TPU v7x, 32 devices: a whole 2x2x4 slice. The times are simulated.
32 devices in a mesh: dp: 8 (over z, y), mp: 4 (over x, core).
Axes of the slice: x: 2, y: 2, z: 4, core: 2. Of those that a mesh axis runs over, the one named last changes fastest.
Arguments:
- hidden_in: float32 [15360, 768], P('dp'), may hold values from -6 to 6
- roi: float32 [3072, 768], P('dp'), may hold values from -135 to 135, as said below
- bn_gain: float32 [768], replicated, may hold values from 0.1 to 1.9
- bn_bias: float32 [768], replicated, may hold values from -3 to 3
- w_qkv: float32 [3, 768, 768], P(None, None, 'mp'), may hold values from -0.21875 to 0.21875
- bias_qv: float32 [2, 768], P(None, 'mp'), may hold values from -3 to 3
- w_out: float32 [768, 768], P('mp'), may hold values from -0.875 to 0.875
- bias_out: float32 [768], replicated, may hold values from -3 to 3
- ln1_gain: float32 [768], replicated, may hold values from 0.1 to 1.9
- ln1_bias: float32 [768], replicated, may hold values from -3 to 3
- w_in: float32 [768, 3072], P(None, 'mp'), may hold values from -0.21875 to 0.21875
- bias_in: float32 [3072], P('mp'), may hold values from -3 to 3
- w_back: float32 [3072, 768], P('mp'), may hold values from -0.109375 to 0.109375
- bias_back: float32 [768], replicated, may hold values from -3 to 3
- ln2_gain: float32 [768], replicated, may hold values from 0.1 to 1.9
- ln2_bias: float32 [768], replicated, may hold values from -3 to 3
- pair_w: float32 [2, 768, 768], P(None, 'mp'), may hold values from -0.15625 to 0.15625
- pair_bias: float32 [768], replicated, may hold values from -3 to 3
- dir_w: float32 [768, 8], replicated, may hold values from -0.21875 to 0.21875
- text_len: int32 [24], P('dp'), may hold values from 30 to 512, as said below
- owner_order: int32 [8, 384], P('dp'), may hold values from 0 to 383, each once within a row
- pair_index: int32 [2048, 2], P('dp'), may hold values from 0 to 384, as said below
- cot_out: float32 [15360, 768], P('dp'), may hold values from -6 to 6
- cot_logits: float32 [2048, 8], P('dp'), may hold values from -6 to 6
Outputs:
- out: float32 [15360, 768], P('dp')
- logits: float32 [2048, 8], P('dp')
- grad_hidden: float32 [15360, 768], P('dp')
- grad_roi: float32 [3072, 768], P('dp')
- grad_bn_gain: float32 [768], replicated
- grad_bn_bias: float32 [768], replicated
- grad_w_qkv: float32 [3, 768, 768], P(None, None, 'mp')
- grad_bias_qv: float32 [2, 768], P(None, 'mp')
- grad_w_out: float32 [768, 768], P('mp')
- grad_bias_out: float32 [768], replicated
- grad_ln1_gain: float32 [768], replicated
- grad_ln1_bias: float32 [768], replicated
- grad_w_in: float32 [768, 3072], P(None, 'mp')
- grad_bias_in: float32 [3072], P('mp')
- grad_w_back: float32 [3072, 768], P('mp')
- grad_bias_back: float32 [768], replicated
- grad_ln2_gain: float32 [768], replicated
- grad_ln2_bias: float32 [768], replicated
- grad_pair_w: float32 [2, 768, 768], P(None, 'mp')
- grad_pair_bias: float32 [768], replicated
- grad_dir_w: float32 [768, 8], replicated
Inputs may be any that keep to these rules, and one draw needn't show every extreme that they name: Document d's first text_len[d] text slots hold text, the rest of its text slots are padding. One document has exactly 512 true text slots, another exactly 30. `owner_order`: row i is a permutation of the 384 segment rows of index i of dp; the k-th entry is sent to owner k // 48. `pair_index`: rows e * 256 to (e + 1) * 256 - 1 are the pair slots of owner e, indexing its received rows; 384 marks an empty slot. Each owner has 192 or more used slots first, then one or more empty ones. `roi`: visual features of the segment rows.
All inputs are finite; a program needn't handle non-finite values.
Results may differ from a plain program's by a relative error of at most 0.0003.
Values sent between devices are 32-bit elements; how exact they have to be, the bound alone decides.
No kernel may reach another device: no remote copies, remote signals or barrier semaphores. Data moves between devices by JAX's collectives and lax.ppermute only.
A program may use at most 192 MiB of HBM per device.

v0:
```python
import jax
import jax.numpy as jnp
from jax import lax
from jax.sharding import PartitionSpec as P

HEAD_DIM = 64
TEXT = 512


EPSILON = 1e-05
NEGATIVE = -1e30
ROOT_HALF = 0.7071067811865476
DENSITY = 0.3989422804014327
HIGHEST = lax.Precision.HIGHEST


def product(operand, other):
    return jnp.dot(operand, other, precision=HIGHEST, preferred_element_type=jnp.float32)


def gelu_slope(preact):
    return (
        0.5 * (1.0 + lax.erf(preact * ROOT_HALF))
        + preact * jnp.exp(-0.5 * preact * preact) * DENSITY
    )


def normalize(values):
    center = values - jnp.mean(values, axis=-1, keepdims=True)
    factor = lax.rsqrt(jnp.mean(center * center, axis=-1, keepdims=True) + EPSILON)
    return (center * factor, factor)


def normalize_back(upstream, normed, factor):
    return factor * (
        upstream
        - jnp.mean(upstream, axis=-1, keepdims=True)
        - normed * jnp.mean(upstream * normed, axis=-1, keepdims=True)
    )


def split_heads(tensor):
    return tensor.reshape(tensor.shape[0], tensor.shape[1] // HEAD_DIM, HEAD_DIM)


def doc_scores(query_rows, key_rows, key_live):
    scores = jnp.einsum(
        "qhd,khd->hqk", split_heads(query_rows), split_heads(key_rows), precision=HIGHEST
    ) * HEAD_DIM ** (-0.5)
    return jnp.where(key_live[None, None, :], scores, NEGATIVE)


def attend(doc_group):
    query_rows, key_rows, value_rows, key_live = doc_group
    scores = doc_scores(query_rows, key_rows, key_live)
    row_top = jnp.max(scores, axis=-1, keepdims=True)
    weights = jnp.exp(scores - row_top)
    weight_sum = jnp.sum(weights, axis=-1, keepdims=True)
    context = jnp.einsum(
        "hqk,khd->qhd", weights / weight_sum, split_heads(value_rows), precision=HIGHEST
    )
    return (context.reshape(query_rows.shape), (row_top + jnp.log(weight_sum))[:, :, 0])


def attend_back(doc_group):
    query_rows, key_rows, value_rows, key_live, logsum, context, upstream = doc_group
    weights = jnp.exp(doc_scores(query_rows, key_rows, key_live) - logsum[:, :, None])
    upstream_heads = split_heads(upstream)
    grad_value = jnp.einsum("hqk,qhd->khd", weights, upstream_heads, precision=HIGHEST)
    grad_weights = jnp.einsum(
        "qhd,khd->hqk", upstream_heads, split_heads(value_rows), precision=HIGHEST
    )
    row_inner = jnp.einsum("qhd,qhd->hq", upstream_heads, split_heads(context), precision=HIGHEST)
    grad_scores = weights * (grad_weights - row_inner[:, :, None]) * HEAD_DIM ** (-0.5)
    grad_query = jnp.einsum("hqk,khd->qhd", grad_scores, split_heads(key_rows), precision=HIGHEST)
    grad_key = jnp.einsum("hqk,qhd->khd", grad_scores, split_heads(query_rows), precision=HIGHEST)
    return (
        grad_query.reshape(query_rows.shape),
        grad_key.reshape(query_rows.shape),
        grad_value.reshape(query_rows.shape),
    )


def per_device(
    hidden_in,
    roi,
    bn_gain,
    bn_bias,
    w_qkv,
    bias_qv,
    w_out,
    bias_out,
    ln1_gain,
    ln1_bias,
    w_in,
    bias_in,
    w_back,
    bias_back,
    ln2_gain,
    ln2_bias,
    pair_w,
    pair_bias,
    dir_w,
    text_len,
    owner_order,
    pair_index,
    cot_out,
    cot_logits,
):
    doc_count = text_len.shape[0]
    slot_count = hidden_in.shape[0] // doc_count
    model_width = hidden_in.shape[1]
    row_count = doc_count * slot_count
    seg_rows = roi.shape[0]
    all_rows = seg_rows * lax.axis_size("dp")
    column_sum = lax.psum(jnp.sum(roi, axis=0), "dp")
    roi_mean = column_sum / all_rows
    roi_center = roi - roi_mean
    roi_var = lax.psum(jnp.sum(roi_center * roi_center, axis=0), "dp") / all_rows
    roi_factor = lax.rsqrt(roi_var + EPSILON)
    roi_normed = roi_center * roi_factor
    roi_out = roi_normed * bn_gain + bn_bias
    doc_blocks = hidden_in.reshape(doc_count, slot_count, model_width)
    doc_blocks = jnp.concatenate(
        [
            doc_blocks[:, :TEXT],
            doc_blocks[:, TEXT:] + roi_out.reshape(doc_count, slot_count - TEXT, model_width),
        ],
        axis=1,
    )
    layer_input = doc_blocks.reshape(row_count, model_width)
    position = jnp.arange(slot_count, dtype=jnp.int32)
    key_live = (position[None, :] < text_len[:, None]) | (position[None, :] >= TEXT)
    query_rows = product(layer_input, w_qkv[0]) + bias_qv[0]
    key_rows = product(layer_input, w_qkv[1])
    value_rows = product(layer_input, w_qkv[2]) + bias_qv[1]
    head_cols = w_qkv.shape[2]

    def per_doc(tensor):
        return tensor.reshape(doc_count, slot_count, tensor.shape[-1])

    context, logsum = lax.map(
        attend, (per_doc(query_rows), per_doc(key_rows), per_doc(value_rows), key_live)
    )
    context = context.reshape(row_count, head_cols)
    attn_part = product(context, w_out)
    first_sum = layer_input + lax.psum(attn_part, "mp") + bias_out
    normed_one, factor_one = normalize(first_sum)
    hidden_one = normed_one * ln1_gain + ln1_bias
    inner_pre = product(hidden_one, w_in) + bias_in
    inner_act = jax.nn.gelu(inner_pre, approximate=False)
    second_sum = hidden_one + lax.psum(product(inner_act, w_back), "mp") + bias_back
    normed_two, factor_two = normalize(second_sum)
    output = normed_two * ln2_gain + ln2_bias
    column_share = model_width // lax.axis_size("mp")
    column_start = lax.axis_index("mp") * column_share
    segments = output.reshape(doc_count, slot_count, model_width)[:, TEXT:].reshape(
        seg_rows, model_width
    )
    seg_columns = lax.dynamic_slice_in_dim(segments, column_start, column_share, 1)
    ordering = owner_order[0]
    received = lax.all_to_all(
        jnp.take(seg_columns, ordering, axis=0), "dp", split_axis=0, concat_axis=0, tiled=True
    )
    candidates = jnp.arange(seg_rows, dtype=jnp.int32)[None, :]
    pick_left = (pair_index[:, 0:1] == candidates).astype(jnp.float32)
    pick_right = (pair_index[:, 1:2] == candidates).astype(jnp.float32)
    left_rows = product(pick_left, received)
    right_rows = product(pick_right, received)
    pair_pre = (
        lax.psum(product(left_rows, pair_w[0]) + product(right_rows, pair_w[1]), "mp") + pair_bias
    )
    pair_act = jax.nn.gelu(pair_pre, approximate=False)
    logits = product(pair_act, dir_w)
    grad_dir_w = product(pair_act.T, cot_logits)
    grad_pair_pre = product(cot_logits, dir_w.T) * gelu_slope(pair_pre)
    grad_pair_bias = jnp.sum(grad_pair_pre, axis=0)
    grad_pair_w = jnp.stack(
        [product(left_rows.T, grad_pair_pre), product(right_rows.T, grad_pair_pre)]
    )
    grad_received = product(pick_left.T, product(grad_pair_pre, pair_w[0].T)) + product(
        pick_right.T, product(grad_pair_pre, pair_w[1].T)
    )
    grad_sent = lax.all_to_all(grad_received, "dp", split_axis=0, concat_axis=0, tiled=True)
    grad_columns = jnp.zeros_like(grad_sent).at[ordering].set(grad_sent)
    grad_segments = lax.all_gather(grad_columns, "mp", axis=1, tiled=True)
    grad_blocks = cot_out.reshape(doc_count, slot_count, model_width)
    grad_output = jnp.concatenate(
        [
            grad_blocks[:, :TEXT],
            grad_blocks[:, TEXT:]
            + grad_segments.reshape(doc_count, slot_count - TEXT, model_width),
        ],
        axis=1,
    ).reshape(row_count, model_width)
    grad_ln2_gain = jnp.sum(grad_output * normed_two, axis=0)
    grad_ln2_bias = jnp.sum(grad_output, axis=0)
    grad_second = normalize_back(grad_output * ln2_gain, normed_two, factor_two)
    grad_bias_back = jnp.sum(grad_second, axis=0)
    grad_w_back = product(inner_act.T, grad_second)
    grad_inner = product(grad_second, w_back.T) * gelu_slope(inner_pre)
    grad_bias_in = jnp.sum(grad_inner, axis=0)
    grad_w_in = product(hidden_one.T, grad_inner)
    grad_hidden_one = grad_second + lax.psum(product(grad_inner, w_in.T), "mp")
    grad_ln1_gain = jnp.sum(grad_hidden_one * normed_one, axis=0)
    grad_ln1_bias = jnp.sum(grad_hidden_one, axis=0)
    grad_first = normalize_back(grad_hidden_one * ln1_gain, normed_one, factor_one)
    grad_bias_out = jnp.sum(grad_first, axis=0)
    grad_w_out = product(context.T, grad_first)
    grad_context = product(grad_first, w_out.T)
    grad_query, grad_key, grad_value = lax.map(
        attend_back,
        (
            per_doc(query_rows),
            per_doc(key_rows),
            per_doc(value_rows),
            key_live,
            logsum,
            per_doc(context),
            per_doc(grad_context),
        ),
    )
    grad_query = grad_query.reshape(row_count, head_cols)
    grad_key = grad_key.reshape(row_count, head_cols)
    grad_value = grad_value.reshape(row_count, head_cols)
    grad_w_qkv = jnp.stack(
        [
            product(layer_input.T, grad_query),
            product(layer_input.T, grad_key),
            product(layer_input.T, grad_value),
        ]
    )
    grad_bias_qv = jnp.stack([jnp.sum(grad_query, axis=0), jnp.sum(grad_value, axis=0)])
    input_part = (
        product(grad_query, w_qkv[0].T)
        + product(grad_key, w_qkv[1].T)
        + product(grad_value, w_qkv[2].T)
    )
    grad_hidden = grad_first + lax.psum(input_part, "mp")
    grad_roi_out = grad_hidden.reshape(doc_count, slot_count, model_width)[:, TEXT:].reshape(
        seg_rows, model_width
    )
    grad_bn_bias, grad_bn_gain = lax.psum(
        (jnp.sum(grad_roi_out, axis=0), jnp.sum(grad_roi_out * roi_normed, axis=0)), "dp"
    )
    grad_roi = (
        bn_gain
        * roi_factor
        * (grad_roi_out - grad_bn_bias / all_rows - roi_normed * grad_bn_gain / all_rows)
    )
    (
        sum_w_qkv,
        sum_bias_qv,
        sum_w_out,
        sum_bias_out,
        sum_ln1_gain,
        sum_ln1_bias,
        sum_w_in,
        sum_bias_in,
        sum_w_back,
        sum_bias_back,
        sum_ln2_gain,
        sum_ln2_bias,
        sum_pair_w,
        sum_pair_bias,
        sum_dir_w,
    ) = lax.psum(
        (
            grad_w_qkv,
            grad_bias_qv,
            grad_w_out,
            grad_bias_out,
            grad_ln1_gain,
            grad_ln1_bias,
            grad_w_in,
            grad_bias_in,
            grad_w_back,
            grad_bias_back,
            grad_ln2_gain,
            grad_ln2_bias,
            grad_pair_w,
            grad_pair_bias,
            grad_dir_w,
        ),
        "dp",
    )
    return (
        output,
        logits,
        grad_hidden,
        grad_roi,
        grad_bn_gain,
        grad_bn_bias,
        sum_w_qkv,
        sum_bias_qv,
        sum_w_out,
        sum_bias_out,
        sum_ln1_gain,
        sum_ln1_bias,
        sum_w_in,
        sum_bias_in,
        sum_w_back,
        sum_bias_back,
        sum_ln2_gain,
        sum_ln2_bias,
        sum_pair_w,
        sum_pair_bias,
        sum_dir_w,
    )


def solution(mesh):
    placed = (
        P("dp", None),
        P("dp", None),
        P(),
        P(),
        P(None, None, "mp"),
        P(None, "mp"),
        P("mp", None),
        P(),
        P(),
        P(),
        P(None, "mp"),
        P("mp"),
        P("mp", None),
        P(),
        P(),
        P(),
        P(None, "mp", None),
        P(),
        P(),
        P("dp"),
        P("dp", None),
        P("dp", None),
        P("dp", None),
        P("dp", None),
    )
    return jax.shard_map(
        per_device,
        mesh=mesh,
        in_specs=placed,
        out_specs=(
            P("dp", None),
            P("dp", None),
            P("dp", None),
            P("dp", None),
            P(),
            P(),
            P(None, None, "mp"),
            P(None, "mp"),
            P("mp", None),
            P(),
            P(),
            P(),
            P(None, "mp"),
            P("mp"),
            P("mp", None),
            P(),
            P(),
            P(),
            P(None, "mp", None),
            P(),
            P(),
        ),
        check_vma=False,
    )
```

profile of v0, /device:TPU:0, one launch (start us, length us, event | category | flops | bytes accessed | tf_op | source)
XLA Modules:
  0.0 1267.7 jit_solution(11706279008520531744)
XLA Ops:
  9.3 23.1 %psum.168 = f32[768]{0:T(1024)S(1)} all-reduce(f32[768]{0:T(1024)S(1)} %reduce_sum.215), channel_id=1, replica_groups=mesh['dp'=8,'mp'=4] {'dp'}, use_global_device_ids=true, to_apply=%region_1.0 | all-reduce | flops 768 | bytes 6144 | tf_op jit(solution)/shard_map/psum | solution.py:116
  33.9 17.1 %psum.169 = f32[768]{0:T(1024)S(1)} all-reduce(f32[768]{0:T(1024)S(1)} %multiply_reduce_fusion.8), channel_id=1, replica_groups=mesh['dp'=8,'mp'=4] {'dp'}, use_global_device_ids=true, to_apply=%region_3.0 | all-reduce | flops 768 | bytes 6144 | tf_op jit(solution)/shard_map/psum | solution.py:119
  58.7 6.9 fusion.62
  65.6 6.9 convolution_add_fusion.1
  72.5 17.7 %convolution_add_fusion = f32[1920,192]{0,1:T(8,128)} fusion(f32[1920,768]{1,0:T(8,128)S(1)} %bitcast.246, f32[192]{0:T(256)S(1)} %bitcast.283, f32[3,768,192]{1,2,0:T(8,128)S(1)} %copy-done.21), kind=kOutput, calls=%fused_computation.92 | convolution fusion | flops 3397754880 | bytes 7963648 | tf_op jit(solution)/shard_map/dot_general | solution.py:18
  90.1 3.6 copy_bitcast_fusion
  95.1 40.8 %while.26 = (s32[]{:T(128)}, f32[3,640,192]{1,2,0:T(8,128)}, f32[3,3,640]{2,1,0:T(4,128)}, f32[3,640,192]{1,2,0:T(8,128)}, pred[3,640]{1,0:T(4,128)(4,1)S(1)}, /...) while((s32[]{:T(128)}, f32[3,640,192]{1,2,0:T(8,128)}, f32[3,3,640]{2,1,0:T(4,128)}, ...), condition=%wide.region_7.8_spmd, body=%wide.region_4.7_spmd.sunk | while | flops 1900951680 | bytes 20712160 | solution.py:142
  96.4 4.7 fusion.191
  103.9 3.9 fusion.193
  109.9 4.7 fusion.191
  117.4 3.9 fusion.193
  123.4 4.7 fusion.191
  130.9 3.9 fusion.193
  138.4 7.7 fusion.105
  146.2 112.0 %all-reduce.9.cloned.1.call-done = f32[1920,768]{1,0:T(8,128)} async-done(((f32[1920,768]{1,0:T(8,128)}), f32[1920,768]{1,0:T(8,128)}) %all-reduce.9.cloned.1.call-update) | async-done | bytes 5898256 | tf_op jit(solution)/shard_map/psum | solution.py:147
  258.2 5.1 fusion.97
  264.3 29.6 %fusion.19 = (f32[1920,768]{1,0:T(8,128)S(1)}, f32[1920,768]{1,0:T(8,128)}) fusion(f32[768]{0:T(1024)S(1)} %copy-done.72, f32[768,768]{1,0:T(8,128)S(1)} %copy-done, f32[768]{0:T(1024)S(1)} %copy-done.60, f32[768]{0:T(1024)S(1)} %copy-done.41, f32[1920]{0:T(1024)S(1)} %add_rsqrt_fusion.1, f32[1920,768]{1,0:T(8,128)S(1)} %get-tuple-element.264, ...), kind=kOutput, calls=%fused_computation.44 | convolution fusion | flops 13691289600 | bytes 20078592 | tf_op jit(solution)/shard_map/dot_general | solution.py:18
  296.4 16.3 %fusion.106 = f32[1920,768]{1,0:T(8,128)} fusion(f32[1920,768]{1,0:T(8,128)S(1)} %get-tuple-element.283, f32[768,768]{1,0:T(8,128)S(1)} %copy-done.70), kind=kOutput, calls=%fused_computation.214 | convolution fusion | flops 13589544960 | bytes 14155776 | tf_op jit(solution)/shard_map/dot_general | solution.py:18
  313.5 112.7 %all-reduce.11.cloned.1.call-done = f32[1920,768]{1,0:T(8,128)} async-done(((f32[1920,768]{1,0:T(8,128)}), f32[1920,768]{1,0:T(8,128)}) %all-reduce.11.cloned.1.call-update) | async-done | bytes 5898256 | tf_op jit(solution)/shard_map/psum | solution.py:152
  426.2 6.0 fusion.96
  440.0 5.5 all-to-all-start
  445.9 11.2 all-to-all-done
  463.0 33.4 %all-reduce.13.cloned.1.call-done = f32[256,768]{1,0:T(8,128)} async-done(((f32[256,768]{1,0:T(8,128)}), f32[256,768]{1,0:T(8,128)}) %all-reduce.13.cloned.1.call-update) | async-done | bytes 786448 | tf_op jit(solution)/shard_map/psum | solution.py:171
  507.4 16.8 %all_to_all.21 = f32[8,48,192]{2,1,0:T(8,128)} all-to-all(f32[8,48,192]{2,1,0:T(8,128)} %bitcast.277), channel_id=1, replica_groups=mesh['dp'=8,'mp'=4] {'dp'}, dimensions={0} | all-to-all | bytes 589824 | tf_op jit(solution)/shard_map/all_to_all | solution.py:184
  524.2 3.0 scatter_custom_fusion
  529.5 5.6 slice_reduce_fusion.1
  535.1 9.8 all-gather.2.cloned.1.call-done
  550.1 3.3 multiply_reduce_fusion.4
  553.4 3.0 fusion.25
  558.9 6.7 fusion.94
  565.6 20.3 %fusion.100 = (f32[768]{0:T(1024)S(1)}, f32[1920,768]{1,0:T(8,128)S(1)}) fusion(f32[1920,768]{1,0:T(8,128)} %get-tuple-element.284, f32[768]{0:T(1024)S(1)} %copy-done.73, f32[1920,768]{1,0:T(8,128)S(1)} %get-tuple-element.257, f32[768,768]{1,0:T(8,128)S(1)} %copy-done.71), kind=kOutput, calls=%fused_computation.208 | convolution fusion | flops 13605764096 | bytes 20060160 | tf_op jit(solution)/shard_map/dot_general | solution.py:18
  588.4 16.2 %fusion.108 = f32[1920,768]{1,0:T(8,128)} fusion(f32[1920,768]{1,0:T(8,128)S(1)} %get-tuple-element.286, f32[768,768]{1,0:T(8,128)S(1)} %copy-done), kind=kOutput, calls=%fused_computation.216 | convolution fusion | flops 13589544960 | bytes 14155776 | tf_op jit(solution)/shard_map/dot_general | solution.py:18
  607.2 110.8 %all-reduce.15.cloned.1.call-done = f32[1920,768]{1,0:T(8,128)} async-done(((f32[1920,768]{1,0:T(8,128)}), f32[1920,768]{1,0:T(8,128)}) %all-reduce.15.cloned.1.call-update) | async-done | bytes 5898256 | tf_op jit(solution)/shard_map/psum | solution.py:204
  718.0 8.3 multiply_reduce_fusion.1
  726.3 4.5 fusion.95
  733.4 5.7 fusion.109
  744.5 92.0 %while.27 = (s32[]{:T(128)}, f32[3,640,192]{1,2,0:T(8,128)}, f32[3,640,192]{1,2,0:T(8,128)}, f32[3,640,192]{1,2,0:T(8,128)}, f32[3,640,192]{1,2,0:T(8,128)}, /*i...) while((s32[]{:T(128)}, f32[3,640,192]{1,2,0:T(8,128)}, ...), condition=%wide.region_22.23_spmd, body=%wide.region_21.22_spmd.sunk | while | flops 4729894912 | bytes 44286608 | solution.py:211
  746.8 4.3 fusion.203
  756.0 5.6 multiply_multiply_fusion.14
  761.6 2.9 fusion.206
  764.5 3.7 fusion.205
  769.2 5.0 fusion.204
  777.3 4.3 fusion.203
  786.5 5.6 multiply_multiply_fusion.14
  795.0 3.7 fusion.205
  799.7 5.0 fusion.204
  807.7 4.3 fusion.203
  817.0 5.6 multiply_multiply_fusion.14
  825.5 3.7 fusion.205
  830.2 5.0 fusion.204
  838.0 6.7 fusion.64
  846.3 5.6 fusion.66
  852.1 8.9 add_add_fusion
  861.0 20.1 %fusion.111 = f32[768,768]{1,0:T(8,128)} fusion(f32[1920,768]{1,0:T(8,128)} %copy-done.74, f32[1920,768]{1,0:T(8,128)} %copy-done.12), kind=kOutput, calls=%fused_computation.219 | convolution fusion | flops 13589544960 | bytes 14155776 | tf_op jit(solution)/shard_map/dot_general | solution.py:18
  881.1 21.8 %fusion.33 = f32[768,768]{1,0:T(8,128)} fusion(f32[1920,768]{1,0:T(8,128)} %copy-done.75, f32[768]{0:T(1024)S(1)} %copy-done.61, f32[768]{0:T(1024)S(1)} %copy-done.42, f32[1920,768]{1,0:T(8,128)} %copy-done.3, f32[1920]{0:T(1024)S(1)} %copy-done.32, f32[1920]{0:T(1024)S(1)} %broadcast_multiply_fusion.5), kind=kOutput, calls=%fused_computation.86 | convolution fusion | flops 13595443200 | bytes 14177280 | tf_op jit(solution)/shard_map/dot_general | solution.py:18
  903.0 4.7 convolution_bitcast_fusion
  907.8 4.7 convolution_bitcast_fusion.1
  912.5 6.4 convolution_bitcast_fusion.2
  920.3 5.1 fusion.110
  931.9 42.5 %all-reduce.17.cloned.1.call-done = f32[1920,768]{1,0:T(8,128)} async-done(((f32[1920,768]{1,0:T(8,128)}), f32[1920,768]{1,0:T(8,128)}) %all-reduce.17.cloned.1.call-update) | async-done | bytes 5898256 | tf_op jit(solution)/shard_map/psum | solution.py:239
  974.5 5.1 add.278
  982.6 41.8 %all-reduce = (f32[768]{0:T(1024)S(1)}, f32[768]{0:T(1024)S(1)}, f32[2,192]{1,0:T(2,128)}, f32[768]{0:T(1024)}, f32[768]{0:T(1024)}, /*index=5*/f32[768]{0:T(102...) all-reduce(f32[768]{0:T(1024)S(1)} %fusion.41, ...), channel_id=1, replica_groups=mesh['dp'=8,'mp'=4] {'dp'}, use_global_device_ids=true, to_apply=%region_27.28 | all-reduce | flops 14208 | bytes 113664 | tf_op jit(solution)/shard_map/psum | solution.py:243
  1025.7 226.1 %all-reduce.19.cloned.1.call-done = (f32[3,768,192]{1,2,0:T(8,128)}, f32[192,768]{1,0:T(8,128)}, f32[768,768]{1,0:T(8,128)}, f32[768,768]{1,0:T(8,128)}, f32[2,192,768]{2,1,0:T(8,128)}) async-done(((f32[3,768,192]{1,2,0:T(8,128)}, f32[192,768]{1,0:T(8,128)}, f32[768,768]{1,0:T(8,128)}, f32[768,768]{1,0:T(8,128)}, f32[2,192,768]{2,1,0:T(8,128)}), (f32[3,768,192]{1,2,0:T(8,128)}, f32[192,768]{1,0:T(8,128)}, ...) | async-done | bytes 8257552 | tf_op jit(solution)/shard_map/psum | solution.py:267
  1251.8 2.9 copy.150
  (309 shorter events, 135.2 us)
Async XLA Ops:
  7.2 257.0 %copy-start = (f32[768,768]{1,0:T(8,128)S(1)}, f32[768,768]{1,0:T(8,128)}, u32[]{:S(2)}) copy-start(f32[768,768]{1,0:T(8,128)} %param.38) | copy-start | bytes 7077892
  7.2 251.0 %all-reduce.9.cloned.1.call-start = ((), (), s32[]{:S(2)}) async-start(), calls=%async_computation.2 | async-start | bytes 11796480 | tf_op jit(solution)/shard_map/psum | solution.py:147
  7.8 45.9 %copy-start.46 = (f32[768]{0:T(1024)S(1)}, f32[768]{0:T(1024)}, u32[]{:S(2)}) copy-start(f32[768]{0:T(1024)} %param.30) | copy-start | bytes 9220
  7.8 46.5 %copy-start.10 = (f32[384,768]{1,0:T(8,128)S(1)}, f32[384,768]{1,0:T(8,128)}, u32[]{:S(2)}) copy-start(f32[384,768]{1,0:T(8,128)} %param.29) | copy-start | bytes 3538948
  32.4 22.1 %copy-start.35 = (f32[768]{0:T(1024)}, f32[768]{0:T(1024)S(1)}, u32[]{:S(2)}) copy-start(f32[768]{0:T(1024)S(1)} %broadcast_multiply_fusion.7) | copy-start | bytes 9220
  51.0 5.8 copy-start.66
  53.7 3.5 copy-start.2
  58.7 13.7 %copy-start.6 = (f32[3,640,768]{2,1,0:T(8,128)}, f32[3,640,768]{2,1,0:T(8,128)S(1)}, u32[]{:S(2)}) copy-start(f32[3,640,768]{2,1,0:T(8,128)S(1)} %pad_maximum_fusion) | copy-start | bytes 17694724
  72.5 21.3 %copy-start.68 = (pred[640]{0:T(1024)(128)(4,1)S(1)}, pred[640]{0:T(1024)(128)(4,1)}, u32[]{:S(2)}) copy-start(pred[640]{0:T(1024)(128)(4,1)} %iota_compare_fusion.7) | copy-start | bytes 1924
  72.5 21.3 %copy-start.69 = (s32[3]{0:T(128)S(1)}, s32[3]{0:T(128)}, u32[]{:S(2)}) copy-start(s32[3]{0:T(128)} %param.47) | copy-start | bytes 40
  95.1 43.4 %copy-start.25 = (f32[192,768]{1,0:T(8,128)S(1)}, f32[192,768]{1,0:T(8,128)}, u32[]{:S(2)}) copy-start(f32[192,768]{1,0:T(8,128)} %param.34) | copy-start | bytes 1769476
  135.8 10.3 copy-start.29
  138.4 119.7 %copy-start.58 = (f32[768]{0:T(1024)S(1)}, f32[768]{0:T(1024)}, u32[]{:S(2)}) copy-start(f32[768]{0:T(1024)} %param.35) | copy-start | bytes 9220
  146.2 280.1 %all-reduce.11.cloned.1.call-start = ((), (), s32[]{:S(2)}) async-start(), calls=%async_computation.3 | async-start | bytes 11796480 | tf_op jit(solution)/shard_map/psum | solution.py:152
  263.3 30.5 %copy-start.3 = (f32[1920,768]{1,0:T(8,128)}, f32[1920,768]{1,0:T(8,128)S(1)}, u32[]{:S(2)}) copy-start(f32[1920,768]{1,0:T(8,128)S(1)} %get-tuple-element.264) | copy-start | bytes 17694724
  264.2 162.0 %copy-start.31 = (f32[1920]{0:T(1024)}, f32[1920]{0:T(1024)S(1)}, u32[]{:S(2)}) copy-start(f32[1920]{0:T(1024)S(1)} %add_rsqrt_fusion.1) | copy-start | bytes 23044
  264.3 32.2 %copy-start.70 = (f32[768,768]{1,0:T(8,128)S(1)}, f32[768,768]{1,0:T(8,128)}, u32[]{:S(2)}) copy-start(f32[768,768]{1,0:T(8,128)} %param.40) | copy-start | bytes 7077892
  312.7 113.6 %copy-start.59 = (f32[768]{0:T(1024)S(1)}, f32[768]{0:T(1024)}, u32[]{:S(2)}) copy-start(f32[768]{0:T(1024)} %param.41) | copy-start | bytes 9220
  313.5 118.7 %copy-start.54 = (s32[384]{0:T(512)}, s32[384]{0:T(512)S(1)}, u32[]{:S(2)}) copy-start(s32[384]{0:T(512)S(1)} %fusion.91) | copy-start | bytes 4612
  434.7 11.1 copy-start.67
  440.0 17.0 %all-to-all-start = ((f32[8,48,192]{2,1,0:T(8,128)}), f32[8,48,192]{2,1,0:T(8,128)S(1)}, u32[]{:S(2)}, u32[]{:S(2)}) async-start(f32[8,48,192]{2,1,0:T(8,128)} %broadcast_select_fusion), calls=%async_computation | async-start | bytes 786432 | tf_op jit(solution)/shard_map/all_to_all | solution.py:162
  445.6 50.8 %all-reduce.13.cloned.1.call-start = ((), (), s32[]{:S(2)}) async-start(), calls=%async_computation.4 | async-start | bytes 1572864 | tf_op jit(solution)/shard_map/psum | solution.py:171
  445.8 11.8 copy-start.52
  445.9 17.1 %copy-start.50 = (s32[256,1]{0,1:T(1,128)}, s32[256,1]{0,1:T(1,128)S(1)}, u32[]{:S(2)}) copy-start(s32[256,1]{0,1:T(1,128)S(1)} %get-tuple-element.279) | copy-start | bytes 3076
  462.9 82.0 %all-gather.2.cloned.1.call-start = ((), (), s32[]{:S(2)}) async-start(), calls=%async_computation.5 | async-start | bytes 1474560 | tf_op jit(solution)/shard_map/all_gather | solution.py:186
  496.4 8.0 copy-start.51
  529.1 188.9 %all-reduce.15.cloned.1.call-start = ((), (), s32[]{:S(2)}) async-start(), calls=%async_computation.6 | async-start | bytes 11796480 | tf_op jit(solution)/shard_map/psum | solution.py:204
  547.5 5.8 slice-start.2
  558.9 6.7 copy-start.71
  558.9 6.7 copy-start.73
  565.6 20.3 %copy-start.12 = (f32[1920,768]{1,0:T(8,128)}, f32[1920,768]{1,0:T(8,128)S(1)}, u32[]{:S(2)}) copy-start(f32[1920,768]{1,0:T(8,128)S(1)} %get-tuple-element.257) | copy-start | bytes 17694724
  604.6 113.4 %copy-start.32 = (f32[1920]{0:T(1024)S(1)}, f32[1920]{0:T(1024)}, u32[]{:S(2)}) copy-start(f32[1920]{0:T(1024)} %copy-done.31) | copy-start | bytes 23044
  604.6 113.4 %copy-start.42 = (f32[768]{0:T(1024)S(1)}, f32[768]{0:T(1024)}, u32[]{:S(2)}) copy-start(f32[768]{0:T(1024)} %param.36) | copy-start | bytes 9220
  604.6 369.8 %all-reduce.17.cloned.1.call-start = ((), (), s32[]{:S(2)}) async-start(), calls=%async_computation.7 | async-start | bytes 11796480 | tf_op jit(solution)/shard_map/psum | solution.py:239
  726.3 7.1 copy-start.26
  739.2 5.3 copy-start.30
  838.0 8.4 copy-start.22
  844.7 7.3 copy-start.13
  861.0 20.2 %copy-start.61 = (f32[768]{0:T(1024)S(1)}, f32[768]{0:T(1024)}, u32[]{:S(2)}) copy-start(f32[768]{0:T(1024)} %param.37) | copy-start | bytes 9220
  861.0 390.8 %all-reduce.19.cloned.1.call-start = ((), (), s32[]{:S(2)}) async-start(), calls=%async_computation.8 | async-start | bytes 16515072 | tf_op jit(solution)/shard_map/psum | solution.py:267
  861.0 41.9 %slice-start = ((s8[4718592]{0:T(1024)(128)(4,1)}), s8[4194304]{0:T(1024)(128)(4,1)S(1)}, s32[]{:S(2)}) async-start(s8[4718592]{0:T(1024)(128)(4,1)} %bitcast.232), calls=%async_computation.9 | async-start | bytes 8388608
  881.1 21.8 %slice-start.1 = ((s8[4718592]{0:T(1024)(128)(4,1)}), s8[524288]{0:T(1024)(128)(4,1)S(1)}, s32[]{:S(2)}) async-start(s8[4718592]{0:T(1024)(128)(4,1)} %bitcast.232), calls=%async_computation.10 | async-start | bytes 1048576
  881.1 21.8 %copy-start.9 = (f32[3,128,768]{2,1,0:T(8,128)S(1)}, f32[3,128,768]{2,1,0:T(8,128)}, u32[]{:S(2)}) copy-start(f32[3,128,768]{2,1,0:T(8,128)} %copy-done.8) | copy-start | bytes 3538948
  881.1 21.8 %copy-start.14 = (f32[3,640,192]{1,2,0:T(8,128)S(1)}, f32[3,640,192]{1,2,0:T(8,128)}, u32[]{:S(2)}) copy-start(f32[3,640,192]{1,2,0:T(8,128)} %get-tuple-element.122) | copy-start | bytes 4423684
  903.0 4.8 copy-start.16
  907.7 12.5 slice-start.4
  912.5 7.8 slice-start.5
  912.5 7.7 copy-start.18
  925.4 4.8 copy-start.45
  925.4 4.8 copy-start.47
  925.4 6.3 copy-start.15
  931.9 50.5 %copy-start.11 = (f32[384,768]{1,0:T(8,128)S(1)}, f32[384,768]{1,0:T(8,128)}, u32[]{:S(2)}) copy-start(f32[384,768]{1,0:T(8,128)} %param.29) | copy-start | bytes 3538948
  931.9 50.5 %copy-start.36 = (f32[768]{0:T(1024)S(1)}, f32[768]{0:T(1024)}, u32[]{:S(2)}) copy-start(f32[768]{0:T(1024)} %copy-done.35) | copy-start | bytes 9220
  931.9 50.5 %copy-start.38 = (f32[768]{0:T(1024)S(1)}, f32[768]{0:T(1024)}, u32[]{:S(2)}) copy-start(f32[768]{0:T(1024)} %copy-done.37) | copy-start | bytes 9220
  931.9 50.7 %copy-start.44 = (f32[768]{0:T(1024)S(1)}, f32[768]{0:T(1024)}, u32[]{:S(2)}) copy-start(f32[768]{0:T(1024)} %get-tuple-element.195) | copy-start | bytes 9220
  931.9 50.7 %copy-start.49 = (f32[768]{0:T(1024)S(1)}, f32[768]{0:T(1024)}, u32[]{:S(2)}) copy-start(f32[768]{0:T(1024)} %get-tuple-element.256) | copy-start | bytes 9220
  931.9 50.7 %copy-start.63 = (f32[768]{0:T(1024)S(1)}, f32[768]{0:T(1024)}, u32[]{:S(2)}) copy-start(f32[768]{0:T(1024)} %get-tuple-element.287) | copy-start | bytes 9220
  931.9 92.5 %copy-start.48 = (f32[768]{0:T(1024)S(1)}, f32[768]{0:T(1024)}, u32[]{:S(2)}) copy-start(f32[768]{0:T(1024)} %get-tuple-element.277) | copy-start | bytes 9220
  1024.4 233.8 %copy-start.64 = (f32[768]{0:T(1024)}, f32[768]{0:T(1024)S(1)}, u32[]{:S(2)}) copy-start(f32[768]{0:T(1024)S(1)} %get-tuple-element.478) | copy-start | bytes 9220
  1024.4 233.8 %copy-start.65 = (f32[768]{0:T(1024)}, f32[768]{0:T(1024)S(1)}, u32[]{:S(2)}) copy-start(f32[768]{0:T(1024)S(1)} %get-tuple-element.477) | copy-start | bytes 9220
  1251.8 5.0 copy-start.24
  1251.8 6.4 copy-start.23
  1254.8 4.9 copy-start.27
  1254.8 5.9 copy-start.1
  (26 other events, 53.5 us)
Sparse Core Ops, SparseCore 0:
  146.3 111.8 all-reduce.8
  312.8 113.3 all-reduce.10
  463.0 33.3 all-reduce.12
  529.2 15.6 all-gather.1
  604.8 113.1 all-reduce.14
  861.1 113.3 all-reduce.16
  981.2 270.5 all-reduce.18
where the time goes:
time: 1280 us; the launch traced here: 1270 us
  waiting for transfers between devices  659 us (51%)
  matrix products  320 us (25%)
  blocking collectives  98.9 us (8%)
  local copies, waits for them, and re-layouts  92.8 us (7%)
  other arithmetic  74.7 us (6%)
  between operations  15.4 us (1%)
    dot_general x31, matrix products, product(): jnp.dot(operand, other, precision=HIGHEST, preferred_element_type=jnp.flo...  229 us
    psum x1, waiting for transfers between devices, per_device(): lax.psum((grad_w_qkv, grad_bias_qv, grad_w_out, grad_bias_out, grad_ln1_g...  226 us
    psum x1, waiting for transfers between devices, per_device(): lax.psum(product(inner_act, w_back), 'mp')  113 us
    psum x1, waiting for transfers between devices, per_device(): first_sum = layer_input + lax.psum(attn_part, 'mp') + bias_out  112 us
    psum x1, waiting for transfers between devices, per_device(): grad_hidden_one = grad_second + lax.psum(product(grad_inner, w_in.T), 'mp')  111 us
    psum x1, waiting for transfers between devices, per_device(): grad_hidden = grad_first + lax.psum(input_part, 'mp')  42.5 us
    psum x1, blocking collectives, per_device(): lax.psum((jnp.sum(grad_roi_out, axis=0), jnp.sum(grad_roi_out * roi_norme...  41.8 us
    psum x1, waiting for transfers between devices, per_device(): lax.psum(product(left_rows, pair_w[0]) + product(right_rows, pair_w[1]),...  33.4 us
  transfers between devices with their start and end apart: 8, of which 8 were waited for; matrix products, arithmetic and copies ran while one was open for 7% of the time, Pallas kernels for 0%

commit v1 on v0

v1 whole, which is shorter than its diff:
```python
import functools

import jax
import jax.numpy as jnp
from jax import lax
from jax.experimental import pallas as pl
from jax.experimental.pallas import tpu as pltpu
from jax.sharding import PartitionSpec as P

HEAD_DIM = 64
TEXT = 512
EPSILON = 1e-05
NEGATIVE = -1e30
ROOT_HALF = 0.7071067811865476
DENSITY = 0.3989422804014327
HIGH = lax.Precision.HIGH
F32 = jnp.float32
BF16 = jnp.bfloat16
VMEM_LIMIT = 56 << 20


def product(operand, other, dims=((1,), (0,))):
    return lax.dot_general(
        operand, other, (dims, ((), ())), precision=HIGH, preferred_element_type=F32
    )


def halves(x):
    hi = x.astype(BF16)
    return hi, (x - hi.astype(F32)).astype(BF16)


def dot(a, b, dims=((1,), (0,))):
    return lax.dot_general(a, b, (dims, ((), ())), preferred_element_type=F32)


ROWS_BY_ROWS = ((1,), (1,))
COLS_BY_COLS = ((0,), (0,))


def dot3(a, b, dims=((1,), (0,))):
    return dot(a[0], b[0], dims) + dot(a[1], b[0], dims) + dot(a[0], b[1], dims)


def gelu_parts(v):
    density = jnp.exp(-0.5 * v * v)
    t = 1.0 / (1.0 + (0.3275911 * ROOT_HALF) * jnp.abs(v))
    poly = t * (
        0.127414796
        + t * (-0.142248368 + t * (0.7107068705 + t * (-0.7265760135 + t * 0.5307027145)))
    )
    tail = poly * density
    phi = jnp.where(v >= 0, 1.0 - tail, tail)
    return v * phi, phi + v * density * DENSITY


def normalize_rows(y):
    center = y - jnp.mean(y, axis=-1, keepdims=True)
    factor = lax.rsqrt(jnp.mean(center * center, axis=-1, keepdims=True) + EPSILON)
    return center * factor, factor


def normalize_rows_back(upstream, normed, factor):
    return factor * (
        upstream
        - jnp.mean(upstream, axis=-1, keepdims=True)
        - normed * jnp.mean(upstream * normed, axis=-1, keepdims=True)
    )


def colsum(x):
    return jnp.sum(x, axis=0, keepdims=True)


def lane_is(rows, width, lane):
    return lax.broadcasted_iota(jnp.int32, (rows, width), 1) == lane


def batch_normed(roi, bn):
    return (roi - bn[0:1]) * bn[1:2]


def split_pieces(pieces, where_hi, where_lo, shift, rows):
    if len(pieces) == 1:
        where_hi[:rows], where_lo[:rows] = halves(pieces[0][...])
    else:
        half = rows // 2
        for piece, place in zip(pieces, (shift, 1 - shift)):
            at = pl.ds(pl.multiple_of(place * half, half), half)
            where_hi[at], where_lo[at] = halves(piece[...])


def attn_fwd_kernel(n_pieces, with_rows, segs, heads, *refs):
    place, lens, hid, roi, bn, bias = refs[:6]
    pieces = refs[6 : 6 + n_pieces]
    refs = refs[6 + n_pieces :]
    qkv, lse, cm_seg, cm_txt, ct_seg, ct_txt = refs[:6]
    refs = refs[6:]
    if with_rows:
        xm_seg, xm_txt = refs[:2]
        refs = refs[2:]
    w_hi, w_lo, x_seg, ctx = refs
    doc = pl.program_id(0)
    c = place[0]
    width = heads * HEAD_DIM
    slots = TEXT + segs

    @pl.when(doc == 0)
    def _():
        split_pieces(pieces, w_hi, w_lo, place[1], w_hi.shape[0])

    x_seg[...] = hid[TEXT:, :] + batch_normed(roi[...], bn) * bn[2:3] + bn[3:4]
    w = (w_hi[...], w_lo[...])
    half = TEXT // 2
    for start in (0, half):
        qkv[start : start + half, :] = dot3(halves(hid[start : start + half, :]), w) + bias[0:1]
    qkv[TEXT:, :] = dot3(halves(x_seg[...]), w) + bias[0:1]

    position = lax.broadcasted_iota(jnp.int32, (slots, HEAD_DIM), 0)
    first = lane_is(slots, HEAD_DIM, 0)
    dead = (position >= lens[doc]) & (position < TEXT)
    key_extra = jnp.where(first & dead, NEGATIVE, 0.0).astype(BF16)
    ones = jnp.where(first, 1.0, 0.0).astype(BF16)
    step = 128
    for h in range(heads):
        at = h * HEAD_DIM
        q_hi, q_lo = halves(qkv[:, at : at + HEAD_DIM] * HEAD_DIM**-0.5)
        k_hi, k_lo = halves(qkv[:, width + at : width + at + HEAD_DIM])
        v_hi, v_lo = halves(qkv[:, 2 * width + at : 2 * width + at + HEAD_DIM])
        q_pack = jnp.concatenate([q_hi, q_lo, q_hi, ones], axis=1)
        k_pack = jnp.concatenate([k_hi, k_hi, k_lo, key_extra], axis=1)
        v_pack = jnp.concatenate([v_hi, v_lo, ones, jnp.zeros_like(ones)], axis=1)
        for start in range(0, slots, step):
            rows = slice(start, start + step)
            scores = dot(q_pack[rows], k_pack, ROWS_BY_ROWS)
            top = jnp.max(scores, axis=-1, keepdims=True)
            p_hi, p_lo = halves(jnp.exp(scores - top))
            mixed = dot(p_hi, v_pack) + dot(p_lo, v_pack)
            total = mixed[:, 2 * HEAD_DIM : 2 * HEAD_DIM + 1]
            ctx[rows, at : at + HEAD_DIM] = (
                mixed[:, :HEAD_DIM] + mixed[:, HEAD_DIM : 2 * HEAD_DIM]
            ) / total
            logsum = top + jnp.log(total)
            if h == 0:
                lse[rows, :] = jnp.broadcast_to(logsum, (step, 128))
            else:
                lse[rows, :] = jnp.where(lane_is(step, 128, h), logsum, lse[rows, :])
    half_seg = segs // 2
    for seg, txt, side in ((cm_seg, cm_txt, c), (ct_seg, ct_txt, 1 - c)):
        seg[...] = ctx[pl.ds(pl.multiple_of(TEXT + side * half_seg, half_seg), half_seg), :]
        txt[...] = ctx[pl.ds(pl.multiple_of(side * half, half), half), :]
    if with_rows:
        xm_seg[...] = x_seg[pl.ds(pl.multiple_of(c * half_seg, half_seg), half_seg), :]
        xm_txt[...] = hid[pl.ds(pl.multiple_of(c * half, half), half), :]


def smem():
    return pl.BlockSpec(memory_space=pltpu.SMEM)


def whole(shape):
    return pl.BlockSpec(shape, lambda *_: (0,) * len(shape))


def attn_fwd(place, lens, hidden, roi, bn, bias, pieces, with_rows):
    docs = lens.shape[0]
    slots, width = hidden.shape[0] // docs, hidden.shape[1]
    segs = slots - TEXT
    cols = pieces[0].shape[1]
    part = cols // 3
    heads = part // HEAD_DIM
    out_rows = [
        (slots, cols),
        (slots, 128),
        (segs // 2, part),
        (TEXT // 2, part),
        (segs // 2, part),
        (TEXT // 2, part),
    ]
    if with_rows:
        out_rows += [(segs // 2, width), (TEXT // 2, width)]
    by_doc = lambda shape: pl.BlockSpec(shape, lambda d: (d, 0))
    return pl.pallas_call(
        functools.partial(attn_fwd_kernel, len(pieces), with_rows, segs, heads),
        grid=(docs,),
        in_specs=[smem(), smem(), by_doc((slots, width)), by_doc((segs, width)), whole(bn.shape), whole(bias.shape)]
        + [whole(p.shape) for p in pieces],
        out_specs=[by_doc(s) for s in out_rows],
        out_shape=[jax.ShapeDtypeStruct((docs * s[0], s[1]), F32) for s in out_rows],
        scratch_shapes=[
            pltpu.VMEM((width, cols), BF16),
            pltpu.VMEM((width, cols), BF16),
            pltpu.VMEM((segs, width), F32),
            pltpu.VMEM((slots, part), F32),
        ],
        compiler_params=pltpu.CompilerParams(vmem_limit_bytes=VMEM_LIMIT),
        name="attn_fwd",
    )(place, lens, hidden, roi, bn, bias, *pieces)


def attn_bwd_kernel(segs, heads, doc, *refs):
    (place, lens, hid, roi, bn) = refs[:5]
    pieces = (refs[5:6], refs[6:8])
    qkvs, lses = refs[8:10], refs[10:12]
    ctxs = (refs[12:16], refs[16:20])
    gcm_seg, gcm_txt, gct_seg, gct_txt = refs[20:24]
    w_sum, b_sum = refs[24:26]
    gx, w_out, b_out = refs[26:29]
    w_hi, w_lo, o_all, g_all, gq, x_all = refs[29:]
    c = place[0]
    width = heads * HEAD_DIM
    slots = TEXT + segs
    half, half_seg = TEXT // 2, segs // 2
    model = hid.shape[1]
    for s in range(2):
        at = s * model
        split_pieces(
            pieces[s], w_hi.at[at : at + model], w_lo.at[at : at + model], place[1], model
        )

    def place_rows(dst, lanes, seg, txt, side):
        dst[pl.ds(pl.multiple_of(TEXT + side * half_seg, half_seg), half_seg), lanes] = seg
        dst[pl.ds(pl.multiple_of(side * half, half), half), lanes] = txt

    for s in range(2):
        lanes = slice(s * width, (s + 1) * width)
        seg_m, txt_m, seg_t, txt_t = ctxs[s]
        place_rows(o_all.at[s], slice(0, width), seg_m[...], txt_m[...], c)
        place_rows(o_all.at[s], slice(0, width), seg_t[...], txt_t[...], 1 - c)
        place_rows(g_all.at[s], slice(0, width), gcm_seg[:, lanes], gcm_txt[:, lanes], c)
        place_rows(g_all.at[s], slice(0, width), gct_seg[:, lanes], gct_txt[:, lanes], 1 - c)
    x_all[:TEXT, :] = hid[:TEXT, :]
    x_all[TEXT:, :] = hid[TEXT:, :] + batch_normed(roi[...], bn) * bn[2:3] + bn[3:4]

    position = lax.broadcasted_iota(jnp.int32, (slots, HEAD_DIM), 0)
    lane = lax.broadcasted_iota(jnp.int32, (slots, HEAD_DIM), 1)
    dead = (position >= lens[doc]) & (position < TEXT)
    key_extra = jnp.where(
        lane == 3, jnp.where(dead, NEGATIVE, 0.0), jnp.where(lane < 3, 1.0, 0.0)
    ).astype(BF16)
    val_extra = jnp.where(lane < 3, 1.0, 0.0).astype(BF16)

    def column_extra(col, last):
        hi = (-col).astype(BF16)
        rest = -col - hi.astype(F32)
        mid = rest.astype(BF16)
        low = (rest - mid.astype(F32)).astype(BF16)
        return jnp.where(
            lane == 0,
            hi.astype(F32),
            jnp.where(
                lane == 1,
                mid.astype(F32),
                jnp.where(lane == 2, low.astype(F32), jnp.where(lane == 3, last, 0.0)),
            ),
        ).astype(BF16)

    step = 128
    scale = HEAD_DIM**-0.5
    for s in range(2):
        qkv = qkvs[s]
        for h in range(heads):
            at = h * HEAD_DIM
            q_hi, q_lo = halves(qkv[:, at : at + HEAD_DIM] * scale)
            k_hi, k_lo = halves(qkv[:, width + at : width + at + HEAD_DIM])
            v_hi, v_lo = halves(qkv[:, 2 * width + at : 2 * width + at + HEAD_DIM])
            g = g_all[s, :, at : at + HEAD_DIM]
            g_hi, g_lo = halves(g)
            inner = jnp.sum(g * o_all[s, :, at : at + HEAD_DIM], axis=-1, keepdims=True)
            q_pack = jnp.concatenate(
                [q_hi, q_lo, q_hi, column_extra(lses[s][:, h : h + 1], 1.0)], axis=1
            )
            k_pack = jnp.concatenate([k_hi, k_hi, k_lo, key_extra], axis=1)
            g_pack = jnp.concatenate([g_hi, g_lo, g_hi, column_extra(inner, 0.0)], axis=1)
            v_pack = jnp.concatenate([v_hi, v_hi, v_lo, val_extra], axis=1)
            q_two = jnp.concatenate([q_hi, q_lo], axis=1)
            k_two = jnp.concatenate([k_hi, k_lo], axis=1)
            g_two = jnp.concatenate([g_hi, g_lo], axis=1)
            grad_q = jnp.zeros((slots, 2 * HEAD_DIM), F32)
            for start in range(0, slots, step):
                rows = slice(start, start + step)
                weights = jnp.exp(dot(k_pack[rows], q_pack, ROWS_BY_ROWS))
                grads = weights * dot(v_pack[rows], g_pack, ROWS_BY_ROWS)
                w_two = halves(weights)
                s_two = halves(grads)
                grad_v = dot(w_two[0], g_two) + dot(w_two[1], g_two)
                grad_k = dot(s_two[0], q_two) + dot(s_two[1], q_two)
                gq[rows, width + at : width + at + HEAD_DIM] = (
                    grad_k[:, :HEAD_DIM] + grad_k[:, HEAD_DIM:]
                )
                gq[rows, 2 * width + at : 2 * width + at + HEAD_DIM] = (
                    grad_v[:, :HEAD_DIM] + grad_v[:, HEAD_DIM:]
                )
                grad_q = (
                    grad_q
                    + dot(s_two[0], k_two[rows], COLS_BY_COLS)
                    + dot(s_two[1], k_two[rows], COLS_BY_COLS)
                )
            gq[:, at : at + HEAD_DIM] = (grad_q[:, :HEAD_DIM] + grad_q[:, HEAD_DIM:]) * scale
        w = (w_hi[s * model : (s + 1) * model, :], w_lo[s * model : (s + 1) * model, :])
        for start in range(0, slots, 2 * step):
            rows = slice(start, min(slots, start + 2 * step))
            part = dot3(halves(gq[rows, :]), w, ROWS_BY_ROWS)
            if s == 0:
                gx[rows, :] = part
            else:
                gx[rows, :] += part
        if s == 0:
            b_out[...] = b_sum[...] + colsum(gq[...])
            w_out[...] = w_sum[...] + dot3(halves(gq[...]), halves(x_all[...]), COLS_BY_COLS)


def attn_bwd(doc, place, lens, hidden, roi, bn, own, other, qkvs, lses, ctxs, grads, w_sum, b_sum):
    docs = lens.shape[0]
    slots, width = hidden.shape[0] // docs, hidden.shape[1]
    segs = slots - TEXT
    cols = own[0].shape[1]
    part = cols // 3
    heads = part // HEAD_DIM
    by_doc = lambda rows, lanes: pl.BlockSpec((rows, lanes), lambda i: (doc, 0))
    half, half_seg = TEXT // 2, segs // 2
    return pl.pallas_call(
        functools.partial(attn_bwd_kernel, segs, heads, doc),
        grid=(1,),
        in_specs=[smem(), smem(), by_doc(slots, width), by_doc(segs, width), whole(bn.shape)]
        + [whole(p.shape) for p in (*own, *other)]
        + [by_doc(slots, cols)] * 2
        + [by_doc(slots, 128)] * 2
        + [by_doc(half_seg, part), by_doc(half, part)] * 4
        + [by_doc(half_seg, 2 * part), by_doc(half, 2 * part)] * 2
        + [whole((cols, width)), whole((1, cols))],
        out_specs=[whole((slots, width)), whole((cols, width)), whole((1, cols))],
        out_shape=[
            jax.ShapeDtypeStruct((slots, width), F32),
            jax.ShapeDtypeStruct((cols, width), F32),
            jax.ShapeDtypeStruct((1, cols), F32),
        ],
        scratch_shapes=[
            pltpu.VMEM((2 * width, cols), BF16),
            pltpu.VMEM((2 * width, cols), BF16),
            pltpu.VMEM((2, slots, part), F32),
            pltpu.VMEM((2, slots, part), F32),
            pltpu.VMEM((slots, cols), F32),
            pltpu.VMEM((slots, width), F32),
        ],
        compiler_params=pltpu.CompilerParams(vmem_limit_bytes=VMEM_LIMIT),
        name="attn_bwd",
    )(place, lens, hidden, roi, bn, *own, *other, *qkvs, *lses, *ctxs[0], *ctxs[1], *grads, w_sum, b_sum)


BIAS_OUT, LN1_GAIN, LN1_BIAS, BIAS_BACK, LN2_GAIN, LN2_BIAS = range(6)
PIECE_SHARDS = (0, 1, 2, 2, 3, 3)


def row_chunks(rows, most=256):
    step = min(rows, most)
    return [slice(start, start + step) for start in range(0, rows, step)]


def piece_place(i, rows, shift):
    if i < 2:
        return 0
    half = rows // 2
    return pl.multiple_of((shift if i % 2 == 0 else 1 - shift) * half, half)


def ffn_fwd_kernel(split, *refs):
    place = refs[0]
    ctx = refs[1:5]
    xres, vec, bias_in = refs[5:8]
    refs = refs[8:]
    if split:
        wo_pieces, wi_pieces, wb_pieces = refs[:6], refs[6:12], refs[12:18]
        refs = refs[18:]
    else:
        wo_ref, wt_ref = refs[:2]
        refs = refs[2:]
    out, n1, f1, n2, f2, act, slope = refs[:7]
    refs = refs[7:]
    if split:
        wo_ref, wt_ref = refs[:2]
        refs = refs[2:]
        wbuf, sems = refs[-2:]
        refs = refs[:-2]
    h_hi, h_lo, acc = refs
    t = pl.program_id(0)
    tiles = 4
    rows = xres.shape[0]
    head_rows = ctx[0].shape[1]
    width = xres.shape[1]

    if split:
        shift = place[1]

        def copies(tile):
            found = []
            for i in range(6):
                if PIECE_SHARDS[i] != tile:
                    continue
                for k, pieces in enumerate((wi_pieces, wb_pieces)):
                    ref = pieces[i]
                    at = piece_place(i, width, shift)
                    found.append(
                        pltpu.make_async_copy(
                            ref, wbuf.at[k, pl.ds(at, ref.shape[0]), :], sems.at[len(found)]
                        )
                    )
            return found

        @pl.when(t == 0)
        def _():
            for copy in copies(0):
                copy.start()
            for i in range(6):
                at = PIECE_SHARDS[i] * head_rows + piece_place(i, head_rows, shift)
                where = pl.ds(at, wo_pieces[i].shape[0])
                wo_ref[0, where, :], wo_ref[1, where, :] = halves(wo_pieces[i][...])

        for tile in range(tiles):

            @pl.when(t == tile)
            def _():
                for copy in copies(tile):
                    copy.wait()

        wt_ref[0, 0], wt_ref[0, 1] = halves(wbuf[0])
        wt_ref[0, 2], wt_ref[0, 3] = halves(wbuf[1])
        for tile in range(tiles - 1):

            @pl.when(t == tile)
            def _():
                for copy in copies(tile + 1):
                    copy.start()

    @pl.when(t == 0)
    def _():
        for r in row_chunks(rows):
            y = xres[r, :] + vec[BIAS_OUT : BIAS_OUT + 1]
            for s in range(4):
                at = slice(s * head_rows, (s + 1) * head_rows)
                y = y + dot3(halves(ctx[s][r, :]), (wo_ref[0, at, :], wo_ref[1, at, :]))
            normed, factor = normalize_rows(y)
            n1[r, :] = normed
            f1[r, :] = jnp.broadcast_to(factor, (factor.shape[0], 128))
            h = normed * vec[LN1_GAIN : LN1_GAIN + 1] + vec[LN1_BIAS : LN1_BIAS + 1]
            h_hi[r, :], h_lo[r, :] = halves(h)
            acc[r, :] = h + vec[BIAS_BACK : BIAS_BACK + 1]

    w_in = (wt_ref[0, 0], wt_ref[0, 1])
    w_back = (wt_ref[0, 2], wt_ref[0, 3])
    bias = bias_in[pl.ds(t, 1), :]
    for r in row_chunks(rows):
        pre = dot3((h_hi[r, :], h_lo[r, :]), w_in) + bias
        value, rise = gelu_parts(pre)
        slope[0, r, :] = rise

        @pl.when(t < 2)
        def _():
            act[0, r, :] = value

        acc[r, :] += dot3(halves(value), w_back)

    @pl.when(t == tiles - 1)
    def _():
        for r in row_chunks(rows):
            normed, factor = normalize_rows(acc[r, :])
            n2[r, :] = normed
            f2[r, :] = jnp.broadcast_to(factor, (factor.shape[0], 128))
            out[r, :] = normed * vec[LN2_GAIN : LN2_GAIN + 1] + vec[LN2_BIAS : LN2_BIAS + 1]


def ffn_fwd(place, ctx, xres, vec, bias_in, wo, wt=None):
    rows, width = xres.shape
    split = wt is None
    f32 = lambda *shape: jax.ShapeDtypeStruct(shape, F32)
    out_shape = [
        f32(rows, width),
        f32(rows, width),
        f32(rows, 128),
        f32(rows, width),
        f32(rows, 128),
        f32(2, rows, width),
        f32(4, rows, width),
    ]
    tile = lambda shape, clip=3: pl.BlockSpec(
        shape, lambda t: (jnp.minimum(t, clip),) + (0,) * (len(shape) - 1)
    )
    out_specs = [whole(s.shape) for s in out_shape[:5]] + [
        tile((1, rows, width), 1),
        tile((1, rows, width)),
    ]
    in_specs = [smem()] + [whole(a.shape) for a in (*ctx, xres, vec, bias_in)]
    scratch = [
        pltpu.VMEM((rows, width), BF16),
        pltpu.VMEM((rows, width), BF16),
        pltpu.VMEM((rows, width), F32),
    ]
    if split:
        w_out, w_in, w_back = wo
        weights = (*w_out, *w_in, *w_back)
        in_specs += [whole(w.shape) for w in w_out] + [pl.BlockSpec(memory_space=pl.ANY)] * 12
        inner = w_in[0].shape[1]
        out_shape += [
            jax.ShapeDtypeStruct((2, width, width), BF16),
            jax.ShapeDtypeStruct((4, 4, width, inner), BF16),
        ]
        out_specs += [whole((2, width, width)), tile((1, 4, width, inner))]
        scratch += [pltpu.VMEM((2, width, inner), F32), pltpu.SemaphoreType.DMA((4,))]
    else:
        weights = (wo, wt)
        in_specs += [whole(wo.shape), tile((1, *wt.shape[1:]))]
    return pl.pallas_call(
        functools.partial(ffn_fwd_kernel, split),
        grid=(4,),
        in_specs=in_specs,
        out_specs=out_specs,
        out_shape=out_shape,
        scratch_shapes=scratch,
        compiler_params=pltpu.CompilerParams(vmem_limit_bytes=VMEM_LIMIT),
        name="ffn_fwd",
    )(place, *ctx, xres, vec, bias_in, *weights)


def ffn_bwd_kernel(*refs):
    gout, n1, f1, n2, f2, slope, vec, wo_ref, wt_ref = refs[:9]
    gs, gi, gf, gcm, gct, sums = refs[9:15]
    s_hi, s_lo, acc = refs[15:]
    t = pl.program_id(0)
    rows = gout.shape[0]
    head_rows = wo_ref.shape[1] // 4
    chunks = row_chunks(rows)

    @pl.when(t == 0)
    def _():
        sums[...] = jnp.zeros_like(sums)
        for r in chunks:
            g = gout[r, :]
            sums[0:1, :] += colsum(g * n2[r, :])
            sums[1:2, :] += colsum(g)
            back = normalize_rows_back(g * vec[LN2_GAIN : LN2_GAIN + 1], n2[r, :], f2[r, 0:1])
            sums[2:3, :] += colsum(back)
            gs[r, :] = back
            acc[r, :] = back
            s_hi[r, :], s_lo[r, :] = halves(back)

    w_in = (wt_ref[0, 0], wt_ref[0, 1])
    w_back = (wt_ref[0, 2], wt_ref[0, 3])
    for r in chunks:
        grad_inner = dot3((s_hi[r, :], s_lo[r, :]), w_back, ROWS_BY_ROWS) * slope[0, r, :]

        @pl.when(t < 2)
        def _():
            gi[0, r, :] = grad_inner
            sums[pl.ds(6 + t, 1), :] += colsum(grad_inner)

        acc[r, :] += dot3(halves(grad_inner), w_in, ROWS_BY_ROWS)

    @pl.when(t == 3)
    def _():
        for r in chunks:
            g = acc[r, :]
            sums[3:4, :] += colsum(g * n1[r, :])
            sums[4:5, :] += colsum(g)
            back = normalize_rows_back(g * vec[LN1_GAIN : LN1_GAIN + 1], n1[r, :], f1[r, 0:1])
            sums[5:6, :] += colsum(back)
            gf[r, :] = back
            two = halves(back)
            for s, (dst, lanes) in enumerate(
                (
                    (gcm, slice(0, head_rows)),
                    (gct, slice(0, head_rows)),
                    (gcm, slice(head_rows, 2 * head_rows)),
                    (gct, slice(head_rows, 2 * head_rows)),
                )
            ):
                at = slice(s * head_rows, (s + 1) * head_rows)
                dst[r, lanes] = dot3(two, (wo_ref[0, at, :], wo_ref[1, at, :]), ROWS_BY_ROWS)


def ffn_bwd(gout, n1, f1, n2, f2, slope, vec, wo, wt):
    rows, width = gout.shape
    f32 = lambda *shape: jax.ShapeDtypeStruct(shape, F32)
    tile = lambda shape, clip=3: pl.BlockSpec(
        shape, lambda t: (jnp.minimum(t, clip),) + (0,) * (len(shape) - 1)
    )
    return pl.pallas_call(
        ffn_bwd_kernel,
        grid=(4,),
        in_specs=[whole(a.shape) for a in (gout, n1, f1, n2, f2)]
        + [tile((1, rows, width)), whole(vec.shape), whole(wo.shape), tile((1, *wt.shape[1:]))],
        out_specs=[
            whole((rows, width)),
            tile((1, rows, width), 1),
            whole((rows, width)),
            whole((rows, width // 2)),
            whole((rows, width // 2)),
            whole((8, width)),
        ],
        out_shape=[
            f32(rows, width),
            f32(2, rows, width),
            f32(rows, width),
            f32(rows, width // 2),
            f32(rows, width // 2),
            f32(8, width),
        ],
        scratch_shapes=[
            pltpu.VMEM((rows, width), BF16),
            pltpu.VMEM((rows, width), BF16),
            pltpu.VMEM((rows, width), F32),
        ],
        compiler_params=pltpu.CompilerParams(vmem_limit_bytes=VMEM_LIMIT),
        name="ffn_bwd",
    )(gout, n1, f1, n2, f2, slope, vec, wo, wt)


def join_kernel(segs, place, ms, mt, ts, tt, out):
    c = place[0]
    half, half_seg = TEXT // 2, segs // 2
    for seg, txt, side in ((ms, mt, c), (ts, tt, 1 - c)):
        out[pl.ds(pl.multiple_of(TEXT + side * half_seg, half_seg), half_seg), :] = seg[...]
        out[pl.ds(pl.multiple_of(side * half, half), half), :] = txt[...]


def join_rows(docs, segs, place, ms, mt, ts, tt):
    width = ms.shape[1]
    slots = TEXT + segs
    by_doc = lambda rows: pl.BlockSpec((rows, width), lambda d: (d, 0))
    return pl.pallas_call(
        functools.partial(join_kernel, segs),
        grid=(docs,),
        in_specs=[smem()] + [by_doc(segs // 2), by_doc(TEXT // 2)] * 2,
        out_specs=by_doc(slots),
        out_shape=jax.ShapeDtypeStruct((docs * slots, width), F32),
        name="join_rows",
    )(place, ms, mt, ts, tt)


def final_kernel(segs, n_parts, *refs):
    place = refs[0]
    mine, theirs = refs[1 : 1 + n_parts], refs[1 + n_parts : 1 + 2 * n_parts]
    ms, mt, ts, tt, roi, bn, out, sums = refs[1 + 2 * n_parts :]
    d = pl.program_id(0)
    join_kernel(segs, place, ms, mt, ts, tt, out)
    for i in range(n_parts):

        @pl.when(d == i)
        def _():
            out[...] += mine[i][...] + theirs[i][...]

    @pl.when(d == 0)
    def _():
        sums[...] = jnp.zeros_like(sums)

    g = out[TEXT:, :]
    sums[0:1, :] += colsum(g)
    sums[1:2, :] += colsum(g * batch_normed(roi[...], bn))


def final_rows(docs, segs, place, mine, theirs, ms, mt, ts, tt, roi, bn):
    width = ms.shape[1]
    slots = TEXT + segs
    by_doc = lambda rows: pl.BlockSpec((rows, width), lambda d: (d, 0))
    return pl.pallas_call(
        functools.partial(final_kernel, segs, len(mine)),
        grid=(docs,),
        in_specs=[smem()]
        + [whole((slots, width))] * (2 * len(mine))
        + [by_doc(segs // 2), by_doc(TEXT // 2)] * 2
        + [by_doc(segs), whole(bn.shape)],
        out_specs=[by_doc(slots), whole((8, width))],
        out_shape=[
            jax.ShapeDtypeStruct((docs * slots, width), F32),
            jax.ShapeDtypeStruct((8, width), F32),
        ],
        compiler_params=pltpu.CompilerParams(vmem_limit_bytes=VMEM_LIMIT),
        name="final_rows",
    )(place, *mine, *theirs, ms, mt, ts, tt, roi, bn)


def swap(x, axis, bit):
    n = lax.axis_size(axis)
    return lax.ppermute(x, axis, [(i, i ^ bit) for i in range(n)])


def butterfly(x, merge):
    bit = 1
    while bit < lax.axis_size("dp"):
        x = merge(x, swap(x, "dp", bit), bit)
        bit *= 2
    return x


def ring_sum(parts):
    n = lax.axis_size("dp")
    order = list(range(0, n, 2)) + list(range(n - 1, 0, -2))
    me = lax.axis_index("dp")
    place = jnp.where(me % 2 == 0, me // 2, n - 1 - me // 2)

    def chunk(i, k):
        sign = 1 if i % 2 == 0 else -1
        size = parts[i].shape[0] // n
        return ((sign * place - k) % n) * size, size

    def take(i, k):
        at, size = chunk(i, k)
        return lax.dynamic_slice_in_dim(parts[i], at, size, 0)

    def send(i, x):
        sign = 1 if i % 2 == 0 else -1
        return lax.ppermute(x, "dp", [(order[k], order[(k + sign) % n]) for k in range(n)])

    count = len(parts)
    held = [take(i, 0) for i in range(count)]
    for step in range(1, n):
        held = [send(i, held[i]) + take(i, step) for i in range(count)]
    total = []
    for i in range(count):
        total.append(lax.dynamic_update_slice_in_dim(parts[i], held[i], chunk(i, -1)[0], 0))
    for step in range(n - 1):
        held = [send(i, held[i]) for i in range(count)]
        for i in range(count):
            total[i] = lax.dynamic_update_slice_in_dim(total[i], held[i], chunk(i, step)[0], 0)
    return total


def per_device(
    hidden_in,
    roi,
    bn_gain,
    bn_bias,
    w_qkv,
    bias_qv,
    w_out,
    bias_out,
    ln1_gain,
    ln1_bias,
    w_in,
    bias_in,
    w_back,
    bias_back,
    ln2_gain,
    ln2_bias,
    pair_w,
    pair_bias,
    dir_w,
    text_len,
    owner_order,
    pair_index,
    cot_out,
    cot_logits,
):
    docs = text_len.shape[0]
    slots = hidden_in.shape[0] // docs
    width = hidden_in.shape[1]
    segs = slots - TEXT
    seg_rows = roi.shape[0]
    n_dp = lax.axis_size("dp")
    all_rows = seg_rows * n_dp
    half, half_seg = TEXT // 2, segs // 2
    m = lax.axis_index("mp")
    c = m % 2
    shift = lax.axis_index("dp") % 2
    place = jnp.stack([c, shift]).astype(jnp.int32)
    part = w_qkv.shape[2]

    def fetch(w):
        size = w.shape[0] // 2
        near = swap(lax.dynamic_slice_in_dim(w, shift * size, size, 0), "mp", 2)
        return near, swap(near, "dp", 1)

    qkv_own = jnp.transpose(w_qkv, (1, 0, 2)).reshape(width, 3 * part)
    qkv_other = fetch(qkv_own)
    small = jnp.zeros((8, width), F32)
    small = small.at[0].set(bias_in)
    small = small.at[1, :part].set(bias_qv[0]).at[2, :part].set(bias_qv[1])

    mean = jnp.mean(roi, axis=0)
    stats = jnp.stack([mean, jnp.sum((roi - mean) ** 2, axis=0)])

    def merge(one, two, count):
        gap = one[0] - two[0]
        return jnp.stack(
            [
                0.5 * (one[0] + two[0]),
                one[1] + two[1] + gap * gap * (0.5 * seg_rows * count),
            ]
        )

    stats = butterfly(stats, merge)
    roi_factor = lax.rsqrt(stats[1] / all_rows + EPSILON)
    bn = jnp.zeros((8, width), F32)
    bn = bn.at[0].set(stats[0]).at[1].set(roi_factor).at[2].set(bn_gain).at[3].set(bn_bias)

    small_x = swap(small, "mp", 2)
    out_own = w_out
    out_x = fetch(w_out)
    in_x = fetch(w_in)
    back_x = fetch(w_back)

    def four(own, far):
        return (own, swap(own, "mp", 1), *far, *(swap(f, "mp", 1) for f in far))

    def qkv_bias(rows):
        return jnp.concatenate([rows[1:2, :part], jnp.zeros((1, part), F32), rows[2:3, :part]], axis=1)

    qkv_a, lse_a, cm_seg_a, cm_txt_a, ct_seg_a, ct_txt_a, x_seg, x_txt = attn_fwd(
        place, text_len, hidden_in, roi, bn, qkv_bias(small), (qkv_own,), True
    )
    qkv_b, lse_b, cm_seg_b, cm_txt_b, ct_seg_b, ct_txt_b = attn_fwd(
        place, text_len, hidden_in, roi, bn, qkv_bias(small_x), qkv_other, False
    )
    from_sib = lambda x: swap(x, "mp", 1)
    ctx_seg = (cm_seg_a, from_sib(ct_seg_a), cm_seg_b, from_sib(ct_seg_b))
    ctx_txt = (cm_txt_a, from_sib(ct_txt_a), cm_txt_b, from_sib(ct_txt_b))
    vec = jnp.stack([bias_out, ln1_gain, ln1_bias, bias_back, ln2_gain, ln2_bias, ln2_bias, ln2_bias])
    bias_rows = jnp.concatenate(
        [small[0:1], from_sib(small)[0:1], small_x[0:1], from_sib(small_x)[0:1]], axis=0
    )
    out_seg, n1_seg, f1_seg, n2_seg, f2_seg, act_seg, slope_seg, wo, wt = ffn_fwd(
        place, ctx_seg, x_seg, vec, bias_rows,
        (four(out_own, out_x), four(w_in, in_x), four(w_back, back_x)),
    )
    out_txt, n1_txt, f1_txt, n2_txt, f2_txt, act_txt, slope_txt = ffn_fwd(
        place, ctx_txt, x_txt, vec, bias_rows, wo, wt
    )

    share = width // lax.axis_size("mp")
    cols = lambda x, who: lax.dynamic_slice_in_dim(x, who * share, share, 1)
    mine, theirs = cols(out_seg, m), from_sib(cols(out_seg, m ^ 1))
    by_core = lambda a, b: (jnp.where(c == 0, a, b), jnp.where(c == 0, b, a))
    columns = jnp.stack(
        [p.reshape(docs, half_seg, share) for p in by_core(mine, theirs)], axis=1
    ).reshape(seg_rows, share)
    ordering = owner_order[0]
    received = lax.all_to_all(
        jnp.take(columns, ordering, axis=0), "dp", split_axis=0, concat_axis=0, tiled=True
    )
    candidates = jnp.arange(seg_rows, dtype=jnp.int32)[None, :]
    pick_left = (pair_index[:, 0:1] == candidates).astype(F32)
    pick_right = (pair_index[:, 1:2] == candidates).astype(F32)
    sides = jnp.concatenate([product(pick_left, received), product(pick_right, received)], axis=1)
    pair_w2 = pair_w.reshape(2 * share, width)
    pair_part = product(sides, pair_w2)
    pair_part = pair_part + from_sib(pair_part)
    pairs_half = pair_part.shape[0] // 2
    piece = lax.dynamic_slice_in_dim(pair_part, c * pairs_half, pairs_half, 0)
    piece = piece + swap(piece, "mp", 2)
    pair_pre = jnp.concatenate(by_core(piece, from_sib(piece)), axis=0) + pair_bias
    root = 0.5 * (1.0 + lax.erf(pair_pre * ROOT_HALF))
    pair_act = pair_pre * root
    logits = product(pair_act, dir_w)
    grad_dir_w = product(cot_logits, pair_act, ((0,), (0,)))
    grad_pair_pre = product(cot_logits, dir_w, ((1,), (1,))) * (
        root + pair_pre * jnp.exp(-0.5 * pair_pre * pair_pre) * DENSITY
    )
    grad_pair_bias = jnp.sum(grad_pair_pre, axis=0)
    grad_pair_w = product(sides, grad_pair_pre, ((0,), (0,)))
    grad_sides = product(grad_pair_pre, pair_w2, ((1,), (1,)))
    grad_received = product(pick_left, grad_sides[:, :share], ((0,), (0,))) + product(
        pick_right, grad_sides[:, share:], ((0,), (0,))
    )
    grad_sent = lax.all_to_all(grad_received, "dp", split_axis=0, concat_axis=0, tiled=True)
    back_order = jnp.zeros_like(ordering).at[ordering].set(jnp.arange(seg_rows, dtype=jnp.int32))
    grad_cols = jnp.take(grad_sent, back_order, axis=0).reshape(docs, 2, half_seg, share)
    rows_of = lambda who: lax.dynamic_index_in_dim(grad_cols, who, 1, keepdims=False).reshape(
        docs * half_seg, share
    )
    grad_mine, grad_theirs = rows_of(c), from_sib(rows_of(1 - c))
    chip_cols = jnp.concatenate(by_core(grad_mine, grad_theirs), axis=1)
    far_cols = swap(chip_cols, "mp", 2)
    low_x = m < 2
    grad_seg = jnp.concatenate(
        [jnp.where(low_x, chip_cols, far_cols), jnp.where(low_x, far_cols, chip_cols)], axis=1
    )

    cot = cot_out.reshape(docs, slots, width)
    cot_seg = lax.dynamic_slice_in_dim(cot, TEXT + c * half_seg, half_seg, 1).reshape(
        docs * half_seg, width
    )
    cot_txt = lax.dynamic_slice_in_dim(cot, c * half, half, 1).reshape(docs * half, width)
    gs_txt, gi_txt, gf_txt, gcm_txt, gct_txt, sums_txt = ffn_bwd(
        cot_txt, n1_txt, f1_txt, n2_txt, f2_txt, slope_txt, vec, wo, wt
    )
    gs_seg, gi_seg, gf_seg, gcm_seg, gct_seg, sums_seg = ffn_bwd(
        cot_seg + grad_seg, n1_seg, f1_seg, n2_seg, f2_seg, slope_seg, vec, wo, wt
    )

    tall = ((0,), (0,))
    h_seg = n1_seg * ln1_gain + ln1_bias
    h_txt = n1_txt * ln1_gain + ln1_bias
    grad_back = [
        product(act_txt[k], gs_txt, tall) + product(act_seg[k], gs_seg, tall) for k in (0, 1)
    ]
    grad_in = [product(h_txt, gi_txt[k], tall) + product(h_seg, gi_seg[k], tall) for k in (0, 1)]
    grad_back_own = grad_back[0] + from_sib(grad_back[1])
    grad_in_own = grad_in[0] + from_sib(grad_in[1])
    sum_w_in, sum_w_back = ring_sum([grad_in_own, grad_back_own])

    grads = (gcm_seg, gcm_txt, from_sib(gct_seg), from_sib(gct_txt))
    ctx_a = (cm_seg_a, cm_txt_a, ct_seg_a, ct_txt_a)
    ctx_b = (cm_seg_b, cm_txt_b, ct_seg_b, ct_txt_b)
    w_sum = jnp.zeros((3 * part, width), F32)
    b_sum = jnp.zeros((1, 3 * part), F32)
    gx = []
    for doc in range(docs):
        gx_doc, w_sum, b_sum = attn_bwd(
            doc, place, text_len, hidden_in, roi, bn, (qkv_own,), qkv_other,
            (qkv_a, qkv_b), (lse_a, lse_b), (ctx_a, ctx_b), grads, w_sum, b_sum,
        )
        gx.append(gx_doc)
    gx_sib = [from_sib(g) for g in gx]
    grad_hidden, bn_sums = final_rows(
        docs, segs, place, gx, gx_sib, gf_seg, gf_txt, from_sib(gf_seg), from_sib(gf_txt), roi, bn
    )

    def out_grad(first):
        return jnp.concatenate(
            [
                product(ctx_txt[first], gf_txt, tall) + product(ctx_seg[first], gf_seg, tall)
            ],
            axis=0,
        )

    grad_out_own = out_grad(0) + from_sib(out_grad(1))
    sum_qkv, sum_rest = ring_sum([w_sum, jnp.concatenate([grad_pair_w, grad_out_own], axis=0)])

    rows = sums_txt + sums_seg
    rows = jnp.concatenate([rows[:6], rows[6:7]]) + from_sib(jnp.concatenate([rows[:6], rows[7:8]]))
    pad = lambda v: jnp.pad(v, (0, width - v.shape[0]))[None]
    vectors = jnp.concatenate(
        [
            rows,
            grad_pair_bias[None],
            grad_dir_w,
            pad(b_sum[0, :part]),
            pad(b_sum[0, 2 * part :]),
            bn_sums[0:2],
        ],
        axis=0,
    )
    vectors = butterfly(vectors, lambda one, two, _: one + two)
    n_dirs = dir_w.shape[1]
    sum_dir_w = vectors[8 : 8 + n_dirs].T
    tail = vectors[8 + n_dirs :]
    sum_bias_qv = tail[0:2, :part]
    grad_bn_bias, grad_bn_gain = tail[2], tail[3]
    grad_roi_out = grad_hidden.reshape(docs, slots, width)[:, TEXT:].reshape(seg_rows, width)
    roi_normed = (roi - bn[0]) * roi_factor
    grad_roi = (
        bn_gain
        * roi_factor
        * (grad_roi_out - grad_bn_bias / all_rows - roi_normed * grad_bn_gain / all_rows)
    )
    output = join_rows(
        docs, segs, place, out_seg, out_txt, from_sib(out_seg), from_sib(out_txt)
    )
    return (
        output,
        logits,
        grad_hidden,
        grad_roi,
        grad_bn_gain,
        grad_bn_bias,
        jnp.transpose(sum_qkv.reshape(3, part, width), (0, 2, 1)),
        sum_bias_qv,
        sum_rest[2 * share :],
        vectors[5],
        vectors[3],
        vectors[4],
        sum_w_in,
        vectors[6],
        sum_w_back,
        vectors[2],
        vectors[0],
        vectors[1],
        sum_rest[: 2 * share].reshape(2, share, width),
        vectors[7],
        sum_dir_w,
    )


def solution(mesh):
    placed = (
        P("dp", None),
        P("dp", None),
        P(),
        P(),
        P(None, None, "mp"),
        P(None, "mp"),
        P("mp", None),
        P(),
        P(),
        P(),
        P(None, "mp"),
        P("mp"),
        P("mp", None),
        P(),
        P(),
        P(),
        P(None, "mp", None),
        P(),
        P(),
        P("dp"),
        P("dp", None),
        P("dp", None),
        P("dp", None),
        P("dp", None),
    )
    return jax.shard_map(
        per_device,
        mesh=mesh,
        in_specs=placed,
        out_specs=(
            P("dp", None),
            P("dp", None),
            P("dp", None),
            P("dp", None),
            P(),
            P(),
            P(None, None, "mp"),
            P(None, "mp"),
            P("mp", None),
            P(),
            P(),
            P(),
            P(None, "mp"),
            P("mp"),
            P("mp", None),
            P(),
            P(),
            P(),
            P(None, "mp", None),
            P(),
            P(),
        ),
        check_vma=False,
    )
```

time: 1280 us -> 862 us (0.67)
  waiting for transfers between devices: 659 us -> 256 us
  Pallas kernels: 0 us -> 337 us
  matrix products: 320 us -> 49.8 us
  blocking collectives: 98.9 us -> 0 us
  starting transfers between devices: 6.42 us -> 91.5 us
  other arithmetic: 74.7 us -> 30.3 us
  between operations: 15.4 us -> 2.56 us
    psum x6 -> x0, waiting for transfers between devices: 638 us -> none  [the longest x1 226 us: per_device(): lax.psum((grad_w_qkv, grad_bias_qv, grad_w_out, grad_bias_out, grad_ln1_g...]
    pallas_call x0 -> x11, Pallas kernels: none -> 337 us  [the longest x3 109 us: attn_bwd(): pl.pallas_call(functools.partial(attn_bwd_kernel, segs, heads, doc), grid...]
    dot_general x52 -> x22, matrix products: 320 us -> 49.8 us  [product(): lax.dot_general(operand, other, (dims, ((), ())), precision=HIGH, preferr...]
    ppermute x0 -> x105, waiting for transfers between devices: none -> 244 us  [the longest x56 155 us: send(): lax.ppermute(x, 'dp', [(order[k], order[(k + sign) % n]) for k in range(n)])]
    ppermute x0 -> x105, starting transfers between devices: none -> 82.8 us  [the longest x56 54.6 us: send(): lax.ppermute(x, 'dp', [(order[k], order[(k + sign) % n]) for k in range(n)])]
    psum x3 -> x0, blocking collectives: 82.1 us -> none  [the longest x1 41.8 us: per_device(): lax.psum((jnp.sum(grad_roi_out, axis=0), jnp.sum(grad_roi_out * roi_norme...]
    reduce_sum x21 -> x2, other arithmetic: 54.6 us -> 2.79 us  [the longest x1 1.42 us: per_device(): stats = jnp.stack([mean, jnp.sum((roi - mean) ** 2, axis=0)])]
    unnamed x169 -> x192, local copies, waits for them, and re-layouts: 26.6 us -> 5.81 us
  transfers between devices with their start and end apart: 8 -> 107, of which waited for: 8 -> 51; matrix products, arithmetic and copies ran while one was open for 7% -> 17% of each run, Pallas kernels for 0% -> 36%
where the time goes in v1:
time: 862 us; the launch traced here: 852 us
  Pallas kernels  337 us (39%)
  waiting for transfers between devices  256 us (30%)
  starting transfers between devices  91.5 us (11%)
  local copies, waits for them, and re-layouts  85.3 us (10%)
  matrix products  49.8 us (6%)
  other arithmetic  30.3 us (4%)
    ppermute x56, waiting for transfers between devices, send(): lax.ppermute(x, 'dp', [(order[k], order[(k + sign) % n]) for k in range(n)])  155 us
    pallas_call x3, Pallas kernels, attn_bwd(): pl.pallas_call(functools.partial(attn_bwd_kernel, segs, heads, doc), grid...  109 us
    ppermute x49, waiting for transfers between devices, swap(): return lax.ppermute(x, axis, [(i, i ^ bit) for i in range(n)])  89.1 us
    pallas_call x2, Pallas kernels, ffn_fwd(): pl.pallas_call(functools.partial(ffn_fwd_kernel, split), grid=(4,), in_sp...  79.5 us
    pallas_call x2, Pallas kernels, ffn_bwd(): pl.pallas_call(ffn_bwd_kernel, grid=(4,), in_specs=[whole(a.shape) for a...  75.5 us
    pallas_call x2, Pallas kernels, attn_fwd(): pl.pallas_call(functools.partial(attn_fwd_kernel, len(pieces), with_rows,...  56 us
    ppermute x56, starting transfers between devices, send(): lax.ppermute(x, 'dp', [(order[k], order[(k + sign) % n]) for k in range(n)])  54.6 us
    dot_general x22, matrix products, product(): lax.dot_general(operand, other, (dims, ((), ())), precision=HIGH, preferr...  49.8 us
  transfers between devices with their start and end apart: 107, of which 51 were waited for; matrix products, arithmetic and copies ran while one was open for 17% of the time, Pallas kernels for 36%

profile of v1, /device:TPU:0, one launch (start us, length us, event | category | flops | bytes accessed | tf_op | source)
XLA Modules:
  0.0 851.8 jit_solution(923355597333131530)
XLA Ops:
  5.6 2.9 collective-permute-start.4
  34.1 2.8 copy.59.refs_6_.refs_5_
  50.7 28.2 %attn_fwd.2 = (f32[1920,576]{1,0:T(8,128)}, f32[1920,128]{1,0:T(8,128)}, f32[192,192]{1,0:T(8,128)}, f32[768,192]{1,0:T(8,128)}, f32[192,192]{1,0:T(8,128)}, /*i...) custom-call(s32[2]{0:T(128)} %pad_add_fusion.refs_0_.place, s32[3]{0:T(128)} %refs_1_.9, ...), custom_call_target="tpu_custom_call" | custom-call | tf_op jit(solution)/shard_map/attn_fwd/pallas_call | solution.py:183
  79.5 15.0 %collective-permute-done.11.refs_10_ = f32[96,768]{1,0:T(8,128)} collective-permute-done((f32[96,768]{1,0:T(8,128)}, f32[96,768]{1,0:T(8,128)}, u32[]{:S(2)}, u32[]{:S(2)}) %collective-permute-start.11) | collective-permute-done | bytes 294944 | tf_op jit(solution)/shard_map/ppermute | solution.py:683
  95.1 8.1 collective-permute-done.12.refs_11_
  108.7 27.8 %attn_fwd.3 = (f32[1920,576]{1,0:T(8,128)}, f32[1920,128]{1,0:T(8,128)}, f32[192,192]{1,0:T(8,128)}, f32[768,192]{1,0:T(8,128)}, f32[192,192]{1,0:T(8,128)}, /*index=5*/f32[768,192]{1,0:T(8,128)}) custom-call(s32[2]{0:T(128)} %pad_add_fusion.refs_0_.place, s32[3]{0:T(128)} %refs_1_.9, f32[1920,768]{1,0:T(8,128)} %refs_2_.9, f32[384,768]{1,0:T(8,128)} %refs_11_.1, ...), custom_call_target="tpu_custom_call" | custom-call | tf_op jit(solution)/shard_map/attn_fwd/pallas_call | solution.py:183
  139.2 27.1 %collective-permute-done.17.refs_17_ = f32[384,768]{1,0:T(8,128)} collective-permute-done((f32[384,768]{1,0:T(8,128)}, f32[384,768]{1,0:T(8,128)}, u32[]{:S(2)}, u32[]{:S(2)}) %collective-permute-start.17) | collective-permute-done | bytes 1179680 | tf_op jit(solution)/shard_map/ppermute | solution.py:683
  166.2 24.8 %collective-permute-done.22.refs_23_ = f32[384,768]{1,0:T(8,128)} collective-permute-done((f32[384,768]{1,0:T(8,128)}, f32[384,768]{1,0:T(8,128)}, u32[]{:S(2)}, u32[]{:S(2)}) %collective-permute-start.22) | collective-permute-done | bytes 1179680 | tf_op jit(solution)/shard_map/ppermute | solution.py:683
  204.7 27.8 %ffn_fwd.2 = (f32[192,768]{1,0:T(8,128)}, f32[192,768]{1,0:T(8,128)}, f32[192,128]{1,0:T(8,128)}, f32[192,768]{1,0:T(8,128)}, f32[192,128]{1,0:T(8,128)}, /*inde...) custom-call(s32[2]{0:T(128)} %pad_add_fusion.refs_0_.place, ...), custom_call_target="tpu_custom_call" | custom-call | tf_op jit(solution)/shard_map/ffn_fwd/pallas_call | solution.py:512
  238.9 5.0 all-to-all-start
  244.0 11.9 %all-to-all-done = f32[8,48,192]{2,1,0:T(8,128)S(1)} async-done(((f32[8,48,192]{2,1,0:T(8,128)}), f32[8,48,192]{2,1,0:T(8,128)S(1)}, u32[]{:S(2)}, u32[]{:S(2)}) %all-to-all-start) | async-done | bytes 294944 | tf_op jit(solution)/shard_map/all_to_all | solution.py:836
  258.0 2.9 scatter_custom_fusion
  262.0 3.3 constant_dynamic-slice_fusion.3
  279.2 51.6 %ffn_fwd.3 = (f32[768,768]{1,0:T(8,128)}, f32[768,768]{1,0:T(8,128)}, f32[768,128]{1,0:T(8,128)}, f32[768,768]{1,0:T(8,128)}, f32[768,128]{1,0:T(8,128)}, /*inde...) custom-call(s32[2]{0:T(128)} %pad_add_fusion.refs_0_.place, f32[768,192]{1,0:T(8,128)} %get-tuple-element.165.refs_1_.refs_13_, ...), custom_call_target="tpu_custom_call" | custom-call | tf_op jit(solution)/shard_map/ffn_fwd/pallas_call | solution.py:512
  330.8 50.4 %ffn_bwd.3 = (f32[768,768]{1,0:T(8,128)}, f32[2,768,768]{2,1,0:T(8,128)}, f32[768,768]{1,0:T(8,128)}, f32[768,384]{1,0:T(8,128)}, f32[768,384]{1,0:T(8,128)}, /*index=5*/f32[8,768]{1,0:T(8,128)}) custom-call(f32[768,768]{1,0:T(8,128)} %bitcast.100, f32[768,768]{1,0:T(8,128)} %get-tuple-element.183.refs_1_, f32[768,128]{1,0:T(8,128)} %get-tuple-element.184.refs_2_, ...), custom_call_target="tpu_custom_call" | custom-call | tf_op jit(solution)/shard_map/ffn_bwd/pallas_call | solution.py:586
  385.3 3.6 all-to-all-start.1
  388.9 6.4 fusion.6
  395.3 6.4 fusion.4
  404.2 6.5 fusion
  411.4 4.9 fusion.2
  421.1 25.2 %ffn_bwd.2 = (f32[192,768]{1,0:T(8,128)}, f32[2,192,768]{2,1,0:T(8,128)}, f32[192,768]{1,0:T(8,128)}, f32[192,384]{1,0:T(8,128)}, f32[192,384]{1,0:T(8,128)}, /*index=5*/f32[8,768]{1,0:T(8,128)}) custom-call(f32[192,768]{1,0:T(8,128)} %maximum_add_fusion.1.refs_0_, f32[192,768]{1,0:T(8,128)} %get-tuple-element.177.refs_1_, ...), custom_call_target="tpu_custom_call" | custom-call | tf_op jit(solution)/shard_map/ffn_bwd/pallas_call | solution.py:586
  449.3 4.0 fusion.25
  457.6 36.1 %attn_bwd.3 = (f32[640,768]{1,0:T(8,128)}, f32[576,768]{1,0:T(8,128)}, f32[1,576]{1,0:T(1,128)}) custom-call(s32[2]{0:T(128)} %pad_add_fusion.refs_0_.place, s32[3]{0:T(128)} %refs_1_.9, f32[1920,768]{1,0:T(8,128)} %refs_2_.9, f32[384,768]{1,0:T(8,128)} %refs_11_.1, f32[8,768]{1,0:T(8,128)} %scatter.35.refs_4_.refs_12_, f32[768,576]{1,0:T(8,128)} %copy.59.refs_6_.refs_5_, ...), custom_call_target="tpu_custom_call" | custom-call | tf_op jit(solution)/shard_map/attn_bwd/pallas_call | solution.py:322
  493.6 36.2 %attn_bwd.4 = (f32[640,768]{1,0:T(8,128)}, f32[576,768]{1,0:T(8,128)}, f32[1,576]{1,0:T(1,128)}) custom-call(s32[2]{0:T(128)} %pad_add_fusion.refs_0_.place, s32[3]{0:T(128)} %refs_1_.9, f32[1920,768]{1,0:T(8,128)} %refs_2_.9, f32[384,768]{1,0:T(8,128)} %refs_11_.1, f32[8,768]{1,0:T(8,128)} %scatter.35.refs_4_.refs_12_, f32[768,576]{1,0:T(8,128)} %copy.59.refs_6_.refs_5_, ...), custom_call_target="tpu_custom_call" | custom-call | tf_op jit(solution)/shard_map/attn_bwd/pallas_call | solution.py:322
  529.9 36.4 %attn_bwd.5 = (f32[640,768]{1,0:T(8,128)}, f32[576,768]{1,0:T(8,128)}, f32[1,576]{1,0:T(1,128)}) custom-call(s32[2]{0:T(128)} %pad_add_fusion.refs_0_.place, s32[3]{0:T(128)} %refs_1_.9, f32[1920,768]{1,0:T(8,128)} %refs_2_.9, f32[384,768]{1,0:T(8,128)} %refs_11_.1, f32[8,768]{1,0:T(8,128)} %scatter.35.refs_4_.refs_12_, f32[768,576]{1,0:T(8,128)} %copy.59.refs_6_.refs_5_, ...), custom_call_target="tpu_custom_call" | custom-call | tf_op jit(solution)/shard_map/attn_bwd/pallas_call | solution.py:322
  569.8 5.3 collective-permute-done.46
  580.9 3.9 collective-permute-done.47
  586.5 5.3 collective-permute-done.61
  593.6 4.4 collective-permute-done.48
  599.8 4.2 collective-permute-done.62
  605.7 4.1 collective-permute-done.49
  611.6 4.2 collective-permute-done.63
  617.6 4.1 collective-permute-done.50
  623.5 4.2 collective-permute-done.64
  629.5 4.8 collective-permute-done.51
  636.1 6.0 collective-permute-done.65
  643.8 4.1 collective-permute-done.52
  649.9 4.0 collective-permute-done.66
  656.8 3.1 collective-permute-done.53
  661.9 2.8 convolution_add_fusion
  668.7 6.2 join_rows.1
  674.9 2.8 fusion.28
  685.1 10.8 %final_rows.1 = (f32[1920,768]{1,0:T(8,128)}, f32[8,768]{1,0:T(8,128)}) custom-call(s32[2]{0:T(128)} %pad_add_fusion.refs_0_.place, f32[640,768]{1,0:T(8,128)} %get-tuple-element.191.refs_1_, f32[640,768]{1,0:T(8,128)} %get-tuple-element.194.refs_2_, f32[640,768]{1,0:T(8,128)} %get-tuple-element.197.refs_3_, f32[640,768]{1,0:T(8,128)} %collective-permute-done.37.refs_4_, ...), custom_call_target="tpu_custom_call" | custom-call | tf_op jit(solution)/shard_map/final_rows/pallas_call | solution.py:664
  707.4 2.8 add_add_fusion
  710.6 3.3 add_add_fusion.1
  719.0 7.4 collective-permute-done.45
  731.9 4.1 collective-permute-done.92
  736.1 2.6 collective-permute-done.77
  741.5 4.5 collective-permute-done.93
  749.0 5.5 collective-permute-done.94
  759.8 4.6 collective-permute-done.95
  767.7 6.5 collective-permute-done.96
  778.0 6.3 collective-permute-done.97
  790.1 5.2 collective-permute-done.98
  795.3 4.7 collective-permute-done.73
  805.6 2.8 collective-permute-done.74
  810.5 3.4 collective-permute-done.100
  814.3 3.3 collective-permute-done.85
  817.7 4.0 collective-permute-done.101
  822.1 3.7 collective-permute-done.86
  825.8 3.1 collective-permute-done.102
  829.6 7.1 collective-permute-done.87
  838.9 4.5 collective-permute-done.88
  843.6 6.6 collective-permute-done.89
  (549 shorter events, 213.5 us)
Async XLA Ops:
  5.6 41.6 %collective-permute-start.4 = (f32[8,768]{1,0:T(8,128)}, f32[8,768]{1,0:T(8,128)}, u32[]{:S(2)}, u32[]{:S(2)}) collective-permute-start(f32[8,768]{1,0:T(8,128)} %scatter.48), channel_id=1, source_target_pairs={{0,2},{1,3},{2,0},{3,1},{4,6},{5,7},{6,4},{7,5},{8,10},{9,11},{10,... | collective-permute-start | bytes 73736 | tf_op jit(solution)/shard_map/ppermute | solution.py:683
  8.5 40.9 %collective-permute-start.8 = (f32[8,768]{1,0:T(8,128)}, f32[8,768]{1,0:T(8,128)}, u32[]{:S(2)}, u32[]{:S(2)}) collective-permute-start(f32[8,768]{1,0:T(8,128)} %scatter.48), channel_id=1, source_target_pairs={{0,1},{1,0},{2,3},{3,2},{4,5},{5,4},{6,7},{7,6},{8,9},{9,8},{10,11... | collective-permute-start | bytes 73736 | tf_op jit(solution)/shard_map/ppermute | solution.py:683
  15.6 24.4 %collective-permute-start.5 = (f32[384,576]{0,1:T(8,128)}, f32[384,576]{0,1:T(8,128)}, u32[]{:S(2)}, u32[]{:S(2)}) collective-permute-start(f32[384,576]{0,1:T(8,128)} %constant_dynamic-slice_fusion.11), channel_id=1, source_target_pairs={{0,2},{1,3},{2,0},{3,1},{4,6},{5,7},{6,4},{7,5},{8,10},{9,11},{10,... | collective-permute-start | bytes 2654216 | tf_op jit(solution)/shard_map/ppermute | solution.py:683
  17.2 119.9 %collective-permute-start.16 = (f32[384,768]{1,0:T(8,128)}, f32[384,768]{1,0:T(8,128)}, u32[]{:S(2)}, u32[]{:S(2)}) collective-permute-start(f32[384,768]{1,0:T(8,128)} %constant_dynamic-slice_fusion.9), channel_id=1, source_target_pairs={{0,2},{1,3},{2,0},{3,1},{4,6},{5,7},{6,4},{7,5},{8,10},{9,11},{10,... | collective-permute-start | bytes 3538952 | tf_op jit(solution)/shard_map/ppermute | solution.py:683
  29.6 9.9 %collective-permute-start.2 = (f32[2,768]{1,0:T(2,128)}, f32[2,768]{1,0:T(2,128)}, u32[]{:S(2)}, u32[]{:S(2)}) collective-permute-start(f32[2,768]{1,0:T(2,128)} %pad_maximum_fusion.10), channel_id=1, source_target_pairs={{0,16},{4,20},{8,24},{12,28},{16,0},{20,4},{24,8},{28,12},{1,17},{... | collective-permute-start | bytes 18440 | tf_op jit(solution)/shard_map/ppermute | solution.py:683
  39.5 98.2 %collective-permute-start.21 = (f32[384,768]{1,0:T(8,128)}, f32[384,768]{1,0:T(8,128)}, u32[]{:S(2)}, u32[]{:S(2)}) collective-permute-start(f32[384,768]{1,0:T(8,128)} %constant_dynamic-slice_fusion.8), channel_id=1, source_target_pairs={{0,2},{1,3},{2,0},{3,1},{4,6},{5,7},{6,4},{7,5},{8,10},{9,11},{10,... | collective-permute-start | bytes 3538952 | tf_op jit(solution)/shard_map/ppermute | solution.py:683
  40.0 63.2 %collective-permute-start.6 = (f32[384,576]{0,1:T(8,128)}, f32[384,576]{0,1:T(8,128)}, u32[]{:S(2)}, u32[]{:S(2)}) collective-permute-start(f32[384,576]{0,1:T(8,128)} %collective-permute-done.5), channel_id=1, source_target_pairs={{0,4},{4,0},{8,12},{12,8},{16,20},{20,16},{24,28},{28,24},{1,5},{5... | collective-permute-start | bytes 2654216 | tf_op jit(solution)/shard_map/ppermute | solution.py:683
  47.2 47.4 %collective-permute-start.11 = (f32[96,768]{1,0:T(8,128)}, f32[96,768]{1,0:T(8,128)}, u32[]{:S(2)}, u32[]{:S(2)}) collective-permute-start(f32[96,768]{1,0:T(8,128)} %constant_dynamic-slice_fusion.10), channel_id=1, source_target_pairs={{0,2},{1,3},{2,0},{3,1},{4,6},{5,7},{6,4},{7,5},{8,10},{9,11},{10,... | collective-permute-start | bytes 884744 | tf_op jit(solution)/shard_map/ppermute | solution.py:683
  49.4 29.5 %collective-permute-start.9 = (f32[8,768]{1,0:T(8,128)}, f32[8,768]{1,0:T(8,128)}, u32[]{:S(2)}, u32[]{:S(2)}) collective-permute-start(f32[8,768]{1,0:T(8,128)} %collective-permute-done.4), channel_id=1, source_target_pairs={{0,1},{1,0},{2,3},{3,2},{4,5},{5,4},{6,7},{7,6},{8,9},{9,8},{10,11... | collective-permute-start | bytes 73736 | tf_op jit(solution)/shard_map/ppermute | solution.py:683
  79.0 16.1 %collective-permute-start.3 = (f32[192,192]{1,0:T(8,128)}, f32[192,192]{1,0:T(8,128)}, u32[]{:S(2)}, u32[]{:S(2)}) collective-permute-start(f32[192,192]{1,0:T(8,128)} %get-tuple-element.160.refs_14_), channel_id=1, source_target_pairs={{0,1},{1,0},{2,3},{3,2},{4,5},{5,4},{6,7},{7,6},{8,9},{9,8},{10,11... | collective-permute-start | bytes 442376 | tf_op jit(solution)/shard_map/ppermute | solution.py:683
  95.1 41.5 %collective-permute-start.10 = (f32[192,768]{1,0:T(8,128)}, f32[192,768]{1,0:T(8,128)}, u32[]{:S(2)}, u32[]{:S(2)}) collective-permute-start(f32[192,768]{1,0:T(8,128)} %refs_8_.1), channel_id=1, source_target_pairs={{0,1},{1,0},{2,3},{3,2},{4,5},{5,4},{6,7},{7,6},{8,9},{9,8},{10,11... | collective-permute-start | bytes 1769480 | tf_op jit(solution)/shard_map/ppermute | solution.py:683
  103.2 33.2 %collective-permute-start.13 = (f32[96,768]{1,0:T(8,128)}, f32[96,768]{1,0:T(8,128)}, u32[]{:S(2)}, u32[]{:S(2)}) collective-permute-start(f32[96,768]{1,0:T(8,128)} %collective-permute-done.11.refs_10_), channel_id=1, source_target_pairs={{0,1},{1,0},{2,3},{3,2},{4,5},{5,4},{6,7},{7,6},{8,9},{9,8},{10,11... | collective-permute-start | bytes 884744 | tf_op jit(solution)/shard_map/ppermute | solution.py:683
  103.2 33.8 %collective-permute-start.14 = (f32[96,768]{1,0:T(8,128)}, f32[96,768]{1,0:T(8,128)}, u32[]{:S(2)}, u32[]{:S(2)}) collective-permute-start(f32[96,768]{1,0:T(8,128)} %collective-permute-done.12.refs_11_), channel_id=1, source_target_pairs={{0,1},{1,0},{2,3},{3,2},{4,5},{5,4},{6,7},{7,6},{8,9},{9,8},{10,11... | collective-permute-start | bytes 884744 | tf_op jit(solution)/shard_map/ppermute | solution.py:683
  136.5 68.2 %collective-permute-start.15 = (f32[768,768]{1,0:T(8,128)S(1)}, f32[768,768]{1,0:T(8,128)}, u32[]{:S(2)}, u32[]{:S(2)}) collective-permute-start(f32[768,768]{1,0:T(8,128)S(1)} %copy-done.29), channel_id=1, source_target_pairs={{0,1},{1,0},{2,3},{3,2},{4,5},{5,4},{6,7},{7,6},{8,9},{9,8},{10,11... | collective-permute-start | bytes 7077896 | tf_op jit(solution)/shard_map/ppermute | solution.py:683
  137.0 67.7 %collective-permute-start.20 = (f32[768,768]{1,0:T(8,128)}, f32[768,768]{1,0:T(8,128)}, u32[]{:S(2)}, u32[]{:S(2)}) collective-permute-start(f32[768,768]{1,0:T(8,128)} %refs_20_.1), channel_id=1, source_target_pairs={{0,1},{1,0},{2,3},{3,2},{4,5},{5,4},{6,7},{7,6},{8,9},{9,8},{10,11... | collective-permute-start | bytes 7077896 | tf_op jit(solution)/shard_map/ppermute | solution.py:683
  137.1 29.1 %collective-permute-start.17 = (f32[384,768]{1,0:T(8,128)}, f32[384,768]{1,0:T(8,128)}, u32[]{:S(2)}, u32[]{:S(2)}) collective-permute-start(f32[384,768]{1,0:T(8,128)} %collective-permute-done.16.refs_16_), channel_id=1, source_target_pairs={{0,4},{4,0},{8,12},{12,8},{16,20},{20,16},{24,28},{28,24},{1,5},{5... | collective-permute-start | bytes 3538952 | tf_op jit(solution)/shard_map/ppermute | solution.py:683
  137.6 53.4 %collective-permute-start.22 = (f32[384,768]{1,0:T(8,128)}, f32[384,768]{1,0:T(8,128)}, u32[]{:S(2)}, u32[]{:S(2)}) collective-permute-start(f32[384,768]{1,0:T(8,128)} %collective-permute-done.21.refs_22_), channel_id=1, source_target_pairs={{0,4},{4,0},{8,12},{12,8},{16,20},{20,16},{24,28},{28,24},{1,5},{5... | collective-permute-start | bytes 3538952 | tf_op jit(solution)/shard_map/ppermute | solution.py:683
  139.2 51.9 %collective-permute-start.18 = (f32[384,768]{1,0:T(8,128)}, f32[384,768]{1,0:T(8,128)}, u32[]{:S(2)}, u32[]{:S(2)}) collective-permute-start(f32[384,768]{1,0:T(8,128)} %collective-permute-done.16.refs_16_), channel_id=1, source_target_pairs={{0,1},{1,0},{2,3},{3,2},{4,5},{5,4},{6,7},{7,6},{8,9},{9,8},{10,11... | collective-permute-start | bytes 3538952 | tf_op jit(solution)/shard_map/ppermute | solution.py:683
  166.2 38.5 %collective-permute-start.23 = (f32[384,768]{1,0:T(8,128)}, f32[384,768]{1,0:T(8,128)}, u32[]{:S(2)}, u32[]{:S(2)}) collective-permute-start(f32[384,768]{1,0:T(8,128)} %collective-permute-done.21.refs_22_), channel_id=1, source_target_pairs={{0,1},{1,0},{2,3},{3,2},{4,5},{5,4},{6,7},{7,6},{8,9},{9,8},{10,11... | collective-permute-start | bytes 3538952 | tf_op jit(solution)/shard_map/ppermute | solution.py:683
  191.0 13.7 %collective-permute-start.19 = (f32[384,768]{1,0:T(8,128)}, f32[384,768]{1,0:T(8,128)}, u32[]{:S(2)}, u32[]{:S(2)}) collective-permute-start(f32[384,768]{1,0:T(8,128)} %collective-permute-done.17.refs_17_), channel_id=1, source_target_pairs={{0,1},{1,0},{2,3},{3,2},{4,5},{5,4},{6,7},{7,6},{8,9},{9,8},{10,11... | collective-permute-start | bytes 3538952 | tf_op jit(solution)/shard_map/ppermute | solution.py:683
  191.0 13.7 %collective-permute-start.24 = (f32[384,768]{1,0:T(8,128)}, f32[384,768]{1,0:T(8,128)}, u32[]{:S(2)}, u32[]{:S(2)}) collective-permute-start(f32[384,768]{1,0:T(8,128)} %collective-permute-done.22.refs_23_), channel_id=1, source_target_pairs={{0,1},{1,0},{2,3},{3,2},{4,5},{5,4},{6,7},{7,6},{8,9},{9,8},{10,11... | collective-permute-start | bytes 3538952 | tf_op jit(solution)/shard_map/ppermute | solution.py:683
  238.9 17.0 %all-to-all-start = ((f32[8,48,192]{2,1,0:T(8,128)}), f32[8,48,192]{2,1,0:T(8,128)S(1)}, u32[]{:S(2)}, u32[]{:S(2)}) async-start(f32[8,48,192]{2,1,0:T(8,128)} %bitcast.9), calls=%async_computation | async-start | bytes 786432 | tf_op jit(solution)/shard_map/all_to_all | solution.py:836
  261.5 11.6 %collective-permute-start.31 = (f32[128,768]{1,0:T(8,128)S(1)}, f32[128,768]{1,0:T(8,128)S(1)}, u32[]{:S(2)}, u32[]{:S(2)}) collective-permute-start(f32[128,768]{1,0:T(8,128)S(1)} %dynamic-slice_add_fusion), channel_id=1, source_target_pairs={{0,2},{1,3},{2,0},{3,1},{4,6},{5,7},{6,4},{7,5},{8,10},{9,11},{10,... | collective-permute-start | bytes 1179656 | tf_op jit(solution)/shard_map/ppermute | solution.py:683
  273.1 108.1 %collective-permute-start.32 = (f32[128,768]{1,0:T(8,128)S(1)}, f32[128,768]{1,0:T(8,128)S(1)}, u32[]{:S(2)}, u32[]{:S(2)}) collective-permute-start(f32[128,768]{1,0:T(8,128)S(1)} %add.610), channel_id=1, source_target_pairs={{0,1},{1,0},{2,3},{3,2},{4,5},{5,4},{6,7},{7,6},{8,9},{9,8},{10,11... | collective-permute-start | bytes 1179656 | tf_op jit(solution)/shard_map/ppermute | solution.py:683
  385.3 16.4 %all-to-all-start.1 = ((f32[8,48,192]{2,1,0:T(8,128)}), f32[8,48,192]{2,1,0:T(8,128)S(1)}, u32[]{:S(2)}, u32[]{:S(2)}) async-start(f32[8,48,192]{2,1,0:T(8,128)} %bitcast.16), calls=%async_computation.1 | async-start | bytes 786432 | tf_op jit(solution)/shard_map/all_to_all | solution.py:863
  416.3 233.5 %collective-permute-start.27 = (f32[192,768]{1,0:T(8,128)}, f32[192,768]{1,0:T(8,128)S(1)}, u32[]{:S(2)}, u32[]{:S(2)}) collective-permute-start(f32[192,768]{1,0:T(8,128)} %get-tuple-element.164.ms), channel_id=1, source_target_pairs={{0,1},{1,0},{2,3},{3,2},{4,5},{5,4},{6,7},{7,6},{8,9},{9,8},{10,11... | collective-permute-start | bytes 1769480 | tf_op jit(solution)/shard_map/ppermute | solution.py:683
  416.3 38.8 %collective-permute-start.36 = (f32[768,384]{1,0:T(8,128)}, f32[768,384]{1,0:T(8,128)S(1)}, u32[]{:S(2)}, u32[]{:S(2)}) collective-permute-start(f32[768,384]{1,0:T(8,128)} %get-tuple-element.190), channel_id=1, source_target_pairs={{0,1},{1,0},{2,3},{3,2},{4,5},{5,4},{6,7},{7,6},{8,9},{9,8},{10,11... | collective-permute-start | bytes 3538952 | tf_op jit(solution)/shard_map/ppermute | solution.py:683
  416.8 238.9 %collective-permute-start.41 = (f32[768,768]{1,0:T(8,128)S(1)}, f32[768,768]{1,0:T(8,128)}, u32[]{:S(2)}, u32[]{:S(2)}) collective-permute-start(f32[768,768]{1,0:T(8,128)S(1)} %copy-done.3), channel_id=1, source_target_pairs={{0,1},{1,0},{2,3},{3,2},{4,5},{5,4},{6,7},{7,6},{8,9},{9,8},{10,11... | collective-permute-start | bytes 7077896 | tf_op jit(solution)/shard_map/ppermute | solution.py:683
  416.8 239.0 %collective-permute-start.28 = (f32[768,768]{1,0:T(8,128)}, f32[768,768]{1,0:T(8,128)}, u32[]{:S(2)}, u32[]{:S(2)}) collective-permute-start(f32[768,768]{1,0:T(8,128)} %get-tuple-element.172.mt), channel_id=1, source_target_pairs={{0,1},{1,0},{2,3},{3,2},{4,5},{5,4},{6,7},{7,6},{8,9},{9,8},{10,11... | collective-permute-start | bytes 7077896 | tf_op jit(solution)/shard_map/ppermute | solution.py:683
  455.2 120.9 %collective-permute-start.60 = (f32[192,768]{1,0:T(8,128)}, f32[192,768]{1,0:T(8,128)S(1)}, u32[]{:S(2)}, u32[]{:S(2)}) collective-permute-start(f32[192,768]{1,0:T(8,128)} %convolution_add_fusion.1), channel_id=1, source_target_pairs={{0,1},{1,0},{2,3},{3,2},{4,5},{5,4},{6,7},{7,6},{8,9},{9,8},{10,11... | collective-permute-start | bytes 1769480 | tf_op jit(solution)/shard_map/ppermute | solution.py:683
  575.1 81.3 %collective-permute-start.40 = (f32[192,768]{1,0:T(8,128)S(1)}, f32[192,768]{1,0:T(8,128)S(1)}, u32[]{:S(2)}, u32[]{:S(2)}) collective-permute-start(f32[192,768]{1,0:T(8,128)S(1)} %copy-done.28), channel_id=1, source_target_pairs={{0,1},{1,0},{2,3},{3,2},{4,5},{5,4},{6,7},{7,6},{8,9},{9,8},{10,11... | collective-permute-start | bytes 1769480 | tf_op jit(solution)/shard_map/ppermute | solution.py:683
  655.7 51.7 %collective-permute-start.90 = (f32[768,768]{1,0:T(8,128)}, f32[768,768]{1,0:T(8,128)}, u32[]{:S(2)}, u32[]{:S(2)}) collective-permute-start(f32[768,768]{1,0:T(8,128)} %fusion.25), channel_id=1, source_target_pairs={{0,1},{1,0},{2,3},{3,2},{4,5},{5,4},{6,7},{7,6},{8,9},{9,8},{10,11... | collective-permute-start | bytes 7077896 | tf_op jit(solution)/shard_map/ppermute | solution.py:683
  655.8 25.2 %collective-permute-start.39 = (f32[640,768]{1,0:T(8,128)}, f32[640,768]{1,0:T(8,128)}, u32[]{:S(2)}, u32[]{:S(2)}) collective-permute-start(f32[640,768]{1,0:T(8,128)} %get-tuple-element.197.refs_3_), channel_id=1, source_target_pairs={{0,1},{1,0},{2,3},{3,2},{4,5},{5,4},{6,7},{7,6},{8,9},{9,8},{10,11... | collective-permute-start | bytes 5898248 | tf_op jit(solution)/shard_map/ppermute | solution.py:683
  656.3 28.5 %collective-permute-start.38 = (f32[640,768]{1,0:T(8,128)}, f32[640,768]{1,0:T(8,128)}, u32[]{:S(2)}, u32[]{:S(2)}) collective-permute-start(f32[640,768]{1,0:T(8,128)} %get-tuple-element.194.refs_2_), channel_id=1, source_target_pairs={{0,1},{1,0},{2,3},{3,2},{4,5},{5,4},{6,7},{7,6},{8,9},{9,8},{10,11... | collective-permute-start | bytes 5898248 | tf_op jit(solution)/shard_map/ppermute | solution.py:683
  656.4 28.7 %collective-permute-start.37 = (f32[640,768]{1,0:T(8,128)}, f32[640,768]{1,0:T(8,128)}, u32[]{:S(2)}, u32[]{:S(2)}) collective-permute-start(f32[640,768]{1,0:T(8,128)} %get-tuple-element.191.refs_1_), channel_id=1, source_target_pairs={{0,1},{1,0},{2,3},{3,2},{4,5},{5,4},{6,7},{7,6},{8,9},{9,8},{10,11... | collective-permute-start | bytes 5898248 | tf_op jit(solution)/shard_map/ppermute | solution.py:683
  666.0 44.6 %collective-permute-start.75 = (f32[768,768]{1,0:T(8,128)}, f32[768,768]{1,0:T(8,128)}, u32[]{:S(2)}, u32[]{:S(2)}) collective-permute-start(f32[768,768]{1,0:T(8,128)} %convolution_add_fusion), channel_id=1, source_target_pairs={{0,1},{1,0},{2,3},{3,2},{4,5},{5,4},{6,7},{7,6},{8,9},{9,8},{10,11... | collective-permute-start | bytes 7077896 | tf_op jit(solution)/shard_map/ppermute | solution.py:683
  681.0 20.7 %collective-permute-start.54 = (f32[72,768]{1,0:T(8,128)}, f32[72,768]{1,0:T(8,128)}, u32[]{:S(2)}, u32[]{:S(2)}) collective-permute-start(f32[72,768]{1,0:T(8,128)} %collective-permute-done.53), channel_id=1, source_target_pairs={{0,8},{8,16},{16,24},{24,28},{28,20},{20,12},{12,4},{4,0},{1,9},{9... | collective-permute-start | bytes 663560 | tf_op jit(solution)/shard_map/ppermute | solution.py:711
  684.8 30.9 %collective-permute-start.68 = (f32[72,768]{1,0:T(8,128)}, f32[72,768]{1,0:T(8,128)}, u32[]{:S(2)}, u32[]{:S(2)}) collective-permute-start(f32[72,768]{1,0:T(8,128)} %get-tuple-element.230), channel_id=1, source_target_pairs={{0,4},{8,0},{16,8},{24,16},{28,24},{20,28},{12,20},{4,12},{1,5},{9... | collective-permute-start | bytes 663560 | tf_op jit(solution)/shard_map/ppermute | solution.py:711
  701.8 30.1 %collective-permute-start.55 = (f32[72,768]{1,0:T(8,128)}, f32[72,768]{1,0:T(8,128)S(1)}, u32[]{:S(2)}, u32[]{:S(2)}) collective-permute-start(f32[72,768]{1,0:T(8,128)} %collective-permute-done.54), channel_id=1, source_target_pairs={{0,8},{8,16},{16,24},{24,28},{28,20},{20,12},{12,4},{4,0},{1,9},{9... | collective-permute-start | bytes 663560 | tf_op jit(solution)/shard_map/ppermute | solution.py:711
  705.9 10.2 %collective-permute-start.44 = (f32[20,768]{1,0:T(8,128)S(1)}, f32[20,768]{1,0:T(8,128)S(1)}, u32[]{:S(2)}, u32[]{:S(2)}) collective-permute-start(f32[20,768]{1,0:T(8,128)S(1)} %add.636), channel_id=1, source_target_pairs={{0,8},{4,12},{8,0},{12,4},{16,24},{20,28},{24,16},{28,20},{1,9},{5... | collective-permute-start | bytes 184328 | tf_op jit(solution)/shard_map/ppermute | solution.py:683
  710.3 18.2 %collective-permute-start.91 = (f32[96,768]{1,0:T(8,128)S(1)}, f32[96,768]{1,0:T(8,128)S(1)}, u32[]{:S(2)}, u32[]{:S(2)}) collective-permute-start(f32[96,768]{1,0:T(8,128)S(1)} %constant_dynamic-slice_fusion), channel_id=1, source_target_pairs={{0,4},{8,0},{16,8},{24,16},{28,24},{20,28},{12,20},{4,12},{1,5},{9... | collective-permute-start | bytes 884744 | tf_op jit(solution)/shard_map/ppermute | solution.py:711
  714.0 14.7 %collective-permute-start.76 = (f32[96,768]{1,0:T(8,128)S(1)}, f32[96,768]{1,0:T(8,128)S(1)}, u32[]{:S(2)}, u32[]{:S(2)}) collective-permute-start(f32[96,768]{1,0:T(8,128)S(1)} %constant_dynamic-slice_fusion.1), channel_id=1, source_target_pairs={{0,8},{8,16},{16,24},{24,28},{28,20},{20,12},{12,4},{4,0},{1,9},{9... | collective-permute-start | bytes 884744 | tf_op jit(solution)/shard_map/ppermute | solution.py:711
  715.7 25.8 %collective-permute-start.69 = (f32[72,768]{1,0:T(8,128)}, f32[72,768]{1,0:T(8,128)S(1)}, u32[]{:S(2)}, u32[]{:S(2)}) collective-permute-start(f32[72,768]{1,0:T(8,128)} %collective-permute-done.68), channel_id=1, source_target_pairs={{0,4},{8,0},{16,8},{24,16},{28,24},{20,28},{12,20},{4,12},{1,5},{9... | collective-permute-start | bytes 663560 | tf_op jit(solution)/shard_map/ppermute | solution.py:711
  716.1 10.4 %collective-permute-start.45 = (f32[20,768]{1,0:T(8,128)S(1)}, f32[20,768]{1,0:T(8,128)S(1)}, u32[]{:S(2)}, u32[]{:S(2)}) collective-permute-start(f32[20,768]{1,0:T(8,128)S(1)} %add.637), channel_id=1, source_target_pairs={{0,16},{4,20},{8,24},{12,28},{16,0},{20,4},{24,8},{28,12},{1,17},{... | collective-permute-start | bytes 184328 | tf_op jit(solution)/shard_map/ppermute | solution.py:683
  728.7 10.0 %collective-permute-start.77 = (f32[96,768]{1,0:T(8,128)S(1)}, f32[96,768]{1,0:T(8,128)S(1)}, u32[]{:S(2)}, u32[]{:S(2)}) collective-permute-start(f32[96,768]{1,0:T(8,128)S(1)} %dynamic-slice_add_fusion.14), channel_id=1, source_target_pairs={{0,8},{8,16},{16,24},{24,28},{28,20},{20,12},{12,4},{4,0},{1,9},{9... | collective-permute-start | bytes 884744 | tf_op jit(solution)/shard_map/ppermute | solution.py:711
  731.9 17.1 %collective-permute-start.56 = (f32[72,768]{1,0:T(8,128)S(1)}, f32[72,768]{1,0:T(8,128)S(1)}, u32[]{:S(2)}, u32[]{:S(2)}) collective-permute-start(f32[72,768]{1,0:T(8,128)S(1)} %collective-permute-done.55), channel_id=1, source_target_pairs={{0,8},{8,16},{16,24},{24,28},{28,20},{20,12},{12,4},{4,0},{1,9},{9... | collective-permute-start | bytes 663560 | tf_op jit(solution)/shard_map/ppermute | solution.py:711
  736.0 10.0 %collective-permute-start.93 = (f32[96,768]{1,0:T(8,128)S(1)}, f32[96,768]{1,0:T(8,128)S(1)}, u32[]{:S(2)}, u32[]{:S(2)}) collective-permute-start(f32[96,768]{1,0:T(8,128)S(1)} %dynamic-slice_add_fusion.6), channel_id=1, source_target_pairs={{0,4},{8,0},{16,8},{24,16},{28,24},{20,28},{12,20},{4,12},{1,5},{9... | collective-permute-start | bytes 884744 | tf_op jit(solution)/shard_map/ppermute | solution.py:711
  741.4 18.2 %collective-permute-start.70 = (f32[72,768]{1,0:T(8,128)S(1)}, f32[72,768]{1,0:T(8,128)S(1)}, u32[]{:S(2)}, u32[]{:S(2)}) collective-permute-start(f32[72,768]{1,0:T(8,128)S(1)} %collective-permute-done.69), channel_id=1, source_target_pairs={{0,4},{8,0},{16,8},{24,16},{28,24},{20,28},{12,20},{4,12},{1,5},{9... | collective-permute-start | bytes 663560 | tf_op jit(solution)/shard_map/ppermute | solution.py:711
  746.9 10.0 %collective-permute-start.79 = (f32[96,768]{1,0:T(8,128)S(1)}, f32[96,768]{1,0:T(8,128)S(1)}, u32[]{:S(2)}, u32[]{:S(2)}) collective-permute-start(f32[96,768]{1,0:T(8,128)S(1)} %dynamic-slice_add_fusion.12), channel_id=1, source_target_pairs={{0,8},{8,16},{16,24},{24,28},{28,20},{20,12},{12,4},{4,0},{1,9},{9... | collective-permute-start | bytes 884744 | tf_op jit(solution)/shard_map/ppermute | solution.py:711
  749.0 18.7 %collective-permute-start.57 = (f32[72,768]{1,0:T(8,128)S(1)}, f32[72,768]{1,0:T(8,128)S(1)}, u32[]{:S(2)}, u32[]{:S(2)}) collective-permute-start(f32[72,768]{1,0:T(8,128)S(1)} %collective-permute-done.56), channel_id=1, source_target_pairs={{0,8},{8,16},{16,24},{24,28},{28,20},{20,12},{12,4},{4,0},{1,9},{9... | collective-permute-start | bytes 663560 | tf_op jit(solution)/shard_map/ppermute | solution.py:711
  759.7 18.3 %collective-permute-start.71 = (f32[72,768]{1,0:T(8,128)S(1)}, f32[72,768]{1,0:T(8,128)S(1)}, u32[]{:S(2)}, u32[]{:S(2)}) collective-permute-start(f32[72,768]{1,0:T(8,128)S(1)} %collective-permute-done.70), channel_id=1, source_target_pairs={{0,4},{8,0},{16,8},{24,16},{28,24},{20,28},{12,20},{4,12},{1,5},{9... | collective-permute-start | bytes 663560 | tf_op jit(solution)/shard_map/ppermute | solution.py:711
  764.3 9.9 %collective-permute-start.96 = (f32[96,768]{1,0:T(8,128)S(1)}, f32[96,768]{1,0:T(8,128)S(1)}, u32[]{:S(2)}, u32[]{:S(2)}) collective-permute-start(f32[96,768]{1,0:T(8,128)S(1)} %dynamic-slice_add_fusion.3), channel_id=1, source_target_pairs={{0,4},{8,0},{16,8},{24,16},{28,24},{20,28},{12,20},{4,12},{1,5},{9... | collective-permute-start | bytes 884744 | tf_op jit(solution)/shard_map/ppermute | solution.py:711
  765.2 10.0 %collective-permute-start.81 = (f32[96,768]{1,0:T(8,128)S(1)}, f32[96,768]{1,0:T(8,128)S(1)}, u32[]{:S(2)}, u32[]{:S(2)}) collective-permute-start(f32[96,768]{1,0:T(8,128)S(1)} %dynamic-slice_add_fusion.10), channel_id=1, source_target_pairs={{0,8},{8,16},{16,24},{24,28},{28,20},{20,12},{12,4},{4,0},{1,9},{9... | collective-permute-start | bytes 884744 | tf_op jit(solution)/shard_map/ppermute | solution.py:711
  767.7 19.6 %collective-permute-start.58 = (f32[72,768]{1,0:T(8,128)S(1)}, f32[72,768]{1,0:T(8,128)S(1)}, u32[]{:S(2)}, u32[]{:S(2)}) collective-permute-start(f32[72,768]{1,0:T(8,128)S(1)} %collective-permute-done.57), channel_id=1, source_target_pairs={{0,8},{8,16},{16,24},{24,28},{28,20},{20,12},{12,4},{4,0},{1,9},{9... | collective-permute-start | bytes 663560 | tf_op jit(solution)/shard_map/ppermute | solution.py:711
  774.3 9.9 %collective-permute-start.97 = (f32[96,768]{1,0:T(8,128)S(1)}, f32[96,768]{1,0:T(8,128)S(1)}, u32[]{:S(2)}, u32[]{:S(2)}) collective-permute-start(f32[96,768]{1,0:T(8,128)S(1)} %dynamic-slice_add_fusion.2), channel_id=1, source_target_pairs={{0,4},{8,0},{16,8},{24,16},{28,24},{20,28},{12,20},{4,12},{1,5},{9... | collective-permute-start | bytes 884744 | tf_op jit(solution)/shard_map/ppermute | solution.py:711
  775.2 9.9 %collective-permute-start.82 = (f32[96,768]{1,0:T(8,128)S(1)}, f32[96,768]{1,0:T(8,128)S(1)}, u32[]{:S(2)}, u32[]{:S(2)}) collective-permute-start(f32[96,768]{1,0:T(8,128)S(1)} %dynamic-slice_add_fusion.9), channel_id=1, source_target_pairs={{0,8},{8,16},{16,24},{24,28},{28,20},{20,12},{12,4},{4,0},{1,9},{9... | collective-permute-start | bytes 884744 | tf_op jit(solution)/shard_map/ppermute | solution.py:711
  778.0 11.0 %collective-permute-start.72 = (f32[72,768]{1,0:T(8,128)S(1)}, f32[72,768]{1,0:T(8,128)S(1)}, u32[]{:S(2)}, u32[]{:S(2)}) collective-permute-start(f32[72,768]{1,0:T(8,128)S(1)} %collective-permute-done.71), channel_id=1, source_target_pairs={{0,4},{8,0},{16,8},{24,16},{28,24},{20,28},{12,20},{4,12},{1,5},{9... | collective-permute-start | bytes 663560 | tf_op jit(solution)/shard_map/ppermute | solution.py:711
  784.3 11.0 %collective-permute-start.98 = (f32[96,768]{1,0:T(8,128)S(1)}, f32[96,768]{1,0:T(8,128)S(1)}, u32[]{:S(2)}, u32[]{:S(2)}) collective-permute-start(f32[96,768]{1,0:T(8,128)S(1)} %dynamic-slice_add_fusion.1), channel_id=1, source_target_pairs={{0,4},{8,0},{16,8},{24,16},{28,24},{20,28},{12,20},{4,12},{1,5},{9... | collective-permute-start | bytes 884744 | tf_op jit(solution)/shard_map/ppermute | solution.py:711
  785.2 14.9 %collective-permute-start.83 = (f32[96,768]{1,0:T(8,128)S(1)}, f32[96,768]{1,0:T(8,128)S(1)}, u32[]{:S(2)}, u32[]{:S(2)}) collective-permute-start(f32[96,768]{1,0:T(8,128)S(1)} %dynamic-slice_add_fusion.8), channel_id=1, source_target_pairs={{0,8},{8,16},{16,24},{24,28},{28,20},{20,12},{12,4},{4,0},{1,9},{9... | collective-permute-start | bytes 884744 | tf_op jit(solution)/shard_map/ppermute | solution.py:711
  787.3 14.8 %collective-permute-start.59 = (f32[72,768]{1,0:T(8,128)S(1)}, f32[72,768]{1,0:T(8,128)S(1)}, u32[]{:S(2)}, u32[]{:S(2)}) collective-permute-start(f32[72,768]{1,0:T(8,128)S(1)} %collective-permute-done.58), channel_id=1, source_target_pairs={{0,8},{8,16},{16,24},{24,28},{28,20},{20,12},{12,4},{4,0},{1,9},{9... | collective-permute-start | bytes 663560 | tf_op jit(solution)/shard_map/ppermute | solution.py:711
  789.0 11.1 %collective-permute-start.73 = (f32[72,768]{1,0:T(8,128)S(1)}, f32[72,768]{1,0:T(8,128)S(1)}, u32[]{:S(2)}, u32[]{:S(2)}) collective-permute-start(f32[72,768]{1,0:T(8,128)S(1)} %collective-permute-done.72), channel_id=1, source_target_pairs={{0,4},{8,0},{16,8},{24,16},{28,24},{20,28},{12,20},{4,12},{1,5},{9... | collective-permute-start | bytes 663560 | tf_op jit(solution)/shard_map/ppermute | solution.py:711
  795.3 10.0 %collective-permute-start.99 = (f32[96,768]{1,0:T(8,128)S(1)}, f32[96,768]{1,0:T(8,128)S(1)}, u32[]{:S(2)}, u32[]{:S(2)}) collective-permute-start(f32[96,768]{1,0:T(8,128)S(1)} %collective-permute-done.98), channel_id=1, source_target_pairs={{0,4},{8,0},{16,8},{24,16},{28,24},{20,28},{12,20},{4,12},{1,5},{9... | collective-permute-start | bytes 884744 | tf_op jit(solution)/shard_map/ppermute | solution.py:711
  800.1 10.3 %collective-permute-start.84 = (f32[96,768]{1,0:T(8,128)S(1)}, f32[96,768]{1,0:T(8,128)S(1)}, u32[]{:S(2)}, u32[]{:S(2)}) collective-permute-start(f32[96,768]{1,0:T(8,128)S(1)} %collective-permute-done.83), channel_id=1, source_target_pairs={{0,8},{8,16},{16,24},{24,28},{28,20},{20,12},{12,4},{4,0},{1,9},{9... | collective-permute-start | bytes 884744 | tf_op jit(solution)/shard_map/ppermute | solution.py:711
  825.7 11.0 %collective-permute-start.87 = (f32[96,768]{1,0:T(8,128)S(1)}, f32[96,768]{1,0:T(8,128)S(1)}, u32[]{:S(2)}, u32[]{:S(2)}) collective-permute-start(f32[96,768]{1,0:T(8,128)S(1)} %collective-permute-done.86), channel_id=1, source_target_pairs={{0,8},{8,16},{16,24},{24,28},{28,20},{20,12},{12,4},{4,0},{1,9},{9... | collective-permute-start | bytes 884744 | tf_op jit(solution)/shard_map/ppermute | solution.py:711
  (139 other events, 1699.5 us)

commit v2 on v0

v2 whole, which is shorter than its diff:
```python
import functools

import jax
import jax.numpy as jnp
from jax import lax
from jax.experimental import pallas as pl
from jax.experimental.pallas import tpu as pltpu
from jax.sharding import PartitionSpec as P

HEAD_DIM = 64
TEXT = 512
EPSILON = 1e-05
NEGATIVE = -1e30
ROOT_HALF = 0.7071067811865476
DENSITY = 0.3989422804014327
HIGH = lax.Precision.HIGH
QUERY_STEP = 256
VMEM_LIMIT = 60 << 20
F32 = jnp.float32
BF16 = jnp.bfloat16


def product(operand, other, dims=((1,), (0,))):
    return lax.dot_general(
        operand, other, (dims, ((), ())), precision=HIGH, preferred_element_type=F32
    )


def halves(x):
    hi = x.astype(BF16)
    return hi, (x - hi.astype(F32)).astype(BF16)


def dot(a, b, dims=((1,), (0,))):
    return lax.dot_general(a, b, (dims, ((), ())), preferred_element_type=F32)


ROWS_BY_ROWS = ((1,), (1,))
COLS_BY_COLS = ((0,), (0,))


def dot3_apart(a, b, dims=((1,), (0,))):
    return dot(a[0], b[0], dims) + dot(a[1], b[0], dims) + dot(a[0], b[1], dims)


def dot3(a, b, dims=((1,), (0,))):
    ka, kb = dims[0][0], dims[1][0]
    return dot(jnp.concatenate([a[0], a[1], a[0]], ka), jnp.concatenate([b[0], b[0], b[1]], kb), dims)


def gelu_parts(v):
    phi = 0.5 + 0.5 * lax.erf(v * ROOT_HALF)
    return v * phi, phi + v * jnp.exp(-0.5 * v * v) * DENSITY


def normalize_rows(y):
    center = y - jnp.mean(y, axis=-1, keepdims=True)
    factor = lax.rsqrt(jnp.mean(center * center, axis=-1, keepdims=True) + EPSILON)
    return center * factor, factor


def normalize_rows_back(upstream, normed, factor):
    return factor * (
        upstream
        - jnp.mean(upstream, axis=-1, keepdims=True)
        - normed * jnp.mean(upstream * normed, axis=-1, keepdims=True)
    )


def colsum(x):
    return jnp.sum(x, axis=0, keepdims=True)


def lane_is(rows, width, lane):
    return lax.broadcasted_iota(jnp.int32, (rows, width), 1) == lane


def cost(products, moved):
    return pl.CostEstimate(flops=6 * products, bytes_accessed=moved, transcendentals=0)


def smem():
    return pl.BlockSpec(memory_space=pltpu.SMEM)


def whole(shape):
    return pl.BlockSpec(shape, lambda *_: (0,) * len(shape), pipeline_mode=pl.Buffered(1))


def sds(*shape):
    return jax.ShapeDtypeStruct(shape, F32)


def batch_normed(roi, stats, rows):
    return (roi - stats[0:1]) * lax.rsqrt(stats[1:2] / rows + EPSILON)


def segment_rows(roi, stats, rows, gain, shift):
    return batch_normed(roi[...], stats, rows) * gain[...][None, :] + shift[...][None, :]


def side_rows(ref, side, half, half_seg):
    return (
        ref.at[pl.ds(pl.multiple_of(TEXT + side * half_seg, half_seg), half_seg)],
        ref.at[pl.ds(pl.multiple_of(side * half, half), half)],
    )


def split_qkv(w, w_hi, w_lo):
    part = w.shape[2]
    for i in range(3):
        lanes = slice(i * part, (i + 1) * part)
        w_hi[:, lanes], w_lo[:, lanes] = halves(w[i])


def attn_fwd_kernel(all_rows, *refs):
    place, lens, hid, roi, stats, gain, shift, w, bias = refs[:9]
    qkv, lse, both_seg, both_txt, xm_seg, xm_txt = refs[9:15]
    w_hi, w_lo, x_seg, ctx, ctx_t = refs[15:]
    doc = pl.program_id(0)
    c = place[0]
    width = w.shape[2]
    heads = width // HEAD_DIM
    slots = hid.shape[0]
    half, half_seg = TEXT // 2, (slots - TEXT) // 2

    @pl.when(doc == 0)
    def _():
        split_qkv(w, w_hi, w_lo)

    x_seg[...] = hid[TEXT:, :] + segment_rows(roi, stats, all_rows, gain, shift)
    wide = (w_hi[...], w_lo[...])
    added = jnp.concatenate([bias[0:1, :], jnp.zeros((1, width), F32), bias[1:2, :]], axis=1)
    for start in (0, half):
        qkv[start : start + half, :] = dot3(halves(hid[start : start + half, :]), wide) + added
    qkv[TEXT:, :] = dot3(halves(x_seg[...]), wide) + added

    position = lax.broadcasted_iota(jnp.int32, (slots, HEAD_DIM), 0)
    first = lane_is(slots, HEAD_DIM, 0)
    dead = (position >= lens[doc]) & (position < TEXT)
    key_extra = jnp.where(first & dead, NEGATIVE, 0.0).astype(BF16)
    ones = jnp.where(first, 1.0, 0.0).astype(BF16)
    one_rows = jnp.ones((16, slots), BF16)
    values = jnp.transpose(qkv[:, 2 * width :])
    for h in range(heads):
        at = h * HEAD_DIM
        q_hi, q_lo = halves(qkv[:, at : at + HEAD_DIM] * HEAD_DIM**-0.5)
        k_hi, k_lo = halves(qkv[:, width + at : width + at + HEAD_DIM])
        v_two = jnp.concatenate([*halves(values[at : at + HEAD_DIM, :]), one_rows], axis=0)
        q_pack = jnp.concatenate([q_hi, q_lo, q_hi, ones], axis=1)
        k_pack = jnp.concatenate([k_hi, k_hi, k_lo, key_extra], axis=1)
        for start in range(0, slots, QUERY_STEP):
            cols = slice(start, min(slots, start + QUERY_STEP))
            scores = dot(k_pack, q_pack[cols], ROWS_BY_ROWS)
            top = jnp.max(scores, axis=0, keepdims=True)
            p_hi, p_lo = halves(jnp.exp(scores - top))
            mixed = dot(v_two, p_hi) + dot(v_two, p_lo)
            total = mixed[2 * HEAD_DIM : 2 * HEAD_DIM + 1]
            ctx_t[at : at + HEAD_DIM, cols] = (
                mixed[:HEAD_DIM] + mixed[HEAD_DIM : 2 * HEAD_DIM]
            ) / total
            lse[h : h + 1, cols] = top + jnp.log(total)
    ctx[...] = jnp.transpose(ctx_t[...])
    for lanes, side in ((slice(0, width), c), (slice(width, 2 * width), 1 - c)):
        at_seg, at_txt = side_rows(ctx, side, half, half_seg)
        both_seg[:, lanes] = at_seg[...]
        both_txt[:, lanes] = at_txt[...]
    xm_seg[...] = x_seg[pl.ds(pl.multiple_of(c * half_seg, half_seg), half_seg), :]
    xm_txt[...] = hid[pl.ds(pl.multiple_of(c * half, half), half), :]


def by_doc(rows, lanes):
    return pl.BlockSpec((rows, lanes), lambda d: (d, 0))


def attn_fwd(all_rows, place, lens, hidden, roi, stats, gain, shift, w, bias):
    docs = lens.shape[0]
    slots, width = hidden.shape[0] // docs, hidden.shape[1]
    segs = slots - TEXT
    part = w.shape[2]
    out_rows = [
        (slots, 3 * part),
        (8, slots),
        (segs // 2, 2 * part),
        (TEXT // 2, 2 * part),
        (segs // 2, width),
        (TEXT // 2, width),
    ]
    return pl.pallas_call(
        functools.partial(attn_fwd_kernel, all_rows),
        grid=(docs,),
        in_specs=[smem(), smem(), by_doc(slots, width), by_doc(segs, width)]
        + [whole(a.shape) for a in (stats, gain, shift, w, bias)],
        out_specs=[by_doc(*s) for s in out_rows],
        out_shape=[sds(docs * s[0], s[1]) for s in out_rows],
        scratch_shapes=[
            pltpu.VMEM((width, 3 * part), BF16),
            pltpu.VMEM((width, 3 * part), BF16),
            pltpu.VMEM((segs, width), F32),
            pltpu.VMEM((slots, part), F32),
            pltpu.VMEM((part, slots), F32),
        ],
        compiler_params=pltpu.CompilerParams(vmem_limit_bytes=VMEM_LIMIT),
        cost_estimate=cost(docs * slots, slots),
        name="attn_fwd",
    )(place, lens, hidden, roi, stats, gain, shift, w, bias)


def attn_bwd_kernel(doc, *refs):
    place, lens, qkv, lse, ctx_seg, ctx_txt, gm_seg, gm_txt, gt_seg, gt_txt, b_sum = refs[:11]
    gq, b_out, o_all, g_all, gq_t = refs[11:]
    c = place[0]
    width = qkv.shape[1] // 3
    heads = width // HEAD_DIM
    slots = qkv.shape[0]
    half, half_seg = TEXT // 2, (slots - TEXT) // 2
    near, far = slice(0, width), slice(width, 2 * width)
    for dst, mine, theirs in (
        (o_all, (ctx_seg, ctx_txt), (ctx_seg, ctx_txt)),
        (g_all, (gm_seg, gm_txt), (gt_seg, gt_txt)),
    ):
        for side, sources, lanes in ((c, mine, near), (1 - c, theirs, far)):
            for place_at, source in zip(side_rows(dst, side, half, half_seg), sources):
                place_at[...] = source[:, lanes]

    position = lax.broadcasted_iota(jnp.int32, (slots, HEAD_DIM), 0)
    first = lane_is(slots, HEAD_DIM, 0)
    dead = (position >= lens[doc]) & (position < TEXT)
    key_extra = jnp.where(first & dead, NEGATIVE, 0.0).astype(BF16)
    ones = jnp.where(first, 1.0, 0.0).astype(BF16)
    none = jnp.zeros_like(ones)
    head_of = lax.broadcasted_iota(jnp.int32, (16, width), 1) // HEAD_DIM
    pick_head = jnp.where(
        head_of == lax.broadcasted_iota(jnp.int32, (16, width), 0), 1.0, 0.0
    ).astype(BF16)
    scale = HEAD_DIM**-0.5
    product_hi, product_lo = halves(g_all[...] * o_all[...])
    inner = dot(pick_head, product_hi, ROWS_BY_ROWS) + dot(pick_head, product_lo, ROWS_BY_ROWS)
    keys_t = jnp.transpose(qkv[:, width : 2 * width])
    for h in range(heads):
        at = h * HEAD_DIM
        q_hi, q_lo = halves(qkv[:, at : at + HEAD_DIM] * scale)
        k_hi, k_lo = halves(qkv[:, width + at : width + at + HEAD_DIM])
        v_hi, v_lo = halves(qkv[:, 2 * width + at : 2 * width + at + HEAD_DIM])
        g_hi, g_lo = halves(g_all[:, at : at + HEAD_DIM])
        k_rows = jnp.concatenate(halves(keys_t[at : at + HEAD_DIM, :]), axis=0)
        q_pack = jnp.concatenate([q_hi, q_lo, q_hi, ones], axis=1)
        k_pack = jnp.concatenate([k_hi, k_hi, k_lo, key_extra], axis=1)
        g_pack = jnp.concatenate([g_hi, g_lo, g_hi, none], axis=1)
        v_pack = jnp.concatenate([v_hi, v_hi, v_lo, none], axis=1)
        q_two = jnp.concatenate([q_hi, q_lo], axis=1)
        g_two = jnp.concatenate([g_hi, g_lo], axis=1)
        weights = jnp.exp(dot(k_pack, q_pack, ROWS_BY_ROWS) - lse[h : h + 1, :])
        grads = weights * (dot(v_pack, g_pack, ROWS_BY_ROWS) - inner[h : h + 1, :])
        w_two = halves(weights)
        s_two = halves(grads)
        grad_v = dot(w_two[0], g_two) + dot(w_two[1], g_two)
        grad_k = dot(s_two[0], q_two) + dot(s_two[1], q_two)
        grad_q = dot(k_rows, s_two[0]) + dot(k_rows, s_two[1])
        gq[:, width + at : width + at + HEAD_DIM] = grad_k[:, :HEAD_DIM] + grad_k[:, HEAD_DIM:]
        gq[:, 2 * width + at : 2 * width + at + HEAD_DIM] = (
            grad_v[:, :HEAD_DIM] + grad_v[:, HEAD_DIM:]
        )
        gq_t[at : at + HEAD_DIM, :] = (grad_q[:HEAD_DIM] + grad_q[HEAD_DIM:]) * scale
    gq[:, :width] = jnp.transpose(gq_t[...])
    b_out[...] = b_sum[...] + colsum(gq[...])


def attn_bwd(doc, place, lens, qkv, lse, ctx, mine, theirs, b_sum):
    docs = lens.shape[0]
    slots, cols = qkv.shape[0] // docs, qkv.shape[1]
    segs = slots - TEXT
    part = cols // 3
    of_doc = lambda rows, lanes: pl.BlockSpec((rows, lanes), lambda i: (doc, 0))
    rows = [of_doc(segs // 2, 2 * part), of_doc(TEXT // 2, 2 * part)]
    return pl.pallas_call(
        functools.partial(attn_bwd_kernel, doc),
        grid=(1,),
        in_specs=[smem(), smem(), of_doc(slots, cols), of_doc(8, slots)] + rows * 3 + [whole((1, cols))],
        out_specs=[whole((slots, cols)), whole((1, cols))],
        out_shape=[sds(slots, cols), sds(1, cols)],
        scratch_shapes=[
            pltpu.VMEM((slots, part), F32),
            pltpu.VMEM((slots, part), F32),
            pltpu.VMEM((part, slots), F32),
        ],
        compiler_params=pltpu.CompilerParams(vmem_limit_bytes=VMEM_LIMIT),
        cost_estimate=cost(slots * part * 16 * slots, 8 * slots * cols),
        name="attn_bwd",
    )(place, lens, qkv, lse, *ctx, *mine, *theirs, b_sum)


def qkv_bwd_kernel(all_rows, *refs):
    place, hid, roi, stats, gain, shift, w, gq, w_sum = refs[:9]
    gx_mine, gx_theirs, w_out = refs[9:12]
    w_hi, w_lo, x_all, gx = refs[12:]
    c = place[0]
    slots = hid.shape[0]
    half, half_seg = TEXT // 2, (slots - TEXT) // 2
    split_qkv(w, w_hi, w_lo)
    x_all[:TEXT, :] = hid[:TEXT, :]
    x_all[TEXT:, :] = hid[TEXT:, :] + segment_rows(roi, stats, all_rows, gain, shift)
    wide = (w_hi[...], w_lo[...])
    for start in range(0, slots, 320):
        rows = slice(start, min(slots, start + 320))
        gx[rows, :] = dot3_apart(halves(gq[rows, :]), wide, ROWS_BY_ROWS)
    w_out[...] = w_sum[...] + dot3_apart(halves(gq[...]), halves(x_all[...]), COLS_BY_COLS)
    for dst, side in ((gx_mine, c), (gx_theirs, 1 - c)):
        at_seg, at_txt = side_rows(gx, side, half, half_seg)
        dst[:half_seg, :] = at_seg[...]
        dst[half_seg:, :] = at_txt[...]


def qkv_bwd(all_rows, doc, docs, place, hidden, roi, stats, gain, shift, w, gq, w_sum):
    slots, width = hidden.shape[0] // docs, hidden.shape[1]
    cols = gq.shape[1]
    of_doc = lambda rows, lanes: pl.BlockSpec((rows, lanes), lambda i: (doc, 0))
    return pl.pallas_call(
        functools.partial(qkv_bwd_kernel, all_rows),
        grid=(1,),
        in_specs=[smem(), of_doc(slots, width), of_doc(slots - TEXT, width)]
        + [whole(a.shape) for a in (stats, gain, shift, w, gq, w_sum)],
        out_specs=[whole((slots // 2, width)), whole((slots // 2, width)), whole((cols, width))],
        out_shape=[sds(slots // 2, width), sds(slots // 2, width), sds(cols, width)],
        scratch_shapes=[
            pltpu.VMEM((width, cols), BF16),
            pltpu.VMEM((width, cols), BF16),
            pltpu.VMEM((slots, width), F32),
            pltpu.VMEM((slots, width), F32),
        ],
        compiler_params=pltpu.CompilerParams(vmem_limit_bytes=VMEM_LIMIT),
        cost_estimate=cost(slots * cols * 2 * width, 12 * slots * width),
        name="qkv_bwd",
    )(place, hidden, roi, stats, gain, shift, w, gq, w_sum)


VECTORS = ("bias_out", "ln1_gain", "ln1_bias", "bias_back", "ln2_gain", "ln2_bias")
TILES = 4
PIECE_SHARDS = (0, 1, 2, 2, 3, 3)


def piece_place(i, rows, shift):
    if i < 2:
        return 0
    half = rows // 2
    return pl.multiple_of((shift if i % 2 == 0 else 1 - shift) * half, half)


def ffn_kernel(forward, backward, names, *refs):
    ref = dict(zip(names, refs))
    place, stage, sems = ref["place"], ref["stage"], ref["sems"]
    wts, acc, a_hi, a_lo = ref["wts"], ref["acc"], ref["a_hi"], ref["a_lo"]
    wo = ref["wo"]
    resident = wts.shape[0] == TILES
    c = place[0]
    shifts = {"wo": place[1], "wi": place[1], "wb": place[2]}
    width = acc.shape[1]
    rows = acc.shape[0]
    part = wo.shape[1] // 4
    row = lambda name: ref[name][...][None, :]

    def two_shards(one, two):
        lane = lax.broadcasted_iota(jnp.int32, (rows, 2 * part), 1)
        return jnp.where(lane < part, ref[one][...], ref[two][...])

    def copies(tile):
        found = []
        for i in range(6):
            if PIECE_SHARDS[i] == tile:
                for k, kind in enumerate(("wi", "wb")):
                    piece = ref[f"{kind}{i}"]
                    if kind == "wi" and i > 1:
                        piece = piece.at[pl.ds(part // 2, width // 2)]
                    at = pl.ds(piece_place(i, width, shifts[kind]), piece.shape[0])
                    found.append(
                        pltpu.make_async_copy(piece, stage.at[k, at, :], sems.at[len(found)])
                    )
        return found

    def start_tile(tile):
        for copy in copies(tile):
            copy.start()

    def ready(tile):
        for copy in copies(tile):
            copy.wait()
        slot = tile if resident else 0
        wts[slot, 0], wts[slot, 1] = halves(stage[0])
        wts[slot, 2], wts[slot, 3] = halves(stage[1])
        if tile + 1 < TILES:
            start_tile(tile + 1)

    def load_wo(count):
        for i in range(count):
            at = PIECE_SHARDS[i] * part + piece_place(i, part, shifts["wo"])
            where = pl.ds(at, ref[f"wo{i}"].shape[0])
            wo[0, where, :], wo[1, where, :] = halves(ref[f"wo{i}"][...])

    def run_forward(loading):
        y = ref["xres"][...] + row("bias_out")
        for one, two, at in (
            ("ctx_own", "ctx_sib", slice(0, 2 * part)),
            ("ctx_far", "ctx_farsib", slice(2 * part, 4 * part)),
        ):
            y = y + dot3(halves(two_shards(one, two)), (wo[0, at, :], wo[1, at, :]))
        normed, factor = normalize_rows(y)
        ref["n1"][...] = normed
        ref["f1"][...] = jnp.broadcast_to(factor, (rows, 128))
        h = normed * row("ln1_gain") + row("ln1_bias")
        ref["h1"][...] = h
        a_hi[...], a_lo[...] = halves(h)
        acc[...] = h + row("bias_back")
        for t in range(TILES):
            if loading:
                ready(t)
            slot = t if resident else 0
            pre = dot3((a_hi[...], a_lo[...]), (wts[slot, 0], wts[slot, 1]))
            value, rise = gelu_parts(pre + row(f"bias_in{t}"))
            ref["slope"][t] = rise
            if t < 2:
                ref[f"act{t}"][...] = value
            acc[...] += dot3(halves(value), (wts[slot, 2], wts[slot, 3]))
        normed, factor = normalize_rows(acc[...])
        ref["n2"][...] = normed
        ref["f2"][...] = jnp.broadcast_to(factor, (rows, 128))
        ref["out"][...] = normed * row("ln2_gain") + row("ln2_bias")

    def run_backward(loading):
        sums = ref["sums"]
        if forward:
            g = ref["gout"][pl.ds(pl.multiple_of(c * rows, rows), rows), :]
        else:
            g = ref["gout"][...]
        n2 = ref["n2"][...]
        sums[0:1, :] += colsum(g * n2)
        sums[1:2, :] += colsum(g)
        back = normalize_rows_back(g * row("ln2_gain"), n2, ref["f2"][:, 0:1])
        sums[2:3, :] += colsum(back)
        ref["gs"][...] = back
        acc[...] = back
        a_hi[...], a_lo[...] = halves(back)
        for t in range(TILES):
            if loading:
                ready(t)
            slot = t if resident else 0
            grad = dot3((a_hi[...], a_lo[...]), (wts[slot, 2], wts[slot, 3]), ROWS_BY_ROWS)
            grad = grad * ref["slope"][t]
            if t < 2:
                ref[f"gi{t}"][...] = grad
                sums[6 + t : 7 + t, :] += colsum(grad)
            acc[...] += dot3(halves(grad), (wts[slot, 0], wts[slot, 1]), ROWS_BY_ROWS)
        g, n1 = acc[...], ref["n1"][...]
        sums[3:4, :] += colsum(g * n1)
        sums[4:5, :] += colsum(g)
        back = normalize_rows_back(g * row("ln1_gain"), n1, ref["f1"][:, 0:1])
        sums[5:6, :] += colsum(back)
        ref["gf"][...] = back
        two = halves(back)
        at = slice(0, 2 * part)
        ref["gb"][...] = dot3(two, (wo[0, at, :], wo[1, at, :]), ROWS_BY_ROWS)
        ref["gwo"][...] = dot3_apart(halves(two_shards("ctx_own", "ctx_sib")), two, COLS_BY_COLS)

    def begin():
        start_tile(0)
        load_wo(6 if forward else 2)
        if backward:
            ref["sums"][...] = jnp.zeros_like(ref["sums"])

    if forward and backward:

        @pl.when(pl.program_id(0) == 0)
        def _():
            begin()
            run_forward(True)
            run_backward(False)

        @pl.when(pl.program_id(0) > 0)
        def _():
            run_forward(False)
            run_backward(False)
    else:
        begin()
        if forward:
            run_forward(True)
        if backward:
            run_backward(True)


def ffn(place, vectors, bias_in, weights, block, offset, total, saved, *, ctx=None, xres=None, gout=None, into=None, start=0, count=None):
    forward, backward = xres is not None, gout is not None
    both = forward and backward
    width = vectors[0].shape[0]
    rows = ctx[0].shape[0]
    blocks = rows // block
    part = width // 4
    w_out, w_in, w_back = weights
    first = offset // block + start
    local = lambda lanes: pl.BlockSpec((block, lanes), lambda r: (start + r, 0))
    shared = pl.BlockSpec((block, width), lambda r: (first + r, 0))
    anywhere = pl.BlockSpec(memory_space=pltpu.HBM)
    names, specs, args = [], [], []

    def take(name, spec, arg):
        names.append(name)
        specs.append(spec)
        args.append(arg)

    take("place", smem(), place)
    for name, a in zip(VECTORS, vectors):
        take(name, whole(a.shape), a)
    for name, a in zip(("ctx_own", "ctx_sib", "ctx_far", "ctx_farsib"), ctx):
        take(name, local(a.shape[1]), a)
    if forward:
        for t in range(TILES):
            take(f"bias_in{t}", whole(bias_in[t].shape), bias_in[t])
        take("xres", local(width), xres)
    if backward:
        if both:
            slots = gout.shape[0] // blocks
            take("gout", pl.BlockSpec((slots, width), lambda r: (start + r, 0)), gout)
        else:
            take("gout", local(width), gout)
    kept = (
        ("n1", (block, width)),
        ("f1", (block, 128)),
        ("n2", (block, width)),
        ("f2", (block, 128)),
        ("slope", (TILES, block, width)),
    )
    if backward and not forward:
        for (name, shape), a in zip(kept, saved):
            take(name, whole(shape), a)
    for i in range(6 if forward else 2):
        piece, height = (w_out[i], part) if i < 2 else (w_in[i], part // 2)
        take(f"wo{i}", whole((height, width)), piece)
    for i in range(6):
        take(f"wi{i}", anywhere, w_in[i])
        take(f"wb{i}", anywhere, w_back[i])
    outs = []
    if forward:
        outs += [("out", local(width), sds(rows, width))]
        outs += [(n, shared, sds(total, width)) for n in ("h1", "act0", "act1")]
        if not backward:
            outs += [(name, whole(shape), sds(*shape)) for name, shape in kept]
    if backward:
        outs += [(n, shared, sds(total, width)) for n in ("gs", "gi0", "gi1", "gf")]
        outs += [("gb", local(2 * part), sds(rows, 2 * part))]
        outs += [("gwo", whole((2 * part, width)), sds(2 * part, width))]
        outs += [("sums", whole((8, width)), sds(8, width))]
    aliases = {}
    if into:
        for k, (name, _, _) in enumerate(outs):
            if name in into:
                aliases[len(args)] = k
                take(name + "_into", anywhere, into[name])
    scratch = [
        ("stage", pltpu.VMEM((2, width, width), F32)),
        ("sems", pltpu.SemaphoreType.DMA((4,))),
        ("wts", pltpu.VMEM((TILES if both else 1, 4, width, width), BF16)),
        ("wo", pltpu.VMEM((2, width, width), BF16)),
        ("acc", pltpu.VMEM((block, width), F32)),
        ("a_hi", pltpu.VMEM((block, width), BF16)),
        ("a_lo", pltpu.VMEM((block, width), BF16)),
    ]
    if both:
        scratch += [(name, pltpu.VMEM(shape, F32)) for name, shape in kept]
    all_names = names + [o[0] for o in outs] + [s[0] for s in scratch]
    passes = (3 if both else 1) * 8
    result = pl.pallas_call(
        functools.partial(ffn_kernel, forward, backward, all_names),
        grid=(count or blocks,),
        in_specs=specs,
        out_specs=[o[1] for o in outs],
        out_shape=[o[2] for o in outs],
        scratch_shapes=[s[1] for s in scratch],
        input_output_aliases=aliases,
        compiler_params=pltpu.CompilerParams(vmem_limit_bytes=VMEM_LIMIT),
        cost_estimate=cost(
            (count or blocks) * block * width * width * (16 if both else 8) + 4 * width**3,
            60 * block * width,
        ),
        name="ffn_" + "fwd" * forward + "bwd" * backward,
    )(*args)
    return {o[0]: r for o, r in zip(outs, result)}


def join_kernel(docs, segs, place, ms, mt, ts, tt, out):
    c = place[0]
    half, half_seg = TEXT // 2, segs // 2
    for seg, txt, side in ((ms, mt, c), (ts, tt, 1 - c)):
        at_seg, at_txt = side_rows(out, side, half, half_seg)
        at_seg[...] = seg[...]
        at_txt[...] = txt[...]


def join_rows(docs, segs, place, ms, mt, ts, tt):
    width = ms.shape[1]
    slots = TEXT + segs
    return pl.pallas_call(
        functools.partial(join_kernel, docs, segs),
        grid=(docs,),
        in_specs=[smem()] + [by_doc(segs // 2, width), by_doc(TEXT // 2, width)] * 2,
        out_specs=by_doc(slots, width),
        out_shape=sds(docs * slots, width),
        cost_estimate=cost(0, 8 * docs * slots * width),
        compiler_params=pltpu.CompilerParams(vmem_limit_bytes=VMEM_LIMIT),
        name="join_rows",
    )(place, ms, mt, ts, tt)


def final_kernel(docs, segs, all_rows, *refs):
    place = refs[0]
    mine, theirs = refs[1 : 1 + docs], refs[1 + docs : 1 + 2 * docs]
    roi, stats, out, sums = refs[1 + 2 * docs :]
    d = pl.program_id(0)
    c = place[0]
    half, half_seg = TEXT // 2, segs // 2

    @pl.when(d == 0)
    def _():
        sums[...] = jnp.zeros_like(sums)

    for i in range(docs):

        @pl.when(d == i)
        def _():
            for source, side in ((mine[i], c), (theirs[i], 1 - c)):
                at_seg, at_txt = side_rows(out, side, half, half_seg)
                at_seg[...] = source[:half_seg, :]
                at_txt[...] = source[half_seg:, :]

    g = out[TEXT:, :]
    sums[0:1, :] += colsum(g)
    sums[1:2, :] += colsum(g * batch_normed(roi[...], stats, all_rows))


def final_rows(all_rows, segs, place, mine, theirs, roi, stats):
    docs = len(mine)
    width = roi.shape[1]
    slots = TEXT + segs
    return pl.pallas_call(
        functools.partial(final_kernel, docs, segs, all_rows),
        grid=(docs,),
        in_specs=[smem()]
        + [whole((slots // 2, width))] * (2 * docs)
        + [by_doc(segs, width), whole(stats.shape)],
        out_specs=[by_doc(slots, width), pl.BlockSpec((8, width), lambda d: (0, 0))],
        out_shape=[sds(docs * slots, width), sds(8, width)],
        compiler_params=pltpu.CompilerParams(vmem_limit_bytes=VMEM_LIMIT),
        cost_estimate=cost(0, 20 * docs * slots * width),
        name="final_rows",
    )(place, *mine, *theirs, roi, stats)


def stats_kernel(roi, stats):
    x = roi[...]
    mean = jnp.mean(x, axis=0, keepdims=True)
    stats[0:1, :] = mean
    stats[1:2, :] = colsum((x - mean) * (x - mean))


def local_stats(roi):
    width = roi.shape[1]
    return pl.pallas_call(
        stats_kernel, out_shape=sds(2, width), name="local_stats"
    )(roi)


def swap(x, axis, bit):
    n = lax.axis_size(axis)
    return lax.ppermute(x, axis, [(i, i ^ bit) for i in range(n)])


def butterfly(x, merge):
    bit = 1
    while bit < lax.axis_size("dp"):
        x = merge(x, swap(x, "dp", bit), bit)
        bit *= 2
    return x


def ring(part, sign):
    n = lax.axis_size("dp")
    order = list(range(0, n, 2)) + list(range(n - 1, 0, -2))
    pairs = [(order[k], order[(k + sign) % n]) for k in range(n)]
    me = lax.axis_index("dp")
    place = sign * jnp.where(me % 2 == 0, me // 2, n - 1 - me // 2)
    size = part.shape[0] // n
    at = lambda k: ((place - k) % n) * size
    held = lax.dynamic_slice_in_dim(part, at(0), size, 0)
    for step in range(1, n):
        got = yield held, "dp", pairs
        held = got + lax.dynamic_slice_in_dim(part, at(step), size, 0)
    pieces = [held]
    for step in range(n - 1):
        held = yield held, "dp", pairs
        pieces.append(held)
    if size % 8 == 0:
        return assemble(jnp.stack([at(k - 1) for k in range(n)]).astype(jnp.int32), pieces)
    total = part
    for k, piece in enumerate(pieces):
        total = lax.dynamic_update_slice_in_dim(total, piece, at(k - 1), 0)
    return total


def assemble_kernel(where, *refs):
    out = refs[-1]
    for k, piece in enumerate(refs[:-1]):
        out[pl.ds(pl.multiple_of(where[k], 8), piece.shape[0]), :] = piece[...]


def assemble(where, pieces):
    size, width = pieces[0].shape
    return pl.pallas_call(
        assemble_kernel,
        in_specs=[smem()] + [pl.BlockSpec(memory_space=pltpu.VMEM)] * len(pieces),
        out_specs=pl.BlockSpec(memory_space=pltpu.VMEM),
        out_shape=sds(size * len(pieces), width),
        compiler_params=pltpu.CompilerParams(vmem_limit_bytes=VMEM_LIMIT),
        cost_estimate=cost(0, 8 * size * len(pieces) * width),
        name="assemble",
    )(where, *pieces)


def halving(part, turn):
    n = lax.axis_size("dp")
    bits = list(range(n.bit_length() - 1))
    bits = bits[turn:] + bits[:turn]
    me = lax.axis_index("dp")
    pairs = lambda bit: [(i, i ^ (1 << bit)) for i in range(n)]
    for bit in bits:
        upper = (me >> bit) % 2
        half = part.shape[0] // 2
        keep, give = (lax.dynamic_slice_in_dim(part, k * half, half, 0) for k in (upper, 1 - upper))
        part = keep + (yield give, "dp", pairs(bit))
    for bit in bits[::-1]:
        upper = (me >> bit) % 2 == 1
        other = yield part, "dp", pairs(bit)
        part = jnp.concatenate(
            [jnp.where(upper, other, part), jnp.where(upper, part, other)], axis=0
        )
    return part


def cube(x):
    n = lax.axis_size("dp")
    bit = 1
    while bit < n:
        x = x + (yield x, "dp", [(i, i ^ bit) for i in range(n)])
        bit *= 2
    return x


class Steps:
    def __init__(self):
        self.active, self.results = {}, {}

    def add(self, name, moves):
        self.active[name] = (moves, next(moves))

    def run(self, work=None, inputs=()):
        names = list(self.active)
        sends = [self.active[name][1][0] for name in names]
        sends, inputs = lax.optimization_barrier((sends, tuple(inputs)))
        got = [lax.ppermute(x, *self.active[name][1][1:]) for name, x in zip(names, sends)]
        done = work(*inputs) if work else ()
        got, done = lax.optimization_barrier((got, done))
        for name, x in zip(names, got):
            moves = self.active.pop(name)[0]
            try:
                self.active[name] = (moves, moves.send(x))
            except StopIteration as stop:
                self.results[name] = stop.value
        return done

    def finish(self):
        while self.active:
            self.run()


def per_device(
    hidden_in,
    roi,
    bn_gain,
    bn_bias,
    w_qkv,
    bias_qv,
    w_out,
    bias_out,
    ln1_gain,
    ln1_bias,
    w_in,
    bias_in,
    w_back,
    bias_back,
    ln2_gain,
    ln2_bias,
    pair_w,
    pair_bias,
    dir_w,
    text_len,
    owner_order,
    pair_index,
    cot_out,
    cot_logits,
):
    docs = text_len.shape[0]
    slots = hidden_in.shape[0] // docs
    width = hidden_in.shape[1]
    segs = slots - TEXT
    seg_rows = roi.shape[0]
    n_dp = lax.axis_size("dp")
    all_rows = seg_rows * n_dp
    half, half_seg = TEXT // 2, segs // 2
    m = lax.axis_index("mp")
    c = m % 2
    dp = lax.axis_index("dp")
    shifts = (dp % 2, dp // 2 % 2)
    place = jnp.stack([c, *shifts]).astype(jnp.int32)
    part = w_qkv.shape[2]
    from_sib = lambda x: swap(x, "mp", 1)
    from_x = lambda x: swap(x, "mp", 2)
    later = lambda w, after: lax.optimization_barrier((w, after))[0]

    def near(k, *arrays):
        parts = []
        for w in arrays:
            size = w.shape[0] // 2
            parts.append(lax.dynamic_slice_in_dim(w, shifts[k] * size, size, 0))
        return from_x(jnp.concatenate(parts, axis=0))

    second = jnp.arange(2, dtype=jnp.int32)[:, None] == 1

    def merge(one, two, count):
        gap = one[0:1] - two[0:1]
        both = one + two
        return jnp.where(second, both + gap * gap * (0.5 * seg_rows * count), 0.5 * both)

    own = (w_out, w_in, w_back)
    close_in = near(0, w_out, w_in)
    close_back = near(1, w_back)
    own_sib = tuple(from_sib(w) for w in own)
    bias_sib, bias_x = from_sib(bias_in), from_x(bias_in)
    bias_xsib = from_sib(bias_x)
    stats = butterfly(local_stats(roi), merge)
    stats, bias_rows = lax.optimization_barrier(
        (stats, (bias_in, bias_sib, bias_x, bias_xsib))
    )
    qkv, lse, both_seg, both_txt, x_seg, x_txt = attn_fwd(
        all_rows, place, text_len, hidden_in, roi, stats, bn_gain, bn_bias, w_qkv, bias_qv
    )

    close, own_sib, both_seg, both_txt = lax.optimization_barrier(
        ((close_in, close_back), own_sib, both_seg, both_txt)
    )
    far = (swap(close[0], "dp", 1), swap(close[1], "dp", 2))
    far_seg, far_txt = from_x(both_seg), from_x(both_txt)
    close_sib = tuple(from_sib(w) for w in close)
    both_sib = (from_sib(both_seg), from_sib(both_txt))
    far, far_seg, far_txt, close_sib, both_sib = lax.optimization_barrier(
        (far, far_seg, far_txt, close_sib, both_sib)
    )
    far_sib = tuple(from_sib(w) for w in far)
    weights = ((w_out, own_sib[0]),) + tuple(
        (own[1 + k], own_sib[1 + k], close[k], far[k], close_sib[k], far_sib[k]) for k in range(2)
    )
    ctx_seg = (both_seg, both_sib[0], far_seg, from_sib(far_seg))
    ctx_txt = (both_txt, both_sib[1], far_txt, from_sib(far_txt))
    vec = (bias_out, ln1_gain, ln1_bias, bias_back, ln2_gain, ln2_bias)
    mine_rows = docs * (half + half_seg)
    txt_rows = docs * half
    seg = ffn(
        place, vec, bias_rows, weights, docs * half_seg, txt_rows, mine_rows, None,
        ctx=ctx_seg, xres=x_seg,
    )

    txt = {name: seg[name] for name in ("h1", "act0", "act1")}
    txt_sums, gwo = [], []

    def text(doc, *first):
        done = ffn(
            place, vec, bias_rows, weights, half, 0, mine_rows, None,
            ctx=ctx_txt, xres=first[0], gout=cot_out, into=txt, start=doc, count=1,
        )
        txt_sums.append(done.pop("sums"))
        gwo.append(done.pop("gwo"))
        txt.update(done)

    share = width // lax.axis_size("mp")
    cols = lambda x, who: lax.dynamic_slice_in_dim(x, who * share, share, 1)
    mine, theirs = cols(seg["out"], m), from_sib(cols(seg["out"], m ^ 1))
    by_core = lambda a, b: (jnp.where(c == 0, a, b), jnp.where(c == 0, b, a))
    columns = jnp.stack(
        [p.reshape(docs, half_seg, share) for p in by_core(mine, theirs)], axis=1
    ).reshape(seg_rows, share)
    ordering = owner_order[0]
    swap_rows = lambda x: lax.all_to_all(x, "dp", split_axis=0, concat_axis=0, tiled=True)
    ordered, x_txt = lax.optimization_barrier((jnp.take(columns, ordering, axis=0), x_txt))
    received = swap_rows(ordered)
    text(0, x_txt)
    received, x_txt = lax.optimization_barrier((received, later(x_txt, txt_sums[0])))
    candidates = jnp.arange(seg_rows, dtype=jnp.int32)[None, :]
    pick_left = (pair_index[:, 0:1] == candidates).astype(F32)
    pick_right = (pair_index[:, 1:2] == candidates).astype(F32)
    sides = jnp.concatenate([product(pick_left, received), product(pick_right, received)], axis=1)
    pair_w2 = pair_w.reshape(2 * share, width)
    pair_part = product(sides, pair_w2)
    pair_part = pair_part + from_sib(pair_part)
    pairs_half = pair_part.shape[0] // 2
    piece = lax.dynamic_slice_in_dim(pair_part, c * pairs_half, pairs_half, 0)
    piece, x_txt = lax.optimization_barrier((piece, x_txt))
    other = from_x(piece)
    if docs > 1:
        text(1, x_txt)
    piece, x_txt = lax.optimization_barrier((piece + later(other, txt_sums[-1]), x_txt))
    pair_pre = jnp.concatenate(by_core(piece, from_sib(piece)), axis=0) + pair_bias
    root = 0.5 * (1.0 + lax.erf(pair_pre * ROOT_HALF))
    pair_act = pair_pre * root
    logits = product(pair_act, dir_w)
    grad_dir_w = product(cot_logits, pair_act, ((0,), (0,)))
    grad_pair_pre = product(cot_logits, dir_w, ((1,), (1,))) * (
        root + pair_pre * jnp.exp(-0.5 * pair_pre * pair_pre) * DENSITY
    )
    grad_pair_bias = jnp.sum(grad_pair_pre, axis=0)
    grad_pair_w = product(sides, grad_pair_pre, ((0,), (0,)))
    grad_sides = product(grad_pair_pre, pair_w2, ((1,), (1,)))
    grad_received = product(pick_left, grad_sides[:, :share], ((0,), (0,))) + product(
        pick_right, grad_sides[:, share:], ((0,), (0,))
    )
    grad_received, x_txt = lax.optimization_barrier((grad_received, x_txt))
    grad_sent = swap_rows(grad_received)
    for doc in range(2, docs):
        text(doc, x_txt)
    grad_sent = later(grad_sent, txt_sums[-1])
    back_order = jnp.zeros_like(ordering).at[ordering].set(jnp.arange(seg_rows, dtype=jnp.int32))
    grad_cols = jnp.take(grad_sent, back_order, axis=0).reshape(docs, 2, half_seg, share)
    rows_of = lambda who: lax.dynamic_index_in_dim(grad_cols, who, 1, keepdims=False).reshape(
        docs * half_seg, share
    )
    grad_mine, grad_theirs = rows_of(c), from_sib(rows_of(1 - c))
    chip_cols = jnp.concatenate(by_core(grad_mine, grad_theirs), axis=1)
    far_cols = from_x(chip_cols)
    low_x = m < 2
    grad_seg = jnp.concatenate(
        [jnp.where(low_x, chip_cols, far_cols), jnp.where(low_x, far_cols, chip_cols)], axis=1
    )
    cot_seg = lax.dynamic_slice_in_dim(
        cot_out.reshape(docs, slots, width), TEXT + c * half_seg, half_seg, 1
    ).reshape(docs * half_seg, width)
    output = join_rows(
        docs, segs, place, seg["out"], txt["out"],
        from_sib(seg["out"]), from_sib(later(txt["out"], grad_cols)),
    )
    grad_seg, output = lax.optimization_barrier((grad_seg, output))
    back = ffn(
        place, vec, bias_rows, weights, docs * half_seg, txt_rows, mine_rows,
        [seg[name] for name in ("n1", "f1", "n2", "f2", "slope")],
        ctx=ctx_seg, gout=cot_seg + grad_seg,
        into={name: txt[name] for name in ("gs", "gi0", "gi1", "gf")},
    )

    tall = ((0,), (0,))
    sib_back = from_sib(product(txt["act1"], back["gs"], tall))
    sib_in = from_sib(product(txt["h1"], back["gi1"], tall))
    grad_back_own = product(txt["act0"], back["gs"], tall) + sib_back
    grad_in_own = product(txt["h1"], back["gi0"], tall) + sib_in
    gf_txt, gf_seg = back["gf"][:txt_rows], back["gf"][txt_rows:]
    gwo = sum(gwo) + back["gwo"]
    grad_out_own = gwo[:part] + from_sib(gwo[part:])

    steps = Steps()
    steps.add("in_out", ring(jnp.concatenate([grad_in_own, grad_out_own], axis=0), 1))
    steps.add("back_pair", ring(jnp.concatenate([grad_back_own, grad_pair_w], axis=0), -1))
    mine = (back["gb"], txt["gb"])
    theirs = tuple(from_sib(g) for g in mine)
    w_sum = jnp.zeros((3 * part, width), F32)
    b_sum = jnp.zeros((1, 3 * part), F32)
    gx = []
    for doc in range(docs):

        def scores(b_sum, doc=doc):
            return attn_bwd(
                doc, place, text_len, qkv, lse, (both_seg, both_txt), mine, theirs, b_sum
            )

        def weights_of(gq, w_sum, doc=doc):
            return qkv_bwd(
                all_rows, doc, docs, place, hidden_in, roi, stats, bn_gain, bn_bias, w_qkv, gq, w_sum
            )

        gq, b_sum = steps.run(scores, (b_sum,))
        gx_mine, gx_theirs, w_sum = steps.run(weights_of, (gq, w_sum))
        chip_sum = gx_mine + from_sib(gx_theirs)
        gx.append((chip_sum, from_x(chip_sum)))
    cut = w_sum.shape[0] * 5 // 9
    steps.add("qkv_low", halving(w_sum[:cut], 0))
    steps.add("qkv_high", halving(w_sum[cut:], 1))
    gh_mine, gh_theirs = [], []
    for doc in range(docs):
        first = jnp.concatenate(
            [gf_seg[doc * half_seg : (doc + 1) * half_seg], gf_txt[doc * half : (doc + 1) * half]],
            axis=0,
        )
        if doc:
            steps.run()
        (far,) = steps.run(lambda x: (x,), (gx[doc][1],))
        gh_mine.append(first + (gx[doc][0] + far))
        gh_theirs.append(from_sib(gh_mine[-1]))
    (gh_theirs[-1],) = steps.run(lambda x: (x,), (gh_theirs[-1],))
    grad_hidden, bn_sums = final_rows(all_rows, segs, place, gh_mine, gh_theirs, roi, stats)

    rows = sum(txt_sums) + back["sums"]
    rows = jnp.concatenate([rows[:6], rows[6:7]]) + from_sib(jnp.concatenate([rows[:6], rows[7:8]]))
    pad = lambda v: jnp.pad(v, (0, width - v.shape[0]))[None]
    vectors = jnp.concatenate(
        [
            rows,
            grad_pair_bias[None],
            grad_dir_w,
            pad(b_sum[0, :part]),
            pad(b_sum[0, 2 * part :]),
            bn_sums[0:2],
        ],
        axis=0,
    )
    steps.add("vectors", cube(vectors))
    steps.finish()
    vectors, in_out, back_pair, low, high = (
        steps.results[name] for name in ("vectors", "in_out", "back_pair", "qkv_low", "qkv_high")
    )
    sum_qkv = jnp.concatenate([low, high], axis=0)
    n_dirs = dir_w.shape[1]
    sum_dir_w = vectors[8 : 8 + n_dirs].T
    tail = vectors[8 + n_dirs :]
    sum_bias_qv = tail[0:2, :part]
    grad_bn_bias, grad_bn_gain = tail[2], tail[3]
    grad_roi_out = grad_hidden.reshape(docs, slots, width)[:, TEXT:].reshape(seg_rows, width)
    roi_factor = lax.rsqrt(stats[1] / all_rows + EPSILON)
    roi_normed = (roi - stats[0]) * roi_factor
    grad_roi = (
        bn_gain
        * roi_factor
        * (grad_roi_out - grad_bn_bias / all_rows - roi_normed * grad_bn_gain / all_rows)
    )
    return (
        output,
        logits,
        grad_hidden,
        grad_roi,
        grad_bn_gain,
        grad_bn_bias,
        jnp.transpose(sum_qkv.reshape(3, part, width), (0, 2, 1)),
        sum_bias_qv,
        in_out[width:],
        vectors[5],
        vectors[3],
        vectors[4],
        in_out[:width],
        vectors[6],
        back_pair[:width],
        vectors[2],
        vectors[0],
        vectors[1],
        back_pair[width:].reshape(2, share, width),
        vectors[7],
        sum_dir_w,
    )


def solution(mesh):
    placed = (
        P("dp", None),
        P("dp", None),
        P(),
        P(),
        P(None, None, "mp"),
        P(None, "mp"),
        P("mp", None),
        P(),
        P(),
        P(),
        P(None, "mp"),
        P("mp"),
        P("mp", None),
        P(),
        P(),
        P(),
        P(None, "mp", None),
        P(),
        P(),
        P("dp"),
        P("dp", None),
        P("dp", None),
        P("dp", None),
        P("dp", None),
    )
    return jax.shard_map(
        per_device,
        mesh=mesh,
        in_specs=placed,
        out_specs=(
            P("dp", None),
            P("dp", None),
            P("dp", None),
            P("dp", None),
            P(),
            P(),
            P(None, None, "mp"),
            P(None, "mp"),
            P("mp", None),
            P(),
            P(),
            P(),
            P(None, "mp"),
            P("mp"),
            P("mp", None),
            P(),
            P(),
            P(),
            P(None, "mp", None),
            P(),
            P(),
        ),
        check_vma=False,
    )
```

time: 1280 us -> 677 us (0.53)
  waiting for transfers between devices: 659 us -> 189 us
  matrix products: 320 us -> 35.6 us
  Pallas kernels: 0 us -> 248 us
  blocking collectives: 98.9 us -> 0 us
  starting transfers between devices: 6.42 us -> 87.5 us
  local copies, waits for them, and re-layouts: 92.8 us -> 52.7 us
  other arithmetic: 74.7 us -> 54.3 us
    psum x6 -> x0, waiting for transfers between devices: 638 us -> none  [the longest x1 226 us: per_device(): lax.psum((grad_w_qkv, grad_bias_qv, grad_w_out, grad_bias_out, grad_ln1_g...]
    dot_general x52 -> x14, matrix products: 320 us -> 35.6 us  [product(): lax.dot_general(operand, other, (dims, ((), ())), precision=HIGH, preferr...]
    pallas_call x0 -> x17, Pallas kernels: none -> 248 us  [the longest x5 147 us: ffn(): pl.pallas_call(functools.partial(ffn_kernel, forward, backward, all_names...]
    ppermute x0 -> x89, waiting for transfers between devices: none -> 189 us  [the longest x43 97.1 us: run(): lax.ppermute(x, *self.active[name][1][1:])]
    psum x3 -> x0, blocking collectives: 82.1 us -> none  [the longest x1 41.8 us: per_device(): lax.psum((jnp.sum(grad_roi_out, axis=0), jnp.sum(grad_roi_out * roi_norme...]
    ppermute x0 -> x89, starting transfers between devices: none -> 77.1 us  [the longest x43 52.3 us: run(): lax.ppermute(x, *self.active[name][1][1:])]
    reduce_sum x21 -> x0, other arithmetic: 54.6 us -> none  [the longest x2 11.1 us: normalize(): center = values - jnp.mean(values, axis=-1, keepdims=True)]
    add x4 -> x36, other arithmetic: 8.86 us -> 41.9 us  [the longest x14 23.8 us: ring(): held = got + lax.dynamic_slice_in_dim(part, at(step), size, 0)]
  transfers between devices with their start and end apart: 8 -> 91, of which waited for: 8 -> 34; matrix products, arithmetic and copies ran while one was open for 7% -> 15% of each run, Pallas kernels for 0% -> 31%
where the time goes in v2:
time: 677 us; the launch traced here: 669 us
  Pallas kernels  248 us (37%)
  waiting for transfers between devices  189 us (28%)
  starting transfers between devices  87.5 us (13%)
  other arithmetic  54.3 us (8%)
  local copies, waits for them, and re-layouts  52.7 us (8%)
  matrix products  35.6 us (5%)
    pallas_call x5, Pallas kernels, ffn(): pl.pallas_call(functools.partial(ffn_kernel, forward, backward, all_names...  147 us
    ppermute x43, waiting for transfers between devices, run(): lax.ppermute(x, *self.active[name][1][1:])  97.1 us
    ppermute x46, waiting for transfers between devices, swap(): return lax.ppermute(x, axis, [(i, i ^ bit) for i in range(n)])  91.7 us
    ppermute x43, starting transfers between devices, run(): lax.ppermute(x, *self.active[name][1][1:])  52.3 us
    dot_general x14, matrix products, product(): lax.dot_general(operand, other, (dims, ((), ())), precision=HIGH, preferr...  35.6 us
    pallas_call x3, Pallas kernels, attn_bwd(): pl.pallas_call(functools.partial(attn_bwd_kernel, doc), grid=(1,), in_spe...  28.1 us
    pallas_call x3, Pallas kernels, qkv_bwd(): pl.pallas_call(functools.partial(qkv_bwd_kernel, all_rows), grid=(1,), in...  28.1 us
    ppermute x46, starting transfers between devices, swap(): return lax.ppermute(x, axis, [(i, i ^ bit) for i in range(n)])  24.8 us
  transfers between devices with their start and end apart: 91, of which 34 were waited for; matrix products, arithmetic and copies ran while one was open for 15% of the time, Pallas kernels for 31%

profile of v2, /device:TPU:0, one launch (start us, length us, event | category | flops | bytes accessed | tf_op | source)
XLA Modules:
  0.0 669.2 jit_solution(13445282498407092707)
XLA Ops:
  1.3 2.2 local_stats.1
  3.4 2.9 collective-permute-start.5
  12.0 2.4 constant_dynamic-slice_fusion.10
  17.6 2.1 collective-permute-done.6
  22.4 2.6 collective-permute-start.7
  30.9 22.3 %attn_fwd.1 = (f32[1920,576]{1,0:T(8,128)}, f32[24,640]{1,0:T(8,128)}, f32[192,384]{1,0:T(8,128)}, f32[768,384]{1,0:T(8,128)}, f32[192,768]{1,0:T(8,128)}, /*index=5*/f32[768,768]{1,0:T(8,128)}) custom-call(s32[3]{0:T(128)} %pad_add_fusion.refs_0_.place, s32[3]{0:T(128)} %refs_1_.22, f32[1920,768]{1,0:T(8,128)} %refs_1_.23, f32[384,768]{1,0:T(8,128)} %refs_7_.2, ...), custom_call_target="tpu_custom_call" | custom-call | flops 11520 | bytes 640 | tf_op jit(solution)/shard_map/attn_fwd/pallas_call | solution.py:189
  53.3 17.5 %collective-permute-done.1.refs_27_.refs_28_.refs_24_ = f32[384,768]{1,0:T(8,128)} collective-permute-done((f32[384,768]{1,0:T(8,128)}, f32[384,768]{1,0:T(8,128)}, u32[]{:S(2)}, u32[]{:S(2)}) %collective-permute-start.1) | collective-permute-done | bytes 1179680 | tf_op jit(solution)/shard_map/ppermute | solution.py:671
  73.7 6.2 collective-permute-done.13.refs_9_
  80.5 17.1 %collective-permute-done.12.refs_29_.refs_30_.refs_26_ = f32[384,768]{1,0:T(8,128)} collective-permute-done((f32[384,768]{1,0:T(8,128)}, f32[384,768]{1,0:T(8,128)}, u32[]{:S(2)}, u32[]{:S(2)}) %collective-permute-start.12) | collective-permute-done | bytes 1179680 | tf_op jit(solution)/shard_map/ppermute | solution.py:671
  97.6 10.8 %collective-permute-done.14.refs_9_ = f32[768,384]{1,0:T(8,128)S(1)} collective-permute-done((f32[768,384]{1,0:T(8,128)}, f32[768,384]{1,0:T(8,128)S(1)}, u32[]{:S(2)}, u32[]{:S(2)}) %collective-permute-start.14) | collective-permute-done | bytes 1179680 | tf_op jit(solution)/shard_map/ppermute | solution.py:671
  111.5 2.6 collective-permute-done.19.refs_10_
  114.8 21.2 %ffn_fwd.1 = (f32[192,768]{1,0:T(8,128)}, f32[960,768]{1,0:T(8,128)}, f32[960,768]{1,0:T(8,128)}, f32[960,768]{1,0:T(8,128)}, f32[192,768]{1,0:T(8,128)}, /*inde...) custom-call(s32[3]{0:T(128)} %pad_add_fusion.refs_0_.place, f32[768]{0:T(1024)} %refs_1_.17, ...), custom_call_target="tpu_custom_call" | custom-call | flops 16307453952 | bytes 8847360 | tf_op jit(solution)/shard_map/ffn_fwd/pallas_call | solution.py:569
  142.3 4.3 all-to-all-start
  146.6 33.7 %ffn_fwdbwd.3 = (f32[768,768]{1,0:T(8,128)}, f32[960,768]{1,0:T(8,128)}, f32[960,768]{1,0:T(8,128)}, f32[960,768]{1,0:T(8,128)}, f32[960,768]{1,0:T(8,128)}, /*i...) custom-call(s32[3]{0:T(128)} %pad_add_fusion.refs_0_.place, ...), custom_call_target="tpu_custom_call", output_to_operand_aliasing={{1}: (35, {}), {2}: (36, {}), {3}: (37, {})} | custom-call | flops 25367150592 | bytes 11796480 | tf_op jit(solution)/shard_map/ffn_fwdbwd/pallas_call | solution.py:569
  182.3 3.1 scatter_custom_fusion
  186.3 33.8 %ffn_fwdbwd.4 = (f32[768,768]{1,0:T(8,128)}, f32[960,768]{1,0:T(8,128)}, f32[960,768]{1,0:T(8,128)}, f32[960,768]{1,0:T(8,128)}, f32[960,768]{1,0:T(8,128)}, /*i...) custom-call(s32[3]{0:T(128)} %pad_add_fusion.refs_0_.place, ...), custom_call_target="tpu_custom_call", output_to_operand_aliasing={{0}: (35, {}), {1}: (36, {}), {2}: (37, {}), {3}: (38, {}),... | custom-call | flops 25367150592 | bytes 11796480 | tf_op jit(solution)/shard_map/ffn_fwdbwd/pallas_call | solution.py:569
  225.6 6.1 all-to-all-start.1
  231.7 33.7 %ffn_fwdbwd.5 = (f32[768,768]{1,0:T(8,128)}, f32[960,768]{1,0:T(8,128)}, f32[960,768]{1,0:T(8,128)}, f32[960,768]{1,0:T(8,128)}, f32[960,768]{1,0:T(8,128)}, /*i...) custom-call(s32[3]{0:T(128)} %pad_add_fusion.refs_0_.place, ...), custom_call_target="tpu_custom_call", output_to_operand_aliasing={{0}: (35, {}), {1}: (36, {}), {2}: (37, {}), {3}: (38, {}),... | custom-call | flops 25367150592 | bytes 11796480 | tf_op jit(solution)/shard_map/ffn_fwdbwd/pallas_call | solution.py:569
  267.9 3.8 collective-permute-done.27
  274.4 7.0 %collective-permute-done.28 = f32[192,384]{1,0:T(8,128)} collective-permute-done((f32[192,384]{1,0:T(8,128)S(1)}, f32[192,384]{1,0:T(8,128)}, u32[]{:S(2)}, u32[]{:S(2)}) %collective-permute-start.28) | collective-permute-done | bytes 294944 | tf_op jit(solution)/shard_map/ppermute | solution.py:671
  282.5 6.5 join_rows.1
  289.8 24.6 %ffn_bwd.1 = (f32[960,768]{1,0:T(8,128)}, f32[960,768]{1,0:T(8,128)}, f32[960,768]{1,0:T(8,128)}, f32[960,768]{1,0:T(8,128)}, f32[192,384]{1,0:T(8,128)}, /*index=5*/f32[384,768]{1,0:T(8,128)}, f32[8,768]{1,0:T(8,128)}) custom-call(s32[3]{0:T(128)} %pad_add_fusion.refs_0_.place, ...), custom_call_target="tpu_custom_call", output_to_operand_aliasing={{0}: (31, {}), {1}: (32, {}), {2}: (33, {}), {3}: (34, {})} | custom-call | flops 16307453952 | bytes 8847360 | tf_op jit(solution)/shard_map/ffn_bwd/pallas_call | solution.py:569
  314.5 8.9 %fusion.68 = f32[768,768]{1,0:T(8,128)} fusion(f32[960,768]{1,0:T(8,128)} %get-tuple-element.331, f32[960,768]{1,0:T(8,128)} %get-tuple-element.330), kind=kOutput, calls=%fused_computation.205 | convolution fusion | flops 3397386240 | bytes 8257536 | tf_op jit(solution)/shard_map/dot_general | solution.py:24
  323.5 6.1 fusion.67
  332.5 2.9 collective-permute-done.32
  336.6 7.7 %convolution_add_fusion = f32[768,768]{1,0:T(8,128)S(1)} fusion(f32[768,768]{1,0:T(8,128)} %collective-permute-done.33, f32[960,768]{1,0:T(8,128)S(1)} %copy-done.30, f32[960,768]{1,0:T(8,128)} %get-tuple-element.330), kind=kOutput, calls=%fused_computation.36 | convolution fusion | flops 3397976064 | bytes 10616832 | tf_op jit(solution)/shard_map/dot_general | solution.py:24
  344.3 6.2 convolution_add_fusion.1
  352.2 2.0 collective-permute-start.35
  354.8 9.4 %attn_bwd.3 = (f32[640,576]{1,0:T(8,128)}, f32[1,576]{1,0:T(1,128)}) custom-call(s32[3]{0:T(128)} %pad_add_fusion.refs_0_.place, s32[3]{0:T(128)} %refs_1_.22, f32[1920,576]{1,0:T(8,128)} %get-tuple-element.334.refs_2_, f32[24,640]{1,0:T(8,128)} %get-tuple-element.335.refs_3_, f32[192,384]{1,0:T(8,128)} %get-tuple-element.249.refs_7_.refs_4_, ...), custom_call_target="tpu_custom_call" | custom-call | flops 7549747200 | bytes 2949120 | tf_op jit(solution)/shard_map/attn_bwd/pallas_call | solution.py:276
  367.8 2.2 collective-permute-start.39
  371.3 9.4 %qkv_bwd.3 = (f32[320,768]{1,0:T(8,128)}, f32[320,768]{1,0:T(8,128)}, f32[576,768]{1,0:T(8,128)}) custom-call(s32[3]{0:T(128)} %pad_add_fusion.refs_0_.place, f32[1920,768]{1,0:T(8,128)} %refs_1_.23, f32[384,768]{1,0:T(8,128)} %refs_7_.2, f32[2,768]{1,0:T(2,128)} %multiply_select_fusion.refs_4_.refs_3_.refs_8_, f32[768]{0:T(1024)} %refs_4_.15, ...), custom_call_target="tpu_custom_call" | custom-call | flops 3397386240 | bytes 5898240 | tf_op jit(solution)/shard_map/qkv_bwd/pallas_call | solution.py:318
  386.6 9.4 %attn_bwd.4 = (f32[640,576]{1,0:T(8,128)}, f32[1,576]{1,0:T(1,128)}) custom-call(s32[3]{0:T(128)} %pad_add_fusion.refs_0_.place, s32[3]{0:T(128)} %refs_1_.22, f32[1920,576]{1,0:T(8,128)} %get-tuple-element.334.refs_2_, f32[24,640]{1,0:T(8,128)} %get-tuple-element.335.refs_3_, f32[192,384]{1,0:T(8,128)} %get-tuple-element.249.refs_7_.refs_4_, ...), custom_call_target="tpu_custom_call" | custom-call | flops 7549747200 | bytes 2949120 | tf_op jit(solution)/shard_map/attn_bwd/pallas_call | solution.py:276
  396.3 2.0 fusion.14
  402.2 9.4 %qkv_bwd.4 = (f32[320,768]{1,0:T(8,128)}, f32[320,768]{1,0:T(8,128)}, f32[576,768]{1,0:T(8,128)}) custom-call(s32[3]{0:T(128)} %pad_add_fusion.refs_0_.place, f32[1920,768]{1,0:T(8,128)} %refs_1_.23, f32[384,768]{1,0:T(8,128)} %refs_7_.2, f32[2,768]{1,0:T(2,128)} %multiply_select_fusion.refs_4_.refs_3_.refs_8_, f32[768]{0:T(1024)} %refs_4_.15, ...), custom_call_target="tpu_custom_call" | custom-call | flops 3397386240 | bytes 5898240 | tf_op jit(solution)/shard_map/qkv_bwd/pallas_call | solution.py:318
  417.7 9.3 %attn_bwd.5 = (f32[640,576]{1,0:T(8,128)}, f32[1,576]{1,0:T(1,128)}) custom-call(s32[3]{0:T(128)} %pad_add_fusion.refs_0_.place, s32[3]{0:T(128)} %refs_1_.22, f32[1920,576]{1,0:T(8,128)} %get-tuple-element.334.refs_2_, f32[24,640]{1,0:T(8,128)} %get-tuple-element.335.refs_3_, f32[192,384]{1,0:T(8,128)} %get-tuple-element.249.refs_7_.refs_4_, ...), custom_call_target="tpu_custom_call" | custom-call | flops 7549747200 | bytes 2949120 | tf_op jit(solution)/shard_map/attn_bwd/pallas_call | solution.py:276
  433.2 2.6 add.506
  437.0 9.4 %qkv_bwd.5 = (f32[320,768]{1,0:T(8,128)}, f32[320,768]{1,0:T(8,128)}, f32[576,768]{1,0:T(8,128)}) custom-call(s32[3]{0:T(128)} %pad_add_fusion.refs_0_.place, f32[1920,768]{1,0:T(8,128)} %refs_1_.23, f32[384,768]{1,0:T(8,128)} %refs_7_.2, f32[2,768]{1,0:T(2,128)} %multiply_select_fusion.refs_4_.refs_3_.refs_8_, f32[768]{0:T(1024)} %refs_4_.15, ...), custom_call_target="tpu_custom_call" | custom-call | flops 3397386240 | bytes 5898240 | tf_op jit(solution)/shard_map/qkv_bwd/pallas_call | solution.py:318
  455.5 3.4 collective-permute-done.49
  463.2 15.3 %collective-permute-done.50 = f32[120,768]{1,0:T(8,128)} collective-permute-done((f32[120,768]{1,0:T(8,128)}, f32[120,768]{1,0:T(8,128)}, u32[]{:S(2)}, u32[]{:S(2)}) %collective-permute-start.50) | collective-permute-done | bytes 368672 | tf_op jit(solution)/shard_map/ppermute | solution.py:765
  488.1 2.2 collective-permute-start.56
  492.5 3.4 collective-permute-start.58
  495.8 9.6 %collective-permute-done.58 = f32[64,768]{1,0:T(8,128)S(1)} collective-permute-done((f32[64,768]{1,0:T(8,128)}, f32[64,768]{1,0:T(8,128)S(1)}, u32[]{:S(2)}, u32[]{:S(2)}) %collective-permute-start.58) | collective-permute-done | bytes 196640 | tf_op jit(solution)/shard_map/ppermute | solution.py:765
  513.4 2.1 collective-permute-start.62
  516.2 10.3 %collective-permute-done.63 = f32[32,768]{1,0:T(8,128)} collective-permute-done((f32[32,768]{1,0:T(8,128)}, f32[32,768]{1,0:T(8,128)}, u32[]{:S(2)}, u32[]{:S(2)}) %collective-permute-start.63) | collective-permute-done | bytes 98336 | tf_op jit(solution)/shard_map/ppermute | solution.py:765
  529.2 4.2 collective-permute-start.66
  536.2 2.1 collective-permute-start.67
  538.5 7.2 %collective-permute-done.68 = f32[32,768]{1,0:T(8,128)S(1)} collective-permute-done((f32[32,768]{1,0:T(8,128)S(1)}, f32[32,768]{1,0:T(8,128)S(1)}, u32[]{:S(2)}, u32[]{:S(2)}) %collective-permute-start.68) | collective-permute-done | bytes 98336 | tf_op jit(solution)/shard_map/ppermute | solution.py:765
  545.7 2.8 collective-permute-done.67
  548.6 9.5 %collective-permute-done.69 = f32[320,768]{1,0:T(8,128)S(1)} collective-permute-done((f32[320,768]{1,0:T(8,128)S(1)}, f32[320,768]{1,0:T(8,128)S(1)}, u32[]{:S(2)}, u32[]{:S(2)}) %collective-permute-start.69) | collective-permute-done | bytes 983072 | tf_op jit(solution)/shard_map/ppermute | solution.py:671
  560.9 3.1 collective-permute-start.73
  565.8 10.3 %collective-permute-done.73 = f32[64,768]{1,0:T(8,128)S(1)} collective-permute-done((f32[64,768]{1,0:T(8,128)S(1)}, f32[64,768]{1,0:T(8,128)S(1)}, u32[]{:S(2)}, u32[]{:S(2)}) %collective-permute-start.73) | collective-permute-done | bytes 196640 | tf_op jit(solution)/shard_map/ppermute | solution.py:765
  576.0 2.3 collective-permute-done.72
  581.7 2.2 collective-permute-start.77
  587.6 5.6 collective-permute-done.77.refs_5_
  596.0 10.6 %collective-permute-done.80 = f32[128,768]{1,0:T(8,128)S(1)} collective-permute-done((f32[128,768]{1,0:T(8,128)S(1)}, f32[128,768]{1,0:T(8,128)S(1)}, u32[]{:S(2)}, u32[]{:S(2)}) %collective-permute-start.80) | collective-permute-done | bytes 393248 | tf_op jit(solution)/shard_map/ppermute | solution.py:765
  608.3 5.9 final_rows.1
  615.0 2.1 concatenate.70
  621.8 7.4 %collective-permute-done.84 = f32[20,768]{1,0:T(8,128)S(1)} collective-permute-done((f32[20,768]{1,0:T(8,128)S(1)}, f32[20,768]{1,0:T(8,128)S(1)}, u32[]{:S(2)}, u32[]{:S(2)}) %collective-permute-start.84) | collective-permute-done | bytes 61472 | tf_op jit(solution)/shard_map/ppermute | solution.py:765
  632.6 10.2 %collective-permute-done.87 = f32[20,768]{1,0:T(8,128)S(1)} collective-permute-done((f32[20,768]{1,0:T(8,128)S(1)}, f32[20,768]{1,0:T(8,128)S(1)}, u32[]{:S(2)}, u32[]{:S(2)}) %collective-permute-start.87) | collective-permute-done | bytes 61472 | tf_op jit(solution)/shard_map/ppermute | solution.py:765
  647.1 4.0 assemble.3
  651.1 3.2 slice.217
  654.3 2.4 slice.221
  656.7 3.6 assemble.2
  660.3 3.4 slice.215
  (461 shorter events, 154.9 us)
Async XLA Ops:
  0.7 70.1 %collective-permute-start.3 = (f32[768,768]{1,0:T(8,128)}, f32[768,768]{1,0:T(8,128)}, u32[]{:S(2)}, u32[]{:S(2)}) collective-permute-start(f32[768,768]{1,0:T(8,128)} %refs_19_.1), channel_id=1, source_target_pairs={{0,1},{1,0},{2,3},{3,2},{4,5},{5,4},{6,7},{7,6},{8,9},{9,8},{10,11... | collective-permute-start | bytes 7077896 | tf_op jit(solution)/shard_map/ppermute | solution.py:671
  1.2 69.6 %collective-permute-start.4 = (f32[768,768]{1,0:T(8,128)}, f32[768,768]{1,0:T(8,128)}, u32[]{:S(2)}, u32[]{:S(2)}) collective-permute-start(f32[768,768]{1,0:T(8,128)} %refs_20_.1), channel_id=1, source_target_pairs={{0,1},{1,0},{2,3},{3,2},{4,5},{5,4},{6,7},{7,6},{8,9},{9,8},{10,11... | collective-permute-start | bytes 7077896 | tf_op jit(solution)/shard_map/ppermute | solution.py:671
  3.4 10.9 %collective-permute-start.5 = (f32[2,768]{1,0:T(2,128)}, f32[2,768]{1,0:T(2,128)S(1)}, u32[]{:S(2)}, u32[]{:S(2)}) collective-permute-start(f32[2,768]{1,0:T(2,128)} %local_stats.1), channel_id=1, source_target_pairs={{0,4},{4,0},{8,12},{12,8},{16,20},{20,16},{24,28},{28,24},{1,5},{5... | collective-permute-start | bytes 18440 | tf_op jit(solution)/shard_map/ppermute | solution.py:671
  11.4 59.3 %collective-permute-start = (f32[480,768]{1,0:T(8,128)}, f32[480,768]{1,0:T(8,128)}, u32[]{:S(2)}, u32[]{:S(2)}) collective-permute-start(f32[480,768]{1,0:T(8,128)} %pad_maximum_fusion.1), channel_id=1, source_target_pairs={{0,2},{1,3},{2,0},{3,1},{4,6},{5,7},{6,4},{7,5},{8,10},{9,11},{10,... | collective-permute-start | bytes 4423688 | tf_op jit(solution)/shard_map/ppermute | solution.py:671
  14.3 56.4 %collective-permute-start.1 = (f32[384,768]{1,0:T(8,128)}, f32[384,768]{1,0:T(8,128)}, u32[]{:S(2)}, u32[]{:S(2)}) collective-permute-start(f32[384,768]{1,0:T(8,128)} %constant_dynamic-slice_fusion.10), channel_id=1, source_target_pairs={{0,2},{1,3},{2,0},{3,1},{4,6},{5,7},{6,4},{7,5},{8,10},{9,11},{10,... | collective-permute-start | bytes 3538952 | tf_op jit(solution)/shard_map/ppermute | solution.py:671
  27.0 26.3 %collective-permute-start.2 = (f32[192,768]{1,0:T(8,128)S(1)}, f32[192,768]{1,0:T(8,128)}, u32[]{:S(2)}, u32[]{:S(2)}) collective-permute-start(f32[192,768]{1,0:T(8,128)S(1)} %copy-done.67), channel_id=1, source_target_pairs={{0,1},{1,0},{2,3},{3,2},{4,5},{5,4},{6,7},{7,6},{8,9},{9,8},{10,11... | collective-permute-start | bytes 1769480 | tf_op jit(solution)/shard_map/ppermute | solution.py:671
  70.8 26.9 %collective-permute-start.12 = (f32[384,768]{1,0:T(8,128)}, f32[384,768]{1,0:T(8,128)}, u32[]{:S(2)}, u32[]{:S(2)}) collective-permute-start(f32[384,768]{1,0:T(8,128)} %collective-permute-done.1.refs_27_.refs_28_.refs_24_), channel_id=1, source_target_pairs={{0,8},{4,12},{8,0},{12,4},{16,24},{20,28},{24,16},{28,20},{1,9},{5... | collective-permute-start | bytes 3538952 | tf_op jit(solution)/shard_map/ppermute | solution.py:671
  72.9 35.6 %collective-permute-start.11 = (f32[480,768]{1,0:T(8,128)}, f32[480,768]{1,0:T(8,128)}, u32[]{:S(2)}, u32[]{:S(2)}) collective-permute-start(f32[480,768]{1,0:T(8,128)} %collective-permute-done.refs_18_.refs_26_.refs_19_.refs_27_.refs_23_), channel_id=1, source_target_pairs={{0,4},{4,0},{8,12},{12,8},{16,20},{20,16},{24,28},{28,24},{1,5},{5... | collective-permute-start | bytes 4423688 | tf_op jit(solution)/shard_map/ppermute | solution.py:671
  73.5 35.1 %collective-permute-start.15 = (f32[480,768]{1,0:T(8,128)}, f32[480,768]{1,0:T(8,128)S(1)}, u32[]{:S(2)}, u32[]{:S(2)}) collective-permute-start(f32[480,768]{1,0:T(8,128)} %collective-permute-done.refs_18_.refs_26_.refs_19_.refs_27_.refs_23_), channel_id=1, source_target_pairs={{0,1},{1,0},{2,3},{3,2},{4,5},{5,4},{6,7},{7,6},{8,9},{9,8},{10,11... | collective-permute-start | bytes 4423688 | tf_op jit(solution)/shard_map/ppermute | solution.py:671
  79.9 28.6 %collective-permute-start.16 = (f32[384,768]{1,0:T(8,128)}, f32[384,768]{1,0:T(8,128)S(1)}, u32[]{:S(2)}, u32[]{:S(2)}) collective-permute-start(f32[384,768]{1,0:T(8,128)} %collective-permute-done.1.refs_27_.refs_28_.refs_24_), channel_id=1, source_target_pairs={{0,1},{1,0},{2,3},{3,2},{4,5},{5,4},{6,7},{7,6},{8,9},{9,8},{10,11... | collective-permute-start | bytes 3538952 | tf_op jit(solution)/shard_map/ppermute | solution.py:671
  79.9 28.6 %collective-permute-start.14 = (f32[768,384]{1,0:T(8,128)}, f32[768,384]{1,0:T(8,128)S(1)}, u32[]{:S(2)}, u32[]{:S(2)}) collective-permute-start(f32[768,384]{1,0:T(8,128)} %get-tuple-element.252.refs_7_.refs_5_), channel_id=1, source_target_pairs={{0,2},{1,3},{2,0},{3,1},{4,6},{5,7},{6,4},{7,5},{8,10},{9,11},{10,... | collective-permute-start | bytes 3538952 | tf_op jit(solution)/shard_map/ppermute | solution.py:671
  111.3 35.2 %collective-permute-start.23 = (f32[768,384]{1,0:T(8,128)}, f32[768,384]{1,0:T(8,128)}, u32[]{:S(2)}, u32[]{:S(2)}) collective-permute-start(f32[768,384]{1,0:T(8,128)} %copy-done.86), channel_id=1, source_target_pairs={{0,1},{1,0},{2,3},{3,2},{4,5},{5,4},{6,7},{7,6},{8,9},{9,8},{10,11... | collective-permute-start | bytes 3538952 | tf_op jit(solution)/shard_map/ppermute | solution.py:671
  142.3 38.0 %all-to-all-start = ((f32[8,48,192]{2,1,0:T(8,128)}), f32[8,48,192]{2,1,0:T(8,128)S(1)}, u32[]{:S(2)}, u32[]{:S(2)}) async-start(f32[8,48,192]{2,1,0:T(8,128)} %bitcast.8), calls=%async_computation | async-start | bytes 786432 | tf_op jit(solution)/shard_map/all_to_all | solution.py:897
  185.5 34.7 %collective-permute-start.25 = (f32[128,768]{1,0:T(8,128)S(1)}, f32[128,768]{1,0:T(8,128)S(1)}, u32[]{:S(2)}, u32[]{:S(2)}) collective-permute-start(f32[128,768]{1,0:T(8,128)S(1)} %dynamic-slice_add_fusion.1), channel_id=1, source_target_pairs={{0,2},{1,3},{2,0},{3,1},{4,6},{5,7},{6,4},{7,5},{8,10},{9,11},{10,... | collective-permute-start | bytes 1179656 | tf_op jit(solution)/shard_map/ppermute | solution.py:671
  225.6 39.8 %all-to-all-start.1 = ((f32[8,48,192]{2,1,0:T(8,128)}), f32[8,48,192]{2,1,0:T(8,128)S(1)}, u32[]{:S(2)}, u32[]{:S(2)}) async-start(f32[8,48,192]{2,1,0:T(8,128)} %bitcast.12), calls=%async_computation.1 | async-start | bytes 786432 | tf_op jit(solution)/shard_map/all_to_all | solution.py:897
  267.2 15.3 %collective-permute-start.30 = (f32[768,768]{1,0:T(8,128)}, f32[768,768]{1,0:T(8,128)}, u32[]{:S(2)}, u32[]{:S(2)}) collective-permute-start(f32[768,768]{1,0:T(8,128)} %get-tuple-element.309.mt), channel_id=1, source_target_pairs={{0,1},{1,0},{2,3},{3,2},{4,5},{5,4},{6,7},{7,6},{8,9},{9,8},{10,11... | collective-permute-start | bytes 7077896 | tf_op jit(solution)/shard_map/ppermute | solution.py:671
  323.4 13.1 %collective-permute-start.33 = (f32[768,768]{1,0:T(8,128)}, f32[768,768]{1,0:T(8,128)}, u32[]{:S(2)}, u32[]{:S(2)}) collective-permute-start(f32[768,768]{1,0:T(8,128)} %fusion.68), channel_id=1, source_target_pairs={{0,1},{1,0},{2,3},{3,2},{4,5},{5,4},{6,7},{7,6},{8,9},{9,8},{10,11... | collective-permute-start | bytes 7077896 | tf_op jit(solution)/shard_map/ppermute | solution.py:671
  329.5 14.7 %collective-permute-start.31 = (f32[768,768]{1,0:T(8,128)}, f32[768,768]{1,0:T(8,128)}, u32[]{:S(2)}, u32[]{:S(2)}) collective-permute-start(f32[768,768]{1,0:T(8,128)} %fusion.67), channel_id=1, source_target_pairs={{0,1},{1,0},{2,3},{3,2},{4,5},{5,4},{6,7},{7,6},{8,9},{9,8},{10,11... | collective-permute-start | bytes 7077896 | tf_op jit(solution)/shard_map/ppermute | solution.py:671
  331.2 23.0 %collective-permute-start.37 = (f32[768,384]{1,0:T(8,128)}, f32[768,384]{1,0:T(8,128)}, u32[]{:S(2)}, u32[]{:S(2)}) collective-permute-start(f32[768,384]{1,0:T(8,128)} %get-tuple-element.337.refs_7_), channel_id=1, source_target_pairs={{0,1},{1,0},{2,3},{3,2},{4,5},{5,4},{6,7},{7,6},{8,9},{9,8},{10,11... | collective-permute-start | bytes 3538952 | tf_op jit(solution)/shard_map/ppermute | solution.py:671
  332.4 21.9 %collective-permute-start.36 = (f32[192,384]{1,0:T(8,128)}, f32[192,384]{1,0:T(8,128)}, u32[]{:S(2)}, u32[]{:S(2)}) collective-permute-start(f32[192,384]{1,0:T(8,128)} %get-tuple-element.336.refs_6_), channel_id=1, source_target_pairs={{0,1},{1,0},{2,3},{3,2},{4,5},{5,4},{6,7},{7,6},{8,9},{9,8},{10,11... | collective-permute-start | bytes 884744 | tf_op jit(solution)/shard_map/ppermute | solution.py:671
  352.2 12.9 %collective-permute-start.35 = (f32[144,768]{1,0:T(8,128)}, f32[144,768]{1,0:T(8,128)S(1)}, u32[]{:S(2)}, u32[]{:S(2)}) collective-permute-start(f32[144,768]{1,0:T(8,128)} %fusion.8), channel_id=1, source_target_pairs={{0,4},{8,0},{16,8},{24,16},{28,24},{20,28},{12,20},{4,12},{1,5},{9... | collective-permute-start | bytes 1327112 | tf_op jit(solution)/shard_map/ppermute | solution.py:765
  367.8 12.9 %collective-permute-start.39 = (f32[144,768]{1,0:T(8,128)}, f32[144,768]{1,0:T(8,128)}, u32[]{:S(2)}, u32[]{:S(2)}) collective-permute-start(f32[144,768]{1,0:T(8,128)} %fusion.10), channel_id=1, source_target_pairs={{0,4},{8,0},{16,8},{24,16},{28,24},{20,28},{12,20},{4,12},{1,5},{9... | collective-permute-start | bytes 1327112 | tf_op jit(solution)/shard_map/ppermute | solution.py:765
  384.4 12.0 %collective-permute-start.42 = (f32[144,768]{1,0:T(8,128)S(1)}, f32[144,768]{1,0:T(8,128)}, u32[]{:S(2)}, u32[]{:S(2)}) collective-permute-start(f32[144,768]{1,0:T(8,128)S(1)} %fusion.12), channel_id=1, source_target_pairs={{0,4},{8,0},{16,8},{24,16},{28,24},{20,28},{12,20},{4,12},{1,5},{9... | collective-permute-start | bytes 1327112 | tf_op jit(solution)/shard_map/ppermute | solution.py:765
  400.2 11.4 %collective-permute-start.44 = (f32[144,768]{1,0:T(8,128)}, f32[144,768]{1,0:T(8,128)}, u32[]{:S(2)}, u32[]{:S(2)}) collective-permute-start(f32[144,768]{1,0:T(8,128)} %fusion.14), channel_id=1, source_target_pairs={{0,4},{8,0},{16,8},{24,16},{28,24},{20,28},{12,20},{4,12},{1,5},{9... | collective-permute-start | bytes 1327112 | tf_op jit(solution)/shard_map/ppermute | solution.py:765
  402.2 31.0 %collective-permute-start.40 = (f32[320,768]{1,0:T(8,128)}, f32[320,768]{1,0:T(8,128)}, u32[]{:S(2)}, u32[]{:S(2)}) collective-permute-start(f32[320,768]{1,0:T(8,128)} %get-tuple-element.352), channel_id=1, source_target_pairs={{0,1},{1,0},{2,3},{3,2},{4,5},{5,4},{6,7},{7,6},{8,9},{9,8},{10,11... | collective-permute-start | bytes 2949128 | tf_op jit(solution)/shard_map/ppermute | solution.py:671
  415.5 12.9 %collective-permute-start.46 = (f32[144,768]{1,0:T(8,128)}, f32[144,768]{1,0:T(8,128)S(1)}, u32[]{:S(2)}, u32[]{:S(2)}) collective-permute-start(f32[144,768]{1,0:T(8,128)} %fusion.16), channel_id=1, source_target_pairs={{0,4},{8,0},{16,8},{24,16},{28,24},{20,28},{12,20},{4,12},{1,5},{9... | collective-permute-start | bytes 1327112 | tf_op jit(solution)/shard_map/ppermute | solution.py:765
  417.1 11.2 %collective-permute-start.45 = (f32[120,768]{1,0:T(8,128)}, f32[120,768]{1,0:T(8,128)}, u32[]{:S(2)}, u32[]{:S(2)}) collective-permute-start(f32[120,768]{1,0:T(8,128)} %fusion.35), channel_id=1, source_target_pairs={{0,8},{8,16},{16,24},{24,28},{28,20},{20,12},{12,4},{4,0},{1,9},{9... | collective-permute-start | bytes 1105928 | tf_op jit(solution)/shard_map/ppermute | solution.py:765
  431.2 15.2 %collective-permute-start.48 = (f32[144,768]{1,0:T(8,128)}, f32[144,768]{1,0:T(8,128)}, u32[]{:S(2)}, u32[]{:S(2)}) collective-permute-start(f32[144,768]{1,0:T(8,128)} %fusion.18), channel_id=1, source_target_pairs={{0,4},{8,0},{16,8},{24,16},{28,24},{20,28},{12,20},{4,12},{1,5},{9... | collective-permute-start | bytes 1327112 | tf_op jit(solution)/shard_map/ppermute | solution.py:765
  432.7 13.6 %collective-permute-start.47 = (f32[120,768]{1,0:T(8,128)}, f32[120,768]{1,0:T(8,128)}, u32[]{:S(2)}, u32[]{:S(2)}) collective-permute-start(f32[120,768]{1,0:T(8,128)} %fusion.37), channel_id=1, source_target_pairs={{0,8},{8,16},{16,24},{24,28},{28,20},{20,12},{12,4},{4,0},{1,9},{9... | collective-permute-start | bytes 1105928 | tf_op jit(solution)/shard_map/ppermute | solution.py:765
  435.8 23.2 %collective-permute-start.49 = (f32[320,768]{1,0:T(8,128)}, f32[320,768]{1,0:T(8,128)}, u32[]{:S(2)}, u32[]{:S(2)}) collective-permute-start(f32[320,768]{1,0:T(8,128)} %add.506), channel_id=1, source_target_pairs={{0,2},{1,3},{2,0},{3,1},{4,6},{5,7},{6,4},{7,5},{8,10},{9,11},{10,... | collective-permute-start | bytes 2949128 | tf_op jit(solution)/shard_map/ppermute | solution.py:671
  458.9 20.8 %collective-permute-start.52 = (f32[160,768]{1,0:T(8,128)}, f32[160,768]{1,0:T(8,128)}, u32[]{:S(2)}, u32[]{:S(2)}) collective-permute-start(f32[160,768]{1,0:T(8,128)} %constant_dynamic-slice_fusion.5), channel_id=1, source_target_pairs={{0,4},{4,0},{8,12},{12,8},{16,20},{20,16},{24,28},{28,24},{1,5},{5... | collective-permute-start | bytes 1474568 | tf_op jit(solution)/shard_map/ppermute | solution.py:765
  460.6 19.1 %collective-permute-start.51 = (f32[144,768]{1,0:T(8,128)}, f32[144,768]{1,0:T(8,128)}, u32[]{:S(2)}, u32[]{:S(2)}) collective-permute-start(f32[144,768]{1,0:T(8,128)} %fusion.20), channel_id=1, source_target_pairs={{0,4},{8,0},{16,8},{24,16},{28,24},{20,28},{12,20},{4,12},{1,5},{9... | collective-permute-start | bytes 1327112 | tf_op jit(solution)/shard_map/ppermute | solution.py:765
  461.2 18.5 %collective-permute-start.53 = (f32[128,768]{1,0:T(8,128)}, f32[128,768]{1,0:T(8,128)}, u32[]{:S(2)}, u32[]{:S(2)}) collective-permute-start(f32[128,768]{1,0:T(8,128)} %constant_dynamic-slice_fusion.4), channel_id=1, source_target_pairs={{0,8},{4,12},{8,0},{12,4},{16,24},{20,28},{24,16},{28,20},{1,9},{5... | collective-permute-start | bytes 1179656 | tf_op jit(solution)/shard_map/ppermute | solution.py:765
  462.8 15.7 %collective-permute-start.50 = (f32[120,768]{1,0:T(8,128)}, f32[120,768]{1,0:T(8,128)}, u32[]{:S(2)}, u32[]{:S(2)}) collective-permute-start(f32[120,768]{1,0:T(8,128)} %fusion.39), channel_id=1, source_target_pairs={{0,8},{8,16},{16,24},{24,28},{28,20},{20,12},{12,4},{4,0},{1,9},{9... | collective-permute-start | bytes 1105928 | tf_op jit(solution)/shard_map/ppermute | solution.py:765
  463.2 27.0 %collective-permute-start.54 = (f32[320,768]{1,0:T(8,128)}, f32[320,768]{1,0:T(8,128)S(1)}, u32[]{:S(2)}, u32[]{:S(2)}) collective-permute-start(f32[320,768]{1,0:T(8,128)} %get-tuple-element.401), channel_id=1, source_target_pairs={{0,1},{1,0},{2,3},{3,2},{4,5},{5,4},{6,7},{7,6},{8,9},{9,8},{10,11... | collective-permute-start | bytes 2949128 | tf_op jit(solution)/shard_map/ppermute | solution.py:671
  488.1 19.0 %collective-permute-start.56 = (f32[144,768]{1,0:T(8,128)}, f32[144,768]{1,0:T(8,128)S(1)}, u32[]{:S(2)}, u32[]{:S(2)}) collective-permute-start(f32[144,768]{1,0:T(8,128)} %fusion.7.refs_0_), channel_id=1, source_target_pairs={{0,4},{8,0},{16,8},{24,16},{28,24},{20,28},{12,20},{4,12},{1,5},{9... | collective-permute-start | bytes 1327112 | tf_op jit(solution)/shard_map/ppermute | solution.py:765
  490.2 16.9 %collective-permute-start.55 = (f32[120,768]{1,0:T(8,128)}, f32[120,768]{1,0:T(8,128)}, u32[]{:S(2)}, u32[]{:S(2)}) collective-permute-start(f32[120,768]{1,0:T(8,128)} %fusion.26.refs_0_), channel_id=1, source_target_pairs={{0,8},{8,16},{16,24},{24,28},{28,20},{20,12},{12,4},{4,0},{1,9},{9... | collective-permute-start | bytes 1105928 | tf_op jit(solution)/shard_map/ppermute | solution.py:765
  490.4 21.0 %collective-permute-start.59 = (f32[320,768]{1,0:T(8,128)S(1)}, f32[320,768]{1,0:T(8,128)}, u32[]{:S(2)}, u32[]{:S(2)}) collective-permute-start(f32[320,768]{1,0:T(8,128)S(1)} %add.543), channel_id=1, source_target_pairs={{0,2},{1,3},{2,0},{3,1},{4,6},{5,7},{6,4},{7,5},{8,10},{9,11},{10,... | collective-permute-start | bytes 2949128 | tf_op jit(solution)/shard_map/ppermute | solution.py:671
  491.7 15.4 %collective-permute-start.57 = (f32[80,768]{1,0:T(8,128)}, f32[80,768]{1,0:T(8,128)}, u32[]{:S(2)}, u32[]{:S(2)}) collective-permute-start(f32[80,768]{1,0:T(8,128)} %constant_dynamic-slice_fusion.3), channel_id=1, source_target_pairs={{0,8},{4,12},{8,0},{12,4},{16,24},{20,28},{24,16},{28,20},{1,9},{5... | collective-permute-start | bytes 737288 | tf_op jit(solution)/shard_map/ppermute | solution.py:765
  492.5 13.0 %collective-permute-start.58 = (f32[64,768]{1,0:T(8,128)}, f32[64,768]{1,0:T(8,128)S(1)}, u32[]{:S(2)}, u32[]{:S(2)}) collective-permute-start(f32[64,768]{1,0:T(8,128)} %constant_dynamic-slice_fusion.2), channel_id=1, source_target_pairs={{0,16},{4,20},{8,24},{12,28},{16,0},{20,4},{24,8},{28,12},{1,17},{... | collective-permute-start | bytes 589832 | tf_op jit(solution)/shard_map/ppermute | solution.py:765
  511.4 15.2 %collective-permute-start.61 = (f32[144,768]{1,0:T(8,128)S(1)}, f32[144,768]{1,0:T(8,128)S(1)}, u32[]{:S(2)}, u32[]{:S(2)}) collective-permute-start(f32[144,768]{1,0:T(8,128)S(1)} %collective-permute-done.56.refs_1_), channel_id=1, source_target_pairs={{0,4},{8,0},{16,8},{24,16},{28,24},{20,28},{12,20},{4,12},{1,5},{9... | collective-permute-start | bytes 1327112 | tf_op jit(solution)/shard_map/ppermute | solution.py:765
  513.1 20.3 %collective-permute-start.64 = (f32[320,768]{1,0:T(8,128)}, f32[320,768]{1,0:T(8,128)}, u32[]{:S(2)}, u32[]{:S(2)}) collective-permute-start(f32[320,768]{1,0:T(8,128)} %get-tuple-element.421), channel_id=1, source_target_pairs={{0,1},{1,0},{2,3},{3,2},{4,5},{5,4},{6,7},{7,6},{8,9},{9,8},{10,11... | collective-permute-start | bytes 2949128 | tf_op jit(solution)/shard_map/ppermute | solution.py:671
  513.1 13.4 %collective-permute-start.60 = (f32[120,768]{1,0:T(8,128)}, f32[120,768]{1,0:T(8,128)}, u32[]{:S(2)}, u32[]{:S(2)}) collective-permute-start(f32[120,768]{1,0:T(8,128)} %collective-permute-done.55.refs_1_), channel_id=1, source_target_pairs={{0,8},{8,16},{16,24},{24,28},{28,20},{20,12},{12,4},{4,0},{1,9},{9... | collective-permute-start | bytes 1105928 | tf_op jit(solution)/shard_map/ppermute | solution.py:765
  513.4 13.1 %collective-permute-start.62 = (f32[40,768]{1,0:T(8,128)S(1)}, f32[40,768]{1,0:T(8,128)}, u32[]{:S(2)}, u32[]{:S(2)}) collective-permute-start(f32[40,768]{1,0:T(8,128)S(1)} %constant_dynamic-slice_fusion.1), channel_id=1, source_target_pairs={{0,16},{4,20},{8,24},{12,28},{16,0},{20,4},{24,8},{28,12},{1,17},{... | collective-permute-start | bytes 368648 | tf_op jit(solution)/shard_map/ppermute | solution.py:765
  515.5 11.0 %collective-permute-start.63 = (f32[32,768]{1,0:T(8,128)}, f32[32,768]{1,0:T(8,128)}, u32[]{:S(2)}, u32[]{:S(2)}) collective-permute-start(f32[32,768]{1,0:T(8,128)} %constant_dynamic-slice_fusion), channel_id=1, source_target_pairs={{0,4},{4,0},{8,12},{12,8},{16,20},{20,16},{24,28},{28,24},{1,5},{5... | collective-permute-start | bytes 294920 | tf_op jit(solution)/shard_map/ppermute | solution.py:765
  529.2 19.3 %collective-permute-start.66 = (f32[144,768]{1,0:T(8,128)S(1)}, f32[144,768]{1,0:T(8,128)}, u32[]{:S(2)}, u32[]{:S(2)}) collective-permute-start(f32[144,768]{1,0:T(8,128)S(1)} %collective-permute-done.61.refs_2_), channel_id=1, source_target_pairs={{0,4},{8,0},{16,8},{24,16},{28,24},{20,28},{12,20},{4,12},{1,5},{9... | collective-permute-start | bytes 1327112 | tf_op jit(solution)/shard_map/ppermute | solution.py:765
  533.4 15.1 %collective-permute-start.65 = (f32[120,768]{1,0:T(8,128)}, f32[120,768]{1,0:T(8,128)}, u32[]{:S(2)}, u32[]{:S(2)}) collective-permute-start(f32[120,768]{1,0:T(8,128)} %collective-permute-done.60.refs_2_), channel_id=1, source_target_pairs={{0,8},{8,16},{16,24},{24,28},{28,20},{20,12},{12,4},{4,0},{1,9},{9... | collective-permute-start | bytes 1105928 | tf_op jit(solution)/shard_map/ppermute | solution.py:765
  534.9 23.2 %collective-permute-start.69 = (f32[320,768]{1,0:T(8,128)S(1)}, f32[320,768]{1,0:T(8,128)S(1)}, u32[]{:S(2)}, u32[]{:S(2)}) collective-permute-start(f32[320,768]{1,0:T(8,128)S(1)} %add.565), channel_id=1, source_target_pairs={{0,2},{1,3},{2,0},{3,1},{4,6},{5,7},{6,4},{7,5},{8,10},{9,11},{10,... | collective-permute-start | bytes 2949128 | tf_op jit(solution)/shard_map/ppermute | solution.py:671
  536.2 12.3 %collective-permute-start.67 = (f32[40,768]{1,0:T(8,128)S(1)}, f32[40,768]{1,0:T(8,128)S(1)}, u32[]{:S(2)}, u32[]{:S(2)}) collective-permute-start(f32[40,768]{1,0:T(8,128)S(1)} %dynamic-slice_add_fusion.5), channel_id=1, source_target_pairs={{0,16},{4,20},{8,24},{12,28},{16,0},{20,4},{24,8},{28,12},{1,17},{... | collective-permute-start | bytes 368648 | tf_op jit(solution)/shard_map/ppermute | solution.py:765
  558.1 20.3 %collective-permute-start.71 = (f32[144,768]{1,0:T(8,128)}, f32[144,768]{1,0:T(8,128)S(1)}, u32[]{:S(2)}, u32[]{:S(2)}) collective-permute-start(f32[144,768]{1,0:T(8,128)} %collective-permute-done.66.refs_3_), channel_id=1, source_target_pairs={{0,4},{8,0},{16,8},{24,16},{28,24},{20,28},{12,20},{4,12},{1,5},{9... | collective-permute-start | bytes 1327112 | tf_op jit(solution)/shard_map/ppermute | solution.py:765
  559.8 18.6 %collective-permute-start.70 = (f32[120,768]{1,0:T(8,128)}, f32[120,768]{1,0:T(8,128)S(1)}, u32[]{:S(2)}, u32[]{:S(2)}) collective-permute-start(f32[120,768]{1,0:T(8,128)} %collective-permute-done.65.refs_3_), channel_id=1, source_target_pairs={{0,8},{8,16},{16,24},{24,28},{28,20},{20,12},{12,4},{4,0},{1,9},{9... | collective-permute-start | bytes 1105928 | tf_op jit(solution)/shard_map/ppermute | solution.py:765
  560.1 18.2 %collective-permute-start.72 = (f32[80,768]{1,0:T(8,128)S(1)}, f32[80,768]{1,0:T(8,128)S(1)}, u32[]{:S(2)}, u32[]{:S(2)}) collective-permute-start(f32[80,768]{1,0:T(8,128)S(1)} %pad_maximum_fusion.10), channel_id=1, source_target_pairs={{0,8},{4,12},{8,0},{12,4},{16,24},{20,28},{24,16},{28,20},{1,9},{5... | collective-permute-start | bytes 737288 | tf_op jit(solution)/shard_map/ppermute | solution.py:765
  560.9 15.2 %collective-permute-start.73 = (f32[64,768]{1,0:T(8,128)S(1)}, f32[64,768]{1,0:T(8,128)S(1)}, u32[]{:S(2)}, u32[]{:S(2)}) collective-permute-start(f32[64,768]{1,0:T(8,128)S(1)} %pad_maximum_fusion.11), channel_id=1, source_target_pairs={{0,16},{4,20},{8,24},{12,28},{16,0},{20,4},{24,8},{28,12},{1,17},{... | collective-permute-start | bytes 589832 | tf_op jit(solution)/shard_map/ppermute | solution.py:765
  565.7 40.9 %collective-permute-start.74 = (f32[320,768]{1,0:T(8,128)S(1)}, f32[320,768]{1,0:T(8,128)S(1)}, u32[]{:S(2)}, u32[]{:S(2)}) collective-permute-start(f32[320,768]{1,0:T(8,128)S(1)} %maximum_add_fusion.refs_1_), channel_id=1, source_target_pairs={{0,1},{1,0},{2,3},{3,2},{4,5},{5,4},{6,7},{7,6},{8,9},{9,8},{10,11... | collective-permute-start | bytes 2949128 | tf_op jit(solution)/shard_map/ppermute | solution.py:671
  580.5 27.8 %collective-permute-start.75 = (f32[320,768]{1,0:T(8,128)S(1)}, f32[320,768]{1,0:T(8,128)}, u32[]{:S(2)}, u32[]{:S(2)}) collective-permute-start(f32[320,768]{1,0:T(8,128)S(1)} %maximum_add_fusion.1.refs_2_), channel_id=1, source_target_pairs={{0,1},{1,0},{2,3},{3,2},{4,5},{5,4},{6,7},{7,6},{8,9},{9,8},{10,11... | collective-permute-start | bytes 2949128 | tf_op jit(solution)/shard_map/ppermute | solution.py:671
  581.7 11.6 %collective-permute-start.77 = (f32[120,768]{1,0:T(8,128)S(1)}, f32[120,768]{1,0:T(8,128)}, u32[]{:S(2)}, u32[]{:S(2)}) collective-permute-start(f32[120,768]{1,0:T(8,128)S(1)} %collective-permute-done.70.refs_4_), channel_id=1, source_target_pairs={{0,8},{8,16},{16,24},{24,28},{28,20},{20,12},{12,4},{4,0},{1,9},{9... | collective-permute-start | bytes 1105928 | tf_op jit(solution)/shard_map/ppermute | solution.py:765
  584.0 22.5 %collective-permute-start.79 = (f32[160,768]{1,0:T(8,128)S(1)}, f32[160,768]{1,0:T(8,128)S(1)}, u32[]{:S(2)}, u32[]{:S(2)}) collective-permute-start(f32[160,768]{1,0:T(8,128)S(1)} %pad_maximum_fusion.3), channel_id=1, source_target_pairs={{0,4},{4,0},{8,12},{12,8},{16,20},{20,16},{24,28},{28,24},{1,5},{5... | collective-permute-start | bytes 1474568 | tf_op jit(solution)/shard_map/ppermute | solution.py:765
  585.6 20.9 %collective-permute-start.78 = (f32[144,768]{1,0:T(8,128)S(1)}, f32[144,768]{1,0:T(8,128)S(1)}, u32[]{:S(2)}, u32[]{:S(2)}) collective-permute-start(f32[144,768]{1,0:T(8,128)S(1)} %collective-permute-done.71.refs_4_), channel_id=1, source_target_pairs={{0,4},{8,0},{16,8},{24,16},{28,24},{20,28},{12,20},{4,12},{1,5},{9... | collective-permute-start | bytes 1327112 | tf_op jit(solution)/shard_map/ppermute | solution.py:765
  593.2 13.3 %collective-permute-start.80 = (f32[128,768]{1,0:T(8,128)S(1)}, f32[128,768]{1,0:T(8,128)S(1)}, u32[]{:S(2)}, u32[]{:S(2)}) collective-permute-start(f32[128,768]{1,0:T(8,128)S(1)} %pad_maximum_fusion.6), channel_id=1, source_target_pairs={{0,8},{4,12},{8,0},{12,4},{16,24},{20,28},{24,16},{28,20},{1,9},{5... | collective-permute-start | bytes 1179656 | tf_op jit(solution)/shard_map/ppermute | solution.py:765
  617.2 12.1 %collective-permute-start.83 = (f32[144,768]{1,0:T(8,128)S(1)}, f32[144,768]{1,0:T(8,128)}, u32[]{:S(2)}, u32[]{:S(2)}) collective-permute-start(f32[144,768]{1,0:T(8,128)S(1)} %collective-permute-done.78.refs_5_), channel_id=1, source_target_pairs={{0,4},{8,0},{16,8},{24,16},{28,24},{20,28},{12,20},{4,12},{1,5},{9... | collective-permute-start | bytes 1327112 | tf_op jit(solution)/shard_map/ppermute | solution.py:765
  617.4 11.9 %collective-permute-start.82 = (f32[120,768]{1,0:T(8,128)}, f32[120,768]{1,0:T(8,128)}, u32[]{:S(2)}, u32[]{:S(2)}) collective-permute-start(f32[120,768]{1,0:T(8,128)} %collective-permute-done.77.refs_5_), channel_id=1, source_target_pairs={{0,8},{8,16},{16,24},{24,28},{28,20},{20,12},{12,4},{4,0},{1,9},{9... | collective-permute-start | bytes 1105928 | tf_op jit(solution)/shard_map/ppermute | solution.py:765
  630.1 12.7 %collective-permute-start.86 = (f32[144,768]{1,0:T(8,128)}, f32[144,768]{1,0:T(8,128)}, u32[]{:S(2)}, u32[]{:S(2)}) collective-permute-start(f32[144,768]{1,0:T(8,128)} %collective-permute-done.83.refs_6_), channel_id=1, source_target_pairs={{0,4},{8,0},{16,8},{24,16},{28,24},{20,28},{12,20},{4,12},{1,5},{9... | collective-permute-start | bytes 1327112 | tf_op jit(solution)/shard_map/ppermute | solution.py:765
  631.8 11.0 %collective-permute-start.85 = (f32[120,768]{1,0:T(8,128)}, f32[120,768]{1,0:T(8,128)}, u32[]{:S(2)}, u32[]{:S(2)}) collective-permute-start(f32[120,768]{1,0:T(8,128)} %collective-permute-done.82.refs_6_), channel_id=1, source_target_pairs={{0,8},{8,16},{16,24},{24,28},{28,20},{20,12},{12,4},{4,0},{1,9},{9... | collective-permute-start | bytes 1105928 | tf_op jit(solution)/shard_map/ppermute | solution.py:765
  642.8 22.8 %collective-permute-start.88 = (f32[20,768]{1,0:T(8,128)S(1)}, f32[20,768]{1,0:T(8,128)S(1)}, u32[]{:S(2)}, u32[]{:S(2)}) collective-permute-start(f32[20,768]{1,0:T(8,128)S(1)} %add.579), channel_id=1, source_target_pairs={{0,16},{4,20},{8,24},{12,28},{16,0},{20,4},{24,8},{28,12},{1,17},{... | collective-permute-start | bytes 184328 | tf_op jit(solution)/shard_map/ppermute | solution.py:765
  (120 other events, 1362.3 us)

commit v3 on v2

--- a/solution.py
+++ b/solution.py
@@ -284,7 +284,7 @@
             pltpu.VMEM((slots, part), F32),
             pltpu.VMEM((part, slots), F32),
         ],
-        compiler_params=pltpu.CompilerParams(vmem_limit_bytes=VMEM_LIMIT),
+        compiler_params=pltpu.CompilerParams(vmem_limit_bytes=32 << 20),
         cost_estimate=cost(slots * part * 16 * slots, 8 * slots * cols),
         name="attn_bwd",
     )(place, lens, qkv, lse, *ctx, *mine, *theirs, b_sum)
@@ -328,7 +328,7 @@
             pltpu.VMEM((slots, width), F32),
             pltpu.VMEM((slots, width), F32),
         ],
-        compiler_params=pltpu.CompilerParams(vmem_limit_bytes=VMEM_LIMIT),
+        compiler_params=pltpu.CompilerParams(vmem_limit_bytes=32 << 20),
         cost_estimate=cost(slots * cols * 2 * width, 12 * slots * width),
         name="qkv_bwd",
     )(place, hidden, roi, stats, gain, shift, w, gq, w_sum)
@@ -372,8 +372,9 @@
                     if kind == "wi" and i > 1:
                         piece = piece.at[pl.ds(part // 2, width // 2)]
                     at = pl.ds(piece_place(i, width, shifts[kind]), piece.shape[0])
+                    where = stage.at[tile % 2, k, at, :]
                     found.append(
-                        pltpu.make_async_copy(piece, stage.at[k, at, :], sems.at[len(found)])
+                        pltpu.make_async_copy(piece, where, sems.at[tile % 2, len(found)])
                     )
         return found
 
@@ -381,14 +382,16 @@
         for copy in copies(tile):
             copy.start()
 
+    slot_of = lambda tile: tile if resident else tile % 2
+
     def ready(tile):
         for copy in copies(tile):
             copy.wait()
-        slot = tile if resident else 0
-        wts[slot, 0], wts[slot, 1] = halves(stage[0])
-        wts[slot, 2], wts[slot, 3] = halves(stage[1])
-        if tile + 1 < TILES:
-            start_tile(tile + 1)
+        slot = slot_of(tile)
+        wts[slot, 0], wts[slot, 1] = halves(stage[tile % 2, 0])
+        wts[slot, 2], wts[slot, 3] = halves(stage[tile % 2, 1])
+        if tile + 2 < TILES:
+            start_tile(tile + 2)
 
     def load_wo(count):
         for i in range(count):
@@ -411,9 +414,11 @@
         a_hi[...], a_lo[...] = halves(h)
         acc[...] = h + row("bias_back")
         for t in range(TILES):
-            if loading:
-                ready(t)
-            slot = t if resident else 0
+            if loading and t == 0:
+                ready(0)
+            if loading and t + 1 < TILES:
+                ready(t + 1)
+            slot = slot_of(t)
             pre = dot3((a_hi[...], a_lo[...]), (wts[slot, 0], wts[slot, 1]))
             value, rise = gelu_parts(pre + row(f"bias_in{t}"))
             ref["slope"][t] = rise
@@ -440,9 +445,11 @@
         acc[...] = back
         a_hi[...], a_lo[...] = halves(back)
         for t in range(TILES):
-            if loading:
-                ready(t)
-            slot = t if resident else 0
+            if loading and t == 0:
+                ready(0)
+            if loading and t + 1 < TILES:
+                ready(t + 1)
+            slot = slot_of(t)
             grad = dot3((a_hi[...], a_lo[...]), (wts[slot, 2], wts[slot, 3]), ROWS_BY_ROWS)
             grad = grad * ref["slope"][t]
             if t < 2:
@@ -462,6 +469,7 @@
 
     def begin():
         start_tile(0)
+        start_tile(1)
         load_wo(6 if forward else 2)
         if backward:
             ref["sums"][...] = jnp.zeros_like(ref["sums"])
@@ -554,9 +562,9 @@
                 aliases[len(args)] = k
                 take(name + "_into", anywhere, into[name])
     scratch = [
-        ("stage", pltpu.VMEM((2, width, width), F32)),
-        ("sems", pltpu.SemaphoreType.DMA((4,))),
-        ("wts", pltpu.VMEM((TILES if both else 1, 4, width, width), BF16)),
+        ("stage", pltpu.VMEM((2, 2, width, width), F32)),
+        ("sems", pltpu.SemaphoreType.DMA((2, 4))),
+        ("wts", pltpu.VMEM((TILES if both else 2, 4, width, width), BF16)),
         ("wo", pltpu.VMEM((2, width, width), BF16)),
         ("acc", pltpu.VMEM((block, width), F32)),
         ("a_hi", pltpu.VMEM((block, width), BF16)),
@@ -679,7 +687,7 @@
     return x
 
 
-def ring(part, sign):
+def ring(part, sign, cuts):
     n = lax.axis_size("dp")
     order = list(range(0, n, 2)) + list(range(n - 1, 0, -2))
     pairs = [(order[k], order[(k + sign) % n]) for k in range(n)]
@@ -696,26 +704,32 @@
         held = yield held, "dp", pairs
         pieces.append(held)
     if size % 8 == 0:
-        return assemble(jnp.stack([at(k - 1) for k in range(n)]).astype(jnp.int32), pieces)
+        where = jnp.stack([at(k - 1) for k in range(n)]).astype(jnp.int32)
+        return assemble(where, pieces, cuts)
     total = part
     for k, piece in enumerate(pieces):
         total = lax.dynamic_update_slice_in_dim(total, piece, at(k - 1), 0)
-    return total
-
-
-def assemble_kernel(where, *refs):
-    out = refs[-1]
-    for k, piece in enumerate(refs[:-1]):
-        out[pl.ds(pl.multiple_of(where[k], 8), piece.shape[0]), :] = piece[...]
-
-
-def assemble(where, pieces):
+    return [total[sum(cuts[:i]) : sum(cuts[: i + 1])] for i in range(len(cuts))]
+
+
+def assemble_kernel(count, where, *refs):
+    outs, total = refs[count:-1], refs[-1]
+    for k, piece in enumerate(refs[:count]):
+        total[pl.ds(pl.multiple_of(where[k], 8), piece.shape[0]), :] = piece[...]
+    at = 0
+    for out in outs:
+        out[...] = total[at : at + out.shape[0], :]
+        at += out.shape[0]
+
+
+def assemble(where, pieces, cuts):
     size, width = pieces[0].shape
     return pl.pallas_call(
-        assemble_kernel,
+        functools.partial(assemble_kernel, len(pieces)),
         in_specs=[smem()] + [pl.BlockSpec(memory_space=pltpu.VMEM)] * len(pieces),
-        out_specs=pl.BlockSpec(memory_space=pltpu.VMEM),
-        out_shape=sds(size * len(pieces), width),
+        out_specs=[pl.BlockSpec(memory_space=pltpu.VMEM)] * len(cuts),
+        out_shape=[sds(rows, width) for rows in cuts],
+        scratch_shapes=[pltpu.VMEM((size * len(pieces), width), F32)],
         compiler_params=pltpu.CompilerParams(vmem_limit_bytes=VMEM_LIMIT),
         cost_estimate=cost(0, 8 * size * len(pieces) * width),
         name="assemble",
@@ -857,15 +871,14 @@
     far_seg, far_txt = from_x(both_seg), from_x(both_txt)
     close_sib = tuple(from_sib(w) for w in close)
     both_sib = (from_sib(both_seg), from_sib(both_txt))
-    far, far_seg, far_txt, close_sib, both_sib = lax.optimization_barrier(
-        (far, far_seg, far_txt, close_sib, both_sib)
+    far, far_seg, close_sib, both_sib = lax.optimization_barrier(
+        (far, far_seg, close_sib, both_sib)
     )
     far_sib = tuple(from_sib(w) for w in far)
     weights = ((w_out, own_sib[0]),) + tuple(
         (own[1 + k], own_sib[1 + k], close[k], far[k], close_sib[k], far_sib[k]) for k in range(2)
     )
     ctx_seg = (both_seg, both_sib[0], far_seg, from_sib(far_seg))
-    ctx_txt = (both_txt, both_sib[1], far_txt, from_sib(far_txt))
     vec = (bias_out, ln1_gain, ln1_bias, bias_back, ln2_gain, ln2_bias)
     mine_rows = docs * (half + half_seg)
     txt_rows = docs * half
@@ -873,6 +886,9 @@
         place, vec, bias_rows, weights, docs * half_seg, txt_rows, mine_rows, None,
         ctx=ctx_seg, xres=x_seg,
     )
+
+    far_txt = later(far_txt, seg["out"])
+    ctx_txt = (both_txt, both_sib[1], far_txt, from_sib(far_txt))
 
     txt = {name: seg[name] for name in ("h1", "act0", "act1")}
     txt_sums, gwo = [], []
@@ -969,8 +985,9 @@
     grad_out_own = gwo[:part] + from_sib(gwo[part:])
 
     steps = Steps()
-    steps.add("in_out", ring(jnp.concatenate([grad_in_own, grad_out_own], axis=0), 1))
-    steps.add("back_pair", ring(jnp.concatenate([grad_back_own, grad_pair_w], axis=0), -1))
+    steps.add("in_out", ring(jnp.concatenate([grad_in_own, grad_out_own], axis=0), 1, (width, part)))
+    back_pair = jnp.concatenate([grad_back_own, grad_pair_w], axis=0)
+    steps.add("back_pair", ring(back_pair, -1, (width, 2 * share)))
     mine = (back["gb"], txt["gb"])
     theirs = tuple(from_sib(g) for g in mine)
     w_sum = jnp.zeros((3 * part, width), F32)
@@ -1051,17 +1068,17 @@
         grad_bn_bias,
         jnp.transpose(sum_qkv.reshape(3, part, width), (0, 2, 1)),
         sum_bias_qv,
-        in_out[width:],
+        in_out[1],
         vectors[5],
         vectors[3],
         vectors[4],
-        in_out[:width],
+        in_out[0],
         vectors[6],
-        back_pair[:width],
+        back_pair[0],
         vectors[2],
         vectors[0],
         vectors[1],
-        back_pair[width:].reshape(2, share, width),
+        back_pair[1].reshape(2, share, width),
         vectors[7],
         sum_dir_w,
     )

time: 677 us -> 647 us (0.956)
  Pallas kernels: 248 us -> 207 us
  waiting for transfers between devices: 189 us -> 200 us
  other arithmetic: 54.3 us -> 45.9 us
    pallas_call x5, Pallas kernels: 147 us -> 125 us  [ffn(): pl.pallas_call(functools.partial(ffn_kernel, forward, backward, all_names...]
    unnamed x187 -> x311, local copies, waits for them, and re-layouts: 9.4 us -> 30.9 us
    pallas_call x3, Pallas kernels: 28.1 us -> 15.7 us  [qkv_bwd(): pl.pallas_call(functools.partial(qkv_bwd_kernel, all_rows), grid=(1,), in...]
    slice x4 -> x0, local copies, waits for them, and re-layouts: 10.9 us -> none  [the longest x1 3.37 us: per_device(): in_out[:width]]
    pallas_call x3, Pallas kernels: 28.1 us -> 20.7 us  [attn_bwd(): pl.pallas_call(functools.partial(attn_bwd_kernel, doc), grid=(1,), in_spe...]
  transfers between devices with their start and end apart: 91 -> 91, of which waited for: 34 -> 37; matrix products, arithmetic and copies ran while one was open for 15% -> 13% of each run, Pallas kernels for 31% -> 27%
where the time goes in v3:
time: 647 us; the launch traced here: 640 us
  Pallas kernels  207 us (32%)
  waiting for transfers between devices  200 us (31%)
  starting transfers between devices  89.9 us (14%)
  local copies, waits for them, and re-layouts  54.9 us (8%)
  other arithmetic  45.9 us (7%)
  matrix products  38.4 us (6%)
    pallas_call x5, Pallas kernels, ffn(): pl.pallas_call(functools.partial(ffn_kernel, forward, backward, all_names...  125 us
    ppermute x43, waiting for transfers between devices, run(): lax.ppermute(x, *self.active[name][1][1:])  102 us
    ppermute x46, waiting for transfers between devices, swap(): return lax.ppermute(x, axis, [(i, i ^ bit) for i in range(n)])  98.4 us
    ppermute x43, starting transfers between devices, run(): lax.ppermute(x, *self.active[name][1][1:])  54.5 us
    dot_general x14, matrix products, product(): lax.dot_general(operand, other, (dims, ((), ())), precision=HIGH, preferr...  38.4 us
    unnamed x311, local copies, waits for them, and re-layouts  30.9 us
    ppermute x46, starting transfers between devices, swap(): return lax.ppermute(x, axis, [(i, i ^ bit) for i in range(n)])  24 us
    pallas_call x1, Pallas kernels, attn_fwd(): pl.pallas_call(functools.partial(attn_fwd_kernel, all_rows), grid=(docs,)...  22.3 us
  transfers between devices with their start and end apart: 91, of which 37 were waited for; matrix products, arithmetic and copies ran while one was open for 13% of the time, Pallas kernels for 27%

profile of v3, /device:TPU:0, one launch (start us, length us, event | category | flops | bytes accessed | tf_op | source)
XLA Modules:
  0.0 639.6 jit_solution(4410776862642909201)
XLA Ops:
  1.3 2.2 local_stats.1
  3.4 2.9 collective-permute-start.5
  12.0 2.4 constant_dynamic-slice_fusion.10
  17.6 2.1 collective-permute-done.6
  22.4 2.6 collective-permute-start.7
  30.9 22.3 %attn_fwd.1 = (f32[1920,576]{1,0:T(8,128)}, f32[24,640]{1,0:T(8,128)}, f32[192,384]{1,0:T(8,128)}, f32[768,384]{1,0:T(8,128)}, f32[192,768]{1,0:T(8,128)}, /*index=5*/f32[768,768]{1,0:T(8,128)}) custom-call(s32[3]{0:T(128)} %pad_add_fusion.refs_0_.place, s32[3]{0:T(128)} %refs_1_.22, f32[1920,768]{1,0:T(8,128)} %refs_1_.23, f32[384,768]{1,0:T(8,128)} %refs_7_.2, ...), custom_call_target="tpu_custom_call" | custom-call | flops 11520 | bytes 640 | tf_op jit(solution)/shard_map/attn_fwd/pallas_call | solution.py:189
  53.3 17.5 %collective-permute-done.1.refs_27_.refs_28_.refs_24_ = f32[384,768]{1,0:T(8,128)} collective-permute-done((f32[384,768]{1,0:T(8,128)}, f32[384,768]{1,0:T(8,128)}, u32[]{:S(2)}, u32[]{:S(2)}) %collective-permute-start.1) | collective-permute-done | bytes 1179680 | tf_op jit(solution)/shard_map/ppermute | solution.py:679
  73.7 4.9 collective-permute-done.13.refs_9_
  79.1 21.3 %collective-permute-done.12.refs_29_.refs_30_.refs_26_ = f32[384,768]{1,0:T(8,128)} collective-permute-done((f32[384,768]{1,0:T(8,128)}, f32[384,768]{1,0:T(8,128)}, u32[]{:S(2)}, u32[]{:S(2)}) %collective-permute-start.12) | collective-permute-done | bytes 1179680 | tf_op jit(solution)/shard_map/ppermute | solution.py:679
  100.4 6.0 collective-permute-done.11.refs_19_.refs_28_.refs_20_.refs_29_.refs_25_
  112.1 17.2 %ffn_fwd.1 = (f32[192,768]{1,0:T(8,128)}, f32[960,768]{1,0:T(8,128)}, f32[960,768]{1,0:T(8,128)}, f32[960,768]{1,0:T(8,128)}, f32[192,768]{1,0:T(8,128)}, /*inde...) custom-call(s32[3]{0:T(128)} %pad_add_fusion.refs_0_.place, f32[768]{0:T(1024)} %refs_1_.17, ...), custom_call_target="tpu_custom_call" | custom-call | flops 16307453952 | bytes 8847360 | tf_op jit(solution)/shard_map/ffn_fwd/pallas_call | solution.py:577
  129.3 6.4 collective-permute-done.22.refs_9_
  142.5 5.3 all-to-all-start
  147.8 29.2 %ffn_fwdbwd.3 = (f32[768,768]{1,0:T(8,128)}, f32[960,768]{1,0:T(8,128)}, f32[960,768]{1,0:T(8,128)}, f32[960,768]{1,0:T(8,128)}, f32[960,768]{1,0:T(8,128)}, /*i...) custom-call(s32[3]{0:T(128)} %pad_add_fusion.refs_0_.place, ...), custom_call_target="tpu_custom_call", output_to_operand_aliasing={{1}: (35, {}), {2}: (36, {}), {3}: (37, {})} | custom-call | flops 25367150592 | bytes 11796480 | tf_op jit(solution)/shard_map/ffn_fwdbwd/pallas_call | solution.py:577
  179.2 3.1 scatter_custom_fusion
  183.9 29.4 %ffn_fwdbwd.4 = (f32[768,768]{1,0:T(8,128)}, f32[960,768]{1,0:T(8,128)}, f32[960,768]{1,0:T(8,128)}, f32[960,768]{1,0:T(8,128)}, f32[960,768]{1,0:T(8,128)}, /*i...) custom-call(s32[3]{0:T(128)} %pad_add_fusion.refs_0_.place, ...), custom_call_target="tpu_custom_call", output_to_operand_aliasing={{0}: (35, {}), {1}: (36, {}), {2}: (37, {}), {3}: (38, {}),... | custom-call | flops 25367150592 | bytes 11796480 | tf_op jit(solution)/shard_map/ffn_fwdbwd/pallas_call | solution.py:577
  219.3 6.2 all-to-all-start.1
  225.5 29.3 %ffn_fwdbwd.5 = (f32[768,768]{1,0:T(8,128)}, f32[960,768]{1,0:T(8,128)}, f32[960,768]{1,0:T(8,128)}, f32[960,768]{1,0:T(8,128)}, f32[960,768]{1,0:T(8,128)}, /*i...) custom-call(s32[3]{0:T(128)} %pad_add_fusion.refs_0_.place, ...), custom_call_target="tpu_custom_call", output_to_operand_aliasing={{0}: (35, {}), {1}: (36, {}), {2}: (37, {}), {3}: (38, {}),... | custom-call | flops 25367150592 | bytes 11796480 | tf_op jit(solution)/shard_map/ffn_fwdbwd/pallas_call | solution.py:577
  257.3 3.8 collective-permute-done.27
  263.0 7.6 %collective-permute-done.28 = f32[192,384]{1,0:T(8,128)S(1)} collective-permute-done((f32[192,384]{1,0:T(8,128)S(1)}, f32[192,384]{1,0:T(8,128)S(1)}, u32[]{:S(2)}, u32[]{:S(2)}) %collective-permute-start.28) | collective-permute-done | bytes 294944 | tf_op jit(solution)/shard_map/ppermute | solution.py:679
  270.8 6.5 %join_rows.1 = f32[1920,768]{1,0:T(8,128)} custom-call(s32[3]{0:T(128)} %pad_add_fusion.refs_0_.place, f32[192,768]{1,0:T(8,128)} %get-tuple-element.271.ms, f32[768,768]{1,0:T(8,128)} %get-tuple-element.313.mt, f32[192,768]{1,0:T(8,128)} %collective-permute-done.29.ts, f32[768,768]{1,0:T(8,128)} %collective-permute-done.30.tt), custom_call_target="tpu_custom_call" | custom-call | bytes 11796480 | tf_op jit(solution)/shard_map/join_rows/pallas_call | solution.py:607
  278.2 20.3 %ffn_bwd.1 = (f32[960,768]{1,0:T(8,128)}, f32[960,768]{1,0:T(8,128)}, f32[960,768]{1,0:T(8,128)}, f32[960,768]{1,0:T(8,128)}, f32[192,384]{1,0:T(8,128)}, /*index=5*/f32[384,768]{1,0:T(8,128)}, f32[8,768]{1,0:T(8,128)}) custom-call(s32[3]{0:T(128)} %pad_add_fusion.refs_0_.place, ...), custom_call_target="tpu_custom_call", output_to_operand_aliasing={{0}: (31, {}), {1}: (32, {}), {2}: (33, {}), {3}: (34, {})} | custom-call | flops 16307453952 | bytes 8847360 | tf_op jit(solution)/shard_map/ffn_bwd/pallas_call | solution.py:577
  298.5 9.0 %fusion.68 = f32[768,768]{1,0:T(8,128)} fusion(f32[960,768]{1,0:T(8,128)} %get-tuple-element.335, f32[960,768]{1,0:T(8,128)} %get-tuple-element.334), kind=kOutput, calls=%fused_computation.205 | convolution fusion | flops 3397386240 | bytes 8257536 | tf_op jit(solution)/shard_map/dot_general | solution.py:24
  307.5 6.1 fusion.67
  317.8 2.5 collective-permute-done.32
  321.5 7.8 %convolution_add_fusion = f32[768,768]{1,0:T(8,128)S(1)} fusion(f32[768,768]{1,0:T(8,128)} %collective-permute-done.33, f32[960,768]{1,0:T(8,128)} %get-tuple-element.333, f32[960,768]{1,0:T(8,128)S(1)} %copy-done.89), kind=kOutput, calls=%fused_computation.36 | convolution fusion | flops 3397976064 | bytes 10616832 | tf_op jit(solution)/shard_map/dot_general | solution.py:24
  329.4 7.5 %convolution_add_fusion.1 = f32[768,768]{1,0:T(8,128)S(1)} fusion(f32[768,768]{1,0:T(8,128)} %collective-permute-done.31, f32[960,768]{1,0:T(8,128)S(1)} %copy-done.88, f32[960,768]{1,0:T(8,128)S(1)} %copy-done.100), kind=kOutput, calls=%fused_computation.37 | convolution fusion | flops 3397976064 | bytes 10616832 | tf_op jit(solution)/shard_map/dot_general | solution.py:24
  337.1 2.1 collective-permute-start.35
  339.8 6.9 %attn_bwd.3 = (f32[640,576]{1,0:T(8,128)S(1)}, f32[1,576]{1,0:T(1,128)S(1)}) custom-call(s32[3]{0:T(128)S(1)} %copy-done.27, s32[3]{0:T(128)S(1)} %copy-done.33, f32[1920,576]{1,0:T(8,128)S(1)} %bitcast.82, f32[24,640]{1,0:T(8,128)S(1)} %copy-done.61, f32[192,384]{1,0:T(8,128)S(1)} %copy-done.52, f32[768,384]{1,0:T(8,128)S(1)} %copy-done.38, ...), custom_call_target="tpu_custom_call" | custom-call | flops 7549747200 | bytes 2949120 | tf_op jit(solution)/shard_map/attn_bwd/pallas_call | solution.py:276
  346.7 3.4 collective-permute-done.34
  354.2 2.7 copy-done.2
  358.9 5.2 qkv_bwd.3
  371.1 2.4 copy-done.36
  373.4 6.9 %attn_bwd.4 = (f32[640,576]{1,0:T(8,128)S(1)}, f32[1,576]{1,0:T(1,128)S(1)}) custom-call(s32[3]{0:T(128)S(1)} %copy-done.28, s32[3]{0:T(128)S(1)} %copy-done.34, f32[1920,576]{1,0:T(8,128)S(1)} %copy-done.36, f32[24,640]{1,0:T(8,128)S(1)} %copy-done.62, f32[192,384]{1,0:T(8,128)S(1)} %copy-done.53, f32[768,384]{1,0:T(8,128)S(1)} %copy-done.39, ...), custom_call_target="tpu_custom_call" | custom-call | flops 7549747200 | bytes 2949120 | tf_op jit(solution)/shard_map/attn_bwd/pallas_call | solution.py:276
  384.3 2.7 copy-done.3
  390.5 5.2 qkv_bwd.4
  402.7 2.4 copy-done.37
  405.1 6.9 %attn_bwd.5 = (f32[640,576]{1,0:T(8,128)S(1)}, f32[1,576]{1,0:T(1,128)S(1)}) custom-call(s32[3]{0:T(128)S(1)} %copy-done.29, s32[3]{0:T(128)S(1)} %copy-done.35, f32[1920,576]{1,0:T(8,128)S(1)} %copy-done.37, f32[24,640]{1,0:T(8,128)S(1)} %copy-done.63, f32[192,384]{1,0:T(8,128)S(1)} %copy-done.54, f32[768,384]{1,0:T(8,128)S(1)} %copy-done.40, ...), custom_call_target="tpu_custom_call" | custom-call | flops 7549747200 | bytes 2949120 | tf_op jit(solution)/shard_map/attn_bwd/pallas_call | solution.py:276
  419.3 2.7 copy-done.4
  424.0 5.2 qkv_bwd.5
  436.4 5.1 collective-permute-done.49
  446.6 15.5 %collective-permute-done.50 = f32[120,768]{1,0:T(8,128)} collective-permute-done((f32[120,768]{1,0:T(8,128)}, f32[120,768]{1,0:T(8,128)}, u32[]{:S(2)}, u32[]{:S(2)}) %collective-permute-start.50) | collective-permute-done | bytes 368672 | tf_op jit(solution)/shard_map/ppermute | solution.py:779
  466.5 2.2 fusion.26.refs_0_
  470.7 2.4 collective-permute-start.56
  474.4 3.8 collective-permute-start.58
  478.2 10.1 %collective-permute-done.58 = f32[64,768]{1,0:T(8,128)S(1)} collective-permute-done((f32[64,768]{1,0:T(8,128)}, f32[64,768]{1,0:T(8,128)S(1)}, u32[]{:S(2)}, u32[]{:S(2)}) %collective-permute-start.58) | collective-permute-done | bytes 196640 | tf_op jit(solution)/shard_map/ppermute | solution.py:779
  496.4 2.1 collective-permute-start.62
  498.9 10.4 %collective-permute-done.63 = f32[32,768]{1,0:T(8,128)} collective-permute-done((f32[32,768]{1,0:T(8,128)}, f32[32,768]{1,0:T(8,128)}, u32[]{:S(2)}, u32[]{:S(2)}) %collective-permute-start.63) | collective-permute-done | bytes 98336 | tf_op jit(solution)/shard_map/ppermute | solution.py:779
  512.2 3.7 collective-permute-start.66
  518.1 2.4 collective-permute-start.67
  520.7 7.6 %collective-permute-done.68 = f32[32,768]{1,0:T(8,128)S(1)} collective-permute-done((f32[32,768]{1,0:T(8,128)S(1)}, f32[32,768]{1,0:T(8,128)S(1)}, u32[]{:S(2)}, u32[]{:S(2)}) %collective-permute-start.68) | collective-permute-done | bytes 98336 | tf_op jit(solution)/shard_map/ppermute | solution.py:779
  528.2 3.3 collective-permute-done.67
  532.6 8.1 %collective-permute-done.69 = f32[320,768]{1,0:T(8,128)S(1)} collective-permute-done((f32[320,768]{1,0:T(8,128)S(1)}, f32[320,768]{1,0:T(8,128)S(1)}, u32[]{:S(2)}, u32[]{:S(2)}) %collective-permute-start.69) | collective-permute-done | bytes 983072 | tf_op jit(solution)/shard_map/ppermute | solution.py:679
  543.7 3.1 collective-permute-start.73
  547.2 11.5 %collective-permute-done.73 = f32[64,768]{1,0:T(8,128)S(1)} collective-permute-done((f32[64,768]{1,0:T(8,128)S(1)}, f32[64,768]{1,0:T(8,128)S(1)}, u32[]{:S(2)}, u32[]{:S(2)}) %collective-permute-start.73) | collective-permute-done | bytes 196640 | tf_op jit(solution)/shard_map/ppermute | solution.py:779
  558.6 2.3 collective-permute-done.72
  564.2 2.5 collective-permute-start.77
  569.4 6.4 collective-permute-done.77.refs_5_
  577.7 11.0 %collective-permute-done.80 = f32[128,768]{1,0:T(8,128)S(1)} collective-permute-done((f32[128,768]{1,0:T(8,128)S(1)}, f32[128,768]{1,0:T(8,128)S(1)}, u32[]{:S(2)}, u32[]{:S(2)}) %collective-permute-start.80) | collective-permute-done | bytes 393248 | tf_op jit(solution)/shard_map/ppermute | solution.py:779
  590.7 5.9 final_rows.1
  603.6 7.4 %collective-permute-done.84 = f32[20,768]{1,0:T(8,128)S(1)} collective-permute-done((f32[20,768]{1,0:T(8,128)S(1)}, f32[20,768]{1,0:T(8,128)S(1)}, u32[]{:S(2)}, u32[]{:S(2)}) %collective-permute-start.84) | collective-permute-done | bytes 61472 | tf_op jit(solution)/shard_map/ppermute | solution.py:779
  614.3 9.4 %collective-permute-done.87 = f32[20,768]{1,0:T(8,128)S(1)} collective-permute-done((f32[20,768]{1,0:T(8,128)S(1)}, f32[20,768]{1,0:T(8,128)S(1)}, u32[]{:S(2)}, u32[]{:S(2)}) %collective-permute-start.87) | collective-permute-done | bytes 61472 | tf_op jit(solution)/shard_map/ppermute | solution.py:779
  627.9 4.1 assemble.3
  632.1 3.9 assemble.2
  (582 shorter events, 156.2 us)
Async XLA Ops:
  0.7 70.1 %collective-permute-start.3 = (f32[768,768]{1,0:T(8,128)}, f32[768,768]{1,0:T(8,128)}, u32[]{:S(2)}, u32[]{:S(2)}) collective-permute-start(f32[768,768]{1,0:T(8,128)} %refs_19_.1), channel_id=1, source_target_pairs={{0,1},{1,0},{2,3},{3,2},{4,5},{5,4},{6,7},{7,6},{8,9},{9,8},{10,11... | collective-permute-start | bytes 7077896 | tf_op jit(solution)/shard_map/ppermute | solution.py:679
  1.2 69.6 %collective-permute-start.4 = (f32[768,768]{1,0:T(8,128)}, f32[768,768]{1,0:T(8,128)}, u32[]{:S(2)}, u32[]{:S(2)}) collective-permute-start(f32[768,768]{1,0:T(8,128)} %refs_20_.1), channel_id=1, source_target_pairs={{0,1},{1,0},{2,3},{3,2},{4,5},{5,4},{6,7},{7,6},{8,9},{9,8},{10,11... | collective-permute-start | bytes 7077896 | tf_op jit(solution)/shard_map/ppermute | solution.py:679
  11.4 59.3 %collective-permute-start = (f32[480,768]{1,0:T(8,128)}, f32[480,768]{1,0:T(8,128)}, u32[]{:S(2)}, u32[]{:S(2)}) collective-permute-start(f32[480,768]{1,0:T(8,128)} %pad_maximum_fusion.1), channel_id=1, source_target_pairs={{0,2},{1,3},{2,0},{3,1},{4,6},{5,7},{6,4},{7,5},{8,10},{9,11},{10,... | collective-permute-start | bytes 4423688 | tf_op jit(solution)/shard_map/ppermute | solution.py:679
  14.3 56.4 %collective-permute-start.1 = (f32[384,768]{1,0:T(8,128)}, f32[384,768]{1,0:T(8,128)}, u32[]{:S(2)}, u32[]{:S(2)}) collective-permute-start(f32[384,768]{1,0:T(8,128)} %constant_dynamic-slice_fusion.10), channel_id=1, source_target_pairs={{0,2},{1,3},{2,0},{3,1},{4,6},{5,7},{6,4},{7,5},{8,10},{9,11},{10,... | collective-permute-start | bytes 3538952 | tf_op jit(solution)/shard_map/ppermute | solution.py:679
  27.0 26.3 %collective-permute-start.2 = (f32[192,768]{1,0:T(8,128)S(1)}, f32[192,768]{1,0:T(8,128)}, u32[]{:S(2)}, u32[]{:S(2)}) collective-permute-start(f32[192,768]{1,0:T(8,128)S(1)} %copy-done.131), channel_id=1, source_target_pairs={{0,1},{1,0},{2,3},{3,2},{4,5},{5,4},{6,7},{7,6},{8,9},{9,8},{10,11... | collective-permute-start | bytes 1769480 | tf_op jit(solution)/shard_map/ppermute | solution.py:679
  71.4 35.0 %collective-permute-start.11 = (f32[480,768]{1,0:T(8,128)}, f32[480,768]{1,0:T(8,128)}, u32[]{:S(2)}, u32[]{:S(2)}) collective-permute-start(f32[480,768]{1,0:T(8,128)} %collective-permute-done.refs_18_.refs_26_.refs_19_.refs_27_.refs_23_), channel_id=1, source_target_pairs={{0,4},{4,0},{8,12},{12,8},{16,20},{20,16},{24,28},{28,24},{1,5},{5... | collective-permute-start | bytes 4423688 | tf_op jit(solution)/shard_map/ppermute | solution.py:679
  71.7 34.7 %collective-permute-start.14 = (f32[480,768]{1,0:T(8,128)}, f32[480,768]{1,0:T(8,128)}, u32[]{:S(2)}, u32[]{:S(2)}) collective-permute-start(f32[480,768]{1,0:T(8,128)} %collective-permute-done.refs_18_.refs_26_.refs_19_.refs_27_.refs_23_), channel_id=1, source_target_pairs={{0,1},{1,0},{2,3},{3,2},{4,5},{5,4},{6,7},{7,6},{8,9},{9,8},{10,11... | collective-permute-start | bytes 4423688 | tf_op jit(solution)/shard_map/ppermute | solution.py:679
  71.9 28.5 %collective-permute-start.12 = (f32[384,768]{1,0:T(8,128)}, f32[384,768]{1,0:T(8,128)}, u32[]{:S(2)}, u32[]{:S(2)}) collective-permute-start(f32[384,768]{1,0:T(8,128)} %collective-permute-done.1.refs_27_.refs_28_.refs_24_), channel_id=1, source_target_pairs={{0,8},{4,12},{8,0},{12,4},{16,24},{20,28},{24,16},{28,20},{1,9},{5... | collective-permute-start | bytes 3538952 | tf_op jit(solution)/shard_map/ppermute | solution.py:679
  78.6 21.9 %collective-permute-start.15 = (f32[384,768]{1,0:T(8,128)}, f32[384,768]{1,0:T(8,128)}, u32[]{:S(2)}, u32[]{:S(2)}) collective-permute-start(f32[384,768]{1,0:T(8,128)} %collective-permute-done.1.refs_27_.refs_28_.refs_24_), channel_id=1, source_target_pairs={{0,1},{1,0},{2,3},{3,2},{4,5},{5,4},{6,7},{7,6},{8,9},{9,8},{10,11... | collective-permute-start | bytes 3538952 | tf_op jit(solution)/shard_map/ppermute | solution.py:679
  78.6 21.8 %collective-permute-start.17 = (f32[768,384]{1,0:T(8,128)}, f32[768,384]{1,0:T(8,128)}, u32[]{:S(2)}, u32[]{:S(2)}) collective-permute-start(f32[768,384]{1,0:T(8,128)} %get-tuple-element.256.refs_7_.refs_5_), channel_id=1, source_target_pairs={{0,1},{1,0},{2,3},{3,2},{4,5},{5,4},{6,7},{7,6},{8,9},{9,8},{10,11... | collective-permute-start | bytes 3538952 | tf_op jit(solution)/shard_map/ppermute | solution.py:679
  106.9 28.8 %collective-permute-start.22 = (f32[768,384]{1,0:T(8,128)}, f32[768,384]{1,0:T(8,128)}, u32[]{:S(2)}, u32[]{:S(2)}) collective-permute-start(f32[768,384]{1,0:T(8,128)} %get-tuple-element.256.refs_7_.refs_5_), channel_id=1, source_target_pairs={{0,2},{1,3},{2,0},{3,1},{4,6},{5,7},{6,4},{7,5},{8,10},{9,11},{10,... | collective-permute-start | bytes 3538952 | tf_op jit(solution)/shard_map/ppermute | solution.py:679
  135.7 12.1 %collective-permute-start.23 = (f32[768,384]{1,0:T(8,128)}, f32[768,384]{1,0:T(8,128)}, u32[]{:S(2)}, u32[]{:S(2)}) collective-permute-start(f32[768,384]{1,0:T(8,128)} %collective-permute-done.22.refs_9_), channel_id=1, source_target_pairs={{0,1},{1,0},{2,3},{3,2},{4,5},{5,4},{6,7},{7,6},{8,9},{9,8},{10,11... | collective-permute-start | bytes 3538952 | tf_op jit(solution)/shard_map/ppermute | solution.py:679
  142.5 34.5 %all-to-all-start = ((f32[8,48,192]{2,1,0:T(8,128)}), f32[8,48,192]{2,1,0:T(8,128)S(1)}, u32[]{:S(2)}, u32[]{:S(2)}) async-start(f32[8,48,192]{2,1,0:T(8,128)} %bitcast.8), calls=%async_computation | async-start | bytes 786432 | tf_op jit(solution)/shard_map/all_to_all | solution.py:913
  182.4 31.0 %collective-permute-start.25 = (f32[128,768]{1,0:T(8,128)S(1)}, f32[128,768]{1,0:T(8,128)S(1)}, u32[]{:S(2)}, u32[]{:S(2)}) collective-permute-start(f32[128,768]{1,0:T(8,128)S(1)} %dynamic-slice_add_fusion.1), channel_id=1, source_target_pairs={{0,2},{1,3},{2,0},{3,1},{4,6},{5,7},{6,4},{7,5},{8,10},{9,11},{10,... | collective-permute-start | bytes 1179656 | tf_op jit(solution)/shard_map/ppermute | solution.py:679
  219.3 35.4 %all-to-all-start.1 = ((f32[8,48,192]{2,1,0:T(8,128)}), f32[8,48,192]{2,1,0:T(8,128)S(1)}, u32[]{:S(2)}, u32[]{:S(2)}) async-start(f32[8,48,192]{2,1,0:T(8,128)} %bitcast.12), calls=%async_computation.1 | async-start | bytes 786432 | tf_op jit(solution)/shard_map/all_to_all | solution.py:913
  256.6 14.2 %collective-permute-start.30 = (f32[768,768]{1,0:T(8,128)}, f32[768,768]{1,0:T(8,128)}, u32[]{:S(2)}, u32[]{:S(2)}) collective-permute-start(f32[768,768]{1,0:T(8,128)} %get-tuple-element.313.mt), channel_id=1, source_target_pairs={{0,1},{1,0},{2,3},{3,2},{4,5},{5,4},{6,7},{7,6},{8,9},{9,8},{10,11... | collective-permute-start | bytes 7077896 | tf_op jit(solution)/shard_map/ppermute | solution.py:679
  307.5 13.9 %collective-permute-start.33 = (f32[768,768]{1,0:T(8,128)}, f32[768,768]{1,0:T(8,128)}, u32[]{:S(2)}, u32[]{:S(2)}) collective-permute-start(f32[768,768]{1,0:T(8,128)} %fusion.68), channel_id=1, source_target_pairs={{0,1},{1,0},{2,3},{3,2},{4,5},{5,4},{6,7},{7,6},{8,9},{9,8},{10,11... | collective-permute-start | bytes 7077896 | tf_op jit(solution)/shard_map/ppermute | solution.py:679
  313.6 15.7 %collective-permute-start.31 = (f32[768,768]{1,0:T(8,128)}, f32[768,768]{1,0:T(8,128)}, u32[]{:S(2)}, u32[]{:S(2)}) collective-permute-start(f32[768,768]{1,0:T(8,128)} %fusion.67), channel_id=1, source_target_pairs={{0,1},{1,0},{2,3},{3,2},{4,5},{5,4},{6,7},{7,6},{8,9},{9,8},{10,11... | collective-permute-start | bytes 7077896 | tf_op jit(solution)/shard_map/ppermute | solution.py:679
  315.4 24.3 %collective-permute-start.37 = (f32[768,384]{1,0:T(8,128)S(1)}, f32[768,384]{1,0:T(8,128)S(1)}, u32[]{:S(2)}, u32[]{:S(2)}) collective-permute-start(f32[768,384]{1,0:T(8,128)S(1)} %copy-done.44), channel_id=1, source_target_pairs={{0,1},{1,0},{2,3},{3,2},{4,5},{5,4},{6,7},{7,6},{8,9},{9,8},{10,11... | collective-permute-start | bytes 3538952 | tf_op jit(solution)/shard_map/ppermute | solution.py:679
  317.7 21.9 %collective-permute-start.36 = (f32[192,384]{1,0:T(8,128)S(1)}, f32[192,384]{1,0:T(8,128)S(1)}, u32[]{:S(2)}, u32[]{:S(2)}) collective-permute-start(f32[192,384]{1,0:T(8,128)S(1)} %copy-done.55), channel_id=1, source_target_pairs={{0,1},{1,0},{2,3},{3,2},{4,5},{5,4},{6,7},{7,6},{8,9},{9,8},{10,11... | collective-permute-start | bytes 884744 | tf_op jit(solution)/shard_map/ppermute | solution.py:679
  337.1 13.0 %collective-permute-start.35 = (f32[144,768]{1,0:T(8,128)S(1)}, f32[144,768]{1,0:T(8,128)S(1)}, u32[]{:S(2)}, u32[]{:S(2)}) collective-permute-start(f32[144,768]{1,0:T(8,128)S(1)} %fusion.8), channel_id=1, source_target_pairs={{0,4},{8,0},{16,8},{24,16},{28,24},{20,28},{12,20},{4,12},{1,5},{9... | collective-permute-start | bytes 1327112 | tf_op jit(solution)/shard_map/ppermute | solution.py:779
  339.2 11.0 %collective-permute-start.34 = (f32[120,768]{1,0:T(8,128)S(1)}, f32[120,768]{1,0:T(8,128)S(1)}, u32[]{:S(2)}, u32[]{:S(2)}) collective-permute-start(f32[120,768]{1,0:T(8,128)S(1)} %fusion.27), channel_id=1, source_target_pairs={{0,8},{8,16},{16,24},{24,28},{28,20},{20,12},{12,4},{4,0},{1,9},{9... | collective-permute-start | bytes 1105928 | tf_op jit(solution)/shard_map/ppermute | solution.py:779
  352.0 12.3 %collective-permute-start.39 = (f32[144,768]{1,0:T(8,128)}, f32[144,768]{1,0:T(8,128)}, u32[]{:S(2)}, u32[]{:S(2)}) collective-permute-start(f32[144,768]{1,0:T(8,128)} %fusion.10), channel_id=1, source_target_pairs={{0,4},{8,0},{16,8},{24,16},{28,24},{20,28},{12,20},{4,12},{1,5},{9... | collective-permute-start | bytes 1327112 | tf_op jit(solution)/shard_map/ppermute | solution.py:779
  368.7 11.6 %collective-permute-start.42 = (f32[144,768]{1,0:T(8,128)S(1)}, f32[144,768]{1,0:T(8,128)S(1)}, u32[]{:S(2)}, u32[]{:S(2)}) collective-permute-start(f32[144,768]{1,0:T(8,128)S(1)} %fusion.12), channel_id=1, source_target_pairs={{0,4},{8,0},{16,8},{24,16},{28,24},{20,28},{12,20},{4,12},{1,5},{9... | collective-permute-start | bytes 1327112 | tf_op jit(solution)/shard_map/ppermute | solution.py:779
  382.2 13.6 %collective-permute-start.44 = (f32[144,768]{1,0:T(8,128)}, f32[144,768]{1,0:T(8,128)}, u32[]{:S(2)}, u32[]{:S(2)}) collective-permute-start(f32[144,768]{1,0:T(8,128)} %fusion.14), channel_id=1, source_target_pairs={{0,4},{8,0},{16,8},{24,16},{28,24},{20,28},{12,20},{4,12},{1,5},{9... | collective-permute-start | bytes 1327112 | tf_op jit(solution)/shard_map/ppermute | solution.py:779
  383.7 12.1 %collective-permute-start.43 = (f32[120,768]{1,0:T(8,128)}, f32[120,768]{1,0:T(8,128)}, u32[]{:S(2)}, u32[]{:S(2)}) collective-permute-start(f32[120,768]{1,0:T(8,128)} %fusion.33), channel_id=1, source_target_pairs={{0,8},{8,16},{16,24},{24,28},{28,20},{20,12},{12,4},{4,0},{1,9},{9... | collective-permute-start | bytes 1105928 | tf_op jit(solution)/shard_map/ppermute | solution.py:779
  384.3 32.7 %collective-permute-start.40 = (f32[320,768]{1,0:T(8,128)}, f32[320,768]{1,0:T(8,128)}, u32[]{:S(2)}, u32[]{:S(2)}) collective-permute-start(f32[320,768]{1,0:T(8,128)} %copy-done.51), channel_id=1, source_target_pairs={{0,1},{1,0},{2,3},{3,2},{4,5},{5,4},{6,7},{7,6},{8,9},{9,8},{10,11... | collective-permute-start | bytes 2949128 | tf_op jit(solution)/shard_map/ppermute | solution.py:679
  400.3 12.6 %collective-permute-start.46 = (f32[144,768]{1,0:T(8,128)S(1)}, f32[144,768]{1,0:T(8,128)S(1)}, u32[]{:S(2)}, u32[]{:S(2)}) collective-permute-start(f32[144,768]{1,0:T(8,128)S(1)} %fusion.16), channel_id=1, source_target_pairs={{0,4},{8,0},{16,8},{24,16},{28,24},{20,28},{12,20},{4,12},{1,5},{9... | collective-permute-start | bytes 1327112 | tf_op jit(solution)/shard_map/ppermute | solution.py:779
  414.7 14.7 %collective-permute-start.48 = (f32[144,768]{1,0:T(8,128)}, f32[144,768]{1,0:T(8,128)}, u32[]{:S(2)}, u32[]{:S(2)}) collective-permute-start(f32[144,768]{1,0:T(8,128)} %fusion.18), channel_id=1, source_target_pairs={{0,4},{8,0},{16,8},{24,16},{28,24},{20,28},{12,20},{4,12},{1,5},{9... | collective-permute-start | bytes 1327112 | tf_op jit(solution)/shard_map/ppermute | solution.py:779
  416.1 13.2 %collective-permute-start.47 = (f32[120,768]{1,0:T(8,128)}, f32[120,768]{1,0:T(8,128)}, u32[]{:S(2)}, u32[]{:S(2)}) collective-permute-start(f32[120,768]{1,0:T(8,128)} %fusion.37), channel_id=1, source_target_pairs={{0,8},{8,16},{16,24},{24,28},{28,20},{20,12},{12,4},{4,0},{1,9},{9... | collective-permute-start | bytes 1105928 | tf_op jit(solution)/shard_map/ppermute | solution.py:779
  418.7 22.9 %collective-permute-start.49 = (f32[320,768]{1,0:T(8,128)S(1)}, f32[320,768]{1,0:T(8,128)S(1)}, u32[]{:S(2)}, u32[]{:S(2)}) collective-permute-start(f32[320,768]{1,0:T(8,128)S(1)} %add.506), channel_id=1, source_target_pairs={{0,2},{1,3},{2,0},{3,1},{4,6},{5,7},{6,4},{7,5},{8,10},{9,11},{10,... | collective-permute-start | bytes 2949128 | tf_op jit(solution)/shard_map/ppermute | solution.py:679
  442.5 20.2 %collective-permute-start.52 = (f32[160,768]{1,0:T(8,128)}, f32[160,768]{1,0:T(8,128)}, u32[]{:S(2)}, u32[]{:S(2)}) collective-permute-start(f32[160,768]{1,0:T(8,128)} %constant_dynamic-slice_fusion.5), channel_id=1, source_target_pairs={{0,4},{4,0},{8,12},{12,8},{16,20},{20,16},{24,28},{28,24},{1,5},{5... | collective-permute-start | bytes 1474568 | tf_op jit(solution)/shard_map/ppermute | solution.py:779
  444.0 18.8 %collective-permute-start.51 = (f32[144,768]{1,0:T(8,128)}, f32[144,768]{1,0:T(8,128)}, u32[]{:S(2)}, u32[]{:S(2)}) collective-permute-start(f32[144,768]{1,0:T(8,128)} %fusion.20), channel_id=1, source_target_pairs={{0,4},{8,0},{16,8},{24,16},{28,24},{20,28},{12,20},{4,12},{1,5},{9... | collective-permute-start | bytes 1327112 | tf_op jit(solution)/shard_map/ppermute | solution.py:779
  444.5 18.2 %collective-permute-start.53 = (f32[128,768]{1,0:T(8,128)}, f32[128,768]{1,0:T(8,128)}, u32[]{:S(2)}, u32[]{:S(2)}) collective-permute-start(f32[128,768]{1,0:T(8,128)} %constant_dynamic-slice_fusion.4), channel_id=1, source_target_pairs={{0,8},{4,12},{8,0},{12,4},{16,24},{20,28},{24,16},{28,20},{1,9},{5... | collective-permute-start | bytes 1179656 | tf_op jit(solution)/shard_map/ppermute | solution.py:779
  446.0 16.1 %collective-permute-start.50 = (f32[120,768]{1,0:T(8,128)}, f32[120,768]{1,0:T(8,128)}, u32[]{:S(2)}, u32[]{:S(2)}) collective-permute-start(f32[120,768]{1,0:T(8,128)} %fusion.39), channel_id=1, source_target_pairs={{0,8},{8,16},{16,24},{24,28},{28,20},{20,12},{12,4},{4,0},{1,9},{9... | collective-permute-start | bytes 1105928 | tf_op jit(solution)/shard_map/ppermute | solution.py:779
  446.6 26.5 %collective-permute-start.54 = (f32[320,768]{1,0:T(8,128)S(1)}, f32[320,768]{1,0:T(8,128)S(1)}, u32[]{:S(2)}, u32[]{:S(2)}) collective-permute-start(f32[320,768]{1,0:T(8,128)S(1)} %copy-done.48), channel_id=1, source_target_pairs={{0,1},{1,0},{2,3},{3,2},{4,5},{5,4},{6,7},{7,6},{8,9},{9,8},{10,11... | collective-permute-start | bytes 2949128 | tf_op jit(solution)/shard_map/ppermute | solution.py:679
  470.7 19.1 %collective-permute-start.56 = (f32[144,768]{1,0:T(8,128)}, f32[144,768]{1,0:T(8,128)}, u32[]{:S(2)}, u32[]{:S(2)}) collective-permute-start(f32[144,768]{1,0:T(8,128)} %fusion.7.refs_0_), channel_id=1, source_target_pairs={{0,4},{8,0},{16,8},{24,16},{28,24},{20,28},{12,20},{4,12},{1,5},{9... | collective-permute-start | bytes 1327112 | tf_op jit(solution)/shard_map/ppermute | solution.py:779
  473.1 16.7 %collective-permute-start.55 = (f32[120,768]{1,0:T(8,128)}, f32[120,768]{1,0:T(8,128)}, u32[]{:S(2)}, u32[]{:S(2)}) collective-permute-start(f32[120,768]{1,0:T(8,128)} %fusion.26.refs_0_), channel_id=1, source_target_pairs={{0,8},{8,16},{16,24},{24,28},{28,20},{20,12},{12,4},{4,0},{1,9},{9... | collective-permute-start | bytes 1105928 | tf_op jit(solution)/shard_map/ppermute | solution.py:779
  473.2 20.9 %collective-permute-start.59 = (f32[320,768]{1,0:T(8,128)S(1)}, f32[320,768]{1,0:T(8,128)}, u32[]{:S(2)}, u32[]{:S(2)}) collective-permute-start(f32[320,768]{1,0:T(8,128)S(1)} %add.543), channel_id=1, source_target_pairs={{0,2},{1,3},{2,0},{3,1},{4,6},{5,7},{6,4},{7,5},{8,10},{9,11},{10,... | collective-permute-start | bytes 2949128 | tf_op jit(solution)/shard_map/ppermute | solution.py:679
  473.8 16.0 %collective-permute-start.57 = (f32[80,768]{1,0:T(8,128)}, f32[80,768]{1,0:T(8,128)}, u32[]{:S(2)}, u32[]{:S(2)}) collective-permute-start(f32[80,768]{1,0:T(8,128)} %constant_dynamic-slice_fusion.3), channel_id=1, source_target_pairs={{0,8},{4,12},{8,0},{12,4},{16,24},{20,28},{24,16},{28,20},{1,9},{5... | collective-permute-start | bytes 737288 | tf_op jit(solution)/shard_map/ppermute | solution.py:779
  474.4 13.8 %collective-permute-start.58 = (f32[64,768]{1,0:T(8,128)}, f32[64,768]{1,0:T(8,128)S(1)}, u32[]{:S(2)}, u32[]{:S(2)}) collective-permute-start(f32[64,768]{1,0:T(8,128)} %constant_dynamic-slice_fusion.2), channel_id=1, source_target_pairs={{0,16},{4,20},{8,24},{12,28},{16,0},{20,4},{24,8},{28,12},{1,17},{... | collective-permute-start | bytes 589832 | tf_op jit(solution)/shard_map/ppermute | solution.py:779
  494.1 15.6 %collective-permute-start.61 = (f32[144,768]{1,0:T(8,128)}, f32[144,768]{1,0:T(8,128)}, u32[]{:S(2)}, u32[]{:S(2)}) collective-permute-start(f32[144,768]{1,0:T(8,128)} %collective-permute-done.56.refs_1_), channel_id=1, source_target_pairs={{0,4},{8,0},{16,8},{24,16},{28,24},{20,28},{12,20},{4,12},{1,5},{9... | collective-permute-start | bytes 1327112 | tf_op jit(solution)/shard_map/ppermute | solution.py:779
  495.8 20.2 %collective-permute-start.64 = (f32[320,768]{1,0:T(8,128)S(1)}, f32[320,768]{1,0:T(8,128)}, u32[]{:S(2)}, u32[]{:S(2)}) collective-permute-start(f32[320,768]{1,0:T(8,128)S(1)} %copy-done.50), channel_id=1, source_target_pairs={{0,1},{1,0},{2,3},{3,2},{4,5},{5,4},{6,7},{7,6},{8,9},{9,8},{10,11... | collective-permute-start | bytes 2949128 | tf_op jit(solution)/shard_map/ppermute | solution.py:679
  495.8 13.9 %collective-permute-start.60 = (f32[120,768]{1,0:T(8,128)}, f32[120,768]{1,0:T(8,128)}, u32[]{:S(2)}, u32[]{:S(2)}) collective-permute-start(f32[120,768]{1,0:T(8,128)} %collective-permute-done.55.refs_1_), channel_id=1, source_target_pairs={{0,8},{8,16},{16,24},{24,28},{28,20},{20,12},{12,4},{4,0},{1,9},{9... | collective-permute-start | bytes 1105928 | tf_op jit(solution)/shard_map/ppermute | solution.py:779
  496.4 13.3 %collective-permute-start.62 = (f32[40,768]{1,0:T(8,128)S(1)}, f32[40,768]{1,0:T(8,128)}, u32[]{:S(2)}, u32[]{:S(2)}) collective-permute-start(f32[40,768]{1,0:T(8,128)S(1)} %constant_dynamic-slice_fusion.1), channel_id=1, source_target_pairs={{0,16},{4,20},{8,24},{12,28},{16,0},{20,4},{24,8},{28,12},{1,17},{... | collective-permute-start | bytes 368648 | tf_op jit(solution)/shard_map/ppermute | solution.py:779
  512.2 19.3 %collective-permute-start.66 = (f32[144,768]{1,0:T(8,128)}, f32[144,768]{1,0:T(8,128)}, u32[]{:S(2)}, u32[]{:S(2)}) collective-permute-start(f32[144,768]{1,0:T(8,128)} %collective-permute-done.61.refs_2_), channel_id=1, source_target_pairs={{0,4},{8,0},{16,8},{24,16},{28,24},{20,28},{12,20},{4,12},{1,5},{9... | collective-permute-start | bytes 1327112 | tf_op jit(solution)/shard_map/ppermute | solution.py:779
  516.0 15.6 %collective-permute-start.65 = (f32[120,768]{1,0:T(8,128)}, f32[120,768]{1,0:T(8,128)}, u32[]{:S(2)}, u32[]{:S(2)}) collective-permute-start(f32[120,768]{1,0:T(8,128)} %collective-permute-done.60.refs_2_), channel_id=1, source_target_pairs={{0,8},{8,16},{16,24},{24,28},{28,20},{20,12},{12,4},{4,0},{1,9},{9... | collective-permute-start | bytes 1105928 | tf_op jit(solution)/shard_map/ppermute | solution.py:779
  517.5 23.2 %collective-permute-start.69 = (f32[320,768]{1,0:T(8,128)S(1)}, f32[320,768]{1,0:T(8,128)S(1)}, u32[]{:S(2)}, u32[]{:S(2)}) collective-permute-start(f32[320,768]{1,0:T(8,128)S(1)} %add.565), channel_id=1, source_target_pairs={{0,2},{1,3},{2,0},{3,1},{4,6},{5,7},{6,4},{7,5},{8,10},{9,11},{10,... | collective-permute-start | bytes 2949128 | tf_op jit(solution)/shard_map/ppermute | solution.py:679
  518.1 13.5 %collective-permute-start.67 = (f32[40,768]{1,0:T(8,128)S(1)}, f32[40,768]{1,0:T(8,128)S(1)}, u32[]{:S(2)}, u32[]{:S(2)}) collective-permute-start(f32[40,768]{1,0:T(8,128)S(1)} %dynamic-slice_add_fusion.5), channel_id=1, source_target_pairs={{0,16},{4,20},{8,24},{12,28},{16,0},{20,4},{24,8},{28,12},{1,17},{... | collective-permute-start | bytes 368648 | tf_op jit(solution)/shard_map/ppermute | solution.py:779
  540.6 20.3 %collective-permute-start.71 = (f32[144,768]{1,0:T(8,128)}, f32[144,768]{1,0:T(8,128)S(1)}, u32[]{:S(2)}, u32[]{:S(2)}) collective-permute-start(f32[144,768]{1,0:T(8,128)} %collective-permute-done.66.refs_3_), channel_id=1, source_target_pairs={{0,4},{8,0},{16,8},{24,16},{28,24},{20,28},{12,20},{4,12},{1,5},{9... | collective-permute-start | bytes 1327112 | tf_op jit(solution)/shard_map/ppermute | solution.py:779
  542.4 18.6 %collective-permute-start.70 = (f32[120,768]{1,0:T(8,128)}, f32[120,768]{1,0:T(8,128)S(1)}, u32[]{:S(2)}, u32[]{:S(2)}) collective-permute-start(f32[120,768]{1,0:T(8,128)} %collective-permute-done.65.refs_3_), channel_id=1, source_target_pairs={{0,8},{8,16},{16,24},{24,28},{28,20},{20,12},{12,4},{4,0},{1,9},{9... | collective-permute-start | bytes 1105928 | tf_op jit(solution)/shard_map/ppermute | solution.py:779
  542.7 18.2 %collective-permute-start.72 = (f32[80,768]{1,0:T(8,128)S(1)}, f32[80,768]{1,0:T(8,128)S(1)}, u32[]{:S(2)}, u32[]{:S(2)}) collective-permute-start(f32[80,768]{1,0:T(8,128)S(1)} %pad_maximum_fusion.10), channel_id=1, source_target_pairs={{0,8},{4,12},{8,0},{12,4},{16,24},{20,28},{24,16},{28,20},{1,9},{5... | collective-permute-start | bytes 737288 | tf_op jit(solution)/shard_map/ppermute | solution.py:779
  543.7 14.9 %collective-permute-start.73 = (f32[64,768]{1,0:T(8,128)S(1)}, f32[64,768]{1,0:T(8,128)S(1)}, u32[]{:S(2)}, u32[]{:S(2)}) collective-permute-start(f32[64,768]{1,0:T(8,128)S(1)} %pad_maximum_fusion.11), channel_id=1, source_target_pairs={{0,16},{4,20},{8,24},{12,28},{16,0},{20,4},{24,8},{28,12},{1,17},{... | collective-permute-start | bytes 589832 | tf_op jit(solution)/shard_map/ppermute | solution.py:779
  547.1 41.6 %collective-permute-start.74 = (f32[320,768]{1,0:T(8,128)S(1)}, f32[320,768]{1,0:T(8,128)S(1)}, u32[]{:S(2)}, u32[]{:S(2)}) collective-permute-start(f32[320,768]{1,0:T(8,128)S(1)} %maximum_add_fusion.refs_1_), channel_id=1, source_target_pairs={{0,1},{1,0},{2,3},{3,2},{4,5},{5,4},{6,7},{7,6},{8,9},{9,8},{10,11... | collective-permute-start | bytes 2949128 | tf_op jit(solution)/shard_map/ppermute | solution.py:679
  563.1 27.6 %collective-permute-start.75 = (f32[320,768]{1,0:T(8,128)S(1)}, f32[320,768]{1,0:T(8,128)}, u32[]{:S(2)}, u32[]{:S(2)}) collective-permute-start(f32[320,768]{1,0:T(8,128)S(1)} %maximum_add_fusion.1.refs_2_), channel_id=1, source_target_pairs={{0,1},{1,0},{2,3},{3,2},{4,5},{5,4},{6,7},{7,6},{8,9},{9,8},{10,11... | collective-permute-start | bytes 2949128 | tf_op jit(solution)/shard_map/ppermute | solution.py:679
  564.2 11.6 %collective-permute-start.77 = (f32[120,768]{1,0:T(8,128)S(1)}, f32[120,768]{1,0:T(8,128)}, u32[]{:S(2)}, u32[]{:S(2)}) collective-permute-start(f32[120,768]{1,0:T(8,128)S(1)} %collective-permute-done.70.refs_4_), channel_id=1, source_target_pairs={{0,8},{8,16},{16,24},{24,28},{28,20},{20,12},{12,4},{4,0},{1,9},{9... | collective-permute-start | bytes 1105928 | tf_op jit(solution)/shard_map/ppermute | solution.py:779
  566.9 21.8 %collective-permute-start.79 = (f32[160,768]{1,0:T(8,128)S(1)}, f32[160,768]{1,0:T(8,128)S(1)}, u32[]{:S(2)}, u32[]{:S(2)}) collective-permute-start(f32[160,768]{1,0:T(8,128)S(1)} %pad_maximum_fusion.3), channel_id=1, source_target_pairs={{0,4},{4,0},{8,12},{12,8},{16,20},{20,16},{24,28},{28,24},{1,5},{5... | collective-permute-start | bytes 1474568 | tf_op jit(solution)/shard_map/ppermute | solution.py:779
  568.0 20.7 %collective-permute-start.78 = (f32[144,768]{1,0:T(8,128)S(1)}, f32[144,768]{1,0:T(8,128)S(1)}, u32[]{:S(2)}, u32[]{:S(2)}) collective-permute-start(f32[144,768]{1,0:T(8,128)S(1)} %collective-permute-done.71.refs_4_), channel_id=1, source_target_pairs={{0,4},{8,0},{16,8},{24,16},{28,24},{20,28},{12,20},{4,12},{1,5},{9... | collective-permute-start | bytes 1327112 | tf_op jit(solution)/shard_map/ppermute | solution.py:779
  575.8 12.9 %collective-permute-start.80 = (f32[128,768]{1,0:T(8,128)S(1)}, f32[128,768]{1,0:T(8,128)S(1)}, u32[]{:S(2)}, u32[]{:S(2)}) collective-permute-start(f32[128,768]{1,0:T(8,128)S(1)} %pad_maximum_fusion.6), channel_id=1, source_target_pairs={{0,8},{4,12},{8,0},{12,4},{16,24},{20,28},{24,16},{28,20},{1,9},{5... | collective-permute-start | bytes 1179656 | tf_op jit(solution)/shard_map/ppermute | solution.py:779
  597.4 13.6 %collective-permute-start.83 = (f32[144,768]{1,0:T(8,128)}, f32[144,768]{1,0:T(8,128)}, u32[]{:S(2)}, u32[]{:S(2)}) collective-permute-start(f32[144,768]{1,0:T(8,128)} %copy-done.124), channel_id=1, source_target_pairs={{0,4},{8,0},{16,8},{24,16},{28,24},{20,28},{12,20},{4,12},{1,5},{9... | collective-permute-start | bytes 1327112 | tf_op jit(solution)/shard_map/ppermute | solution.py:779
  598.9 12.1 %collective-permute-start.82 = (f32[120,768]{1,0:T(8,128)}, f32[120,768]{1,0:T(8,128)}, u32[]{:S(2)}, u32[]{:S(2)}) collective-permute-start(f32[120,768]{1,0:T(8,128)} %collective-permute-done.77.refs_5_), channel_id=1, source_target_pairs={{0,8},{8,16},{16,24},{24,28},{28,20},{20,12},{12,4},{4,0},{1,9},{9... | collective-permute-start | bytes 1105928 | tf_op jit(solution)/shard_map/ppermute | solution.py:779
  611.0 12.7 %collective-permute-start.86 = (f32[144,768]{1,0:T(8,128)}, f32[144,768]{1,0:T(8,128)S(1)}, u32[]{:S(2)}, u32[]{:S(2)}) collective-permute-start(f32[144,768]{1,0:T(8,128)} %collective-permute-done.83.refs_6_), channel_id=1, source_target_pairs={{0,4},{8,0},{16,8},{24,16},{28,24},{20,28},{12,20},{4,12},{1,5},{9... | collective-permute-start | bytes 1327112 | tf_op jit(solution)/shard_map/ppermute | solution.py:779
  612.6 11.0 %collective-permute-start.85 = (f32[120,768]{1,0:T(8,128)}, f32[120,768]{1,0:T(8,128)S(1)}, u32[]{:S(2)}, u32[]{:S(2)}) collective-permute-start(f32[120,768]{1,0:T(8,128)} %collective-permute-done.82.refs_6_), channel_id=1, source_target_pairs={{0,8},{8,16},{16,24},{24,28},{28,20},{20,12},{12,4},{4,0},{1,9},{9... | collective-permute-start | bytes 1105928 | tf_op jit(solution)/shard_map/ppermute | solution.py:779
  623.7 12.2 %collective-permute-start.88 = (f32[20,768]{1,0:T(8,128)S(1)}, f32[20,768]{1,0:T(8,128)S(1)}, u32[]{:S(2)}, u32[]{:S(2)}) collective-permute-start(f32[20,768]{1,0:T(8,128)S(1)} %add.579), channel_id=1, source_target_pairs={{0,16},{4,20},{8,24},{12,28},{16,0},{20,4},{24,8},{28,12},{1,17},{... | collective-permute-start | bytes 184328 | tf_op jit(solution)/shard_map/ppermute | solution.py:779
  (182 other events, 1483.7 us)

commit v4 on v3

--- a/solution.py
+++ b/solution.py
@@ -1010,8 +1010,10 @@
         chip_sum = gx_mine + from_sib(gx_theirs)
         gx.append((chip_sum, from_x(chip_sum)))
     cut = w_sum.shape[0] * 5 // 9
-    steps.add("qkv_low", halving(w_sum[:cut], 0))
-    steps.add("qkv_high", halving(w_sum[cut:], 1))
+    qkv_steps = Steps()
+    qkv_steps.add("qkv_low", halving(w_sum[:cut], 0))
+    qkv_steps.add("qkv_high", halving(w_sum[cut:], 1))
+    qkv_steps.finish()
     gh_mine, gh_theirs = [], []
     for doc in range(docs):
         first = jnp.concatenate(
@@ -1042,6 +1044,7 @@
     )
     steps.add("vectors", cube(vectors))
     steps.finish()
+    steps.results.update(qkv_steps.results)
     vectors, in_out, back_pair, low, high = (
         steps.results[name] for name in ("vectors", "in_out", "back_pair", "qkv_low", "qkv_high")
     )

time: 647 us -> 604 us (0.934)
  waiting for transfers between devices: 200 us -> 181 us
  other arithmetic: 45.9 us -> 29.9 us
  local copies, waits for them, and re-layouts: 54.9 us -> 47.3 us
    ppermute x43, waiting for transfers between devices: 102 us -> 86.2 us  [run(): lax.ppermute(x, *self.active[name][1][1:])]
    add x14, other arithmetic: 19.5 us -> 10.4 us  [ring(): held = got + lax.dynamic_slice_in_dim(part, at(step), size, 0)]
    unnamed x311 -> x305, local copies, waits for them, and re-layouts: 30.9 us -> 23.1 us
    add x6, other arithmetic: 6.81 us -> 0.21 us  [halving(): part = keep + (yield (give, 'dp', pairs(bit)))]
  transfers between devices with their start and end apart: 91 -> 91, of which waited for: 37 -> 37; matrix products, arithmetic and copies ran while one was open for 13% -> 11% of each run, Pallas kernels for 27% -> 30%
where the time goes in v4:
time: 604 us; the launch traced here: 596 us
  Pallas kernels  208 us (34%)
  waiting for transfers between devices  181 us (30%)
  starting transfers between devices  87.8 us (15%)
  local copies, waits for them, and re-layouts  47.3 us (8%)
  matrix products  39.7 us (7%)
  other arithmetic  29.9 us (5%)
    pallas_call x5, Pallas kernels, ffn(): pl.pallas_call(functools.partial(ffn_kernel, forward, backward, all_names...  125 us
    ppermute x46, waiting for transfers between devices, swap(): return lax.ppermute(x, axis, [(i, i ^ bit) for i in range(n)])  94.4 us
    ppermute x43, waiting for transfers between devices, run(): lax.ppermute(x, *self.active[name][1][1:])  86.2 us
    ppermute x43, starting transfers between devices, run(): lax.ppermute(x, *self.active[name][1][1:])  52.3 us
    dot_general x14, matrix products, product(): lax.dot_general(operand, other, (dims, ((), ())), precision=HIGH, preferr...  39.7 us
    ppermute x46, starting transfers between devices, swap(): return lax.ppermute(x, axis, [(i, i ^ bit) for i in range(n)])  24 us
    unnamed x305, local copies, waits for them, and re-layouts  23.1 us
    pallas_call x1, Pallas kernels, attn_fwd(): pl.pallas_call(functools.partial(attn_fwd_kernel, all_rows), grid=(docs,)...  22.3 us
  transfers between devices with their start and end apart: 91, of which 37 were waited for; matrix products, arithmetic and copies ran while one was open for 11% of the time, Pallas kernels for 30%

profile of v4, /device:TPU:0, one launch (start us, length us, event | category | flops | bytes accessed | tf_op | source)
XLA Modules:
  0.0 596.3 jit_solution(1376774831386583376)
XLA Ops:
  1.3 2.2 local_stats.1
  3.4 2.9 collective-permute-start.5
  12.0 2.4 constant_dynamic-slice_fusion.10
  17.6 2.1 collective-permute-done.6
  22.4 2.6 collective-permute-start.7
  25.0 1.9 collective-permute-done.7
  27.1 1.9 copy.78.refs_7_.refs_6_
  30.9 22.3 %attn_fwd.1 = (f32[1920,576]{1,0:T(8,128)}, f32[24,640]{1,0:T(8,128)}, f32[192,384]{1,0:T(8,128)}, f32[768,384]{1,0:T(8,128)}, f32[192,768]{1,0:T(8,128)}, /*index=5*/f32[768,768]{1,0:T(8,128)}) custom-call(s32[3]{0:T(128)} %pad_add_fusion.refs_0_.place, s32[3]{0:T(128)} %refs_1_.22, f32[1920,768]{1,0:T(8,128)} %refs_1_.23, f32[384,768]{1,0:T(8,128)} %refs_7_.2, ...), custom_call_target="tpu_custom_call" | custom-call | flops 11520 | bytes 640 | tf_op jit(solution)/shard_map/attn_fwd/pallas_call | solution.py:189
  53.3 17.5 %collective-permute-done.1.refs_27_.refs_28_.refs_24_ = f32[384,768]{1,0:T(8,128)} collective-permute-done((f32[384,768]{1,0:T(8,128)}, f32[384,768]{1,0:T(8,128)}, u32[]{:S(2)}, u32[]{:S(2)}) %collective-permute-start.1) | collective-permute-done | bytes 1179680 | tf_op jit(solution)/shard_map/ppermute | solution.py:679
  73.7 4.9 collective-permute-done.13.refs_9_
  79.1 21.3 %collective-permute-done.12.refs_29_.refs_30_.refs_26_ = f32[384,768]{1,0:T(8,128)} collective-permute-done((f32[384,768]{1,0:T(8,128)}, f32[384,768]{1,0:T(8,128)}, u32[]{:S(2)}, u32[]{:S(2)}) %collective-permute-start.12) | collective-permute-done | bytes 1179680 | tf_op jit(solution)/shard_map/ppermute | solution.py:679
  100.4 6.0 collective-permute-done.11.refs_19_.refs_28_.refs_20_.refs_29_.refs_25_
  112.2 17.2 %ffn_fwd.1 = (f32[192,768]{1,0:T(8,128)}, f32[960,768]{1,0:T(8,128)}, f32[960,768]{1,0:T(8,128)}, f32[960,768]{1,0:T(8,128)}, f32[192,768]{1,0:T(8,128)}, /*inde...) custom-call(s32[3]{0:T(128)} %pad_add_fusion.refs_0_.place, f32[768]{0:T(1024)} %refs_1_.17, ...), custom_call_target="tpu_custom_call" | custom-call | flops 16307453952 | bytes 8847360 | tf_op jit(solution)/shard_map/ffn_fwd/pallas_call | solution.py:577
  129.4 6.4 %collective-permute-done.22.refs_9_ = f32[768,384]{1,0:T(8,128)} collective-permute-done((f32[768,384]{1,0:T(8,128)}, f32[768,384]{1,0:T(8,128)}, u32[]{:S(2)}, u32[]{:S(2)}) %collective-permute-start.22) | collective-permute-done | bytes 1179680 | tf_op jit(solution)/shard_map/ppermute | solution.py:679
  142.6 5.3 all-to-all-start
  147.9 29.2 %ffn_fwdbwd.3 = (f32[768,768]{1,0:T(8,128)}, f32[960,768]{1,0:T(8,128)}, f32[960,768]{1,0:T(8,128)}, f32[960,768]{1,0:T(8,128)}, f32[960,768]{1,0:T(8,128)}, /*i...) custom-call(s32[3]{0:T(128)} %pad_add_fusion.refs_0_.place, ...), custom_call_target="tpu_custom_call", output_to_operand_aliasing={{1}: (35, {}), {2}: (36, {}), {3}: (37, {})} | custom-call | flops 25367150592 | bytes 11796480 | tf_op jit(solution)/shard_map/ffn_fwdbwd/pallas_call | solution.py:577
  179.2 3.1 scatter_custom_fusion
  184.0 29.4 %ffn_fwdbwd.4 = (f32[768,768]{1,0:T(8,128)}, f32[960,768]{1,0:T(8,128)}, f32[960,768]{1,0:T(8,128)}, f32[960,768]{1,0:T(8,128)}, f32[960,768]{1,0:T(8,128)}, /*i...) custom-call(s32[3]{0:T(128)} %pad_add_fusion.refs_0_.place, ...), custom_call_target="tpu_custom_call", output_to_operand_aliasing={{0}: (35, {}), {1}: (36, {}), {2}: (37, {}), {3}: (38, {}),... | custom-call | flops 25367150592 | bytes 11796480 | tf_op jit(solution)/shard_map/ffn_fwdbwd/pallas_call | solution.py:577
  219.4 6.1 %all-to-all-start.1 = ((f32[8,48,192]{2,1,0:T(8,128)}), f32[8,48,192]{2,1,0:T(8,128)S(1)}, u32[]{:S(2)}, u32[]{:S(2)}) async-start(f32[8,48,192]{2,1,0:T(8,128)} %bitcast.12), calls=%async_computation.1 | async-start | bytes 786432 | tf_op jit(solution)/shard_map/all_to_all | solution.py:913
  225.5 29.3 %ffn_fwdbwd.5 = (f32[768,768]{1,0:T(8,128)}, f32[960,768]{1,0:T(8,128)}, f32[960,768]{1,0:T(8,128)}, f32[960,768]{1,0:T(8,128)}, f32[960,768]{1,0:T(8,128)}, /*i...) custom-call(s32[3]{0:T(128)} %pad_add_fusion.refs_0_.place, ...), custom_call_target="tpu_custom_call", output_to_operand_aliasing={{0}: (35, {}), {1}: (36, {}), {2}: (37, {}), {3}: (38, {}),... | custom-call | flops 25367150592 | bytes 11796480 | tf_op jit(solution)/shard_map/ffn_fwdbwd/pallas_call | solution.py:577
  257.4 3.8 collective-permute-done.27
  263.2 7.5 %collective-permute-done.28 = f32[192,384]{1,0:T(8,128)S(1)} collective-permute-done((f32[192,384]{1,0:T(8,128)S(1)}, f32[192,384]{1,0:T(8,128)S(1)}, u32[]{:S(2)}, u32[]{:S(2)}) %collective-permute-start.28) | collective-permute-done | bytes 294944 | tf_op jit(solution)/shard_map/ppermute | solution.py:679
  271.7 6.5 %join_rows.1 = f32[1920,768]{1,0:T(8,128)} custom-call(s32[3]{0:T(128)} %pad_add_fusion.refs_0_.place, f32[192,768]{1,0:T(8,128)} %get-tuple-element.271.ms, f32[768,768]{1,0:T(8,128)} %get-tuple-element.313.mt, f32[192,768]{1,0:T(8,128)} %copy-done.105, f32[768,768]{1,0:T(8,128)} %collective-permute-done.30.tt), custom_call_target="tpu_custom_call" | custom-call | bytes 11796480 | tf_op jit(solution)/shard_map/join_rows/pallas_call | solution.py:607
  279.0 20.3 %ffn_bwd.1 = (f32[960,768]{1,0:T(8,128)}, f32[960,768]{1,0:T(8,128)}, f32[960,768]{1,0:T(8,128)}, f32[960,768]{1,0:T(8,128)}, f32[192,384]{1,0:T(8,128)}, /*index=5*/f32[384,768]{1,0:T(8,128)}, f32[8,768]{1,0:T(8,128)}) custom-call(s32[3]{0:T(128)} %pad_add_fusion.refs_0_.place, ...), custom_call_target="tpu_custom_call", output_to_operand_aliasing={{0}: (31, {}), {1}: (32, {}), {2}: (33, {}), {3}: (34, {})} | custom-call | flops 16307453952 | bytes 8847360 | tf_op jit(solution)/shard_map/ffn_bwd/pallas_call | solution.py:577
  299.4 9.0 %fusion.68 = f32[768,768]{1,0:T(8,128)} fusion(f32[960,768]{1,0:T(8,128)} %get-tuple-element.335, f32[960,768]{1,0:T(8,128)} %get-tuple-element.334), kind=kOutput, calls=%fused_computation.205 | convolution fusion | flops 3397386240 | bytes 8257536 | tf_op jit(solution)/shard_map/dot_general | solution.py:24
  308.4 6.1 %fusion.67 = f32[768,768]{1,0:T(8,128)} fusion(f32[960,768]{1,0:T(8,128)S(1)} %copy-done.70, f32[960,768]{1,0:T(8,128)S(1)} %copy-done.83), kind=kOutput, calls=%fused_computation.204 | convolution fusion | flops 3397386240 | bytes 8257536 | tf_op jit(solution)/shard_map/dot_general | solution.py:24
  316.7 1.9 fusion.40
  318.7 2.5 collective-permute-done.32
  322.3 7.8 %convolution_add_fusion = f32[768,768]{1,0:T(8,128)S(1)} fusion(f32[768,768]{1,0:T(8,128)} %collective-permute-done.33, f32[960,768]{1,0:T(8,128)} %get-tuple-element.333, f32[960,768]{1,0:T(8,128)S(1)} %copy-done.72), kind=kOutput, calls=%fused_computation.36 | convolution fusion | flops 3397976064 | bytes 10616832 | tf_op jit(solution)/shard_map/dot_general | solution.py:24
  330.2 7.5 %convolution_add_fusion.1 = f32[768,768]{1,0:T(8,128)S(1)} fusion(f32[768,768]{1,0:T(8,128)} %collective-permute-done.31, f32[960,768]{1,0:T(8,128)S(1)} %copy-done.71, f32[960,768]{1,0:T(8,128)S(1)} %copy-done.82), kind=kOutput, calls=%fused_computation.37 | convolution fusion | flops 3397976064 | bytes 10616832 | tf_op jit(solution)/shard_map/dot_general | solution.py:24
  338.0 2.1 collective-permute-start.35
  340.7 7.0 %attn_bwd.3 = (f32[640,576]{1,0:T(8,128)S(1)}, f32[1,576]{1,0:T(1,128)S(1)}) custom-call(s32[3]{0:T(128)S(1)} %copy-done.19, s32[3]{0:T(128)S(1)} %copy-done.24, f32[1920,576]{1,0:T(8,128)S(1)} %bitcast.84, f32[24,640]{1,0:T(8,128)S(1)} %copy-done.48, f32[192,384]{1,0:T(8,128)S(1)} %copy-done.39, f32[768,384]{1,0:T(8,128)S(1)} %copy-done.29, ...), custom_call_target="tpu_custom_call" | custom-call | flops 7549747200 | bytes 2949120 | tf_op jit(solution)/shard_map/attn_bwd/pallas_call | solution.py:276
  347.7 3.3 collective-permute-done.34
  355.0 2.7 copy-done.2
  359.8 5.5 qkv_bwd.3
  366.2 2.4 fusion.12
  372.3 2.4 copy-done.27
  374.7 7.0 %attn_bwd.4 = (f32[640,576]{1,0:T(8,128)S(1)}, f32[1,576]{1,0:T(1,128)S(1)}) custom-call(s32[3]{0:T(128)S(1)} %copy-done.21, s32[3]{0:T(128)S(1)} %copy-done.25, f32[1920,576]{1,0:T(8,128)S(1)} %copy-done.27, f32[24,640]{1,0:T(8,128)S(1)} %copy-done.49, f32[192,384]{1,0:T(8,128)S(1)} %copy-done.40, f32[768,384]{1,0:T(8,128)S(1)} %copy-done.30, ...), custom_call_target="tpu_custom_call" | custom-call | flops 7549747200 | bytes 2949120 | tf_op jit(solution)/shard_map/attn_bwd/pallas_call | solution.py:276
  385.7 2.7 copy-done.3
  391.9 5.5 qkv_bwd.4
  402.9 2.4 copy-done.28
  405.3 7.0 %attn_bwd.5 = (f32[640,576]{1,0:T(8,128)S(1)}, f32[1,576]{1,0:T(1,128)S(1)}) custom-call(s32[3]{0:T(128)S(1)} %copy-done.23, s32[3]{0:T(128)S(1)} %copy-done.26, f32[1920,576]{1,0:T(8,128)S(1)} %copy-done.28, f32[24,640]{1,0:T(8,128)S(1)} %copy-done.50, f32[192,384]{1,0:T(8,128)S(1)} %copy-done.41, f32[768,384]{1,0:T(8,128)S(1)} %copy-done.31, ...), custom_call_target="tpu_custom_call" | custom-call | flops 7549747200 | bytes 2949120 | tf_op jit(solution)/shard_map/attn_bwd/pallas_call | solution.py:276
  417.9 5.5 qkv_bwd.5
  429.9 12.0 %collective-permute-done.49 = f32[320,768]{1,0:T(8,128)S(1)} collective-permute-done((f32[320,768]{1,0:T(8,128)S(1)}, f32[320,768]{1,0:T(8,128)S(1)}, u32[]{:S(2)}, u32[]{:S(2)}) %collective-permute-start.49) | collective-permute-done | bytes 983072 | tf_op jit(solution)/shard_map/ppermute | solution.py:679
  445.7 7.3 %collective-permute-done.50 = f32[120,768]{1,0:T(8,128)S(1)} collective-permute-done((f32[120,768]{1,0:T(8,128)S(1)}, f32[120,768]{1,0:T(8,128)S(1)}, u32[]{:S(2)}, u32[]{:S(2)}) %collective-permute-start.50) | collective-permute-done | bytes 368672 | tf_op jit(solution)/shard_map/ppermute | solution.py:779
  453.0 2.2 collective-permute-start.80
  455.2 1.9 collective-permute-done.51
  459.1 6.5 %collective-permute-done.80 = f32[64,768]{1,0:T(8,128)S(1)} collective-permute-done((f32[64,768]{1,0:T(8,128)S(1)}, f32[64,768]{1,0:T(8,128)S(1)}, u32[]{:S(2)}, u32[]{:S(2)}) %collective-permute-start.80) | collective-permute-done | bytes 196640 | tf_op jit(solution)/shard_map/ppermute | solution.py:779
  468.9 6.3 %collective-permute-done.82 = f32[32,768]{1,0:T(8,128)S(1)} collective-permute-done((f32[32,768]{1,0:T(8,128)S(1)}, f32[32,768]{1,0:T(8,128)S(1)}, u32[]{:S(2)}, u32[]{:S(2)}) %collective-permute-start.82) | collective-permute-done | bytes 98336 | tf_op jit(solution)/shard_map/ppermute | solution.py:779
  475.2 7.6 %collective-permute-done.81 = f32[40,768]{1,0:T(8,128)S(1)} collective-permute-done((f32[40,768]{1,0:T(8,128)S(1)}, f32[40,768]{1,0:T(8,128)S(1)}, u32[]{:S(2)}, u32[]{:S(2)}) %collective-permute-start.81) | collective-permute-done | bytes 122912 | tf_op jit(solution)/shard_map/ppermute | solution.py:779
  483.2 2.0 collective-permute-start.56
  487.6 6.6 %collective-permute-done.56.refs_2_ = f32[120,768]{1,0:T(8,128)S(1)} collective-permute-done((f32[120,768]{1,0:T(8,128)S(1)}, f32[120,768]{1,0:T(8,128)S(1)}, u32[]{:S(2)}, u32[]{:S(2)}) %collective-permute-start.56) | collective-permute-done | bytes 368672 | tf_op jit(solution)/shard_map/ppermute | solution.py:779
  498.8 6.1 %collective-permute-done.59.refs_3_ = f32[120,768]{1,0:T(8,128)S(1)} collective-permute-done((f32[120,768]{1,0:T(8,128)S(1)}, f32[120,768]{1,0:T(8,128)S(1)}, u32[]{:S(2)}, u32[]{:S(2)}) %collective-permute-start.59) | collective-permute-done | bytes 368672 | tf_op jit(solution)/shard_map/ppermute | solution.py:779
  509.2 6.6 %collective-permute-done.62.refs_4_ = f32[120,768]{1,0:T(8,128)S(1)} collective-permute-done((f32[120,768]{1,0:T(8,128)S(1)}, f32[120,768]{1,0:T(8,128)S(1)}, u32[]{:S(2)}, u32[]{:S(2)}) %collective-permute-start.62) | collective-permute-done | bytes 368672 | tf_op jit(solution)/shard_map/ppermute | solution.py:779
  515.8 4.4 collective-permute-start.86
  521.9 4.7 collective-permute-done.86
  532.3 7.4 %collective-permute-done.67.refs_5_ = f32[120,768]{1,0:T(8,128)S(1)} collective-permute-done((f32[120,768]{1,0:T(8,128)S(1)}, f32[120,768]{1,0:T(8,128)S(1)}, u32[]{:S(2)}, u32[]{:S(2)}) %collective-permute-start.67) | collective-permute-done | bytes 368672 | tf_op jit(solution)/shard_map/ppermute | solution.py:779
  541.5 5.9 final_rows.1
  548.2 2.2 concatenate.66
  558.8 9.5 %collective-permute-done.88 = f32[128,768]{1,0:T(8,128)} collective-permute-done((f32[128,768]{1,0:T(8,128)}, f32[128,768]{1,0:T(8,128)}, u32[]{:S(2)}, u32[]{:S(2)}) %collective-permute-start.88) | collective-permute-done | bytes 393248 | tf_op jit(solution)/shard_map/ppermute | solution.py:779
  569.3 2.0 collective-permute-start.73
  572.9 6.4 %collective-permute-done.75 = f32[20,768]{1,0:T(8,128)S(1)} collective-permute-done((f32[20,768]{1,0:T(8,128)S(1)}, f32[20,768]{1,0:T(8,128)S(1)}, u32[]{:S(2)}, u32[]{:S(2)}) %collective-permute-start.75) | collective-permute-done | bytes 61472 | tf_op jit(solution)/shard_map/ppermute | solution.py:779
  583.8 4.1 assemble.3
  588.0 3.9 assemble.2
  (577 shorter events, 135.1 us)
Async XLA Ops:
  0.7 70.1 %collective-permute-start.3 = (f32[768,768]{1,0:T(8,128)}, f32[768,768]{1,0:T(8,128)}, u32[]{:S(2)}, u32[]{:S(2)}) collective-permute-start(f32[768,768]{1,0:T(8,128)} %refs_19_.1), channel_id=1, source_target_pairs={{0,1},{1,0},{2,3},{3,2},{4,5},{5,4},{6,7},{7,6},{8,9},{9,8},{10,11... | collective-permute-start | bytes 7077896 | tf_op jit(solution)/shard_map/ppermute | solution.py:679
  1.2 69.6 %collective-permute-start.4 = (f32[768,768]{1,0:T(8,128)}, f32[768,768]{1,0:T(8,128)}, u32[]{:S(2)}, u32[]{:S(2)}) collective-permute-start(f32[768,768]{1,0:T(8,128)} %refs_20_.1), channel_id=1, source_target_pairs={{0,1},{1,0},{2,3},{3,2},{4,5},{5,4},{6,7},{7,6},{8,9},{9,8},{10,11... | collective-permute-start | bytes 7077896 | tf_op jit(solution)/shard_map/ppermute | solution.py:679
  3.4 10.9 %collective-permute-start.5 = (f32[2,768]{1,0:T(2,128)}, f32[2,768]{1,0:T(2,128)S(1)}, u32[]{:S(2)}, u32[]{:S(2)}) collective-permute-start(f32[2,768]{1,0:T(2,128)} %local_stats.1), channel_id=1, source_target_pairs={{0,4},{4,0},{8,12},{12,8},{16,20},{20,16},{24,28},{28,24},{1,5},{5... | collective-permute-start | bytes 18440 | tf_op jit(solution)/shard_map/ppermute | solution.py:679
  11.4 59.3 %collective-permute-start = (f32[480,768]{1,0:T(8,128)}, f32[480,768]{1,0:T(8,128)}, u32[]{:S(2)}, u32[]{:S(2)}) collective-permute-start(f32[480,768]{1,0:T(8,128)} %pad_maximum_fusion.1), channel_id=1, source_target_pairs={{0,2},{1,3},{2,0},{3,1},{4,6},{5,7},{6,4},{7,5},{8,10},{9,11},{10,... | collective-permute-start | bytes 4423688 | tf_op jit(solution)/shard_map/ppermute | solution.py:679
  14.3 56.4 %collective-permute-start.1 = (f32[384,768]{1,0:T(8,128)}, f32[384,768]{1,0:T(8,128)}, u32[]{:S(2)}, u32[]{:S(2)}) collective-permute-start(f32[384,768]{1,0:T(8,128)} %constant_dynamic-slice_fusion.10), channel_id=1, source_target_pairs={{0,2},{1,3},{2,0},{3,1},{4,6},{5,7},{6,4},{7,5},{8,10},{9,11},{10,... | collective-permute-start | bytes 3538952 | tf_op jit(solution)/shard_map/ppermute | solution.py:679
  27.0 26.3 %collective-permute-start.2 = (f32[192,768]{1,0:T(8,128)S(1)}, f32[192,768]{1,0:T(8,128)}, u32[]{:S(2)}, u32[]{:S(2)}) collective-permute-start(f32[192,768]{1,0:T(8,128)S(1)} %copy-done.119), channel_id=1, source_target_pairs={{0,1},{1,0},{2,3},{3,2},{4,5},{5,4},{6,7},{7,6},{8,9},{9,8},{10,11... | collective-permute-start | bytes 1769480 | tf_op jit(solution)/shard_map/ppermute | solution.py:679
  71.4 35.0 %collective-permute-start.11 = (f32[480,768]{1,0:T(8,128)}, f32[480,768]{1,0:T(8,128)}, u32[]{:S(2)}, u32[]{:S(2)}) collective-permute-start(f32[480,768]{1,0:T(8,128)} %collective-permute-done.refs_18_.refs_26_.refs_19_.refs_27_.refs_23_), channel_id=1, source_target_pairs={{0,4},{4,0},{8,12},{12,8},{16,20},{20,16},{24,28},{28,24},{1,5},{5... | collective-permute-start | bytes 4423688 | tf_op jit(solution)/shard_map/ppermute | solution.py:679
  71.7 34.7 %collective-permute-start.14 = (f32[480,768]{1,0:T(8,128)}, f32[480,768]{1,0:T(8,128)S(1)}, u32[]{:S(2)}, u32[]{:S(2)}) collective-permute-start(f32[480,768]{1,0:T(8,128)} %collective-permute-done.refs_18_.refs_26_.refs_19_.refs_27_.refs_23_), channel_id=1, source_target_pairs={{0,1},{1,0},{2,3},{3,2},{4,5},{5,4},{6,7},{7,6},{8,9},{9,8},{10,11... | collective-permute-start | bytes 4423688 | tf_op jit(solution)/shard_map/ppermute | solution.py:679
  71.9 28.5 %collective-permute-start.12 = (f32[384,768]{1,0:T(8,128)}, f32[384,768]{1,0:T(8,128)}, u32[]{:S(2)}, u32[]{:S(2)}) collective-permute-start(f32[384,768]{1,0:T(8,128)} %collective-permute-done.1.refs_27_.refs_28_.refs_24_), channel_id=1, source_target_pairs={{0,8},{4,12},{8,0},{12,4},{16,24},{20,28},{24,16},{28,20},{1,9},{5... | collective-permute-start | bytes 3538952 | tf_op jit(solution)/shard_map/ppermute | solution.py:679
  78.6 21.8 %collective-permute-start.15 = (f32[384,768]{1,0:T(8,128)}, f32[384,768]{1,0:T(8,128)S(1)}, u32[]{:S(2)}, u32[]{:S(2)}) collective-permute-start(f32[384,768]{1,0:T(8,128)} %collective-permute-done.1.refs_27_.refs_28_.refs_24_), channel_id=1, source_target_pairs={{0,1},{1,0},{2,3},{3,2},{4,5},{5,4},{6,7},{7,6},{8,9},{9,8},{10,11... | collective-permute-start | bytes 3538952 | tf_op jit(solution)/shard_map/ppermute | solution.py:679
  78.6 21.8 %collective-permute-start.17 = (f32[768,384]{1,0:T(8,128)}, f32[768,384]{1,0:T(8,128)S(1)}, u32[]{:S(2)}, u32[]{:S(2)}) collective-permute-start(f32[768,384]{1,0:T(8,128)} %get-tuple-element.256.refs_7_.refs_5_), channel_id=1, source_target_pairs={{0,1},{1,0},{2,3},{3,2},{4,5},{5,4},{6,7},{7,6},{8,9},{9,8},{10,11... | collective-permute-start | bytes 3538952 | tf_op jit(solution)/shard_map/ppermute | solution.py:679
  107.5 28.2 %collective-permute-start.22 = (f32[768,384]{1,0:T(8,128)}, f32[768,384]{1,0:T(8,128)}, u32[]{:S(2)}, u32[]{:S(2)}) collective-permute-start(f32[768,384]{1,0:T(8,128)} %get-tuple-element.256.refs_7_.refs_5_), channel_id=1, source_target_pairs={{0,2},{1,3},{2,0},{3,1},{4,6},{5,7},{6,4},{7,5},{8,10},{9,11},{10,... | collective-permute-start | bytes 3538952 | tf_op jit(solution)/shard_map/ppermute | solution.py:679
  135.8 12.1 %collective-permute-start.23 = (f32[768,384]{1,0:T(8,128)}, f32[768,384]{1,0:T(8,128)}, u32[]{:S(2)}, u32[]{:S(2)}) collective-permute-start(f32[768,384]{1,0:T(8,128)} %collective-permute-done.22.refs_9_), channel_id=1, source_target_pairs={{0,1},{1,0},{2,3},{3,2},{4,5},{5,4},{6,7},{7,6},{8,9},{9,8},{10,11... | collective-permute-start | bytes 3538952 | tf_op jit(solution)/shard_map/ppermute | solution.py:679
  142.6 34.5 %all-to-all-start = ((f32[8,48,192]{2,1,0:T(8,128)}), f32[8,48,192]{2,1,0:T(8,128)S(1)}, u32[]{:S(2)}, u32[]{:S(2)}) async-start(f32[8,48,192]{2,1,0:T(8,128)} %bitcast.8), calls=%async_computation | async-start | bytes 786432 | tf_op jit(solution)/shard_map/all_to_all | solution.py:913
  182.4 31.0 %collective-permute-start.25 = (f32[128,768]{1,0:T(8,128)S(1)}, f32[128,768]{1,0:T(8,128)S(1)}, u32[]{:S(2)}, u32[]{:S(2)}) collective-permute-start(f32[128,768]{1,0:T(8,128)S(1)} %dynamic-slice_add_fusion.1), channel_id=1, source_target_pairs={{0,2},{1,3},{2,0},{3,1},{4,6},{5,7},{6,4},{7,5},{8,10},{9,11},{10,... | collective-permute-start | bytes 1179656 | tf_op jit(solution)/shard_map/ppermute | solution.py:679
  219.4 35.5 %all-to-all-start.1 = ((f32[8,48,192]{2,1,0:T(8,128)}), f32[8,48,192]{2,1,0:T(8,128)S(1)}, u32[]{:S(2)}, u32[]{:S(2)}) async-start(f32[8,48,192]{2,1,0:T(8,128)} %bitcast.12), calls=%async_computation.1 | async-start | bytes 786432 | tf_op jit(solution)/shard_map/all_to_all | solution.py:913
  256.7 14.2 %collective-permute-start.30 = (f32[768,768]{1,0:T(8,128)}, f32[768,768]{1,0:T(8,128)}, u32[]{:S(2)}, u32[]{:S(2)}) collective-permute-start(f32[768,768]{1,0:T(8,128)} %get-tuple-element.313.mt), channel_id=1, source_target_pairs={{0,1},{1,0},{2,3},{3,2},{4,5},{5,4},{6,7},{7,6},{8,9},{9,8},{10,11... | collective-permute-start | bytes 7077896 | tf_op jit(solution)/shard_map/ppermute | solution.py:679
  308.4 13.9 %collective-permute-start.33 = (f32[768,768]{1,0:T(8,128)}, f32[768,768]{1,0:T(8,128)}, u32[]{:S(2)}, u32[]{:S(2)}) collective-permute-start(f32[768,768]{1,0:T(8,128)} %fusion.68), channel_id=1, source_target_pairs={{0,1},{1,0},{2,3},{3,2},{4,5},{5,4},{6,7},{7,6},{8,9},{9,8},{10,11... | collective-permute-start | bytes 7077896 | tf_op jit(solution)/shard_map/ppermute | solution.py:679
  314.5 15.7 %collective-permute-start.31 = (f32[768,768]{1,0:T(8,128)}, f32[768,768]{1,0:T(8,128)}, u32[]{:S(2)}, u32[]{:S(2)}) collective-permute-start(f32[768,768]{1,0:T(8,128)} %fusion.67), channel_id=1, source_target_pairs={{0,1},{1,0},{2,3},{3,2},{4,5},{5,4},{6,7},{7,6},{8,9},{9,8},{10,11... | collective-permute-start | bytes 7077896 | tf_op jit(solution)/shard_map/ppermute | solution.py:679
  316.2 24.3 %collective-permute-start.37 = (f32[768,384]{1,0:T(8,128)S(1)}, f32[768,384]{1,0:T(8,128)S(1)}, u32[]{:S(2)}, u32[]{:S(2)}) collective-permute-start(f32[768,384]{1,0:T(8,128)S(1)} %copy-done.35), channel_id=1, source_target_pairs={{0,1},{1,0},{2,3},{3,2},{4,5},{5,4},{6,7},{7,6},{8,9},{9,8},{10,11... | collective-permute-start | bytes 3538952 | tf_op jit(solution)/shard_map/ppermute | solution.py:679
  318.6 21.9 %collective-permute-start.36 = (f32[192,384]{1,0:T(8,128)S(1)}, f32[192,384]{1,0:T(8,128)S(1)}, u32[]{:S(2)}, u32[]{:S(2)}) collective-permute-start(f32[192,384]{1,0:T(8,128)S(1)} %copy-done.42), channel_id=1, source_target_pairs={{0,1},{1,0},{2,3},{3,2},{4,5},{5,4},{6,7},{7,6},{8,9},{9,8},{10,11... | collective-permute-start | bytes 884744 | tf_op jit(solution)/shard_map/ppermute | solution.py:679
  338.0 13.0 %collective-permute-start.35 = (f32[144,768]{1,0:T(8,128)S(1)}, f32[144,768]{1,0:T(8,128)S(1)}, u32[]{:S(2)}, u32[]{:S(2)}) collective-permute-start(f32[144,768]{1,0:T(8,128)S(1)} %fusion.8), channel_id=1, source_target_pairs={{0,4},{8,0},{16,8},{24,16},{28,24},{20,28},{12,20},{4,12},{1,5},{9... | collective-permute-start | bytes 1327112 | tf_op jit(solution)/shard_map/ppermute | solution.py:779
  340.1 11.0 %collective-permute-start.34 = (f32[120,768]{1,0:T(8,128)S(1)}, f32[120,768]{1,0:T(8,128)S(1)}, u32[]{:S(2)}, u32[]{:S(2)}) collective-permute-start(f32[120,768]{1,0:T(8,128)S(1)} %fusion.27), channel_id=1, source_target_pairs={{0,8},{8,16},{16,24},{24,28},{28,20},{20,12},{12,4},{4,0},{1,9},{9... | collective-permute-start | bytes 1105928 | tf_op jit(solution)/shard_map/ppermute | solution.py:779
  352.8 12.5 %collective-permute-start.39 = (f32[144,768]{1,0:T(8,128)}, f32[144,768]{1,0:T(8,128)}, u32[]{:S(2)}, u32[]{:S(2)}) collective-permute-start(f32[144,768]{1,0:T(8,128)} %fusion.10), channel_id=1, source_target_pairs={{0,4},{8,0},{16,8},{24,16},{28,24},{20,28},{12,20},{4,12},{1,5},{9... | collective-permute-start | bytes 1327112 | tf_op jit(solution)/shard_map/ppermute | solution.py:779
  354.3 11.0 %collective-permute-start.38 = (f32[120,768]{1,0:T(8,128)}, f32[120,768]{1,0:T(8,128)}, u32[]{:S(2)}, u32[]{:S(2)}) collective-permute-start(f32[120,768]{1,0:T(8,128)} %fusion.29), channel_id=1, source_target_pairs={{0,8},{8,16},{16,24},{24,28},{28,20},{20,12},{12,4},{4,0},{1,9},{9... | collective-permute-start | bytes 1105928 | tf_op jit(solution)/shard_map/ppermute | solution.py:779
  370.0 11.7 %collective-permute-start.42 = (f32[144,768]{1,0:T(8,128)S(1)}, f32[144,768]{1,0:T(8,128)S(1)}, u32[]{:S(2)}, u32[]{:S(2)}) collective-permute-start(f32[144,768]{1,0:T(8,128)S(1)} %fusion.12), channel_id=1, source_target_pairs={{0,4},{8,0},{16,8},{24,16},{28,24},{20,28},{12,20},{4,12},{1,5},{9... | collective-permute-start | bytes 1327112 | tf_op jit(solution)/shard_map/ppermute | solution.py:779
  371.6 10.2 %collective-permute-start.41 = (f32[120,768]{1,0:T(8,128)S(1)}, f32[120,768]{1,0:T(8,128)S(1)}, u32[]{:S(2)}, u32[]{:S(2)}) collective-permute-start(f32[120,768]{1,0:T(8,128)S(1)} %fusion.31), channel_id=1, source_target_pairs={{0,8},{8,16},{16,24},{24,28},{28,20},{20,12},{12,4},{4,0},{1,9},{9... | collective-permute-start | bytes 1105928 | tf_op jit(solution)/shard_map/ppermute | solution.py:779
  383.6 13.8 %collective-permute-start.44 = (f32[144,768]{1,0:T(8,128)}, f32[144,768]{1,0:T(8,128)}, u32[]{:S(2)}, u32[]{:S(2)}) collective-permute-start(f32[144,768]{1,0:T(8,128)} %fusion.14), channel_id=1, source_target_pairs={{0,4},{8,0},{16,8},{24,16},{28,24},{20,28},{12,20},{4,12},{1,5},{9... | collective-permute-start | bytes 1327112 | tf_op jit(solution)/shard_map/ppermute | solution.py:779
  385.1 12.3 %collective-permute-start.43 = (f32[120,768]{1,0:T(8,128)}, f32[120,768]{1,0:T(8,128)}, u32[]{:S(2)}, u32[]{:S(2)}) collective-permute-start(f32[120,768]{1,0:T(8,128)} %fusion.33), channel_id=1, source_target_pairs={{0,8},{8,16},{16,24},{24,28},{28,20},{20,12},{12,4},{4,0},{1,9},{9... | collective-permute-start | bytes 1105928 | tf_op jit(solution)/shard_map/ppermute | solution.py:779
  385.7 31.5 %collective-permute-start.40 = (f32[320,768]{1,0:T(8,128)}, f32[320,768]{1,0:T(8,128)S(1)}, u32[]{:S(2)}, u32[]{:S(2)}) collective-permute-start(f32[320,768]{1,0:T(8,128)} %copy-done.38), channel_id=1, source_target_pairs={{0,1},{1,0},{2,3},{3,2},{4,5},{5,4},{6,7},{7,6},{8,9},{9,8},{10,11... | collective-permute-start | bytes 2949128 | tf_op jit(solution)/shard_map/ppermute | solution.py:679
  400.6 12.6 %collective-permute-start.46 = (f32[144,768]{1,0:T(8,128)S(1)}, f32[144,768]{1,0:T(8,128)S(1)}, u32[]{:S(2)}, u32[]{:S(2)}) collective-permute-start(f32[144,768]{1,0:T(8,128)S(1)} %fusion.16), channel_id=1, source_target_pairs={{0,4},{8,0},{16,8},{24,16},{28,24},{20,28},{12,20},{4,12},{1,5},{9... | collective-permute-start | bytes 1327112 | tf_op jit(solution)/shard_map/ppermute | solution.py:779
  402.1 10.9 %collective-permute-start.45 = (f32[120,768]{1,0:T(8,128)S(1)}, f32[120,768]{1,0:T(8,128)S(1)}, u32[]{:S(2)}, u32[]{:S(2)}) collective-permute-start(f32[120,768]{1,0:T(8,128)S(1)} %fusion.35), channel_id=1, source_target_pairs={{0,8},{8,16},{16,24},{24,28},{28,20},{20,12},{12,4},{4,0},{1,9},{9... | collective-permute-start | bytes 1105928 | tf_op jit(solution)/shard_map/ppermute | solution.py:779
  413.5 11.9 %collective-permute-start.48 = (f32[144,768]{1,0:T(8,128)S(1)}, f32[144,768]{1,0:T(8,128)S(1)}, u32[]{:S(2)}, u32[]{:S(2)}) collective-permute-start(f32[144,768]{1,0:T(8,128)S(1)} %fusion.18), channel_id=1, source_target_pairs={{0,4},{8,0},{16,8},{24,16},{28,24},{20,28},{12,20},{4,12},{1,5},{9... | collective-permute-start | bytes 1327112 | tf_op jit(solution)/shard_map/ppermute | solution.py:779
  417.2 12.0 %collective-permute-start.52 = (f32[320,768]{1,0:T(8,128)S(1)}, f32[320,768]{1,0:T(8,128)S(1)}, u32[]{:S(2)}, u32[]{:S(2)}) collective-permute-start(f32[320,768]{1,0:T(8,128)S(1)} %get-tuple-element.402), channel_id=1, source_target_pairs={{0,1},{1,0},{2,3},{3,2},{4,5},{5,4},{6,7},{7,6},{8,9},{9,8},{10,11... | collective-permute-start | bytes 2949128 | tf_op jit(solution)/shard_map/ppermute | solution.py:679
  417.3 24.6 %collective-permute-start.49 = (f32[320,768]{1,0:T(8,128)S(1)}, f32[320,768]{1,0:T(8,128)S(1)}, u32[]{:S(2)}, u32[]{:S(2)}) collective-permute-start(f32[320,768]{1,0:T(8,128)S(1)} %add.506), channel_id=1, source_target_pairs={{0,2},{1,3},{2,0},{3,1},{4,6},{5,7},{6,4},{7,5},{8,10},{9,11},{10,... | collective-permute-start | bytes 2949128 | tf_op jit(solution)/shard_map/ppermute | solution.py:679
  425.6 18.4 %collective-permute-start.77 = (f32[160,768]{1,0:T(8,128)S(1)}, f32[160,768]{1,0:T(8,128)S(1)}, u32[]{:S(2)}, u32[]{:S(2)}) collective-permute-start(f32[160,768]{1,0:T(8,128)S(1)} %constant_dynamic-slice_fusion.5), channel_id=1, source_target_pairs={{0,4},{4,0},{8,12},{12,8},{16,20},{20,16},{24,28},{28,24},{1,5},{5... | collective-permute-start | bytes 1474568 | tf_op jit(solution)/shard_map/ppermute | solution.py:779
  427.3 55.5 %collective-permute-start.58 = (f32[320,768]{1,0:T(8,128)S(1)}, f32[320,768]{1,0:T(8,128)S(1)}, u32[]{:S(2)}, u32[]{:S(2)}) collective-permute-start(f32[320,768]{1,0:T(8,128)S(1)} %get-tuple-element.414), channel_id=1, source_target_pairs={{0,1},{1,0},{2,3},{3,2},{4,5},{5,4},{6,7},{7,6},{8,9},{9,8},{10,11... | collective-permute-start | bytes 2949128 | tf_op jit(solution)/shard_map/ppermute | solution.py:679
  427.4 16.0 %collective-permute-start.78 = (f32[128,768]{1,0:T(8,128)S(1)}, f32[128,768]{1,0:T(8,128)S(1)}, u32[]{:S(2)}, u32[]{:S(2)}) collective-permute-start(f32[128,768]{1,0:T(8,128)S(1)} %constant_dynamic-slice_fusion.4), channel_id=1, source_target_pairs={{0,8},{4,12},{8,0},{12,4},{16,24},{20,28},{24,16},{28,20},{1,9},{5... | collective-permute-start | bytes 1179656 | tf_op jit(solution)/shard_map/ppermute | solution.py:779
  429.3 53.8 %collective-permute-start.55 = (f32[320,768]{1,0:T(8,128)S(1)}, f32[320,768]{1,0:T(8,128)S(1)}, u32[]{:S(2)}, u32[]{:S(2)}) collective-permute-start(f32[320,768]{1,0:T(8,128)S(1)} %add.539), channel_id=1, source_target_pairs={{0,2},{1,3},{2,0},{3,1},{4,6},{5,7},{6,4},{7,5},{8,10},{9,11},{10,... | collective-permute-start | bytes 2949128 | tf_op jit(solution)/shard_map/ppermute | solution.py:679
  441.9 15.2 %collective-permute-start.51 = (f32[144,768]{1,0:T(8,128)S(1)}, f32[144,768]{1,0:T(8,128)S(1)}, u32[]{:S(2)}, u32[]{:S(2)}) collective-permute-start(f32[144,768]{1,0:T(8,128)S(1)} %fusion.20), channel_id=1, source_target_pairs={{0,4},{8,0},{16,8},{24,16},{28,24},{20,28},{12,20},{4,12},{1,5},{9... | collective-permute-start | bytes 1327112 | tf_op jit(solution)/shard_map/ppermute | solution.py:779
  444.1 22.7 %collective-permute-start.79 = (f32[80,768]{1,0:T(8,128)S(1)}, f32[80,768]{1,0:T(8,128)S(1)}, u32[]{:S(2)}, u32[]{:S(2)}) collective-permute-start(f32[80,768]{1,0:T(8,128)S(1)} %constant_dynamic-slice_fusion.3), channel_id=1, source_target_pairs={{0,8},{4,12},{8,0},{12,4},{16,24},{20,28},{24,16},{28,20},{1,9},{5... | collective-permute-start | bytes 737288 | tf_op jit(solution)/shard_map/ppermute | solution.py:779
  453.0 12.6 %collective-permute-start.80 = (f32[64,768]{1,0:T(8,128)S(1)}, f32[64,768]{1,0:T(8,128)S(1)}, u32[]{:S(2)}, u32[]{:S(2)}) collective-permute-start(f32[64,768]{1,0:T(8,128)S(1)} %constant_dynamic-slice_fusion.2), channel_id=1, source_target_pairs={{0,16},{4,20},{8,24},{12,28},{16,0},{20,4},{24,8},{28,12},{1,17},{... | collective-permute-start | bytes 589832 | tf_op jit(solution)/shard_map/ppermute | solution.py:779
  457.4 25.7 %collective-permute-start.54 = (f32[144,768]{1,0:T(8,128)S(1)}, f32[144,768]{1,0:T(8,128)S(1)}, u32[]{:S(2)}, u32[]{:S(2)}) collective-permute-start(f32[144,768]{1,0:T(8,128)S(1)} %fusion.7.refs_0_), channel_id=1, source_target_pairs={{0,4},{8,0},{16,8},{24,16},{28,24},{20,28},{12,20},{4,12},{1,5},{9... | collective-permute-start | bytes 1327112 | tf_op jit(solution)/shard_map/ppermute | solution.py:779
  465.6 17.5 %collective-permute-start.53 = (f32[120,768]{1,0:T(8,128)S(1)}, f32[120,768]{1,0:T(8,128)S(1)}, u32[]{:S(2)}, u32[]{:S(2)}) collective-permute-start(f32[120,768]{1,0:T(8,128)S(1)} %fusion.26.refs_0_), channel_id=1, source_target_pairs={{0,8},{8,16},{16,24},{24,28},{28,20},{20,12},{12,4},{4,0},{1,9},{9... | collective-permute-start | bytes 1105928 | tf_op jit(solution)/shard_map/ppermute | solution.py:779
  483.0 22.8 %collective-permute-start.61 = (f32[320,768]{1,0:T(8,128)S(1)}, f32[320,768]{1,0:T(8,128)S(1)}, u32[]{:S(2)}, u32[]{:S(2)}) collective-permute-start(f32[320,768]{1,0:T(8,128)S(1)} %add.548), channel_id=1, source_target_pairs={{0,2},{1,3},{2,0},{3,1},{4,6},{5,7},{6,4},{7,5},{8,10},{9,11},{10,... | collective-permute-start | bytes 2949128 | tf_op jit(solution)/shard_map/ppermute | solution.py:679
  483.1 12.5 %collective-permute-start.57 = (f32[144,768]{1,0:T(8,128)S(1)}, f32[144,768]{1,0:T(8,128)S(1)}, u32[]{:S(2)}, u32[]{:S(2)}) collective-permute-start(f32[144,768]{1,0:T(8,128)S(1)} %collective-permute-done.54.refs_1_), channel_id=1, source_target_pairs={{0,4},{8,0},{16,8},{24,16},{28,24},{20,28},{12,20},{4,12},{1,5},{9... | collective-permute-start | bytes 1327112 | tf_op jit(solution)/shard_map/ppermute | solution.py:779
  483.2 11.1 %collective-permute-start.56 = (f32[120,768]{1,0:T(8,128)S(1)}, f32[120,768]{1,0:T(8,128)S(1)}, u32[]{:S(2)}, u32[]{:S(2)}) collective-permute-start(f32[120,768]{1,0:T(8,128)S(1)} %collective-permute-done.53.refs_1_), channel_id=1, source_target_pairs={{0,8},{8,16},{16,24},{24,28},{28,20},{20,12},{12,4},{4,0},{1,9},{9... | collective-permute-start | bytes 1105928 | tf_op jit(solution)/shard_map/ppermute | solution.py:779
  485.2 13.6 %collective-permute-start.83 = (f32[40,768]{1,0:T(8,128)S(1)}, f32[40,768]{1,0:T(8,128)S(1)}, u32[]{:S(2)}, u32[]{:S(2)}) collective-permute-start(f32[40,768]{1,0:T(8,128)S(1)} %dynamic-slice_add_fusion.5), channel_id=1, source_target_pairs={{0,16},{4,20},{8,24},{12,28},{16,0},{20,4},{24,8},{28,12},{1,17},{... | collective-permute-start | bytes 368648 | tf_op jit(solution)/shard_map/ppermute | solution.py:779
  486.0 11.9 %collective-permute-start.84 = (f32[32,768]{1,0:T(8,128)S(1)}, f32[32,768]{1,0:T(8,128)S(1)}, u32[]{:S(2)}, u32[]{:S(2)}) collective-permute-start(f32[32,768]{1,0:T(8,128)S(1)} %dynamic-slice_add_fusion.6), channel_id=1, source_target_pairs={{0,4},{4,0},{8,12},{12,8},{16,20},{20,16},{24,28},{28,24},{1,5},{5... | collective-permute-start | bytes 294920 | tf_op jit(solution)/shard_map/ppermute | solution.py:779
  497.8 22.9 %collective-permute-start.69 = (f32[7,768]{1,0:T(8,128)S(1)}, f32[7,768]{1,0:T(8,128)S(1)}, u32[]{:S(2)}, u32[]{:S(2)}) collective-permute-start(f32[7,768]{1,0:T(8,128)S(1)} %pad_maximum_fusion.12), channel_id=1, source_target_pairs={{0,1},{1,0},{2,3},{3,2},{4,5},{5,4},{6,7},{7,6},{8,9},{9,8},{10,11... | collective-permute-start | bytes 64520 | tf_op jit(solution)/shard_map/ppermute | solution.py:679
  498.8 40.9 %collective-permute-start.64 = (f32[320,768]{1,0:T(8,128)S(1)}, f32[320,768]{1,0:T(8,128)S(1)}, u32[]{:S(2)}, u32[]{:S(2)}) collective-permute-start(f32[320,768]{1,0:T(8,128)S(1)} %maximum_add_fusion.refs_1_), channel_id=1, source_target_pairs={{0,1},{1,0},{2,3},{3,2},{4,5},{5,4},{6,7},{7,6},{8,9},{9,8},{10,11... | collective-permute-start | bytes 2949128 | tf_op jit(solution)/shard_map/ppermute | solution.py:679
  505.7 14.5 %collective-permute-start.63 = (f32[144,768]{1,0:T(8,128)S(1)}, f32[144,768]{1,0:T(8,128)S(1)}, u32[]{:S(2)}, u32[]{:S(2)}) collective-permute-start(f32[144,768]{1,0:T(8,128)S(1)} %collective-permute-done.60.refs_3_), channel_id=1, source_target_pairs={{0,4},{8,0},{16,8},{24,16},{28,24},{20,28},{12,20},{4,12},{1,5},{9... | collective-permute-start | bytes 1327112 | tf_op jit(solution)/shard_map/ppermute | solution.py:779
  507.9 18.8 %collective-permute-start.85 = (f32[80,768]{1,0:T(8,128)S(1)}, f32[80,768]{1,0:T(8,128)S(1)}, u32[]{:S(2)}, u32[]{:S(2)}) collective-permute-start(f32[80,768]{1,0:T(8,128)S(1)} %pad_maximum_fusion.10), channel_id=1, source_target_pairs={{0,8},{4,12},{8,0},{12,4},{16,24},{20,28},{24,16},{28,20},{1,9},{5... | collective-permute-start | bytes 737288 | tf_op jit(solution)/shard_map/ppermute | solution.py:779
  515.8 10.8 %collective-permute-start.86 = (f32[64,768]{1,0:T(8,128)S(1)}, f32[64,768]{1,0:T(8,128)S(1)}, u32[]{:S(2)}, u32[]{:S(2)}) collective-permute-start(f32[64,768]{1,0:T(8,128)S(1)} %pad_maximum_fusion.11), channel_id=1, source_target_pairs={{0,16},{4,20},{8,24},{12,28},{16,0},{20,4},{24,8},{28,12},{1,17},{... | collective-permute-start | bytes 589832 | tf_op jit(solution)/shard_map/ppermute | solution.py:779
  520.7 20.7 %collective-permute-start.65 = (f32[320,768]{1,0:T(8,128)S(1)}, f32[320,768]{1,0:T(8,128)}, u32[]{:S(2)}, u32[]{:S(2)}) collective-permute-start(f32[320,768]{1,0:T(8,128)S(1)} %maximum_add_fusion.1.refs_2_), channel_id=1, source_target_pairs={{0,1},{1,0},{2,3},{3,2},{4,5},{5,4},{6,7},{7,6},{8,9},{9,8},{10,11... | collective-permute-start | bytes 2949128 | tf_op jit(solution)/shard_map/ppermute | solution.py:679
  526.8 12.9 %collective-permute-start.68 = (f32[144,768]{1,0:T(8,128)S(1)}, f32[144,768]{1,0:T(8,128)S(1)}, u32[]{:S(2)}, u32[]{:S(2)}) collective-permute-start(f32[144,768]{1,0:T(8,128)S(1)} %collective-permute-done.63.refs_4_), channel_id=1, source_target_pairs={{0,4},{8,0},{16,8},{24,16},{28,24},{20,28},{12,20},{4,12},{1,5},{9... | collective-permute-start | bytes 1327112 | tf_op jit(solution)/shard_map/ppermute | solution.py:779
  527.0 12.6 %collective-permute-start.67 = (f32[120,768]{1,0:T(8,128)S(1)}, f32[120,768]{1,0:T(8,128)S(1)}, u32[]{:S(2)}, u32[]{:S(2)}) collective-permute-start(f32[120,768]{1,0:T(8,128)S(1)} %collective-permute-done.62.refs_4_), channel_id=1, source_target_pairs={{0,8},{8,16},{16,24},{24,28},{28,20},{20,12},{12,4},{4,0},{1,9},{9... | collective-permute-start | bytes 1105928 | tf_op jit(solution)/shard_map/ppermute | solution.py:779
  529.7 38.6 %collective-permute-start.87 = (f32[160,768]{1,0:T(8,128)S(1)}, f32[160,768]{1,0:T(8,128)S(1)}, u32[]{:S(2)}, u32[]{:S(2)}) collective-permute-start(f32[160,768]{1,0:T(8,128)S(1)} %pad_maximum_fusion.3), channel_id=1, source_target_pairs={{0,4},{4,0},{8,12},{12,8},{16,20},{20,16},{24,28},{28,24},{1,5},{5... | collective-permute-start | bytes 1474568 | tf_op jit(solution)/shard_map/ppermute | solution.py:779
  550.4 17.9 %collective-permute-start.71 = (f32[144,768]{1,0:T(8,128)}, f32[144,768]{1,0:T(8,128)}, u32[]{:S(2)}, u32[]{:S(2)}) collective-permute-start(f32[144,768]{1,0:T(8,128)} %copy-done.110), channel_id=1, source_target_pairs={{0,4},{8,0},{16,8},{24,16},{28,24},{20,28},{12,20},{4,12},{1,5},{9... | collective-permute-start | bytes 1327112 | tf_op jit(solution)/shard_map/ppermute | solution.py:779
  550.9 17.4 %collective-permute-start.88 = (f32[128,768]{1,0:T(8,128)}, f32[128,768]{1,0:T(8,128)}, u32[]{:S(2)}, u32[]{:S(2)}) collective-permute-start(f32[128,768]{1,0:T(8,128)} %pad_maximum_fusion.6), channel_id=1, source_target_pairs={{0,8},{4,12},{8,0},{12,4},{16,24},{20,28},{24,16},{28,20},{1,9},{5... | collective-permute-start | bytes 1179656 | tf_op jit(solution)/shard_map/ppermute | solution.py:779
  552.5 15.8 %collective-permute-start.70 = (f32[120,768]{1,0:T(8,128)}, f32[120,768]{1,0:T(8,128)}, u32[]{:S(2)}, u32[]{:S(2)}) collective-permute-start(f32[120,768]{1,0:T(8,128)} %copy-done.116), channel_id=1, source_target_pairs={{0,8},{8,16},{16,24},{24,28},{28,20},{20,12},{12,4},{4,0},{1,9},{9... | collective-permute-start | bytes 1105928 | tf_op jit(solution)/shard_map/ppermute | solution.py:779
  555.3 13.0 %collective-permute-start.72 = (f32[20,768]{1,0:T(8,128)S(1)}, f32[20,768]{1,0:T(8,128)S(1)}, u32[]{:S(2)}, u32[]{:S(2)}) collective-permute-start(f32[20,768]{1,0:T(8,128)S(1)} %concatenate.66), channel_id=1, source_target_pairs={{0,4},{4,0},{8,12},{12,8},{16,20},{20,16},{24,28},{28,24},{1,5},{5... | collective-permute-start | bytes 184328 | tf_op jit(solution)/shard_map/ppermute | solution.py:779
  569.2 10.2 %collective-permute-start.74 = (f32[144,768]{1,0:T(8,128)}, f32[144,768]{1,0:T(8,128)S(1)}, u32[]{:S(2)}, u32[]{:S(2)}) collective-permute-start(f32[144,768]{1,0:T(8,128)} %collective-permute-done.71.refs_6_), channel_id=1, source_target_pairs={{0,4},{8,0},{16,8},{24,16},{28,24},{20,28},{12,20},{4,12},{1,5},{9... | collective-permute-start | bytes 1327112 | tf_op jit(solution)/shard_map/ppermute | solution.py:779
  580.1 11.8 %collective-permute-start.76 = (f32[20,768]{1,0:T(8,128)}, f32[20,768]{1,0:T(8,128)}, u32[]{:S(2)}, u32[]{:S(2)}) collective-permute-start(f32[20,768]{1,0:T(8,128)} %add.558), channel_id=1, source_target_pairs={{0,16},{4,20},{8,24},{12,28},{16,0},{20,4},{24,8},{28,12},{1,17},{... | collective-permute-start | bytes 184328 | tf_op jit(solution)/shard_map/ppermute | solution.py:779
  (179 other events, 1713.8 us)

commit v5 on v4

--- a/solution.py
+++ b/solution.py
@@ -992,7 +992,16 @@
     theirs = tuple(from_sib(g) for g in mine)
     w_sum = jnp.zeros((3 * part, width), F32)
     b_sum = jnp.zeros((1, 3 * part), F32)
-    gx = []
+    gx, gh_mine, gh_theirs = [], [], []
+
+    def finish_rows(doc, chip_sum, far):
+        first = jnp.concatenate(
+            [gf_seg[doc * half_seg : (doc + 1) * half_seg], gf_txt[doc * half : (doc + 1) * half]],
+            axis=0,
+        )
+        gh_mine.append(first + (chip_sum + far))
+        gh_theirs.append(from_sib(gh_mine[-1]))
+
     for doc in range(docs):
 
         def scores(b_sum, doc=doc):
@@ -1001,12 +1010,15 @@
             )
 
         def weights_of(gq, w_sum, doc=doc):
-            return qkv_bwd(
+            grads = qkv_bwd(
                 all_rows, doc, docs, place, hidden_in, roi, stats, bn_gain, bn_bias, w_qkv, gq, w_sum
             )
+            return (*grads, *(far for _, far in gx[-1:]))
 
         gq, b_sum = steps.run(scores, (b_sum,))
-        gx_mine, gx_theirs, w_sum = steps.run(weights_of, (gq, w_sum))
+        gx_mine, gx_theirs, w_sum, *far = steps.run(weights_of, (gq, w_sum))
+        if far:
+            finish_rows(doc - 1, gx[-1][0], far[0])
         chip_sum = gx_mine + from_sib(gx_theirs)
         gx.append((chip_sum, from_x(chip_sum)))
     cut = w_sum.shape[0] * 5 // 9
@@ -1014,18 +1026,10 @@
     qkv_steps.add("qkv_low", halving(w_sum[:cut], 0))
     qkv_steps.add("qkv_high", halving(w_sum[cut:], 1))
     qkv_steps.finish()
-    gh_mine, gh_theirs = [], []
-    for doc in range(docs):
-        first = jnp.concatenate(
-            [gf_seg[doc * half_seg : (doc + 1) * half_seg], gf_txt[doc * half : (doc + 1) * half]],
-            axis=0,
-        )
-        if doc:
-            steps.run()
-        (far,) = steps.run(lambda x: (x,), (gx[doc][1],))
-        gh_mine.append(first + (gx[doc][0] + far))
-        gh_theirs.append(from_sib(gh_mine[-1]))
-    (gh_theirs[-1],) = steps.run(lambda x: (x,), (gh_theirs[-1],))
+    steps.run()
+    (far,) = steps.run(lambda: (gx[-1][1],))
+    finish_rows(docs - 1, gx[-1][0], far)
+    (gh_theirs[-1],) = steps.run(lambda: (gh_theirs[-1],))
     grad_hidden, bn_sums = final_rows(all_rows, segs, place, gh_mine, gh_theirs, roi, stats)
 
     rows = sum(txt_sums) + back["sums"]

time: 604 us -> 614 us (1.017)
  waiting for transfers between devices: 181 us -> 211 us
  local copies, waits for them, and re-layouts: 47.3 us -> 33.5 us
    ppermute x43, waiting for transfers between devices: 86.2 us -> 110 us  [run(): lax.ppermute(x, *self.active[name][1][1:])]
    unnamed x305 -> x183, local copies, waits for them, and re-layouts: 23.1 us -> 10.1 us
    ppermute x46, waiting for transfers between devices: 94.4 us -> 101 us  [swap(): return lax.ppermute(x, axis, [(i, i ^ bit) for i in range(n)])]
  transfers between devices with their start and end apart: 91 -> 91, of which waited for: 37 -> 48; matrix products, arithmetic and copies ran while one was open for 11% -> 12% of each run, Pallas kernels for 30% -> 28%
where the time goes in v5:
time: 614 us; the launch traced here: 607 us
  waiting for transfers between devices  211 us (34%)
  Pallas kernels  207 us (34%)
  starting transfers between devices  89.6 us (15%)
  matrix products  37.4 us (6%)
  local copies, waits for them, and re-layouts  33.5 us (5%)
  other arithmetic  26.1 us (4%)
    pallas_call x5, Pallas kernels, ffn(): pl.pallas_call(functools.partial(ffn_kernel, forward, backward, all_names...  125 us
    ppermute x43, waiting for transfers between devices, run(): lax.ppermute(x, *self.active[name][1][1:])  110 us
    ppermute x46, waiting for transfers between devices, swap(): return lax.ppermute(x, axis, [(i, i ^ bit) for i in range(n)])  101 us
    ppermute x43, starting transfers between devices, run(): lax.ppermute(x, *self.active[name][1][1:])  54 us
    dot_general x14, matrix products, product(): lax.dot_general(operand, other, (dims, ((), ())), precision=HIGH, preferr...  37.4 us
    ppermute x46, starting transfers between devices, swap(): return lax.ppermute(x, axis, [(i, i ^ bit) for i in range(n)])  24.2 us
    pallas_call x1, Pallas kernels, attn_fwd(): pl.pallas_call(functools.partial(attn_fwd_kernel, all_rows), grid=(docs,)...  22.3 us
    pallas_call x3, Pallas kernels, attn_bwd(): pl.pallas_call(functools.partial(attn_bwd_kernel, doc), grid=(1,), in_spe...  20.7 us
  transfers between devices with their start and end apart: 91, of which 48 were waited for; matrix products, arithmetic and copies ran while one was open for 12% of the time, Pallas kernels for 28%

profile of v5, /device:TPU:0, one launch (start us, length us, event | category | flops | bytes accessed | tf_op | source)
XLA Modules:
  0.0 607.1 jit_solution(9450857309149133663)
XLA Ops:
  1.3 2.2 local_stats.1
  3.4 2.9 collective-permute-start.5
  12.0 2.4 constant_dynamic-slice_fusion.10
  17.6 2.1 collective-permute-done.6
  22.4 2.6 collective-permute-start.7
  30.9 22.3 %attn_fwd.1 = (f32[1920,576]{1,0:T(8,128)}, f32[24,640]{1,0:T(8,128)}, f32[192,384]{1,0:T(8,128)}, f32[768,384]{1,0:T(8,128)}, f32[192,768]{1,0:T(8,128)}, /*index=5*/f32[768,768]{1,0:T(8,128)}) custom-call(s32[3]{0:T(128)} %pad_add_fusion.refs_0_.place, s32[3]{0:T(128)} %refs_1_.22, f32[1920,768]{1,0:T(8,128)} %refs_1_.23, f32[384,768]{1,0:T(8,128)} %refs_7_.2, ...), custom_call_target="tpu_custom_call" | custom-call | flops 11520 | bytes 640 | tf_op jit(solution)/shard_map/attn_fwd/pallas_call | solution.py:189
  53.3 17.5 %collective-permute-done.1.refs_27_.refs_28_.refs_24_ = f32[384,768]{1,0:T(8,128)} collective-permute-done((f32[384,768]{1,0:T(8,128)}, f32[384,768]{1,0:T(8,128)}, u32[]{:S(2)}, u32[]{:S(2)}) %collective-permute-start.1) | collective-permute-done | bytes 1179680 | tf_op jit(solution)/shard_map/ppermute | solution.py:679
  73.7 4.9 collective-permute-done.13.refs_9_
  79.1 21.3 %collective-permute-done.12.refs_29_.refs_30_.refs_26_ = f32[384,768]{1,0:T(8,128)} collective-permute-done((f32[384,768]{1,0:T(8,128)}, f32[384,768]{1,0:T(8,128)}, u32[]{:S(2)}, u32[]{:S(2)}) %collective-permute-start.12) | collective-permute-done | bytes 1179680 | tf_op jit(solution)/shard_map/ppermute | solution.py:679
  100.4 6.0 collective-permute-done.11.refs_19_.refs_28_.refs_20_.refs_29_.refs_25_
  112.1 17.2 %ffn_fwd.1 = (f32[192,768]{1,0:T(8,128)}, f32[960,768]{1,0:T(8,128)}, f32[960,768]{1,0:T(8,128)}, f32[960,768]{1,0:T(8,128)}, f32[192,768]{1,0:T(8,128)}, /*inde...) custom-call(s32[3]{0:T(128)} %pad_add_fusion.refs_0_.place, f32[768]{0:T(1024)} %refs_1_.17, ...), custom_call_target="tpu_custom_call" | custom-call | flops 16307453952 | bytes 8847360 | tf_op jit(solution)/shard_map/ffn_fwd/pallas_call | solution.py:577
  129.4 6.3 %collective-permute-done.22.refs_9_ = f32[768,384]{1,0:T(8,128)} collective-permute-done((f32[768,384]{1,0:T(8,128)}, f32[768,384]{1,0:T(8,128)}, u32[]{:S(2)}, u32[]{:S(2)}) %collective-permute-start.22) | collective-permute-done | bytes 1179680 | tf_op jit(solution)/shard_map/ppermute | solution.py:679
  142.5 5.3 all-to-all-start
  147.8 29.2 %ffn_fwdbwd.3 = (f32[768,768]{1,0:T(8,128)}, f32[960,768]{1,0:T(8,128)}, f32[960,768]{1,0:T(8,128)}, f32[960,768]{1,0:T(8,128)}, f32[960,768]{1,0:T(8,128)}, /*i...) custom-call(s32[3]{0:T(128)} %pad_add_fusion.refs_0_.place, ...), custom_call_target="tpu_custom_call", output_to_operand_aliasing={{1}: (35, {}), {2}: (36, {}), {3}: (37, {})} | custom-call | flops 25367150592 | bytes 11796480 | tf_op jit(solution)/shard_map/ffn_fwdbwd/pallas_call | solution.py:577
  179.0 3.1 scatter_custom_fusion
  183.7 29.4 %ffn_fwdbwd.4 = (f32[768,768]{1,0:T(8,128)}, f32[960,768]{1,0:T(8,128)}, f32[960,768]{1,0:T(8,128)}, f32[960,768]{1,0:T(8,128)}, f32[960,768]{1,0:T(8,128)}, /*i...) custom-call(s32[3]{0:T(128)} %pad_add_fusion.refs_0_.place, ...), custom_call_target="tpu_custom_call", output_to_operand_aliasing={{0}: (35, {}), {1}: (36, {}), {2}: (37, {}), {3}: (38, {}),... | custom-call | flops 25367150592 | bytes 11796480 | tf_op jit(solution)/shard_map/ffn_fwdbwd/pallas_call | solution.py:577
  218.5 6.2 %all-to-all-start.1 = ((f32[8,48,192]{2,1,0:T(8,128)}), f32[8,48,192]{2,1,0:T(8,128)S(1)}, u32[]{:S(2)}, u32[]{:S(2)}) async-start(f32[8,48,192]{2,1,0:T(8,128)} %bitcast.12), calls=%async_computation.1 | async-start | bytes 786432 | tf_op jit(solution)/shard_map/all_to_all | solution.py:913
  224.7 29.3 %ffn_fwdbwd.5 = (f32[768,768]{1,0:T(8,128)}, f32[960,768]{1,0:T(8,128)}, f32[960,768]{1,0:T(8,128)}, f32[960,768]{1,0:T(8,128)}, f32[960,768]{1,0:T(8,128)}, /*i...) custom-call(s32[3]{0:T(128)} %pad_add_fusion.refs_0_.place, ...), custom_call_target="tpu_custom_call", output_to_operand_aliasing={{0}: (35, {}), {1}: (36, {}), {2}: (37, {}), {3}: (38, {}),... | custom-call | flops 25367150592 | bytes 11796480 | tf_op jit(solution)/shard_map/ffn_fwdbwd/pallas_call | solution.py:577
  256.5 3.8 collective-permute-done.27
  262.3 7.7 %collective-permute-done.28 = f32[192,384]{1,0:T(8,128)} collective-permute-done((f32[192,384]{1,0:T(8,128)S(1)}, f32[192,384]{1,0:T(8,128)}, u32[]{:S(2)}, u32[]{:S(2)}) %collective-permute-start.28) | collective-permute-done | bytes 294944 | tf_op jit(solution)/shard_map/ppermute | solution.py:679
  271.1 6.5 %join_rows.1 = f32[1920,768]{1,0:T(8,128)} custom-call(s32[3]{0:T(128)} %pad_add_fusion.refs_0_.place, f32[192,768]{1,0:T(8,128)} %get-tuple-element.269.ms, f32[768,768]{1,0:T(8,128)} %get-tuple-element.311.mt, f32[192,768]{1,0:T(8,128)} %collective-permute-done.29.ts, f32[768,768]{1,0:T(8,128)} %collective-permute-done.30.tt), custom_call_target="tpu_custom_call" | custom-call | bytes 11796480 | tf_op jit(solution)/shard_map/join_rows/pallas_call | solution.py:607
  278.5 20.3 %ffn_bwd.1 = (f32[960,768]{1,0:T(8,128)}, f32[960,768]{1,0:T(8,128)}, f32[960,768]{1,0:T(8,128)}, f32[960,768]{1,0:T(8,128)}, f32[192,384]{1,0:T(8,128)}, /*index=5*/f32[384,768]{1,0:T(8,128)}, f32[8,768]{1,0:T(8,128)}) custom-call(s32[3]{0:T(128)} %pad_add_fusion.refs_0_.place, ...), custom_call_target="tpu_custom_call", output_to_operand_aliasing={{0}: (31, {}), {1}: (32, {}), {2}: (33, {}), {3}: (34, {})} | custom-call | flops 16307453952 | bytes 8847360 | tf_op jit(solution)/shard_map/ffn_bwd/pallas_call | solution.py:577
  298.8 8.9 %fusion.68 = f32[768,768]{1,0:T(8,128)} fusion(f32[960,768]{1,0:T(8,128)} %get-tuple-element.333, f32[960,768]{1,0:T(8,128)} %get-tuple-element.332), kind=kOutput, calls=%fused_computation.205 | convolution fusion | flops 3397386240 | bytes 8257536 | tf_op jit(solution)/shard_map/dot_general | solution.py:24
  307.8 6.1 fusion.67
  321.7 7.4 %convolution_add_fusion = f32[768,768]{1,0:T(8,128)S(1)} fusion(f32[768,768]{1,0:T(8,128)} %collective-permute-done.33, f32[960,768]{1,0:T(8,128)} %get-tuple-element.331, f32[960,768]{1,0:T(8,128)S(1)} %copy-done.27), kind=kOutput, calls=%fused_computation.36 | convolution fusion | flops 3397976064 | bytes 10616832 | tf_op jit(solution)/shard_map/dot_general | solution.py:24
  329.2 7.0 %convolution_add_fusion.1 = f32[768,768]{1,0:T(8,128)S(1)} fusion(f32[768,768]{1,0:T(8,128)} %collective-permute-done.31, f32[960,768]{1,0:T(8,128)S(1)} %copy-done.26, f32[960,768]{1,0:T(8,128)S(1)} %copy-done.42), kind=kOutput, calls=%fused_computation.37 | convolution fusion | flops 3397976064 | bytes 10616832 | tf_op jit(solution)/shard_map/dot_general | solution.py:24
  336.5 2.1 collective-permute-start.35
  339.1 6.9 %attn_bwd.3 = (f32[640,576]{1,0:T(8,128)S(1)}, f32[1,576]{1,0:T(1,128)S(1)}) custom-call(s32[3]{0:T(128)S(1)} %copy-done.9, s32[3]{0:T(128)S(1)} %copy-done.10, f32[1920,576]{1,0:T(8,128)S(1)} %bitcast.84, f32[24,640]{1,0:T(8,128)S(1)} %copy-done.15, f32[192,384]{1,0:T(8,128)S(1)} %copy-done.13, f32[768,384]{1,0:T(8,128)S(1)} %copy-done.11, ...), custom_call_target="tpu_custom_call" | custom-call | flops 7549747200 | bytes 2949120 | tf_op jit(solution)/shard_map/attn_bwd/pallas_call | solution.py:276
  346.0 3.5 collective-permute-done.34
  354.9 5.3 qkv_bwd.3
  366.3 6.9 %attn_bwd.4 = (f32[640,576]{1,0:T(8,128)S(1)}, f32[1,576]{1,0:T(1,128)S(1)}) custom-call(s32[3]{0:T(128)S(1)} %copy-done.9, s32[3]{0:T(128)S(1)} %copy-done.10, f32[1920,576]{1,0:T(8,128)S(1)} %bitcast.84, f32[24,640]{1,0:T(8,128)S(1)} %copy-done.15, f32[192,384]{1,0:T(8,128)S(1)} %copy-done.13, f32[768,384]{1,0:T(8,128)S(1)} %copy-done.11, ...), custom_call_target="tpu_custom_call" | custom-call | flops 7549747200 | bytes 2949120 | tf_op jit(solution)/shard_map/attn_bwd/pallas_call | solution.py:276
  373.2 3.3 collective-permute-done.41
  383.4 5.2 qkv_bwd.4
  388.6 2.3 collective-permute-done.43
  391.3 8.7 %collective-permute-done.45 = f32[320,768]{1,0:T(8,128)S(1)} collective-permute-done((f32[320,768]{1,0:T(8,128)S(1)}, f32[320,768]{1,0:T(8,128)S(1)}, u32[]{:S(2)}, u32[]{:S(2)}) %collective-permute-start.45) | collective-permute-done | bytes 983072 | tf_op jit(solution)/shard_map/ppermute | solution.py:679
  405.9 6.9 %attn_bwd.5 = (f32[640,576]{1,0:T(8,128)S(1)}, f32[1,576]{1,0:T(1,128)S(1)}) custom-call(s32[3]{0:T(128)S(1)} %copy-done.9, s32[3]{0:T(128)S(1)} %copy-done.10, f32[1920,576]{1,0:T(8,128)S(1)} %bitcast.84, f32[24,640]{1,0:T(8,128)S(1)} %copy-done.15, f32[192,384]{1,0:T(8,128)S(1)} %copy-done.13, f32[768,384]{1,0:T(8,128)S(1)} %copy-done.11, ...), custom_call_target="tpu_custom_call" | custom-call | flops 7549747200 | bytes 2949120 | tf_op jit(solution)/shard_map/attn_bwd/pallas_call | solution.py:276
  412.8 3.6 collective-permute-done.47
  420.7 5.3 qkv_bwd.5
  426.0 4.0 collective-permute-done.49
  430.2 9.8 %collective-permute-done.51 = f32[320,768]{1,0:T(8,128)S(1)} collective-permute-done((f32[320,768]{1,0:T(8,128)S(1)}, f32[320,768]{1,0:T(8,128)S(1)}, u32[]{:S(2)}, u32[]{:S(2)}) %collective-permute-start.51) | collective-permute-done | bytes 983072 | tf_op jit(solution)/shard_map/ppermute | solution.py:679
  446.3 7.5 %collective-permute-done.53 = f32[120,768]{1,0:T(8,128)S(1)} collective-permute-done((f32[120,768]{1,0:T(8,128)S(1)}, f32[120,768]{1,0:T(8,128)S(1)}, u32[]{:S(2)}, u32[]{:S(2)}) %collective-permute-start.53) | collective-permute-done | bytes 368672 | tf_op jit(solution)/shard_map/ppermute | solution.py:779
  454.3 5.5 collective-permute-done.74
  459.8 2.0 collective-permute-done.73
  462.1 4.0 collective-permute-start.76
  466.2 5.3 collective-permute-done.76
  476.0 3.1 collective-permute-done.78
  479.1 2.5 collective-permute-start.56
  481.7 7.4 %collective-permute-done.55.refs_1_ = f32[120,768]{1,0:T(8,128)S(1)} collective-permute-done((f32[120,768]{1,0:T(8,128)S(1)}, f32[120,768]{1,0:T(8,128)S(1)}, u32[]{:S(2)}, u32[]{:S(2)}) %collective-permute-start.55) | collective-permute-done | bytes 368672 | tf_op jit(solution)/shard_map/ppermute | solution.py:779
  492.0 4.5 collective-permute-start.80
  496.8 2.3 collective-permute-done.80
  502.7 5.8 collective-permute-done.60.refs_2_
  508.9 2.3 collective-permute-done.61.refs_2_
  513.2 5.9 final_rows.1
  521.4 2.6 collective-permute-start.82
  526.0 13.7 %collective-permute-done.82 = f32[64,768]{1,0:T(8,128)S(1)} collective-permute-done((f32[64,768]{1,0:T(8,128)}, f32[64,768]{1,0:T(8,128)S(1)}, u32[]{:S(2)}, u32[]{:S(2)}) %collective-permute-start.82) | collective-permute-done | bytes 196640 | tf_op jit(solution)/shard_map/ppermute | solution.py:779
  539.7 5.2 collective-permute-done.66
  545.8 2.0 collective-permute-start.67
  549.5 11.2 %collective-permute-done.69 = f32[20,768]{1,0:T(8,128)S(1)} collective-permute-done((f32[20,768]{1,0:T(8,128)S(1)}, f32[20,768]{1,0:T(8,128)S(1)}, u32[]{:S(2)}, u32[]{:S(2)}) %collective-permute-start.69) | collective-permute-done | bytes 61472 | tf_op jit(solution)/shard_map/ppermute | solution.py:779
  560.7 2.0 collective-permute-start.84
  567.0 14.2 %collective-permute-done.84 = f32[128,768]{1,0:T(8,128)} collective-permute-done((f32[128,768]{1,0:T(8,128)}, f32[128,768]{1,0:T(8,128)}, u32[]{:S(2)}, u32[]{:S(2)}) %collective-permute-start.84) | collective-permute-done | bytes 393248 | tf_op jit(solution)/shard_map/ppermute | solution.py:779
  581.4 2.1 collective-permute-start.85
  594.8 3.0 collective-permute-done.87.refs_7_
  598.7 4.2 assemble.3
  602.9 3.7 assemble.2
  (455 shorter events, 130.9 us)
Async XLA Ops:
  0.7 70.1 %collective-permute-start.3 = (f32[768,768]{1,0:T(8,128)}, f32[768,768]{1,0:T(8,128)}, u32[]{:S(2)}, u32[]{:S(2)}) collective-permute-start(f32[768,768]{1,0:T(8,128)} %refs_19_.1), channel_id=1, source_target_pairs={{0,1},{1,0},{2,3},{3,2},{4,5},{5,4},{6,7},{7,6},{8,9},{9,8},{10,11... | collective-permute-start | bytes 7077896 | tf_op jit(solution)/shard_map/ppermute | solution.py:679
  1.2 69.6 %collective-permute-start.4 = (f32[768,768]{1,0:T(8,128)}, f32[768,768]{1,0:T(8,128)}, u32[]{:S(2)}, u32[]{:S(2)}) collective-permute-start(f32[768,768]{1,0:T(8,128)} %refs_20_.1), channel_id=1, source_target_pairs={{0,1},{1,0},{2,3},{3,2},{4,5},{5,4},{6,7},{7,6},{8,9},{9,8},{10,11... | collective-permute-start | bytes 7077896 | tf_op jit(solution)/shard_map/ppermute | solution.py:679
  3.4 10.9 %collective-permute-start.5 = (f32[2,768]{1,0:T(2,128)}, f32[2,768]{1,0:T(2,128)S(1)}, u32[]{:S(2)}, u32[]{:S(2)}) collective-permute-start(f32[2,768]{1,0:T(2,128)} %local_stats.1), channel_id=1, source_target_pairs={{0,4},{4,0},{8,12},{12,8},{16,20},{20,16},{24,28},{28,24},{1,5},{5... | collective-permute-start | bytes 18440 | tf_op jit(solution)/shard_map/ppermute | solution.py:679
  11.4 59.3 %collective-permute-start = (f32[480,768]{1,0:T(8,128)}, f32[480,768]{1,0:T(8,128)}, u32[]{:S(2)}, u32[]{:S(2)}) collective-permute-start(f32[480,768]{1,0:T(8,128)} %pad_maximum_fusion.1), channel_id=1, source_target_pairs={{0,2},{1,3},{2,0},{3,1},{4,6},{5,7},{6,4},{7,5},{8,10},{9,11},{10,... | collective-permute-start | bytes 4423688 | tf_op jit(solution)/shard_map/ppermute | solution.py:679
  14.3 56.4 %collective-permute-start.1 = (f32[384,768]{1,0:T(8,128)}, f32[384,768]{1,0:T(8,128)}, u32[]{:S(2)}, u32[]{:S(2)}) collective-permute-start(f32[384,768]{1,0:T(8,128)} %constant_dynamic-slice_fusion.10), channel_id=1, source_target_pairs={{0,2},{1,3},{2,0},{3,1},{4,6},{5,7},{6,4},{7,5},{8,10},{9,11},{10,... | collective-permute-start | bytes 3538952 | tf_op jit(solution)/shard_map/ppermute | solution.py:679
  27.0 26.3 %collective-permute-start.2 = (f32[192,768]{1,0:T(8,128)S(1)}, f32[192,768]{1,0:T(8,128)}, u32[]{:S(2)}, u32[]{:S(2)}) collective-permute-start(f32[192,768]{1,0:T(8,128)S(1)} %copy-done.68), channel_id=1, source_target_pairs={{0,1},{1,0},{2,3},{3,2},{4,5},{5,4},{6,7},{7,6},{8,9},{9,8},{10,11... | collective-permute-start | bytes 1769480 | tf_op jit(solution)/shard_map/ppermute | solution.py:679
  71.4 35.0 %collective-permute-start.11 = (f32[480,768]{1,0:T(8,128)}, f32[480,768]{1,0:T(8,128)}, u32[]{:S(2)}, u32[]{:S(2)}) collective-permute-start(f32[480,768]{1,0:T(8,128)} %collective-permute-done.refs_18_.refs_26_.refs_19_.refs_27_.refs_23_), channel_id=1, source_target_pairs={{0,4},{4,0},{8,12},{12,8},{16,20},{20,16},{24,28},{28,24},{1,5},{5... | collective-permute-start | bytes 4423688 | tf_op jit(solution)/shard_map/ppermute | solution.py:679
  71.7 34.7 %collective-permute-start.14 = (f32[480,768]{1,0:T(8,128)}, f32[480,768]{1,0:T(8,128)}, u32[]{:S(2)}, u32[]{:S(2)}) collective-permute-start(f32[480,768]{1,0:T(8,128)} %collective-permute-done.refs_18_.refs_26_.refs_19_.refs_27_.refs_23_), channel_id=1, source_target_pairs={{0,1},{1,0},{2,3},{3,2},{4,5},{5,4},{6,7},{7,6},{8,9},{9,8},{10,11... | collective-permute-start | bytes 4423688 | tf_op jit(solution)/shard_map/ppermute | solution.py:679
  71.9 28.5 %collective-permute-start.12 = (f32[384,768]{1,0:T(8,128)}, f32[384,768]{1,0:T(8,128)}, u32[]{:S(2)}, u32[]{:S(2)}) collective-permute-start(f32[384,768]{1,0:T(8,128)} %collective-permute-done.1.refs_27_.refs_28_.refs_24_), channel_id=1, source_target_pairs={{0,8},{4,12},{8,0},{12,4},{16,24},{20,28},{24,16},{28,20},{1,9},{5... | collective-permute-start | bytes 3538952 | tf_op jit(solution)/shard_map/ppermute | solution.py:679
  78.6 21.9 %collective-permute-start.15 = (f32[384,768]{1,0:T(8,128)}, f32[384,768]{1,0:T(8,128)}, u32[]{:S(2)}, u32[]{:S(2)}) collective-permute-start(f32[384,768]{1,0:T(8,128)} %collective-permute-done.1.refs_27_.refs_28_.refs_24_), channel_id=1, source_target_pairs={{0,1},{1,0},{2,3},{3,2},{4,5},{5,4},{6,7},{7,6},{8,9},{9,8},{10,11... | collective-permute-start | bytes 3538952 | tf_op jit(solution)/shard_map/ppermute | solution.py:679
  78.6 21.8 %collective-permute-start.17 = (f32[768,384]{1,0:T(8,128)}, f32[768,384]{1,0:T(8,128)}, u32[]{:S(2)}, u32[]{:S(2)}) collective-permute-start(f32[768,384]{1,0:T(8,128)} %get-tuple-element.254.refs_7_.refs_5_), channel_id=1, source_target_pairs={{0,1},{1,0},{2,3},{3,2},{4,5},{5,4},{6,7},{7,6},{8,9},{9,8},{10,11... | collective-permute-start | bytes 3538952 | tf_op jit(solution)/shard_map/ppermute | solution.py:679
  106.9 28.8 %collective-permute-start.22 = (f32[768,384]{1,0:T(8,128)}, f32[768,384]{1,0:T(8,128)}, u32[]{:S(2)}, u32[]{:S(2)}) collective-permute-start(f32[768,384]{1,0:T(8,128)} %get-tuple-element.254.refs_7_.refs_5_), channel_id=1, source_target_pairs={{0,2},{1,3},{2,0},{3,1},{4,6},{5,7},{6,4},{7,5},{8,10},{9,11},{10,... | collective-permute-start | bytes 3538952 | tf_op jit(solution)/shard_map/ppermute | solution.py:679
  135.7 12.1 %collective-permute-start.23 = (f32[768,384]{1,0:T(8,128)}, f32[768,384]{1,0:T(8,128)}, u32[]{:S(2)}, u32[]{:S(2)}) collective-permute-start(f32[768,384]{1,0:T(8,128)} %collective-permute-done.22.refs_9_), channel_id=1, source_target_pairs={{0,1},{1,0},{2,3},{3,2},{4,5},{5,4},{6,7},{7,6},{8,9},{9,8},{10,11... | collective-permute-start | bytes 3538952 | tf_op jit(solution)/shard_map/ppermute | solution.py:679
  142.5 34.5 %all-to-all-start = ((f32[8,48,192]{2,1,0:T(8,128)}), f32[8,48,192]{2,1,0:T(8,128)S(1)}, u32[]{:S(2)}, u32[]{:S(2)}) async-start(f32[8,48,192]{2,1,0:T(8,128)} %bitcast.8), calls=%async_computation | async-start | bytes 786432 | tf_op jit(solution)/shard_map/all_to_all | solution.py:913
  182.2 31.0 %collective-permute-start.25 = (f32[128,768]{1,0:T(8,128)S(1)}, f32[128,768]{1,0:T(8,128)S(1)}, u32[]{:S(2)}, u32[]{:S(2)}) collective-permute-start(f32[128,768]{1,0:T(8,128)S(1)} %dynamic-slice_add_fusion.1), channel_id=1, source_target_pairs={{0,2},{1,3},{2,0},{3,1},{4,6},{5,7},{6,4},{7,5},{8,10},{9,11},{10,... | collective-permute-start | bytes 1179656 | tf_op jit(solution)/shard_map/ppermute | solution.py:679
  218.5 35.5 %all-to-all-start.1 = ((f32[8,48,192]{2,1,0:T(8,128)}), f32[8,48,192]{2,1,0:T(8,128)S(1)}, u32[]{:S(2)}, u32[]{:S(2)}) async-start(f32[8,48,192]{2,1,0:T(8,128)} %bitcast.12), calls=%async_computation.1 | async-start | bytes 786432 | tf_op jit(solution)/shard_map/all_to_all | solution.py:913
  255.9 15.3 %collective-permute-start.30 = (f32[768,768]{1,0:T(8,128)}, f32[768,768]{1,0:T(8,128)}, u32[]{:S(2)}, u32[]{:S(2)}) collective-permute-start(f32[768,768]{1,0:T(8,128)} %get-tuple-element.311.mt), channel_id=1, source_target_pairs={{0,1},{1,0},{2,3},{3,2},{4,5},{5,4},{6,7},{7,6},{8,9},{9,8},{10,11... | collective-permute-start | bytes 7077896 | tf_op jit(solution)/shard_map/ppermute | solution.py:679
  261.1 10.0 %collective-permute-start.29 = (f32[192,768]{1,0:T(8,128)S(1)}, f32[192,768]{1,0:T(8,128)}, u32[]{:S(2)}, u32[]{:S(2)}) collective-permute-start(f32[192,768]{1,0:T(8,128)S(1)} %copy-done.47), channel_id=1, source_target_pairs={{0,1},{1,0},{2,3},{3,2},{4,5},{5,4},{6,7},{7,6},{8,9},{9,8},{10,11... | collective-permute-start | bytes 1769480 | tf_op jit(solution)/shard_map/ppermute | solution.py:679
  307.8 13.9 %collective-permute-start.33 = (f32[768,768]{1,0:T(8,128)}, f32[768,768]{1,0:T(8,128)}, u32[]{:S(2)}, u32[]{:S(2)}) collective-permute-start(f32[768,768]{1,0:T(8,128)} %fusion.68), channel_id=1, source_target_pairs={{0,1},{1,0},{2,3},{3,2},{4,5},{5,4},{6,7},{7,6},{8,9},{9,8},{10,11... | collective-permute-start | bytes 7077896 | tf_op jit(solution)/shard_map/ppermute | solution.py:679
  313.9 15.3 %collective-permute-start.31 = (f32[768,768]{1,0:T(8,128)}, f32[768,768]{1,0:T(8,128)}, u32[]{:S(2)}, u32[]{:S(2)}) collective-permute-start(f32[768,768]{1,0:T(8,128)} %fusion.67), channel_id=1, source_target_pairs={{0,1},{1,0},{2,3},{3,2},{4,5},{5,4},{6,7},{7,6},{8,9},{9,8},{10,11... | collective-permute-start | bytes 7077896 | tf_op jit(solution)/shard_map/ppermute | solution.py:679
  316.6 22.4 %collective-permute-start.37 = (f32[768,384]{1,0:T(8,128)S(1)}, f32[768,384]{1,0:T(8,128)S(1)}, u32[]{:S(2)}, u32[]{:S(2)}) collective-permute-start(f32[768,384]{1,0:T(8,128)S(1)} %copy-done.12), channel_id=1, source_target_pairs={{0,1},{1,0},{2,3},{3,2},{4,5},{5,4},{6,7},{7,6},{8,9},{9,8},{10,11... | collective-permute-start | bytes 3538952 | tf_op jit(solution)/shard_map/ppermute | solution.py:679
  320.0 19.0 %collective-permute-start.36 = (f32[192,384]{1,0:T(8,128)S(1)}, f32[192,384]{1,0:T(8,128)S(1)}, u32[]{:S(2)}, u32[]{:S(2)}) collective-permute-start(f32[192,384]{1,0:T(8,128)S(1)} %copy-done.14), channel_id=1, source_target_pairs={{0,1},{1,0},{2,3},{3,2},{4,5},{5,4},{6,7},{7,6},{8,9},{9,8},{10,11... | collective-permute-start | bytes 884744 | tf_op jit(solution)/shard_map/ppermute | solution.py:679
  336.5 13.0 %collective-permute-start.35 = (f32[144,768]{1,0:T(8,128)S(1)}, f32[144,768]{1,0:T(8,128)S(1)}, u32[]{:S(2)}, u32[]{:S(2)}) collective-permute-start(f32[144,768]{1,0:T(8,128)S(1)} %fusion.8), channel_id=1, source_target_pairs={{0,4},{8,0},{16,8},{24,16},{28,24},{20,28},{12,20},{4,12},{1,5},{9... | collective-permute-start | bytes 1327112 | tf_op jit(solution)/shard_map/ppermute | solution.py:779
  338.6 11.0 %collective-permute-start.34 = (f32[120,768]{1,0:T(8,128)S(1)}, f32[120,768]{1,0:T(8,128)S(1)}, u32[]{:S(2)}, u32[]{:S(2)}) collective-permute-start(f32[120,768]{1,0:T(8,128)S(1)} %fusion.27), channel_id=1, source_target_pairs={{0,8},{8,16},{16,24},{24,28},{28,20},{20,12},{12,4},{4,0},{1,9},{9... | collective-permute-start | bytes 1105928 | tf_op jit(solution)/shard_map/ppermute | solution.py:779
  349.8 11.6 %collective-permute-start.39 = (f32[144,768]{1,0:T(8,128)S(1)}, f32[144,768]{1,0:T(8,128)S(1)}, u32[]{:S(2)}, u32[]{:S(2)}) collective-permute-start(f32[144,768]{1,0:T(8,128)S(1)} %fusion.10), channel_id=1, source_target_pairs={{0,4},{8,0},{16,8},{24,16},{28,24},{20,28},{12,20},{4,12},{1,5},{9... | collective-permute-start | bytes 1327112 | tf_op jit(solution)/shard_map/ppermute | solution.py:779
  351.3 9.8 %collective-permute-start.38 = (f32[120,768]{1,0:T(8,128)S(1)}, f32[120,768]{1,0:T(8,128)S(1)}, u32[]{:S(2)}, u32[]{:S(2)}) collective-permute-start(f32[120,768]{1,0:T(8,128)S(1)} %fusion.29), channel_id=1, source_target_pairs={{0,8},{8,16},{16,24},{24,28},{28,20},{20,12},{12,4},{4,0},{1,9},{9... | collective-permute-start | bytes 1105928 | tf_op jit(solution)/shard_map/ppermute | solution.py:779
  362.2 14.5 %collective-permute-start.40 = (f32[320,768]{1,0:T(8,128)S(1)}, f32[320,768]{1,0:T(8,128)S(1)}, u32[]{:S(2)}, u32[]{:S(2)}) collective-permute-start(f32[320,768]{1,0:T(8,128)S(1)} %get-tuple-element.354), channel_id=1, source_target_pairs={{0,1},{1,0},{2,3},{3,2},{4,5},{5,4},{6,7},{7,6},{8,9},{9,8},{10,11... | collective-permute-start | bytes 2949128 | tf_op jit(solution)/shard_map/ppermute | solution.py:679
  364.1 12.5 %collective-permute-start.42 = (f32[144,768]{1,0:T(8,128)}, f32[144,768]{1,0:T(8,128)S(1)}, u32[]{:S(2)}, u32[]{:S(2)}) collective-permute-start(f32[144,768]{1,0:T(8,128)} %fusion.12), channel_id=1, source_target_pairs={{0,4},{8,0},{16,8},{24,16},{28,24},{20,28},{12,20},{4,12},{1,5},{9... | collective-permute-start | bytes 1327112 | tf_op jit(solution)/shard_map/ppermute | solution.py:779
  365.6 10.9 %collective-permute-start.41 = (f32[120,768]{1,0:T(8,128)}, f32[120,768]{1,0:T(8,128)S(1)}, u32[]{:S(2)}, u32[]{:S(2)}) collective-permute-start(f32[120,768]{1,0:T(8,128)} %fusion.31), channel_id=1, source_target_pairs={{0,8},{8,16},{16,24},{24,28},{28,20},{20,12},{12,4},{4,0},{1,9},{9... | collective-permute-start | bytes 1105928 | tf_op jit(solution)/shard_map/ppermute | solution.py:779
  376.8 23.2 %collective-permute-start.45 = (f32[320,768]{1,0:T(8,128)S(1)}, f32[320,768]{1,0:T(8,128)S(1)}, u32[]{:S(2)}, u32[]{:S(2)}) collective-permute-start(f32[320,768]{1,0:T(8,128)S(1)} %add.506), channel_id=1, source_target_pairs={{0,2},{1,3},{2,0},{3,1},{4,6},{5,7},{6,4},{7,5},{8,10},{9,11},{10,... | collective-permute-start | bytes 2949128 | tf_op jit(solution)/shard_map/ppermute | solution.py:679
  379.5 11.8 %collective-permute-start.44 = (f32[144,768]{1,0:T(8,128)}, f32[144,768]{1,0:T(8,128)}, u32[]{:S(2)}, u32[]{:S(2)}) collective-permute-start(f32[144,768]{1,0:T(8,128)} %fusion.14), channel_id=1, source_target_pairs={{0,4},{8,0},{16,8},{24,16},{28,24},{20,28},{12,20},{4,12},{1,5},{9... | collective-permute-start | bytes 1327112 | tf_op jit(solution)/shard_map/ppermute | solution.py:779
  380.9 10.0 %collective-permute-start.43 = (f32[120,768]{1,0:T(8,128)}, f32[120,768]{1,0:T(8,128)}, u32[]{:S(2)}, u32[]{:S(2)}) collective-permute-start(f32[120,768]{1,0:T(8,128)} %fusion.33), channel_id=1, source_target_pairs={{0,8},{8,16},{16,24},{24,28},{28,20},{20,12},{12,4},{4,0},{1,9},{9... | collective-permute-start | bytes 1105928 | tf_op jit(solution)/shard_map/ppermute | solution.py:779
  400.0 16.5 %collective-permute-start.46 = (f32[320,768]{1,0:T(8,128)S(1)}, f32[320,768]{1,0:T(8,128)S(1)}, u32[]{:S(2)}, u32[]{:S(2)}) collective-permute-start(f32[320,768]{1,0:T(8,128)S(1)} %get-tuple-element.376), channel_id=1, source_target_pairs={{0,1},{1,0},{2,3},{3,2},{4,5},{5,4},{6,7},{7,6},{8,9},{9,8},{10,11... | collective-permute-start | bytes 2949128 | tf_op jit(solution)/shard_map/ppermute | solution.py:679
  403.7 12.8 %collective-permute-start.48 = (f32[144,768]{1,0:T(8,128)}, f32[144,768]{1,0:T(8,128)S(1)}, u32[]{:S(2)}, u32[]{:S(2)}) collective-permute-start(f32[144,768]{1,0:T(8,128)} %fusion.16), channel_id=1, source_target_pairs={{0,4},{8,0},{16,8},{24,16},{28,24},{20,28},{12,20},{4,12},{1,5},{9... | collective-permute-start | bytes 1327112 | tf_op jit(solution)/shard_map/ppermute | solution.py:779
  405.2 11.1 %collective-permute-start.47 = (f32[120,768]{1,0:T(8,128)}, f32[120,768]{1,0:T(8,128)S(1)}, u32[]{:S(2)}, u32[]{:S(2)}) collective-permute-start(f32[120,768]{1,0:T(8,128)} %fusion.35), channel_id=1, source_target_pairs={{0,8},{8,16},{16,24},{24,28},{28,20},{20,12},{12,4},{4,0},{1,9},{9... | collective-permute-start | bytes 1105928 | tf_op jit(solution)/shard_map/ppermute | solution.py:779
  416.6 23.5 %collective-permute-start.51 = (f32[320,768]{1,0:T(8,128)S(1)}, f32[320,768]{1,0:T(8,128)S(1)}, u32[]{:S(2)}, u32[]{:S(2)}) collective-permute-start(f32[320,768]{1,0:T(8,128)S(1)} %add.521), channel_id=1, source_target_pairs={{0,2},{1,3},{2,0},{3,1},{4,6},{5,7},{6,4},{7,5},{8,10},{9,11},{10,... | collective-permute-start | bytes 2949128 | tf_op jit(solution)/shard_map/ppermute | solution.py:679
  418.4 11.9 %collective-permute-start.50 = (f32[144,768]{1,0:T(8,128)S(1)}, f32[144,768]{1,0:T(8,128)S(1)}, u32[]{:S(2)}, u32[]{:S(2)}) collective-permute-start(f32[144,768]{1,0:T(8,128)S(1)} %fusion.18), channel_id=1, source_target_pairs={{0,4},{8,0},{16,8},{24,16},{28,24},{20,28},{12,20},{4,12},{1,5},{9... | collective-permute-start | bytes 1327112 | tf_op jit(solution)/shard_map/ppermute | solution.py:779
  420.0 10.0 %collective-permute-start.49 = (f32[120,768]{1,0:T(8,128)S(1)}, f32[120,768]{1,0:T(8,128)S(1)}, u32[]{:S(2)}, u32[]{:S(2)}) collective-permute-start(f32[120,768]{1,0:T(8,128)S(1)} %fusion.37), channel_id=1, source_target_pairs={{0,8},{8,16},{16,24},{24,28},{28,20},{20,12},{12,4},{4,0},{1,9},{9... | collective-permute-start | bytes 1105928 | tf_op jit(solution)/shard_map/ppermute | solution.py:779
  420.7 76.1 %collective-permute-start.63 = (f32[7,768]{1,0:T(8,128)S(1)}, f32[7,768]{1,0:T(8,128)S(1)}, u32[]{:S(2)}, u32[]{:S(2)}) collective-permute-start(f32[7,768]{1,0:T(8,128)S(1)} %pad_maximum_fusion.12), channel_id=1, source_target_pairs={{0,1},{1,0},{2,3},{3,2},{4,5},{5,4},{6,7},{7,6},{8,9},{9,8},{10,11... | collective-permute-start | bytes 64520 | tf_op jit(solution)/shard_map/ppermute | solution.py:679
  440.4 13.4 %collective-permute-start.54 = (f32[144,768]{1,0:T(8,128)S(1)}, f32[144,768]{1,0:T(8,128)S(1)}, u32[]{:S(2)}, u32[]{:S(2)}) collective-permute-start(f32[144,768]{1,0:T(8,128)S(1)} %fusion.20), channel_id=1, source_target_pairs={{0,4},{8,0},{16,8},{24,16},{28,24},{20,28},{12,20},{4,12},{1,5},{9... | collective-permute-start | bytes 1327112 | tf_op jit(solution)/shard_map/ppermute | solution.py:779
  442.0 11.8 %collective-permute-start.53 = (f32[120,768]{1,0:T(8,128)S(1)}, f32[120,768]{1,0:T(8,128)S(1)}, u32[]{:S(2)}, u32[]{:S(2)}) collective-permute-start(f32[120,768]{1,0:T(8,128)S(1)} %fusion.39), channel_id=1, source_target_pairs={{0,8},{8,16},{16,24},{24,28},{28,20},{20,12},{12,4},{4,0},{1,9},{9... | collective-permute-start | bytes 1105928 | tf_op jit(solution)/shard_map/ppermute | solution.py:779
  442.8 19.0 %collective-permute-start.73 = (f32[160,768]{1,0:T(8,128)S(1)}, f32[160,768]{1,0:T(8,128)S(1)}, u32[]{:S(2)}, u32[]{:S(2)}) collective-permute-start(f32[160,768]{1,0:T(8,128)S(1)} %constant_dynamic-slice_fusion.5), channel_id=1, source_target_pairs={{0,4},{4,0},{8,12},{12,8},{16,20},{20,16},{24,28},{28,24},{1,5},{5... | collective-permute-start | bytes 1474568 | tf_op jit(solution)/shard_map/ppermute | solution.py:779
  444.4 15.4 %collective-permute-start.74 = (f32[128,768]{1,0:T(8,128)S(1)}, f32[128,768]{1,0:T(8,128)S(1)}, u32[]{:S(2)}, u32[]{:S(2)}) collective-permute-start(f32[128,768]{1,0:T(8,128)S(1)} %constant_dynamic-slice_fusion.4), channel_id=1, source_target_pairs={{0,8},{4,12},{8,0},{12,4},{16,24},{20,28},{24,16},{28,20},{1,9},{5... | collective-permute-start | bytes 1179656 | tf_op jit(solution)/shard_map/ppermute | solution.py:779
  453.8 57.4 %collective-permute-start.58 = (f32[320,768]{1,0:T(8,128)S(1)}, f32[320,768]{1,0:T(8,128)S(1)}, u32[]{:S(2)}, u32[]{:S(2)}) collective-permute-start(f32[320,768]{1,0:T(8,128)S(1)} %maximum_add_fusion.refs_1_), channel_id=1, source_target_pairs={{0,1},{1,0},{2,3},{3,2},{4,5},{5,4},{6,7},{7,6},{8,9},{9,8},{10,11... | collective-permute-start | bytes 2949128 | tf_op jit(solution)/shard_map/ppermute | solution.py:679
  453.8 18.0 %collective-permute-start.52 = (f32[320,768]{1,0:T(8,128)S(1)}, f32[320,768]{1,0:T(8,128)S(1)}, u32[]{:S(2)}, u32[]{:S(2)}) collective-permute-start(f32[320,768]{1,0:T(8,128)S(1)} %get-tuple-element.398), channel_id=1, source_target_pairs={{0,1},{1,0},{2,3},{3,2},{4,5},{5,4},{6,7},{7,6},{8,9},{9,8},{10,11... | collective-permute-start | bytes 2949128 | tf_op jit(solution)/shard_map/ppermute | solution.py:679
  462.0 9.8 %collective-permute-start.75 = (f32[80,768]{1,0:T(8,128)S(1)}, f32[80,768]{1,0:T(8,128)S(1)}, u32[]{:S(2)}, u32[]{:S(2)}) collective-permute-start(f32[80,768]{1,0:T(8,128)S(1)} %constant_dynamic-slice_fusion.3), channel_id=1, source_target_pairs={{0,8},{4,12},{8,0},{12,4},{16,24},{20,28},{24,16},{28,20},{1,9},{5... | collective-permute-start | bytes 737288 | tf_op jit(solution)/shard_map/ppermute | solution.py:779
  472.0 20.0 %collective-permute-start.57 = (f32[320,768]{1,0:T(8,128)S(1)}, f32[320,768]{1,0:T(8,128)S(1)}, u32[]{:S(2)}, u32[]{:S(2)}) collective-permute-start(f32[320,768]{1,0:T(8,128)S(1)} %add.536), channel_id=1, source_target_pairs={{0,2},{1,3},{2,0},{3,1},{4,6},{5,7},{6,4},{7,5},{8,10},{9,11},{10,... | collective-permute-start | bytes 2949128 | tf_op jit(solution)/shard_map/ppermute | solution.py:679
  479.1 10.0 %collective-permute-start.56 = (f32[144,768]{1,0:T(8,128)S(1)}, f32[144,768]{1,0:T(8,128)S(1)}, u32[]{:S(2)}, u32[]{:S(2)}) collective-permute-start(f32[144,768]{1,0:T(8,128)S(1)} %fusion.7.refs_0_), channel_id=1, source_target_pairs={{0,4},{8,0},{16,8},{24,16},{28,24},{20,28},{12,20},{4,12},{1,5},{9... | collective-permute-start | bytes 1327112 | tf_op jit(solution)/shard_map/ppermute | solution.py:779
  489.1 24.1 %collective-permute-start.59 = (f32[320,768]{1,0:T(8,128)S(1)}, f32[320,768]{1,0:T(8,128)}, u32[]{:S(2)}, u32[]{:S(2)}) collective-permute-start(f32[320,768]{1,0:T(8,128)S(1)} %maximum_add_fusion.1.refs_2_), channel_id=1, source_target_pairs={{0,1},{1,0},{2,3},{3,2},{4,5},{5,4},{6,7},{7,6},{8,9},{9,8},{10,11... | collective-permute-start | bytes 2949128 | tf_op jit(solution)/shard_map/ppermute | solution.py:679
  489.1 10.0 %collective-permute-start.79 = (f32[40,768]{1,0:T(8,128)S(1)}, f32[40,768]{1,0:T(8,128)S(1)}, u32[]{:S(2)}, u32[]{:S(2)}) collective-permute-start(f32[40,768]{1,0:T(8,128)S(1)} %dynamic-slice_add_fusion.5), channel_id=1, source_target_pairs={{0,16},{4,20},{8,24},{12,28},{16,0},{20,4},{24,8},{28,12},{1,17},{... | collective-permute-start | bytes 368648 | tf_op jit(solution)/shard_map/ppermute | solution.py:779
  496.7 14.4 %collective-permute-start.62 = (f32[320,768]{1,0:T(8,128)S(1)}, f32[320,768]{1,0:T(8,128)S(1)}, u32[]{:S(2)}, u32[]{:S(2)}) collective-permute-start(f32[320,768]{1,0:T(8,128)S(1)} %maximum_add_fusion.2.refs_3_), channel_id=1, source_target_pairs={{0,1},{1,0},{2,3},{3,2},{4,5},{5,4},{6,7},{7,6},{8,9},{9,8},{10,11... | collective-permute-start | bytes 2949128 | tf_op jit(solution)/shard_map/ppermute | solution.py:679
  500.0 11.1 %collective-permute-start.61 = (f32[144,768]{1,0:T(8,128)S(1)}, f32[144,768]{1,0:T(8,128)S(1)}, u32[]{:S(2)}, u32[]{:S(2)}) collective-permute-start(f32[144,768]{1,0:T(8,128)S(1)} %collective-permute-done.56.refs_1_), channel_id=1, source_target_pairs={{0,4},{8,0},{16,8},{24,16},{28,24},{20,28},{12,20},{4,12},{1,5},{9... | collective-permute-start | bytes 1327112 | tf_op jit(solution)/shard_map/ppermute | solution.py:779
  508.5 31.2 %collective-permute-start.81 = (f32[80,768]{1,0:T(8,128)}, f32[80,768]{1,0:T(8,128)S(1)}, u32[]{:S(2)}, u32[]{:S(2)}) collective-permute-start(f32[80,768]{1,0:T(8,128)} %pad_maximum_fusion.10), channel_id=1, source_target_pairs={{0,8},{4,12},{8,0},{12,4},{16,24},{20,28},{24,16},{28,20},{1,9},{5... | collective-permute-start | bytes 737288 | tf_op jit(solution)/shard_map/ppermute | solution.py:779
  520.0 24.9 %collective-permute-start.65 = (f32[144,768]{1,0:T(8,128)}, f32[144,768]{1,0:T(8,128)}, u32[]{:S(2)}, u32[]{:S(2)}) collective-permute-start(f32[144,768]{1,0:T(8,128)} %copy-done.60), channel_id=1, source_target_pairs={{0,4},{8,0},{16,8},{24,16},{28,24},{20,28},{12,20},{4,12},{1,5},{9... | collective-permute-start | bytes 1327112 | tf_op jit(solution)/shard_map/ppermute | solution.py:779
  521.4 18.2 %collective-permute-start.82 = (f32[64,768]{1,0:T(8,128)}, f32[64,768]{1,0:T(8,128)S(1)}, u32[]{:S(2)}, u32[]{:S(2)}) collective-permute-start(f32[64,768]{1,0:T(8,128)} %pad_maximum_fusion.11), channel_id=1, source_target_pairs={{0,16},{4,20},{8,24},{12,28},{16,0},{20,4},{24,8},{28,12},{1,17},{... | collective-permute-start | bytes 589832 | tf_op jit(solution)/shard_map/ppermute | solution.py:779
  524.0 20.9 %collective-permute-start.64 = (f32[120,768]{1,0:T(8,128)}, f32[120,768]{1,0:T(8,128)}, u32[]{:S(2)}, u32[]{:S(2)}) collective-permute-start(f32[120,768]{1,0:T(8,128)} %copy-done.65), channel_id=1, source_target_pairs={{0,8},{8,16},{16,24},{24,28},{28,20},{20,12},{12,4},{4,0},{1,9},{9... | collective-permute-start | bytes 1105928 | tf_op jit(solution)/shard_map/ppermute | solution.py:779
  544.9 15.7 %collective-permute-start.68 = (f32[144,768]{1,0:T(8,128)}, f32[144,768]{1,0:T(8,128)}, u32[]{:S(2)}, u32[]{:S(2)}) collective-permute-start(f32[144,768]{1,0:T(8,128)} %collective-permute-done.65.refs_3_), channel_id=1, source_target_pairs={{0,4},{8,0},{16,8},{24,16},{28,24},{20,28},{12,20},{4,12},{1,5},{9... | collective-permute-start | bytes 1327112 | tf_op jit(solution)/shard_map/ppermute | solution.py:779
  545.8 14.9 %collective-permute-start.67 = (f32[120,768]{1,0:T(8,128)}, f32[120,768]{1,0:T(8,128)}, u32[]{:S(2)}, u32[]{:S(2)}) collective-permute-start(f32[120,768]{1,0:T(8,128)} %collective-permute-done.64.refs_3_), channel_id=1, source_target_pairs={{0,8},{8,16},{16,24},{24,28},{28,20},{20,12},{12,4},{4,0},{1,9},{9... | collective-permute-start | bytes 1105928 | tf_op jit(solution)/shard_map/ppermute | solution.py:779
  547.8 12.8 %collective-permute-start.69 = (f32[20,768]{1,0:T(8,128)S(1)}, f32[20,768]{1,0:T(8,128)S(1)}, u32[]{:S(2)}, u32[]{:S(2)}) collective-permute-start(f32[20,768]{1,0:T(8,128)S(1)} %add.557), channel_id=1, source_target_pairs={{0,8},{4,12},{8,0},{12,4},{16,24},{20,28},{24,16},{28,20},{1,9},{5... | collective-permute-start | bytes 184328 | tf_op jit(solution)/shard_map/ppermute | solution.py:779
  548.7 32.5 %collective-permute-start.83 = (f32[160,768]{1,0:T(8,128)}, f32[160,768]{1,0:T(8,128)S(1)}, u32[]{:S(2)}, u32[]{:S(2)}) collective-permute-start(f32[160,768]{1,0:T(8,128)} %pad_maximum_fusion.3), channel_id=1, source_target_pairs={{0,4},{4,0},{8,12},{12,8},{16,20},{20,16},{24,28},{28,24},{1,5},{5... | collective-permute-start | bytes 1474568 | tf_op jit(solution)/shard_map/ppermute | solution.py:779
  560.7 20.5 %collective-permute-start.71 = (f32[144,768]{1,0:T(8,128)}, f32[144,768]{1,0:T(8,128)S(1)}, u32[]{:S(2)}, u32[]{:S(2)}) collective-permute-start(f32[144,768]{1,0:T(8,128)} %collective-permute-done.68.refs_4_), channel_id=1, source_target_pairs={{0,4},{8,0},{16,8},{24,16},{28,24},{20,28},{12,20},{4,12},{1,5},{9... | collective-permute-start | bytes 1327112 | tf_op jit(solution)/shard_map/ppermute | solution.py:779
  560.7 20.5 %collective-permute-start.84 = (f32[128,768]{1,0:T(8,128)}, f32[128,768]{1,0:T(8,128)}, u32[]{:S(2)}, u32[]{:S(2)}) collective-permute-start(f32[128,768]{1,0:T(8,128)} %pad_maximum_fusion.6), channel_id=1, source_target_pairs={{0,8},{4,12},{8,0},{12,4},{16,24},{20,28},{24,16},{28,20},{1,9},{5... | collective-permute-start | bytes 1179656 | tf_op jit(solution)/shard_map/ppermute | solution.py:779
  562.8 18.5 %collective-permute-start.70 = (f32[120,768]{1,0:T(8,128)}, f32[120,768]{1,0:T(8,128)}, u32[]{:S(2)}, u32[]{:S(2)}) collective-permute-start(f32[120,768]{1,0:T(8,128)} %collective-permute-done.67.refs_4_), channel_id=1, source_target_pairs={{0,8},{8,16},{16,24},{24,28},{28,20},{20,12},{12,4},{4,0},{1,9},{9... | collective-permute-start | bytes 1105928 | tf_op jit(solution)/shard_map/ppermute | solution.py:779
  564.0 17.2 %collective-permute-start.72 = (f32[20,768]{1,0:T(8,128)S(1)}, f32[20,768]{1,0:T(8,128)S(1)}, u32[]{:S(2)}, u32[]{:S(2)}) collective-permute-start(f32[20,768]{1,0:T(8,128)S(1)} %add.558), channel_id=1, source_target_pairs={{0,16},{4,20},{8,24},{12,28},{16,0},{20,4},{24,8},{28,12},{1,17},{... | collective-permute-start | bytes 184328 | tf_op jit(solution)/shard_map/ppermute | solution.py:779
  (118 other events, 1345.8 us)

commit v6 on v4

--- a/solution.py
+++ b/solution.py
@@ -1022,10 +1022,10 @@
         )
         if doc:
             steps.run()
-        (far,) = steps.run(lambda x: (x,), (gx[doc][1],))
+        (far,) = steps.run(lambda doc=doc: (gx[doc][1],))
         gh_mine.append(first + (gx[doc][0] + far))
         gh_theirs.append(from_sib(gh_mine[-1]))
-    (gh_theirs[-1],) = steps.run(lambda x: (x,), (gh_theirs[-1],))
+    (gh_theirs[-1],) = steps.run(lambda: (gh_theirs[-1],))
     grad_hidden, bn_sums = final_rows(all_rows, segs, place, gh_mine, gh_theirs, roi, stats)
 
     rows = sum(txt_sums) + back["sums"]

time: 604 us -> 601 us (level)
    ppermute x46, waiting for transfers between devices: 94.4 us -> 101 us  [swap(): return lax.ppermute(x, axis, [(i, i ^ bit) for i in range(n)])]
    ppermute x43, waiting for transfers between devices: 86.2 us -> 79.9 us  [run(): lax.ppermute(x, *self.active[name][1][1:])]
    unnamed x305 -> x299, local copies, waits for them, and re-layouts: 23.1 us -> 23.1 us
where the time goes in v6:
time: 601 us; the launch traced here: 594 us
  Pallas kernels  208 us (35%)
  waiting for transfers between devices  181 us (30%)
  starting transfers between devices  85 us (14%)
  local copies, waits for them, and re-layouts  47.3 us (8%)
  matrix products  39.7 us (7%)
  other arithmetic  30.4 us (5%)
    pallas_call x5, Pallas kernels, ffn(): pl.pallas_call(functools.partial(ffn_kernel, forward, backward, all_names...  125 us
    ppermute x46, waiting for transfers between devices, swap(): return lax.ppermute(x, axis, [(i, i ^ bit) for i in range(n)])  101 us
    ppermute x43, waiting for transfers between devices, run(): lax.ppermute(x, *self.active[name][1][1:])  79.9 us
    ppermute x43, starting transfers between devices, run(): lax.ppermute(x, *self.active[name][1][1:])  48.5 us
    dot_general x14, matrix products, product(): lax.dot_general(operand, other, (dims, ((), ())), precision=HIGH, preferr...  39.7 us
    ppermute x46, starting transfers between devices, swap(): return lax.ppermute(x, axis, [(i, i ^ bit) for i in range(n)])  25.1 us
    unnamed x299, local copies, waits for them, and re-layouts  23.1 us
    pallas_call x1, Pallas kernels, attn_fwd(): pl.pallas_call(functools.partial(attn_fwd_kernel, all_rows), grid=(docs,)...  22.3 us
  transfers between devices with their start and end apart: 91, of which 37 were waited for; matrix products, arithmetic and copies ran while one was open for 11% of the time, Pallas kernels for 30%

profile of v6, /device:TPU:0, one launch (start us, length us, event | category | flops | bytes accessed | tf_op | source)
XLA Modules:
  0.0 594.1 jit_solution(2702242953488137110)
XLA Ops:
  1.3 2.2 local_stats.1
  3.4 2.9 collective-permute-start.5
  12.0 2.4 constant_dynamic-slice_fusion.10
  17.6 2.1 collective-permute-done.6
  22.4 2.6 collective-permute-start.7
  25.0 1.9 collective-permute-done.7
  30.9 22.3 %attn_fwd.1 = (f32[1920,576]{1,0:T(8,128)}, f32[24,640]{1,0:T(8,128)}, f32[192,384]{1,0:T(8,128)}, f32[768,384]{1,0:T(8,128)}, f32[192,768]{1,0:T(8,128)}, /*index=5*/f32[768,768]{1,0:T(8,128)}) custom-call(s32[3]{0:T(128)} %pad_add_fusion.refs_0_.place, s32[3]{0:T(128)} %refs_1_.22, f32[1920,768]{1,0:T(8,128)} %refs_1_.23, f32[384,768]{1,0:T(8,128)} %refs_7_.2, ...), custom_call_target="tpu_custom_call" | custom-call | flops 11520 | bytes 640 | tf_op jit(solution)/shard_map/attn_fwd/pallas_call | solution.py:189
  53.3 17.5 %collective-permute-done.1.refs_27_.refs_28_.refs_24_ = f32[384,768]{1,0:T(8,128)} collective-permute-done((f32[384,768]{1,0:T(8,128)}, f32[384,768]{1,0:T(8,128)}, u32[]{:S(2)}, u32[]{:S(2)}) %collective-permute-start.1) | collective-permute-done | bytes 1179680 | tf_op jit(solution)/shard_map/ppermute | solution.py:679
  73.7 4.9 collective-permute-done.13.refs_9_
  79.1 21.3 %collective-permute-done.12.refs_29_.refs_30_.refs_26_ = f32[384,768]{1,0:T(8,128)} collective-permute-done((f32[384,768]{1,0:T(8,128)}, f32[384,768]{1,0:T(8,128)}, u32[]{:S(2)}, u32[]{:S(2)}) %collective-permute-start.12) | collective-permute-done | bytes 1179680 | tf_op jit(solution)/shard_map/ppermute | solution.py:679
  100.4 6.0 %collective-permute-done.11.refs_19_.refs_28_.refs_20_.refs_29_.refs_25_ = f32[480,768]{1,0:T(8,128)} collective-permute-done((f32[480,768]{1,0:T(8,128)}, f32[480,768]{1,0:T(8,128)}, u32[]{:S(2)}, u32[]{:S(2)}) %collective-permute-start.11) | collective-permute-done | bytes 1474592 | tf_op jit(solution)/shard_map/ppermute | solution.py:679
  112.2 17.2 %ffn_fwd.1 = (f32[192,768]{1,0:T(8,128)}, f32[960,768]{1,0:T(8,128)}, f32[960,768]{1,0:T(8,128)}, f32[960,768]{1,0:T(8,128)}, f32[192,768]{1,0:T(8,128)}, /*inde...) custom-call(s32[3]{0:T(128)} %pad_add_fusion.refs_0_.place, f32[768]{0:T(1024)} %refs_1_.17, ...), custom_call_target="tpu_custom_call" | custom-call | flops 16307453952 | bytes 8847360 | tf_op jit(solution)/shard_map/ffn_fwd/pallas_call | solution.py:577
  129.4 6.4 %collective-permute-done.22.refs_9_ = f32[768,384]{1,0:T(8,128)} collective-permute-done((f32[768,384]{1,0:T(8,128)}, f32[768,384]{1,0:T(8,128)}, u32[]{:S(2)}, u32[]{:S(2)}) %collective-permute-start.22) | collective-permute-done | bytes 1179680 | tf_op jit(solution)/shard_map/ppermute | solution.py:679
  142.6 5.3 all-to-all-start
  147.9 29.2 %ffn_fwdbwd.3 = (f32[768,768]{1,0:T(8,128)}, f32[960,768]{1,0:T(8,128)}, f32[960,768]{1,0:T(8,128)}, f32[960,768]{1,0:T(8,128)}, f32[960,768]{1,0:T(8,128)}, /*i...) custom-call(s32[3]{0:T(128)} %pad_add_fusion.refs_0_.place, ...), custom_call_target="tpu_custom_call", output_to_operand_aliasing={{1}: (35, {}), {2}: (36, {}), {3}: (37, {})} | custom-call | flops 25367150592 | bytes 11796480 | tf_op jit(solution)/shard_map/ffn_fwdbwd/pallas_call | solution.py:577
  179.2 3.1 scatter_custom_fusion
  184.0 29.4 %ffn_fwdbwd.4 = (f32[768,768]{1,0:T(8,128)}, f32[960,768]{1,0:T(8,128)}, f32[960,768]{1,0:T(8,128)}, f32[960,768]{1,0:T(8,128)}, f32[960,768]{1,0:T(8,128)}, /*i...) custom-call(s32[3]{0:T(128)} %pad_add_fusion.refs_0_.place, ...), custom_call_target="tpu_custom_call", output_to_operand_aliasing={{0}: (35, {}), {1}: (36, {}), {2}: (37, {}), {3}: (38, {}),... | custom-call | flops 25367150592 | bytes 11796480 | tf_op jit(solution)/shard_map/ffn_fwdbwd/pallas_call | solution.py:577
  219.4 6.1 %all-to-all-start.1 = ((f32[8,48,192]{2,1,0:T(8,128)}), f32[8,48,192]{2,1,0:T(8,128)S(1)}, u32[]{:S(2)}, u32[]{:S(2)}) async-start(f32[8,48,192]{2,1,0:T(8,128)} %bitcast.12), calls=%async_computation.1 | async-start | bytes 786432 | tf_op jit(solution)/shard_map/all_to_all | solution.py:913
  225.6 29.3 %ffn_fwdbwd.5 = (f32[768,768]{1,0:T(8,128)}, f32[960,768]{1,0:T(8,128)}, f32[960,768]{1,0:T(8,128)}, f32[960,768]{1,0:T(8,128)}, f32[960,768]{1,0:T(8,128)}, /*i...) custom-call(s32[3]{0:T(128)} %pad_add_fusion.refs_0_.place, ...), custom_call_target="tpu_custom_call", output_to_operand_aliasing={{0}: (35, {}), {1}: (36, {}), {2}: (37, {}), {3}: (38, {}),... | custom-call | flops 25367150592 | bytes 11796480 | tf_op jit(solution)/shard_map/ffn_fwdbwd/pallas_call | solution.py:577
  257.4 3.8 collective-permute-done.27
  263.2 7.5 %collective-permute-done.28 = f32[192,384]{1,0:T(8,128)S(1)} collective-permute-done((f32[192,384]{1,0:T(8,128)S(1)}, f32[192,384]{1,0:T(8,128)S(1)}, u32[]{:S(2)}, u32[]{:S(2)}) %collective-permute-start.28) | collective-permute-done | bytes 294944 | tf_op jit(solution)/shard_map/ppermute | solution.py:679
  271.7 6.5 %join_rows.1 = f32[1920,768]{1,0:T(8,128)} custom-call(s32[3]{0:T(128)} %pad_add_fusion.refs_0_.place, f32[192,768]{1,0:T(8,128)} %get-tuple-element.267.ms, f32[768,768]{1,0:T(8,128)} %get-tuple-element.309.mt, f32[192,768]{1,0:T(8,128)} %copy-done.105, f32[768,768]{1,0:T(8,128)} %collective-permute-done.30.tt), custom_call_target="tpu_custom_call" | custom-call | bytes 11796480 | tf_op jit(solution)/shard_map/join_rows/pallas_call | solution.py:607
  279.1 20.3 %ffn_bwd.1 = (f32[960,768]{1,0:T(8,128)}, f32[960,768]{1,0:T(8,128)}, f32[960,768]{1,0:T(8,128)}, f32[960,768]{1,0:T(8,128)}, f32[192,384]{1,0:T(8,128)}, /*index=5*/f32[384,768]{1,0:T(8,128)}, f32[8,768]{1,0:T(8,128)}) custom-call(s32[3]{0:T(128)} %pad_add_fusion.refs_0_.place, ...), custom_call_target="tpu_custom_call", output_to_operand_aliasing={{0}: (31, {}), {1}: (32, {}), {2}: (33, {}), {3}: (34, {})} | custom-call | flops 16307453952 | bytes 8847360 | tf_op jit(solution)/shard_map/ffn_bwd/pallas_call | solution.py:577
  299.4 8.9 %fusion.68 = f32[768,768]{1,0:T(8,128)} fusion(f32[960,768]{1,0:T(8,128)} %get-tuple-element.331, f32[960,768]{1,0:T(8,128)} %get-tuple-element.330), kind=kOutput, calls=%fused_computation.205 | convolution fusion | flops 3397386240 | bytes 8257536 | tf_op jit(solution)/shard_map/dot_general | solution.py:24
  308.4 6.1 %fusion.67 = f32[768,768]{1,0:T(8,128)} fusion(f32[960,768]{1,0:T(8,128)S(1)} %copy-done.70, f32[960,768]{1,0:T(8,128)S(1)} %copy-done.83), kind=kOutput, calls=%fused_computation.204 | convolution fusion | flops 3397386240 | bytes 8257536 | tf_op jit(solution)/shard_map/dot_general | solution.py:24
  316.7 1.9 fusion.40
  318.7 2.5 collective-permute-done.32
  322.3 7.8 %convolution_add_fusion = f32[768,768]{1,0:T(8,128)S(1)} fusion(f32[768,768]{1,0:T(8,128)} %collective-permute-done.33, f32[960,768]{1,0:T(8,128)} %get-tuple-element.329, f32[960,768]{1,0:T(8,128)S(1)} %copy-done.72), kind=kOutput, calls=%fused_computation.36 | convolution fusion | flops 3397976064 | bytes 10616832 | tf_op jit(solution)/shard_map/dot_general | solution.py:24
  330.2 7.5 %convolution_add_fusion.1 = f32[768,768]{1,0:T(8,128)S(1)} fusion(f32[768,768]{1,0:T(8,128)} %collective-permute-done.31, f32[960,768]{1,0:T(8,128)S(1)} %copy-done.71, f32[960,768]{1,0:T(8,128)S(1)} %copy-done.82), kind=kOutput, calls=%fused_computation.37 | convolution fusion | flops 3397976064 | bytes 10616832 | tf_op jit(solution)/shard_map/dot_general | solution.py:24
  338.0 2.1 collective-permute-start.35
  340.6 7.0 %attn_bwd.3 = (f32[640,576]{1,0:T(8,128)S(1)}, f32[1,576]{1,0:T(1,128)S(1)}) custom-call(s32[3]{0:T(128)S(1)} %copy-done.19, s32[3]{0:T(128)S(1)} %copy-done.24, f32[1920,576]{1,0:T(8,128)S(1)} %bitcast.84, f32[24,640]{1,0:T(8,128)S(1)} %copy-done.48, f32[192,384]{1,0:T(8,128)S(1)} %copy-done.39, f32[768,384]{1,0:T(8,128)S(1)} %copy-done.29, ...), custom_call_target="tpu_custom_call" | custom-call | flops 7549747200 | bytes 2949120 | tf_op jit(solution)/shard_map/attn_bwd/pallas_call | solution.py:276
  347.7 3.3 collective-permute-done.34
  355.0 2.7 copy-done.2
  359.8 5.5 qkv_bwd.3
  366.2 2.4 fusion.12
  372.3 2.4 copy-done.27
  374.7 7.0 %attn_bwd.4 = (f32[640,576]{1,0:T(8,128)S(1)}, f32[1,576]{1,0:T(1,128)S(1)}) custom-call(s32[3]{0:T(128)S(1)} %copy-done.21, s32[3]{0:T(128)S(1)} %copy-done.25, f32[1920,576]{1,0:T(8,128)S(1)} %copy-done.27, f32[24,640]{1,0:T(8,128)S(1)} %copy-done.49, f32[192,384]{1,0:T(8,128)S(1)} %copy-done.40, f32[768,384]{1,0:T(8,128)S(1)} %copy-done.30, ...), custom_call_target="tpu_custom_call" | custom-call | flops 7549747200 | bytes 2949120 | tf_op jit(solution)/shard_map/attn_bwd/pallas_call | solution.py:276
  385.6 2.7 copy-done.3
  391.9 5.5 qkv_bwd.4
  402.9 2.4 copy-done.28
  405.3 7.0 %attn_bwd.5 = (f32[640,576]{1,0:T(8,128)S(1)}, f32[1,576]{1,0:T(1,128)S(1)}) custom-call(s32[3]{0:T(128)S(1)} %copy-done.23, s32[3]{0:T(128)S(1)} %copy-done.26, f32[1920,576]{1,0:T(8,128)S(1)} %copy-done.28, f32[24,640]{1,0:T(8,128)S(1)} %copy-done.50, f32[192,384]{1,0:T(8,128)S(1)} %copy-done.41, f32[768,384]{1,0:T(8,128)S(1)} %copy-done.31, ...), custom_call_target="tpu_custom_call" | custom-call | flops 7549747200 | bytes 2949120 | tf_op jit(solution)/shard_map/attn_bwd/pallas_call | solution.py:276
  417.9 5.5 qkv_bwd.5
  431.2 10.4 %collective-permute-done.51 = f32[320,768]{1,0:T(8,128)} collective-permute-done((f32[320,768]{1,0:T(8,128)S(1)}, f32[320,768]{1,0:T(8,128)}, u32[]{:S(2)}, u32[]{:S(2)}) %collective-permute-start.51) | collective-permute-done | bytes 983072 | tf_op jit(solution)/shard_map/ppermute | solution.py:679
  442.1 3.0 collective-permute-done.78
  447.2 4.2 collective-permute-start.80
  451.5 5.4 collective-permute-done.80
  457.1 2.2 collective-permute-start.82
  459.5 2.0 collective-permute-start.53
  463.4 11.9 %collective-permute-done.81 = f32[40,768]{1,0:T(8,128)S(1)} collective-permute-done((f32[40,768]{1,0:T(8,128)S(1)}, f32[40,768]{1,0:T(8,128)S(1)}, u32[]{:S(2)}, u32[]{:S(2)}) %collective-permute-start.81) | collective-permute-done | bytes 122912 | tf_op jit(solution)/shard_map/ppermute | solution.py:779
  478.1 2.2 collective-permute-start.84
  481.8 2.4 collective-permute-done.84
  484.2 4.7 collective-permute-done.83
  490.4 2.0 collective-permute-start.59
  492.5 8.7 %collective-permute-done.59.refs_3_ = f32[120,768]{1,0:T(8,128)S(1)} collective-permute-done((f32[120,768]{1,0:T(8,128)S(1)}, f32[120,768]{1,0:T(8,128)S(1)}, u32[]{:S(2)}, u32[]{:S(2)}) %collective-permute-start.59) | collective-permute-done | bytes 368672 | tf_op jit(solution)/shard_map/ppermute | solution.py:779
  505.1 8.0 %collective-permute-done.63 = f32[320,768]{1,0:T(8,128)S(1)} collective-permute-done((f32[320,768]{1,0:T(8,128)S(1)}, f32[320,768]{1,0:T(8,128)S(1)}, u32[]{:S(2)}, u32[]{:S(2)}) %collective-permute-start.63) | collective-permute-done | bytes 983072 | tf_op jit(solution)/shard_map/ppermute | solution.py:679
  515.6 9.3 %collective-permute-done.86 = f32[64,768]{1,0:T(8,128)S(1)} collective-permute-done((f32[64,768]{1,0:T(8,128)S(1)}, f32[64,768]{1,0:T(8,128)S(1)}, u32[]{:S(2)}, u32[]{:S(2)}) %collective-permute-start.86) | collective-permute-done | bytes 196640 | tf_op jit(solution)/shard_map/ppermute | solution.py:779
  525.1 2.1 collective-permute-start.67
  528.7 4.9 collective-permute-done.66.refs_5_
  538.0 5.9 final_rows.1
  544.8 2.2 concatenate.66
  554.7 11.2 %collective-permute-done.88 = f32[128,768]{1,0:T(8,128)S(1)} collective-permute-done((f32[128,768]{1,0:T(8,128)}, f32[128,768]{1,0:T(8,128)S(1)}, u32[]{:S(2)}, u32[]{:S(2)}) %collective-permute-start.88) | collective-permute-done | bytes 393248 | tf_op jit(solution)/shard_map/ppermute | solution.py:779
  569.7 7.3 %collective-permute-done.75 = f32[20,768]{1,0:T(8,128)S(1)} collective-permute-done((f32[20,768]{1,0:T(8,128)S(1)}, f32[20,768]{1,0:T(8,128)S(1)}, u32[]{:S(2)}, u32[]{:S(2)}) %collective-permute-start.75) | collective-permute-done | bytes 61472 | tf_op jit(solution)/shard_map/ppermute | solution.py:779
  581.6 4.1 assemble.3
  585.7 3.9 assemble.2
  (571 shorter events, 132.6 us)
Async XLA Ops:
  0.7 70.1 %collective-permute-start.3 = (f32[768,768]{1,0:T(8,128)}, f32[768,768]{1,0:T(8,128)}, u32[]{:S(2)}, u32[]{:S(2)}) collective-permute-start(f32[768,768]{1,0:T(8,128)} %refs_19_.1), channel_id=1, source_target_pairs={{0,1},{1,0},{2,3},{3,2},{4,5},{5,4},{6,7},{7,6},{8,9},{9,8},{10,11... | collective-permute-start | bytes 7077896 | tf_op jit(solution)/shard_map/ppermute | solution.py:679
  1.2 69.6 %collective-permute-start.4 = (f32[768,768]{1,0:T(8,128)}, f32[768,768]{1,0:T(8,128)}, u32[]{:S(2)}, u32[]{:S(2)}) collective-permute-start(f32[768,768]{1,0:T(8,128)} %refs_20_.1), channel_id=1, source_target_pairs={{0,1},{1,0},{2,3},{3,2},{4,5},{5,4},{6,7},{7,6},{8,9},{9,8},{10,11... | collective-permute-start | bytes 7077896 | tf_op jit(solution)/shard_map/ppermute | solution.py:679
  3.4 10.9 %collective-permute-start.5 = (f32[2,768]{1,0:T(2,128)}, f32[2,768]{1,0:T(2,128)S(1)}, u32[]{:S(2)}, u32[]{:S(2)}) collective-permute-start(f32[2,768]{1,0:T(2,128)} %local_stats.1), channel_id=1, source_target_pairs={{0,4},{4,0},{8,12},{12,8},{16,20},{20,16},{24,28},{28,24},{1,5},{5... | collective-permute-start | bytes 18440 | tf_op jit(solution)/shard_map/ppermute | solution.py:679
  11.4 59.3 %collective-permute-start = (f32[480,768]{1,0:T(8,128)}, f32[480,768]{1,0:T(8,128)}, u32[]{:S(2)}, u32[]{:S(2)}) collective-permute-start(f32[480,768]{1,0:T(8,128)} %pad_maximum_fusion.1), channel_id=1, source_target_pairs={{0,2},{1,3},{2,0},{3,1},{4,6},{5,7},{6,4},{7,5},{8,10},{9,11},{10,... | collective-permute-start | bytes 4423688 | tf_op jit(solution)/shard_map/ppermute | solution.py:679
  14.3 56.4 %collective-permute-start.1 = (f32[384,768]{1,0:T(8,128)}, f32[384,768]{1,0:T(8,128)}, u32[]{:S(2)}, u32[]{:S(2)}) collective-permute-start(f32[384,768]{1,0:T(8,128)} %constant_dynamic-slice_fusion.10), channel_id=1, source_target_pairs={{0,2},{1,3},{2,0},{3,1},{4,6},{5,7},{6,4},{7,5},{8,10},{9,11},{10,... | collective-permute-start | bytes 3538952 | tf_op jit(solution)/shard_map/ppermute | solution.py:679
  27.0 26.3 %collective-permute-start.2 = (f32[192,768]{1,0:T(8,128)S(1)}, f32[192,768]{1,0:T(8,128)}, u32[]{:S(2)}, u32[]{:S(2)}) collective-permute-start(f32[192,768]{1,0:T(8,128)S(1)} %copy-done.119), channel_id=1, source_target_pairs={{0,1},{1,0},{2,3},{3,2},{4,5},{5,4},{6,7},{7,6},{8,9},{9,8},{10,11... | collective-permute-start | bytes 1769480 | tf_op jit(solution)/shard_map/ppermute | solution.py:679
  71.4 35.0 %collective-permute-start.11 = (f32[480,768]{1,0:T(8,128)}, f32[480,768]{1,0:T(8,128)}, u32[]{:S(2)}, u32[]{:S(2)}) collective-permute-start(f32[480,768]{1,0:T(8,128)} %collective-permute-done.refs_18_.refs_26_.refs_19_.refs_27_.refs_23_), channel_id=1, source_target_pairs={{0,4},{4,0},{8,12},{12,8},{16,20},{20,16},{24,28},{28,24},{1,5},{5... | collective-permute-start | bytes 4423688 | tf_op jit(solution)/shard_map/ppermute | solution.py:679
  71.7 34.7 %collective-permute-start.14 = (f32[480,768]{1,0:T(8,128)}, f32[480,768]{1,0:T(8,128)S(1)}, u32[]{:S(2)}, u32[]{:S(2)}) collective-permute-start(f32[480,768]{1,0:T(8,128)} %collective-permute-done.refs_18_.refs_26_.refs_19_.refs_27_.refs_23_), channel_id=1, source_target_pairs={{0,1},{1,0},{2,3},{3,2},{4,5},{5,4},{6,7},{7,6},{8,9},{9,8},{10,11... | collective-permute-start | bytes 4423688 | tf_op jit(solution)/shard_map/ppermute | solution.py:679
  71.9 28.5 %collective-permute-start.12 = (f32[384,768]{1,0:T(8,128)}, f32[384,768]{1,0:T(8,128)}, u32[]{:S(2)}, u32[]{:S(2)}) collective-permute-start(f32[384,768]{1,0:T(8,128)} %collective-permute-done.1.refs_27_.refs_28_.refs_24_), channel_id=1, source_target_pairs={{0,8},{4,12},{8,0},{12,4},{16,24},{20,28},{24,16},{28,20},{1,9},{5... | collective-permute-start | bytes 3538952 | tf_op jit(solution)/shard_map/ppermute | solution.py:679
  78.6 21.8 %collective-permute-start.15 = (f32[384,768]{1,0:T(8,128)}, f32[384,768]{1,0:T(8,128)S(1)}, u32[]{:S(2)}, u32[]{:S(2)}) collective-permute-start(f32[384,768]{1,0:T(8,128)} %collective-permute-done.1.refs_27_.refs_28_.refs_24_), channel_id=1, source_target_pairs={{0,1},{1,0},{2,3},{3,2},{4,5},{5,4},{6,7},{7,6},{8,9},{9,8},{10,11... | collective-permute-start | bytes 3538952 | tf_op jit(solution)/shard_map/ppermute | solution.py:679
  78.6 21.8 %collective-permute-start.17 = (f32[768,384]{1,0:T(8,128)}, f32[768,384]{1,0:T(8,128)S(1)}, u32[]{:S(2)}, u32[]{:S(2)}) collective-permute-start(f32[768,384]{1,0:T(8,128)} %get-tuple-element.252.refs_7_.refs_5_), channel_id=1, source_target_pairs={{0,1},{1,0},{2,3},{3,2},{4,5},{5,4},{6,7},{7,6},{8,9},{9,8},{10,11... | collective-permute-start | bytes 3538952 | tf_op jit(solution)/shard_map/ppermute | solution.py:679
  107.5 28.2 %collective-permute-start.22 = (f32[768,384]{1,0:T(8,128)}, f32[768,384]{1,0:T(8,128)}, u32[]{:S(2)}, u32[]{:S(2)}) collective-permute-start(f32[768,384]{1,0:T(8,128)} %get-tuple-element.252.refs_7_.refs_5_), channel_id=1, source_target_pairs={{0,2},{1,3},{2,0},{3,1},{4,6},{5,7},{6,4},{7,5},{8,10},{9,11},{10,... | collective-permute-start | bytes 3538952 | tf_op jit(solution)/shard_map/ppermute | solution.py:679
  135.8 12.1 %collective-permute-start.23 = (f32[768,384]{1,0:T(8,128)}, f32[768,384]{1,0:T(8,128)}, u32[]{:S(2)}, u32[]{:S(2)}) collective-permute-start(f32[768,384]{1,0:T(8,128)} %collective-permute-done.22.refs_9_), channel_id=1, source_target_pairs={{0,1},{1,0},{2,3},{3,2},{4,5},{5,4},{6,7},{7,6},{8,9},{9,8},{10,11... | collective-permute-start | bytes 3538952 | tf_op jit(solution)/shard_map/ppermute | solution.py:679
  142.6 34.5 %all-to-all-start = ((f32[8,48,192]{2,1,0:T(8,128)}), f32[8,48,192]{2,1,0:T(8,128)S(1)}, u32[]{:S(2)}, u32[]{:S(2)}) async-start(f32[8,48,192]{2,1,0:T(8,128)} %bitcast.8), calls=%async_computation | async-start | bytes 786432 | tf_op jit(solution)/shard_map/all_to_all | solution.py:913
  182.5 31.0 %collective-permute-start.25 = (f32[128,768]{1,0:T(8,128)S(1)}, f32[128,768]{1,0:T(8,128)S(1)}, u32[]{:S(2)}, u32[]{:S(2)}) collective-permute-start(f32[128,768]{1,0:T(8,128)S(1)} %dynamic-slice_add_fusion.1), channel_id=1, source_target_pairs={{0,2},{1,3},{2,0},{3,1},{4,6},{5,7},{6,4},{7,5},{8,10},{9,11},{10,... | collective-permute-start | bytes 1179656 | tf_op jit(solution)/shard_map/ppermute | solution.py:679
  219.4 35.5 %all-to-all-start.1 = ((f32[8,48,192]{2,1,0:T(8,128)}), f32[8,48,192]{2,1,0:T(8,128)S(1)}, u32[]{:S(2)}, u32[]{:S(2)}) async-start(f32[8,48,192]{2,1,0:T(8,128)} %bitcast.12), calls=%async_computation.1 | async-start | bytes 786432 | tf_op jit(solution)/shard_map/all_to_all | solution.py:913
  256.7 14.2 %collective-permute-start.30 = (f32[768,768]{1,0:T(8,128)}, f32[768,768]{1,0:T(8,128)}, u32[]{:S(2)}, u32[]{:S(2)}) collective-permute-start(f32[768,768]{1,0:T(8,128)} %get-tuple-element.309.mt), channel_id=1, source_target_pairs={{0,1},{1,0},{2,3},{3,2},{4,5},{5,4},{6,7},{7,6},{8,9},{9,8},{10,11... | collective-permute-start | bytes 7077896 | tf_op jit(solution)/shard_map/ppermute | solution.py:679
  308.3 13.9 %collective-permute-start.33 = (f32[768,768]{1,0:T(8,128)}, f32[768,768]{1,0:T(8,128)}, u32[]{:S(2)}, u32[]{:S(2)}) collective-permute-start(f32[768,768]{1,0:T(8,128)} %fusion.68), channel_id=1, source_target_pairs={{0,1},{1,0},{2,3},{3,2},{4,5},{5,4},{6,7},{7,6},{8,9},{9,8},{10,11... | collective-permute-start | bytes 7077896 | tf_op jit(solution)/shard_map/ppermute | solution.py:679
  314.5 15.7 %collective-permute-start.31 = (f32[768,768]{1,0:T(8,128)}, f32[768,768]{1,0:T(8,128)}, u32[]{:S(2)}, u32[]{:S(2)}) collective-permute-start(f32[768,768]{1,0:T(8,128)} %fusion.67), channel_id=1, source_target_pairs={{0,1},{1,0},{2,3},{3,2},{4,5},{5,4},{6,7},{7,6},{8,9},{9,8},{10,11... | collective-permute-start | bytes 7077896 | tf_op jit(solution)/shard_map/ppermute | solution.py:679
  316.2 24.3 %collective-permute-start.37 = (f32[768,384]{1,0:T(8,128)S(1)}, f32[768,384]{1,0:T(8,128)S(1)}, u32[]{:S(2)}, u32[]{:S(2)}) collective-permute-start(f32[768,384]{1,0:T(8,128)S(1)} %copy-done.35), channel_id=1, source_target_pairs={{0,1},{1,0},{2,3},{3,2},{4,5},{5,4},{6,7},{7,6},{8,9},{9,8},{10,11... | collective-permute-start | bytes 3538952 | tf_op jit(solution)/shard_map/ppermute | solution.py:679
  318.6 21.9 %collective-permute-start.36 = (f32[192,384]{1,0:T(8,128)S(1)}, f32[192,384]{1,0:T(8,128)S(1)}, u32[]{:S(2)}, u32[]{:S(2)}) collective-permute-start(f32[192,384]{1,0:T(8,128)S(1)} %copy-done.42), channel_id=1, source_target_pairs={{0,1},{1,0},{2,3},{3,2},{4,5},{5,4},{6,7},{7,6},{8,9},{9,8},{10,11... | collective-permute-start | bytes 884744 | tf_op jit(solution)/shard_map/ppermute | solution.py:679
  338.0 13.0 %collective-permute-start.35 = (f32[144,768]{1,0:T(8,128)S(1)}, f32[144,768]{1,0:T(8,128)S(1)}, u32[]{:S(2)}, u32[]{:S(2)}) collective-permute-start(f32[144,768]{1,0:T(8,128)S(1)} %fusion.8), channel_id=1, source_target_pairs={{0,4},{8,0},{16,8},{24,16},{28,24},{20,28},{12,20},{4,12},{1,5},{9... | collective-permute-start | bytes 1327112 | tf_op jit(solution)/shard_map/ppermute | solution.py:779
  340.1 11.0 %collective-permute-start.34 = (f32[120,768]{1,0:T(8,128)S(1)}, f32[120,768]{1,0:T(8,128)S(1)}, u32[]{:S(2)}, u32[]{:S(2)}) collective-permute-start(f32[120,768]{1,0:T(8,128)S(1)} %fusion.27), channel_id=1, source_target_pairs={{0,8},{8,16},{16,24},{24,28},{28,20},{20,12},{12,4},{4,0},{1,9},{9... | collective-permute-start | bytes 1105928 | tf_op jit(solution)/shard_map/ppermute | solution.py:779
  352.8 12.5 %collective-permute-start.39 = (f32[144,768]{1,0:T(8,128)}, f32[144,768]{1,0:T(8,128)}, u32[]{:S(2)}, u32[]{:S(2)}) collective-permute-start(f32[144,768]{1,0:T(8,128)} %fusion.10), channel_id=1, source_target_pairs={{0,4},{8,0},{16,8},{24,16},{28,24},{20,28},{12,20},{4,12},{1,5},{9... | collective-permute-start | bytes 1327112 | tf_op jit(solution)/shard_map/ppermute | solution.py:779
  354.3 11.0 %collective-permute-start.38 = (f32[120,768]{1,0:T(8,128)}, f32[120,768]{1,0:T(8,128)}, u32[]{:S(2)}, u32[]{:S(2)}) collective-permute-start(f32[120,768]{1,0:T(8,128)} %fusion.29), channel_id=1, source_target_pairs={{0,8},{8,16},{16,24},{24,28},{28,20},{20,12},{12,4},{4,0},{1,9},{9... | collective-permute-start | bytes 1105928 | tf_op jit(solution)/shard_map/ppermute | solution.py:779
  370.0 11.7 %collective-permute-start.42 = (f32[144,768]{1,0:T(8,128)S(1)}, f32[144,768]{1,0:T(8,128)S(1)}, u32[]{:S(2)}, u32[]{:S(2)}) collective-permute-start(f32[144,768]{1,0:T(8,128)S(1)} %fusion.12), channel_id=1, source_target_pairs={{0,4},{8,0},{16,8},{24,16},{28,24},{20,28},{12,20},{4,12},{1,5},{9... | collective-permute-start | bytes 1327112 | tf_op jit(solution)/shard_map/ppermute | solution.py:779
  383.6 13.8 %collective-permute-start.44 = (f32[144,768]{1,0:T(8,128)}, f32[144,768]{1,0:T(8,128)}, u32[]{:S(2)}, u32[]{:S(2)}) collective-permute-start(f32[144,768]{1,0:T(8,128)} %fusion.14), channel_id=1, source_target_pairs={{0,4},{8,0},{16,8},{24,16},{28,24},{20,28},{12,20},{4,12},{1,5},{9... | collective-permute-start | bytes 1327112 | tf_op jit(solution)/shard_map/ppermute | solution.py:779
  385.1 12.3 %collective-permute-start.43 = (f32[120,768]{1,0:T(8,128)}, f32[120,768]{1,0:T(8,128)}, u32[]{:S(2)}, u32[]{:S(2)}) collective-permute-start(f32[120,768]{1,0:T(8,128)} %fusion.33), channel_id=1, source_target_pairs={{0,8},{8,16},{16,24},{24,28},{28,20},{20,12},{12,4},{4,0},{1,9},{9... | collective-permute-start | bytes 1105928 | tf_op jit(solution)/shard_map/ppermute | solution.py:779
  385.6 31.5 %collective-permute-start.40 = (f32[320,768]{1,0:T(8,128)}, f32[320,768]{1,0:T(8,128)S(1)}, u32[]{:S(2)}, u32[]{:S(2)}) collective-permute-start(f32[320,768]{1,0:T(8,128)} %copy-done.38), channel_id=1, source_target_pairs={{0,1},{1,0},{2,3},{3,2},{4,5},{5,4},{6,7},{7,6},{8,9},{9,8},{10,11... | collective-permute-start | bytes 2949128 | tf_op jit(solution)/shard_map/ppermute | solution.py:679
  400.5 12.6 %collective-permute-start.46 = (f32[144,768]{1,0:T(8,128)S(1)}, f32[144,768]{1,0:T(8,128)S(1)}, u32[]{:S(2)}, u32[]{:S(2)}) collective-permute-start(f32[144,768]{1,0:T(8,128)S(1)} %fusion.16), channel_id=1, source_target_pairs={{0,4},{8,0},{16,8},{24,16},{28,24},{20,28},{12,20},{4,12},{1,5},{9... | collective-permute-start | bytes 1327112 | tf_op jit(solution)/shard_map/ppermute | solution.py:779
  402.1 10.9 %collective-permute-start.45 = (f32[120,768]{1,0:T(8,128)S(1)}, f32[120,768]{1,0:T(8,128)S(1)}, u32[]{:S(2)}, u32[]{:S(2)}) collective-permute-start(f32[120,768]{1,0:T(8,128)S(1)} %fusion.35), channel_id=1, source_target_pairs={{0,8},{8,16},{16,24},{24,28},{28,20},{20,12},{12,4},{4,0},{1,9},{9... | collective-permute-start | bytes 1105928 | tf_op jit(solution)/shard_map/ppermute | solution.py:779
  413.4 11.9 %collective-permute-start.48 = (f32[144,768]{1,0:T(8,128)S(1)}, f32[144,768]{1,0:T(8,128)S(1)}, u32[]{:S(2)}, u32[]{:S(2)}) collective-permute-start(f32[144,768]{1,0:T(8,128)S(1)} %fusion.18), channel_id=1, source_target_pairs={{0,4},{8,0},{16,8},{24,16},{28,24},{20,28},{12,20},{4,12},{1,5},{9... | collective-permute-start | bytes 1327112 | tf_op jit(solution)/shard_map/ppermute | solution.py:779
  417.1 12.3 %collective-permute-start.52 = (f32[320,768]{1,0:T(8,128)S(1)}, f32[320,768]{1,0:T(8,128)S(1)}, u32[]{:S(2)}, u32[]{:S(2)}) collective-permute-start(f32[320,768]{1,0:T(8,128)S(1)} %get-tuple-element.397), channel_id=1, source_target_pairs={{0,1},{1,0},{2,3},{3,2},{4,5},{5,4},{6,7},{7,6},{8,9},{9,8},{10,11... | collective-permute-start | bytes 2949128 | tf_op jit(solution)/shard_map/ppermute | solution.py:679
  417.3 24.3 %collective-permute-start.51 = (f32[320,768]{1,0:T(8,128)S(1)}, f32[320,768]{1,0:T(8,128)}, u32[]{:S(2)}, u32[]{:S(2)}) collective-permute-start(f32[320,768]{1,0:T(8,128)S(1)} %add.506), channel_id=1, source_target_pairs={{0,2},{1,3},{2,0},{3,1},{4,6},{5,7},{6,4},{7,5},{8,10},{9,11},{10,... | collective-permute-start | bytes 2949128 | tf_op jit(solution)/shard_map/ppermute | solution.py:679
  425.7 16.5 %collective-permute-start.50 = (f32[144,768]{1,0:T(8,128)S(1)}, f32[144,768]{1,0:T(8,128)S(1)}, u32[]{:S(2)}, u32[]{:S(2)}) collective-permute-start(f32[144,768]{1,0:T(8,128)S(1)} %fusion.20), channel_id=1, source_target_pairs={{0,4},{8,0},{16,8},{24,16},{28,24},{20,28},{12,20},{4,12},{1,5},{9... | collective-permute-start | bytes 1327112 | tf_op jit(solution)/shard_map/ppermute | solution.py:779
  427.2 14.4 %collective-permute-start.49 = (f32[120,768]{1,0:T(8,128)S(1)}, f32[120,768]{1,0:T(8,128)S(1)}, u32[]{:S(2)}, u32[]{:S(2)}) collective-permute-start(f32[120,768]{1,0:T(8,128)S(1)} %fusion.39), channel_id=1, source_target_pairs={{0,8},{8,16},{16,24},{24,28},{28,20},{20,12},{12,4},{4,0},{1,9},{9... | collective-permute-start | bytes 1105928 | tf_op jit(solution)/shard_map/ppermute | solution.py:779
  427.8 19.1 %collective-permute-start.77 = (f32[160,768]{1,0:T(8,128)S(1)}, f32[160,768]{1,0:T(8,128)S(1)}, u32[]{:S(2)}, u32[]{:S(2)}) collective-permute-start(f32[160,768]{1,0:T(8,128)S(1)} %constant_dynamic-slice_fusion.5), channel_id=1, source_target_pairs={{0,4},{4,0},{8,12},{12,8},{16,20},{20,16},{24,28},{28,24},{1,5},{5... | collective-permute-start | bytes 1474568 | tf_op jit(solution)/shard_map/ppermute | solution.py:779
  429.4 15.8 %collective-permute-start.78 = (f32[128,768]{1,0:T(8,128)S(1)}, f32[128,768]{1,0:T(8,128)S(1)}, u32[]{:S(2)}, u32[]{:S(2)}) collective-permute-start(f32[128,768]{1,0:T(8,128)S(1)} %constant_dynamic-slice_fusion.4), channel_id=1, source_target_pairs={{0,8},{4,12},{8,0},{12,4},{16,24},{20,28},{24,16},{28,20},{1,9},{5... | collective-permute-start | bytes 1179656 | tf_op jit(solution)/shard_map/ppermute | solution.py:779
  441.6 36.5 %collective-permute-start.58 = (f32[320,768]{1,0:T(8,128)S(1)}, f32[320,768]{1,0:T(8,128)S(1)}, u32[]{:S(2)}, u32[]{:S(2)}) collective-permute-start(f32[320,768]{1,0:T(8,128)S(1)} %get-tuple-element.406), channel_id=1, source_target_pairs={{0,1},{1,0},{2,3},{3,2},{4,5},{5,4},{6,7},{7,6},{8,9},{9,8},{10,11... | collective-permute-start | bytes 2949128 | tf_op jit(solution)/shard_map/ppermute | solution.py:679
  441.6 47.3 %collective-permute-start.57 = (f32[320,768]{1,0:T(8,128)S(1)}, f32[320,768]{1,0:T(8,128)S(1)}, u32[]{:S(2)}, u32[]{:S(2)}) collective-permute-start(f32[320,768]{1,0:T(8,128)S(1)} %add.539), channel_id=1, source_target_pairs={{0,2},{1,3},{2,0},{3,1},{4,6},{5,7},{6,4},{7,5},{8,10},{9,11},{10,... | collective-permute-start | bytes 2949128 | tf_op jit(solution)/shard_map/ppermute | solution.py:679
  459.4 15.9 %collective-permute-start.54 = (f32[144,768]{1,0:T(8,128)S(1)}, f32[144,768]{1,0:T(8,128)S(1)}, u32[]{:S(2)}, u32[]{:S(2)}) collective-permute-start(f32[144,768]{1,0:T(8,128)S(1)} %fusion.7.refs_0_), channel_id=1, source_target_pairs={{0,4},{8,0},{16,8},{24,16},{28,24},{20,28},{12,20},{4,12},{1,5},{9... | collective-permute-start | bytes 1327112 | tf_op jit(solution)/shard_map/ppermute | solution.py:779
  459.5 15.8 %collective-permute-start.53 = (f32[120,768]{1,0:T(8,128)S(1)}, f32[120,768]{1,0:T(8,128)S(1)}, u32[]{:S(2)}, u32[]{:S(2)}) collective-permute-start(f32[120,768]{1,0:T(8,128)S(1)} %fusion.26.refs_0_), channel_id=1, source_target_pairs={{0,8},{8,16},{16,24},{24,28},{28,20},{20,12},{12,4},{4,0},{1,9},{9... | collective-permute-start | bytes 1105928 | tf_op jit(solution)/shard_map/ppermute | solution.py:779
  463.0 12.3 %collective-permute-start.81 = (f32[40,768]{1,0:T(8,128)S(1)}, f32[40,768]{1,0:T(8,128)S(1)}, u32[]{:S(2)}, u32[]{:S(2)}) collective-permute-start(f32[40,768]{1,0:T(8,128)S(1)} %constant_dynamic-slice_fusion.1), channel_id=1, source_target_pairs={{0,16},{4,20},{8,24},{12,28},{16,0},{20,4},{24,8},{28,12},{1,17},{... | collective-permute-start | bytes 368648 | tf_op jit(solution)/shard_map/ppermute | solution.py:779
  475.4 15.0 %collective-permute-start.56 = (f32[144,768]{1,0:T(8,128)S(1)}, f32[144,768]{1,0:T(8,128)S(1)}, u32[]{:S(2)}, u32[]{:S(2)}) collective-permute-start(f32[144,768]{1,0:T(8,128)S(1)} %collective-permute-done.54.refs_1_), channel_id=1, source_target_pairs={{0,4},{8,0},{16,8},{24,16},{28,24},{20,28},{12,20},{4,12},{1,5},{9... | collective-permute-start | bytes 1327112 | tf_op jit(solution)/shard_map/ppermute | solution.py:779
  475.6 14.7 %collective-permute-start.55 = (f32[120,768]{1,0:T(8,128)S(1)}, f32[120,768]{1,0:T(8,128)S(1)}, u32[]{:S(2)}, u32[]{:S(2)}) collective-permute-start(f32[120,768]{1,0:T(8,128)S(1)} %collective-permute-done.53.refs_1_), channel_id=1, source_target_pairs={{0,8},{8,16},{16,24},{24,28},{28,20},{20,12},{12,4},{4,0},{1,9},{9... | collective-permute-start | bytes 1105928 | tf_op jit(solution)/shard_map/ppermute | solution.py:779
  477.5 11.4 %collective-permute-start.83 = (f32[40,768]{1,0:T(8,128)S(1)}, f32[40,768]{1,0:T(8,128)S(1)}, u32[]{:S(2)}, u32[]{:S(2)}) collective-permute-start(f32[40,768]{1,0:T(8,128)S(1)} %dynamic-slice_add_fusion.5), channel_id=1, source_target_pairs={{0,16},{4,20},{8,24},{12,28},{16,0},{20,4},{24,8},{28,12},{1,17},{... | collective-permute-start | bytes 368648 | tf_op jit(solution)/shard_map/ppermute | solution.py:779
  484.2 30.2 %collective-permute-start.69 = (f32[7,768]{1,0:T(8,128)S(1)}, f32[7,768]{1,0:T(8,128)S(1)}, u32[]{:S(2)}, u32[]{:S(2)}) collective-permute-start(f32[7,768]{1,0:T(8,128)S(1)} %pad_maximum_fusion.12), channel_id=1, source_target_pairs={{0,1},{1,0},{2,3},{3,2},{4,5},{5,4},{6,7},{7,6},{8,9},{9,8},{10,11... | collective-permute-start | bytes 64520 | tf_op jit(solution)/shard_map/ppermute | solution.py:679
  488.9 47.3 %collective-permute-start.64 = (f32[320,768]{1,0:T(8,128)S(1)}, f32[320,768]{1,0:T(8,128)S(1)}, u32[]{:S(2)}, u32[]{:S(2)}) collective-permute-start(f32[320,768]{1,0:T(8,128)S(1)} %maximum_add_fusion.refs_1_), channel_id=1, source_target_pairs={{0,1},{1,0},{2,3},{3,2},{4,5},{5,4},{6,7},{7,6},{8,9},{9,8},{10,11... | collective-permute-start | bytes 2949128 | tf_op jit(solution)/shard_map/ppermute | solution.py:679
  488.9 24.2 %collective-permute-start.63 = (f32[320,768]{1,0:T(8,128)S(1)}, f32[320,768]{1,0:T(8,128)S(1)}, u32[]{:S(2)}, u32[]{:S(2)}) collective-permute-start(f32[320,768]{1,0:T(8,128)S(1)} %add.548), channel_id=1, source_target_pairs={{0,2},{1,3},{2,0},{3,1},{4,6},{5,7},{6,4},{7,5},{8,10},{9,11},{10,... | collective-permute-start | bytes 2949128 | tf_op jit(solution)/shard_map/ppermute | solution.py:679
  490.4 12.4 %collective-permute-start.60 = (f32[144,768]{1,0:T(8,128)S(1)}, f32[144,768]{1,0:T(8,128)S(1)}, u32[]{:S(2)}, u32[]{:S(2)}) collective-permute-start(f32[144,768]{1,0:T(8,128)S(1)} %collective-permute-done.56.refs_2_), channel_id=1, source_target_pairs={{0,4},{8,0},{16,8},{24,16},{28,24},{20,28},{12,20},{4,12},{1,5},{9... | collective-permute-start | bytes 1327112 | tf_op jit(solution)/shard_map/ppermute | solution.py:779
  490.4 10.8 %collective-permute-start.59 = (f32[120,768]{1,0:T(8,128)S(1)}, f32[120,768]{1,0:T(8,128)S(1)}, u32[]{:S(2)}, u32[]{:S(2)}) collective-permute-start(f32[120,768]{1,0:T(8,128)S(1)} %collective-permute-done.55.refs_2_), channel_id=1, source_target_pairs={{0,8},{8,16},{16,24},{24,28},{28,20},{20,12},{12,4},{4,0},{1,9},{9... | collective-permute-start | bytes 1105928 | tf_op jit(solution)/shard_map/ppermute | solution.py:779
  502.7 11.5 %collective-permute-start.62 = (f32[144,768]{1,0:T(8,128)S(1)}, f32[144,768]{1,0:T(8,128)S(1)}, u32[]{:S(2)}, u32[]{:S(2)}) collective-permute-start(f32[144,768]{1,0:T(8,128)S(1)} %collective-permute-done.60.refs_3_), channel_id=1, source_target_pairs={{0,4},{8,0},{16,8},{24,16},{28,24},{20,28},{12,20},{4,12},{1,5},{9... | collective-permute-start | bytes 1327112 | tf_op jit(solution)/shard_map/ppermute | solution.py:779
  513.0 11.8 %collective-permute-start.85 = (f32[80,768]{1,0:T(8,128)S(1)}, f32[80,768]{1,0:T(8,128)S(1)}, u32[]{:S(2)}, u32[]{:S(2)}) collective-permute-start(f32[80,768]{1,0:T(8,128)S(1)} %pad_maximum_fusion.10), channel_id=1, source_target_pairs={{0,8},{4,12},{8,0},{12,4},{16,24},{20,28},{24,16},{28,20},{1,9},{5... | collective-permute-start | bytes 737288 | tf_op jit(solution)/shard_map/ppermute | solution.py:779
  513.1 11.8 %collective-permute-start.86 = (f32[64,768]{1,0:T(8,128)S(1)}, f32[64,768]{1,0:T(8,128)S(1)}, u32[]{:S(2)}, u32[]{:S(2)}) collective-permute-start(f32[64,768]{1,0:T(8,128)S(1)} %pad_maximum_fusion.11), channel_id=1, source_target_pairs={{0,16},{4,20},{8,24},{12,28},{16,0},{20,4},{24,8},{28,12},{1,17},{... | collective-permute-start | bytes 589832 | tf_op jit(solution)/shard_map/ppermute | solution.py:779
  514.2 23.8 %collective-permute-start.65 = (f32[320,768]{1,0:T(8,128)S(1)}, f32[320,768]{1,0:T(8,128)}, u32[]{:S(2)}, u32[]{:S(2)}) collective-permute-start(f32[320,768]{1,0:T(8,128)S(1)} %maximum_add_fusion.1.refs_2_), channel_id=1, source_target_pairs={{0,1},{1,0},{2,3},{3,2},{4,5},{5,4},{6,7},{7,6},{8,9},{9,8},{10,11... | collective-permute-start | bytes 2949128 | tf_op jit(solution)/shard_map/ppermute | solution.py:679
  514.4 21.7 %collective-permute-start.68 = (f32[320,768]{1,0:T(8,128)S(1)}, f32[320,768]{1,0:T(8,128)S(1)}, u32[]{:S(2)}, u32[]{:S(2)}) collective-permute-start(f32[320,768]{1,0:T(8,128)S(1)} %maximum_add_fusion.2.refs_3_), channel_id=1, source_target_pairs={{0,1},{1,0},{2,3},{3,2},{4,5},{5,4},{6,7},{7,6},{8,9},{9,8},{10,11... | collective-permute-start | bytes 2949128 | tf_op jit(solution)/shard_map/ppermute | solution.py:679
  525.1 11.0 %collective-permute-start.67 = (f32[144,768]{1,0:T(8,128)S(1)}, f32[144,768]{1,0:T(8,128)S(1)}, u32[]{:S(2)}, u32[]{:S(2)}) collective-permute-start(f32[144,768]{1,0:T(8,128)S(1)} %collective-permute-done.62.refs_4_), channel_id=1, source_target_pairs={{0,4},{8,0},{16,8},{24,16},{28,24},{20,28},{12,20},{4,12},{1,5},{9... | collective-permute-start | bytes 1327112 | tf_op jit(solution)/shard_map/ppermute | solution.py:779
  533.6 32.4 %collective-permute-start.87 = (f32[160,768]{1,0:T(8,128)}, f32[160,768]{1,0:T(8,128)}, u32[]{:S(2)}, u32[]{:S(2)}) collective-permute-start(f32[160,768]{1,0:T(8,128)} %pad_maximum_fusion.3), channel_id=1, source_target_pairs={{0,4},{4,0},{8,12},{12,8},{16,20},{20,16},{24,28},{28,24},{1,5},{5... | collective-permute-start | bytes 1474568 | tf_op jit(solution)/shard_map/ppermute | solution.py:779
  547.0 19.0 %collective-permute-start.71 = (f32[144,768]{1,0:T(8,128)}, f32[144,768]{1,0:T(8,128)S(1)}, u32[]{:S(2)}, u32[]{:S(2)}) collective-permute-start(f32[144,768]{1,0:T(8,128)} %copy-done.110), channel_id=1, source_target_pairs={{0,4},{8,0},{16,8},{24,16},{28,24},{20,28},{12,20},{4,12},{1,5},{9... | collective-permute-start | bytes 1327112 | tf_op jit(solution)/shard_map/ppermute | solution.py:779
  548.7 17.2 %collective-permute-start.88 = (f32[128,768]{1,0:T(8,128)}, f32[128,768]{1,0:T(8,128)S(1)}, u32[]{:S(2)}, u32[]{:S(2)}) collective-permute-start(f32[128,768]{1,0:T(8,128)} %pad_maximum_fusion.6), channel_id=1, source_target_pairs={{0,8},{4,12},{8,0},{12,4},{16,24},{20,28},{24,16},{28,20},{1,9},{5... | collective-permute-start | bytes 1179656 | tf_op jit(solution)/shard_map/ppermute | solution.py:779
  549.0 16.9 %collective-permute-start.70 = (f32[120,768]{1,0:T(8,128)}, f32[120,768]{1,0:T(8,128)}, u32[]{:S(2)}, u32[]{:S(2)}) collective-permute-start(f32[120,768]{1,0:T(8,128)} %copy-done.117), channel_id=1, source_target_pairs={{0,8},{8,16},{16,24},{24,28},{28,20},{20,12},{12,4},{4,0},{1,9},{9... | collective-permute-start | bytes 1105928 | tf_op jit(solution)/shard_map/ppermute | solution.py:779
  552.6 13.4 %collective-permute-start.72 = (f32[20,768]{1,0:T(8,128)S(1)}, f32[20,768]{1,0:T(8,128)S(1)}, u32[]{:S(2)}, u32[]{:S(2)}) collective-permute-start(f32[20,768]{1,0:T(8,128)S(1)} %concatenate.66), channel_id=1, source_target_pairs={{0,4},{4,0},{8,12},{12,8},{16,20},{20,16},{24,28},{28,24},{1,5},{5... | collective-permute-start | bytes 184328 | tf_op jit(solution)/shard_map/ppermute | solution.py:779
  566.0 11.0 %collective-permute-start.74 = (f32[144,768]{1,0:T(8,128)S(1)}, f32[144,768]{1,0:T(8,128)S(1)}, u32[]{:S(2)}, u32[]{:S(2)}) collective-permute-start(f32[144,768]{1,0:T(8,128)S(1)} %collective-permute-done.71.refs_6_), channel_id=1, source_target_pairs={{0,4},{8,0},{16,8},{24,16},{28,24},{20,28},{12,20},{4,12},{1,5},{9... | collective-permute-start | bytes 1327112 | tf_op jit(solution)/shard_map/ppermute | solution.py:779
  577.8 11.8 %collective-permute-start.76 = (f32[20,768]{1,0:T(8,128)}, f32[20,768]{1,0:T(8,128)}, u32[]{:S(2)}, u32[]{:S(2)}) collective-permute-start(f32[20,768]{1,0:T(8,128)} %add.558), channel_id=1, source_target_pairs={{0,16},{4,20},{8,24},{12,28},{16,0},{20,4},{24,8},{28,12},{1,17},{... | collective-permute-start | bytes 184328 | tf_op jit(solution)/shard_map/ppermute | solution.py:779
  (176 other events, 1543.9 us)
